TPU v7x, 512 devices: a whole 4x8x8 slice. The times are simulated.
512 devices in a mesh: ctx: 64 (over y, x, core), pp: 8 (over z).
Axes of the slice: x: 4, y: 8, z: 8, core: 2. Of those that a mesh axis runs over, the one named last changes fastest.
Arguments:
- inputs: bfloat16 [8, 2, 4096, 2048], P('pp', None, 'ctx'), may hold values from -6 to 6
- saved_keys: bfloat16 [8, 2, 4096, 512], P('pp', None, 'ctx'), may hold values from -6 to 6
- saved_values: bfloat16 [8, 2, 4096, 512], P('pp', None, 'ctx'), may hold values from -5 to 5
- query_gain: float32 [8, 2048], P('pp'), may hold values from 0.25 to 1.75
- first_grads: bfloat16 [8, 4096, 2048], P('pp', 'ctx'), may hold values from -5 to 5
- head_grads: bfloat16 [1, 4096, 2048], P(None, 'ctx'), may hold values from -5 to 5
- window: int32 [8, 4], P('pp'), may hold values from 1 to 7, as said below
- stride: int32 [8, 4], P('pp'), may hold values from 16 to 32, as said below
Outputs:
- grads_out: bfloat16 [8, 2, 4096, 2048], P('pp', None, 'ctx')
- key_grads: bfloat16 [8, 2, 4096, 512], P('pp', None, 'ctx')
- value_grads: bfloat16 [8, 2, 4096, 512], P('pp', None, 'ctx')
Inputs may be any that keep to these rules, and one draw needn't show every extreme that they name: `window`: every entry is 1 to 7; some entry equals 7 and some equals 1. `stride`: every entry is 16 or 32; both occur.
All inputs are finite; a program needn't handle non-finite values.
Results may differ from a plain program's by a relative error of at most 0.014.
Values may be sent and summed in bfloat16 or wider, within the bound.
No kernel may reach another device: no remote copies, remote signals or barrier semaphores. Data moves between devices by JAX's collectives and lax.ppermute only.
A program may use at most 64 MiB of HBM per device.

v0:
```python
import jax
import jax.numpy as jnp
from jax import lax
from jax.sharding import PartitionSpec as P

BLK = 64
WIN = 7
STRIDE = 16
HEAD_DIM = 128


def shifted(block, axis, distance):
    devices = range(lax.axis_size(axis))
    route = [(i - distance, i) for i in devices if i - distance in devices]
    return lax.ppermute(block, axis, route)


def broadcast(array, axis, root):
    mine = lax.axis_index(axis) == root
    return lax.psum(jnp.where(mine, array, jnp.zeros_like(array)), axis)


def block_allowed(block, window, stride, summary_count):
    row_ids = jnp.arange(BLK, dtype=jnp.int32)
    query_pos = block * BLK + row_ids
    col_ids = jnp.arange(WIN * BLK, dtype=jnp.int32)
    key_block = block - WIN + 1 + col_ids // BLK
    key_pos = (block - WIN + 1) * BLK + col_ids
    local_ok = (key_block[None, None, :] >= 0) & (
        key_pos[None, None, :] <= query_pos[None, :, None]
    )
    local_ok = local_ok & ((block - key_block)[None, None, :] < window[:, None, None])
    strided_block = STRIDE * (jnp.arange(summary_count * BLK, dtype=jnp.int32) // BLK)
    strided_ok = strided_block[None, None, :] % stride[:, None, None] == 0
    strided_ok = strided_ok & (strided_block[None, None, :] <= block - window[:, None, None])
    heads = window.shape[0]
    strided_ok = jnp.broadcast_to(strided_ok, (heads, BLK, summary_count * BLK))
    return jnp.concatenate([local_ok, strided_ok], axis=2)


def head_backward(operands):
    query_h, key_h, value_h, grad_h, allowed_h = operands
    scale = HEAD_DIM ** (-0.5)
    group_size = query_h.shape[0] // allowed_h.shape[0]
    allowed_rows = jnp.tile(allowed_h, (group_size, 1))
    contract = (((1,), (1,)), ((), ()))
    scores = lax.dot_general(query_h, key_h, contract, preferred_element_type=jnp.float32) * scale
    scores = jnp.where(allowed_rows, scores, jnp.float32(-1e30))
    row_peak = jnp.max(scores, axis=1, keepdims=True)
    weights = jnp.exp(scores - row_peak)
    probs = weights / jnp.sum(weights, axis=1, keepdims=True)
    grad_prob = lax.dot_general(grad_h, value_h, contract, preferred_element_type=jnp.float32)
    row_delta = jnp.sum(probs * grad_prob, axis=1, keepdims=True)
    dscore = (probs * (grad_prob - row_delta) * scale).astype(jnp.bfloat16)
    probs_round = probs.astype(jnp.bfloat16)
    across = (((0,), (0,)), ((), ()))
    dquery = jnp.dot(dscore, key_h, preferred_element_type=jnp.float32)
    key_grad = lax.dot_general(dscore, query_h, across, preferred_element_type=jnp.float32)
    value_grad = lax.dot_general(probs_round, grad_h, across, preferred_element_type=jnp.float32)
    return (dquery, key_grad, value_grad)


def local_backward(inputs, gain, kv_all, grad_out, allowed):
    kv_heads = allowed.shape[0]
    rows, feat = inputs.shape
    group_size = feat // (kv_heads * HEAD_DIM)
    kv_width = kv_heads * HEAD_DIM
    key_count = kv_all.shape[0]
    queries = (inputs.astype(jnp.float32) * gain).astype(jnp.bfloat16)

    def regroup(matrix):
        shaped = matrix.reshape(rows, kv_heads, group_size, HEAD_DIM).transpose(1, 2, 0, 3)
        return shaped.reshape(kv_heads, group_size * rows, HEAD_DIM)

    key_heads = kv_all[:, :kv_width].reshape(key_count, kv_heads, HEAD_DIM).transpose(1, 0, 2)
    value_heads = kv_all[:, kv_width:].reshape(key_count, kv_heads, HEAD_DIM).transpose(1, 0, 2)
    dquery, key_grad, value_grad = lax.map(
        head_backward, (regroup(queries), key_heads, value_heads, regroup(grad_out), allowed)
    )
    dquery = (
        dquery.reshape(kv_heads, group_size, rows, HEAD_DIM)
        .transpose(2, 0, 1, 3)
        .reshape(rows, feat)
    )
    result = (grad_out.astype(jnp.float32) + gain * dquery).astype(jnp.bfloat16)
    key_grad = key_grad.transpose(1, 0, 2).reshape(key_count, kv_width)
    value_grad = value_grad.transpose(1, 0, 2).reshape(key_count, kv_width)
    return (result, jnp.concatenate([key_grad, value_grad], axis=1))


def pick_owned(combined, block_index):
    slot = jnp.minimum(block_index // STRIDE, combined.shape[0] - 1)
    owned_row = lax.dynamic_index_in_dim(combined, slot, 0, keepdims=False)
    return jnp.where(block_index % STRIDE == 0, owned_row, jnp.float32(0.0))


def body(inputs, saved_keys, saved_values, query_gain, first_grads, head_grads, window, stride):
    block_index = lax.axis_index("ctx")
    section_index = lax.axis_index("pp")
    section_count = lax.axis_size("pp")
    summary_count = lax.axis_size("ctx") // STRIDE
    tick_count = inputs.shape[1]
    kv_width = saved_keys.shape[-1]
    paired = jnp.concatenate([saved_keys[0], saved_values[0]], axis=-1)
    behind = [paired]
    for offset in range(1, WIN):
        behind.append(shifted(paired, "ctx", offset))
    nearby = jnp.stack(behind[::-1], axis=1)
    nearby = nearby.reshape(tick_count, WIN * BLK, 2 * kv_width)
    owners = [
        broadcast(paired, "ctx", owner_index * STRIDE) for owner_index in range(summary_count)
    ]
    summary = jnp.stack(owners, axis=1).reshape(tick_count, summary_count * BLK, 2 * kv_width)
    allowed = block_allowed(block_index, window[0], stride[0], summary_count)
    results = []
    finished = []
    previous = first_grads[0]
    for step_index in range(tick_count):
        if step_index == 0:
            grad_out = first_grads[0]
        else:
            incoming = shifted(previous, "pp", -1)
            grad_out = jnp.where(
                section_index == section_count - 1, head_grads[step_index - 1], incoming
            )
        kv_all = jnp.concatenate([nearby[step_index], summary[step_index]], axis=0)
        result, local_part = local_backward(
            inputs[0, step_index], query_gain[0], kv_all, grad_out, allowed
        )
        own_total = local_part[(WIN - 1) * BLK : WIN * BLK]
        for offset in range(1, WIN):
            start = (WIN - 1 - offset) * BLK
            piece = local_part[start : start + BLK].astype(jnp.bfloat16)
            own_total = own_total + shifted(piece, "ctx", -offset).astype(jnp.float32)
        summary_part = local_part[WIN * BLK :].reshape(summary_count, BLK, 2 * kv_width)
        combined = lax.psum(summary_part, "ctx")
        finished.append(own_total + pick_owned(combined, block_index))
        results.append(result)
        previous = result
    totals = jnp.stack(finished, axis=0)
    grads_out = jnp.stack(results, axis=0)[None]
    key_grads = totals[:, :, :kv_width].astype(jnp.bfloat16)[None]
    value_grads = totals[:, :, kv_width:].astype(jnp.bfloat16)[None]
    return (grads_out, key_grads, value_grads)


def solution(mesh):
    in_specs = (
        P("pp", None, "ctx", None),
        P("pp", None, "ctx", None),
        P("pp", None, "ctx", None),
        P("pp", None),
        P("pp", "ctx", None),
        P(None, "ctx", None),
        P("pp", None),
        P("pp", None),
    )
    out_specs = (P("pp", None, "ctx", None), P("pp", None, "ctx", None), P("pp", None, "ctx", None))
    return jax.shard_map(body, mesh=mesh, in_specs=in_specs, out_specs=out_specs, check_vma=False)
```

profile of v0, /device:TPU:25, one launch (start us, length us, event | category | flops | bytes accessed | tf_op | source)
XLA Modules:
  0.0 532.1 jit_solution(817379970787281829)
XLA Ops:
  7.3 2.2 select_bitcast_fusion
  9.4 4.4 collective-permute-start
  13.8 5.5 %collective-permute-start.1 = (bf16[2,64,1024]{2,1,0:T(8,128)(2,1)}, bf16[2,64,1024]{2,1,0:T(8,128)(2,1)}, u32[]{:S(2)}, u32[]{:S(2)}) collective-permute-start(bf16[2,64,1024]{2,1,0:T(8,128)(2,1)} %get-tuple-element.203), channel_id=1, source_target_pairs={{0,40},{8,48},{16,56},{24,64},{32,72},{40,80},{48,88},{56,96},{64,... | collective-permute-start | bytes 786440 | tf_op jit(solution)/shard_map/ppermute | solution.py:15
  19.3 2.2 collective-permute-start.2
  21.6 4.3 collective-permute-start.3
  25.9 2.5 collective-permute-start.4
  31.5 3.4 collective-permute-start.5
  39.2 5.2 collective-permute-done.4
  45.7 180.7 %all-reduce.7.cloned.1.call-done = (bf16[2,1,64,1024]{3,2,0,1:T(8,128)(2,1)}, bf16[2,1,64,1024]{3,2,0,1:T(8,128)(2,1)}, bf16[2,1,64,1024]{3,2,0,1:T(8,128)(2,1)}, bf16[2,1,64,1024]{3,2,0,1:T(8,128)(2,1)}) async-done(((bf16[2,1,64,1024]{3,2,0,1:T(8,128)(2,1)}, bf16[2,1,64,1024]{3,2,0,1:T(8,128)(2,1)}, bf16[2,1,64,1024]{3,2,0,1:T(8,128)(2,1)}, bf16[2,1,64,1024]{3,2,0,1:T(8,128)(2,1)}), ...) | async-done | bytes 1048592 | tf_op jit(solution)/shard_map/psum | solution.py:20
  236.3 17.9 %while.28 = (s32[]{:T(128)}, f32[4,256,128]{2,1,0:T(8,128)}, f32[4,704,128]{2,1,0:T(8,128)S(1)}, f32[4,704,128]{2,1,0:T(8,128)}, pred[4,64,704]{2,1,0:T(8,128)(4...) while((s32[]{:T(128)}, f32[4,256,128]{2,1,0:T(8,128)}, ...), condition=%wide.region_8.9_spmd, body=%wide.region_4.8_spmd.sunk | while | flops 233929984 | bytes 8654961 | solution.py:77
  264.0 2.4 reshape.411
  270.8 2.4 reshape.414
  286.1 28.3 %while.29 = (s32[]{:T(128)}, f32[4,256,128]{2,1,0:T(8,128)}, f32[4,704,128]{2,1,0:T(8,128)}, f32[4,704,128]{2,1,0:T(8,128)}, pred[4,64,704]{2,1,0:T(8,128)(4,1)S...) while((s32[]{:T(128)}, f32[4,256,128]{2,1,0:T(8,128)}, ...), condition=%wide.region_13.14_spmd, body=%wide.region_9.13_spmd.sunk | while | flops 233929984 | bytes 9703565 | solution.py:77
  323.2 3.2 convert.24
  332.9 5.8 %collective-permute-start.17 = (bf16[64,1024]{1,0:T(8,128)(2,1)S(1)}, bf16[64,1024]{1,0:T(8,128)(2,1)S(1)}, u32[]{:S(2)}, u32[]{:S(2)}) collective-permute-start(bf16[64,1024]{1,0:T(8,128)(2,1)S(1)} %get-tuple-element.185), channel_id=1, source_target_pairs={{40,0},{48,8},{56,16},{64,24},{72,32},{80,40},{88,48},{96,56},{104... | collective-permute-start | bytes 393224 | tf_op jit(solution)/shard_map/ppermute | solution.py:15
  338.8 4.6 collective-permute-start.16
  343.4 2.5 collective-permute-start.15
  345.9 3.0 collective-permute-start.14
  349.0 3.0 collective-permute-start.13
  352.8 2.7 collective-permute-start.11
  355.6 2.5 collective-permute-start.10
  358.1 2.8 collective-permute-start.9
  363.5 2.3 collective-permute-start.7
  365.8 155.9 %all-reduce.5.cloned.1.call-done = (f32[4,64,1024]{2,1,0:T(8,128)}, f32[4,64,1024]{2,1,0:T(8,128)}) async-done(((f32[4,64,1024]{2,1,0:T(8,128)}, f32[4,64,1024]{2,1,0:T(8,128)}), (f32[4,64,1024]{2,1,0:T(8,128)}, f32[4,64,1024]{2,1,0:T(8,128)})) %all-reduce.5.cloned.1.call-update) | async-done | bytes 2097168 | tf_op jit(solution)/shard_map/psum | solution.py:136
  (241 shorter events, 113.5 us)
Async XLA Ops:
  7.2 21.4 %copy-start.27 = (s32[1,4]{1,0:T(1,128)S(1)}, s32[1,4]{1,0:T(1,128)}, u32[]{:S(2)}) copy-start(s32[1,4]{1,0:T(1,128)} %param.18) | copy-start | bytes 52
  7.2 21.5 %copy-start.15 = (bf16[1,2,64,2048]{3,2,1,0:T(8,128)(2,1)S(1)}, bf16[1,2,64,2048]{3,2,1,0:T(8,128)(2,1)}, u32[]{:S(2)}) copy-start(bf16[1,2,64,2048]{3,2,1,0:T(8,128)(2,1)} %param.12) | copy-start | bytes 1572868
  7.2 219.2 %all-reduce.7.cloned.1.call-start = ((), (), s32[]{:S(2)}) async-start(), calls=%async_computation.1 | async-start | bytes 2097152 | tf_op jit(solution)/shard_map/psum | solution.py:20
  9.4 22.1 %collective-permute-start = (bf16[2,64,1024]{2,1,0:T(8,128)(2,1)}, bf16[2,64,1024]{2,1,0:T(8,128)(2,1)}, u32[]{:S(2)}, u32[]{:S(2)}) collective-permute-start(bf16[2,64,1024]{2,1,0:T(8,128)(2,1)} %get-tuple-element.203), channel_id=1, source_target_pairs={{0,48},{8,56},{16,64},{24,72},{32,80},{40,88},{48,96},{56,104},{64... | collective-permute-start | bytes 786440 | tf_op jit(solution)/shard_map/ppermute | solution.py:15
  13.8 22.1 %collective-permute-start.1 = (bf16[2,64,1024]{2,1,0:T(8,128)(2,1)}, bf16[2,64,1024]{2,1,0:T(8,128)(2,1)}, u32[]{:S(2)}, u32[]{:S(2)}) collective-permute-start(bf16[2,64,1024]{2,1,0:T(8,128)(2,1)} %get-tuple-element.203), channel_id=1, source_target_pairs={{0,40},{8,48},{16,56},{24,64},{32,72},{40,80},{48,88},{56,96},{64,... | collective-permute-start | bytes 786440 | tf_op jit(solution)/shard_map/ppermute | solution.py:15
  19.3 17.6 %collective-permute-start.2 = (bf16[2,64,1024]{2,1,0:T(8,128)(2,1)}, bf16[2,64,1024]{2,1,0:T(8,128)(2,1)}, u32[]{:S(2)}, u32[]{:S(2)}) collective-permute-start(bf16[2,64,1024]{2,1,0:T(8,128)(2,1)} %get-tuple-element.203), channel_id=1, source_target_pairs={{0,32},{8,40},{16,48},{24,56},{32,64},{40,72},{48,80},{56,88},{64,... | collective-permute-start | bytes 786440 | tf_op jit(solution)/shard_map/ppermute | solution.py:15
  21.6 17.6 %collective-permute-start.3 = (bf16[2,64,1024]{2,1,0:T(8,128)(2,1)}, bf16[2,64,1024]{2,1,0:T(8,128)(2,1)S(1)}, u32[]{:S(2)}, u32[]{:S(2)}) collective-permute-start(bf16[2,64,1024]{2,1,0:T(8,128)(2,1)} %get-tuple-element.203), channel_id=1, source_target_pairs={{0,24},{8,32},{16,40},{24,48},{32,56},{40,64},{48,72},{56,80},{64,... | collective-permute-start | bytes 786440 | tf_op jit(solution)/shard_map/ppermute | solution.py:15
  25.9 18.5 %collective-permute-start.4 = (bf16[2,64,1024]{2,1,0:T(8,128)(2,1)}, bf16[2,64,1024]{2,1,0:T(8,128)(2,1)S(1)}, u32[]{:S(2)}, u32[]{:S(2)}) collective-permute-start(bf16[2,64,1024]{2,1,0:T(8,128)(2,1)} %get-tuple-element.203), channel_id=1, source_target_pairs={{0,16},{8,24},{16,32},{24,40},{32,48},{40,56},{48,64},{56,72},{64,... | collective-permute-start | bytes 786440 | tf_op jit(solution)/shard_map/ppermute | solution.py:15
  28.5 493.3 %all-reduce.5.cloned.1.call-start = ((), (), s32[]{:S(2)}) async-start(), calls=%async_computation | async-start | bytes 4194304 | tf_op jit(solution)/shard_map/psum | solution.py:136
  31.5 12.9 %collective-permute-start.5 = (bf16[2,64,1024]{2,1,0:T(8,128)(2,1)}, bf16[2,64,1024]{2,1,0:T(8,128)(2,1)S(1)}, u32[]{:S(2)}, u32[]{:S(2)}) collective-permute-start(bf16[2,64,1024]{2,1,0:T(8,128)(2,1)} %get-tuple-element.203), channel_id=1, source_target_pairs={{0,8},{8,16},{16,24},{24,32},{32,40},{40,48},{48,56},{56,64},{64,7... | collective-permute-start | bytes 786440 | tf_op jit(solution)/shard_map/ppermute | solution.py:15
  269.3 8.3 %collective-permute-start.6 = (bf16[64,2048]{1,0:T(8,128)(2,1)}, bf16[64,2048]{1,0:T(8,128)(2,1)}, u32[]{:S(2)}, u32[]{:S(2)}) collective-permute-start(bf16[64,2048]{1,0:T(8,128)(2,1)} %fusion.60), channel_id=1, source_target_pairs={{1,0},{2,1},{3,2},{4,3},{5,4},{6,5},{7,6},{9,8},{10,9},{11,10},{12... | collective-permute-start | bytes 786440 | tf_op jit(solution)/shard_map/ppermute | solution.py:15
  321.1 24.8 %collective-permute-start.12 = (bf16[64,1024]{1,0:T(8,128)(2,1)}, bf16[64,1024]{1,0:T(8,128)(2,1)S(1)}, u32[]{:S(2)}, u32[]{:S(2)}) collective-permute-start(bf16[64,1024]{1,0:T(8,128)(2,1)} %get-tuple-element.178), channel_id=1, source_target_pairs={{48,0},{56,8},{64,16},{72,24},{80,32},{88,40},{96,48},{104,56},{11... | collective-permute-start | bytes 393224 | tf_op jit(solution)/shard_map/ppermute | solution.py:15
  329.6 22.4 %copy-start.14 = (bf16[1,64,2048]{2,1,0:T(8,128)(2,1)S(1)}, bf16[1,64,2048]{2,1,0:T(8,128)(2,1)}, u32[]{:S(2)}) copy-start(bf16[1,64,2048]{2,1,0:T(8,128)(2,1)} %fusion.58) | copy-start | bytes 786436
  330.9 18.1 %collective-permute-start.18 = (bf16[64,1024]{1,0:T(8,128)(2,1)S(1)}, bf16[64,1024]{1,0:T(8,128)(2,1)S(1)}, u32[]{:S(2)}, u32[]{:S(2)}) collective-permute-start(bf16[64,1024]{1,0:T(8,128)(2,1)S(1)} %get-tuple-element.184), channel_id=1, source_target_pairs={{48,0},{56,8},{64,16},{72,24},{80,32},{88,40},{96,48},{104,56},{11... | collective-permute-start | bytes 393224 | tf_op jit(solution)/shard_map/ppermute | solution.py:15
  332.9 19.9 %collective-permute-start.17 = (bf16[64,1024]{1,0:T(8,128)(2,1)S(1)}, bf16[64,1024]{1,0:T(8,128)(2,1)S(1)}, u32[]{:S(2)}, u32[]{:S(2)}) collective-permute-start(bf16[64,1024]{1,0:T(8,128)(2,1)S(1)} %get-tuple-element.185), channel_id=1, source_target_pairs={{40,0},{48,8},{56,16},{64,24},{72,32},{80,40},{88,48},{96,56},{104... | collective-permute-start | bytes 393224 | tf_op jit(solution)/shard_map/ppermute | solution.py:15
  338.8 16.8 %collective-permute-start.16 = (bf16[64,1024]{1,0:T(8,128)(2,1)S(1)}, bf16[64,1024]{1,0:T(8,128)(2,1)S(1)}, u32[]{:S(2)}, u32[]{:S(2)}) collective-permute-start(bf16[64,1024]{1,0:T(8,128)(2,1)S(1)} %get-tuple-element.186), channel_id=1, source_target_pairs={{32,0},{40,8},{48,16},{56,24},{64,32},{72,40},{80,48},{88,56},{96,... | collective-permute-start | bytes 393224 | tf_op jit(solution)/shard_map/ppermute | solution.py:15
  343.4 14.7 %collective-permute-start.15 = (bf16[64,1024]{1,0:T(8,128)(2,1)S(1)}, bf16[64,1024]{1,0:T(8,128)(2,1)S(1)}, u32[]{:S(2)}, u32[]{:S(2)}) collective-permute-start(bf16[64,1024]{1,0:T(8,128)(2,1)S(1)} %get-tuple-element.187), channel_id=1, source_target_pairs={{24,0},{32,8},{40,16},{48,24},{56,32},{64,40},{72,48},{80,56},{88,... | collective-permute-start | bytes 393224 | tf_op jit(solution)/shard_map/ppermute | solution.py:15
  345.9 15.0 %collective-permute-start.14 = (bf16[64,1024]{1,0:T(8,128)(2,1)S(1)}, bf16[64,1024]{1,0:T(8,128)(2,1)S(1)}, u32[]{:S(2)}, u32[]{:S(2)}) collective-permute-start(bf16[64,1024]{1,0:T(8,128)(2,1)S(1)} %get-tuple-element.188), channel_id=1, source_target_pairs={{16,0},{24,8},{32,16},{40,24},{48,32},{56,40},{64,48},{72,56},{80,... | collective-permute-start | bytes 393224 | tf_op jit(solution)/shard_map/ppermute | solution.py:15
  349.0 13.9 %collective-permute-start.13 = (bf16[64,1024]{1,0:T(8,128)(2,1)S(1)}, bf16[64,1024]{1,0:T(8,128)(2,1)S(1)}, u32[]{:S(2)}, u32[]{:S(2)}) collective-permute-start(bf16[64,1024]{1,0:T(8,128)(2,1)S(1)} %get-tuple-element.183), channel_id=1, source_target_pairs={{8,0},{16,8},{24,16},{32,24},{40,32},{48,40},{56,48},{64,56},{72,6... | collective-permute-start | bytes 393224 | tf_op jit(solution)/shard_map/ppermute | solution.py:15
  352.8 170.3 %collective-permute-start.11 = (bf16[64,1024]{1,0:T(8,128)(2,1)}, bf16[64,1024]{1,0:T(8,128)(2,1)}, u32[]{:S(2)}, u32[]{:S(2)}) collective-permute-start(bf16[64,1024]{1,0:T(8,128)(2,1)} %get-tuple-element.179), channel_id=1, source_target_pairs={{40,0},{48,8},{56,16},{64,24},{72,32},{80,40},{88,48},{96,56},{104... | collective-permute-start | bytes 393224 | tf_op jit(solution)/shard_map/ppermute | solution.py:15
  355.6 167.6 %collective-permute-start.10 = (bf16[64,1024]{1,0:T(8,128)(2,1)}, bf16[64,1024]{1,0:T(8,128)(2,1)}, u32[]{:S(2)}, u32[]{:S(2)}) collective-permute-start(bf16[64,1024]{1,0:T(8,128)(2,1)} %get-tuple-element.180), channel_id=1, source_target_pairs={{32,0},{40,8},{48,16},{56,24},{64,32},{72,40},{80,48},{88,56},{96,... | collective-permute-start | bytes 393224 | tf_op jit(solution)/shard_map/ppermute | solution.py:15
  358.1 165.0 %collective-permute-start.9 = (bf16[64,1024]{1,0:T(8,128)(2,1)}, bf16[64,1024]{1,0:T(8,128)(2,1)}, u32[]{:S(2)}, u32[]{:S(2)}) collective-permute-start(bf16[64,1024]{1,0:T(8,128)(2,1)} %get-tuple-element.181), channel_id=1, source_target_pairs={{24,0},{32,8},{40,16},{48,24},{56,32},{64,40},{72,48},{80,56},{88,... | collective-permute-start | bytes 393224 | tf_op jit(solution)/shard_map/ppermute | solution.py:15
  360.9 162.2 %collective-permute-start.8 = (bf16[64,1024]{1,0:T(8,128)(2,1)}, bf16[64,1024]{1,0:T(8,128)(2,1)}, u32[]{:S(2)}, u32[]{:S(2)}) collective-permute-start(bf16[64,1024]{1,0:T(8,128)(2,1)} %get-tuple-element.182), channel_id=1, source_target_pairs={{16,0},{24,8},{32,16},{40,24},{48,32},{56,40},{64,48},{72,56},{80,... | collective-permute-start | bytes 393224 | tf_op jit(solution)/shard_map/ppermute | solution.py:15
  363.5 159.6 %collective-permute-start.7 = (bf16[64,1024]{1,0:T(8,128)(2,1)S(1)}, bf16[64,1024]{1,0:T(8,128)(2,1)}, u32[]{:S(2)}, u32[]{:S(2)}) collective-permute-start(bf16[64,1024]{1,0:T(8,128)(2,1)S(1)} %get-tuple-element.177), channel_id=1, source_target_pairs={{8,0},{16,8},{24,16},{32,24},{40,32},{48,40},{56,48},{64,56},{72,6... | collective-permute-start | bytes 393224 | tf_op jit(solution)/shard_map/ppermute | solution.py:15
  (29 other events, 112.7 us)
Sparse Core Ops, SparseCore 0:
  28.6 197.7 all-reduce.6
  319.2 202.5 all-reduce.4
where the time goes:
time: 534 us; the launch traced here: 532 us
  waiting for transfers between devices  345 us (65%)
  starting transfers between devices  59.1 us (11%)
  local copies, waits for them, and re-layouts  53 us (10%)
  matrix products  40.5 us (8%)
  other arithmetic  19.6 us (4%)
  between operations  14.8 us (3%)
    psum x1, waiting for transfers between devices, broadcast(): return lax.psum(jnp.where(mine, array, jnp.zeros_like(array)), axis)  181 us
    psum x1, waiting for transfers between devices, body(): combined = lax.psum(summary_part, 'ctx')  156 us
    ppermute x19, starting transfers between devices, shifted(): return lax.ppermute(block, axis, route)  59 us
    unnamed x67, local copies, waits for them, and re-layouts  12.3 us
    dot_general x8, matrix products, head_backward(): dquery = jnp.dot(dscore, key_h, preferred_element_type=jnp.float32)  11.4 us
  transfers between devices with their start and end apart: 21, of which 5 were waited for; matrix products, arithmetic and copies ran while one was open for 5% of the time, Pallas kernels for 0%

commit v1 on v0

v1 whole, which is shorter than its diff:
```python
import functools

import jax
import jax.numpy as jnp
from jax import lax
from jax.experimental import pallas as pl
from jax.experimental.pallas import tpu as pltpu
from jax.sharding import PartitionSpec as P

BLK = 64
WIN = 7
STRIDE = 16
HEAD_DIM = 128
GROUP = 4
HALF_HEADS = 2
HALF_KV = HALF_HEADS * HEAD_DIM
HALF_FEAT = HALF_HEADS * GROUP * HEAD_DIM
SCALE = HEAD_DIM**-0.5
LOG2E = 1.4426950408889634
NEG = -1e30
NT = (((1,), (1,)), ((), ()))
TN = (((0,), (0,)), ((), ()))


def route(array, axis, move):
    size = lax.axis_size(axis)
    pairs = [(i, move(i)) for i in range(size)]
    return lax.ppermute(array, axis, [(a, b) for a, b in pairs if b is not None and 0 <= b < size])


def sibling(array):
    return route(array, "ctx", lambda i: i ^ 1)


def attention_kernel(has_head, *refs):
    meta, gain, q_mine, q_other, g_mine, g_other = refs[:6]
    refs = refs[6:]
    if has_head:
        h_mine, h_other = refs[:2]
        refs = refs[2:]
    pairs, strided = refs[:4], refs[4:8]
    result, own, back1, back2, back3, part0, part1, part2, part3 = refs[8:]
    backs = (own, back1, back2, back3)
    parts = (part0, part1, part2, part3)
    index = meta[0]
    blocks = (index, jnp.bitwise_xor(index, 1))
    group = index // STRIDE
    for h in range(HALF_HEADS):
        window = meta[2 + h]
        stride = meta[4 + h]
        q_rows, g_rows = [], []
        for half, (q_ref, g_ref) in enumerate(((q_mine, g_mine), (q_other, g_other))):
            for j in range(GROUP):
                at = slice((h * GROUP + j) * HEAD_DIM, (h * GROUP + j + 1) * HEAD_DIM)
                q_rows.append((q_ref[:, at].astype(jnp.float32) * gain[:, at]).astype(jnp.bfloat16))
                grad = g_ref[:, at]
                if has_head:
                    top = (h_mine, h_other)[half][:, at]
                    grad = jnp.where(meta[1] == 1, top, grad)
                g_rows.append(grad)
        q = jnp.concatenate(q_rows, axis=0)
        g = jnp.concatenate(g_rows, axis=0)
        k_at = slice(h * HEAD_DIM, (h + 1) * HEAD_DIM)
        v_at = slice(HALF_KV + h * HEAD_DIM, HALF_KV + (h + 1) * HEAD_DIM)
        k = jnp.concatenate([r[:, k_at] for r in pairs + strided], axis=0)
        v = jnp.concatenate([r[:, v_at] for r in pairs + strided], axis=0)
        scores = lax.dot_general(k, q, NT, preferred_element_type=jnp.float32)
        wide = GROUP * BLK
        key_row = lax.broadcasted_iota(jnp.int32, (BLK, wide), 0)
        query_row = lax.broadcasted_iota(jnp.int32, (BLK, wide), 1) % BLK
        rows = []
        for slot in range(12):
            cells = []
            for half in range(2):
                query_block = blocks[half]
                if slot < 8:
                    key_block = blocks[slot % 2] - 2 * (slot // 2)
                    gap = query_block - key_block
                    ok = (key_block >= 0) & (gap >= 0) & (gap < WIN)
                    ok = ok & ((gap < window) | (key_block % stride == 0))
                else:
                    key_block = STRIDE * (group - (slot - 8))
                    ok = (key_block >= 0) & (key_block <= query_block - WIN)
                    ok = ok & (key_block % stride == 0)
                cell = scores[slot * BLK : (slot + 1) * BLK, half * wide : (half + 1) * wide]
                if slot == half:
                    cell = jnp.where(key_row <= query_row, cell, NEG)
                else:
                    cell = jnp.where(ok, cell, NEG)
                cells.append(cell)
            rows.append(jnp.concatenate(cells, axis=1))
        scores = jnp.concatenate(rows, axis=0)
        peak = jnp.max(scores, axis=0, keepdims=True)
        weights = jnp.exp2((scores - peak) * (SCALE * LOG2E))
        probs = weights * (1.0 / jnp.sum(weights, axis=0, keepdims=True))
        grad_prob = lax.dot_general(v, g, NT, preferred_element_type=jnp.float32)
        delta = jnp.sum(probs * grad_prob, axis=0, keepdims=True)
        dscore = (probs * (grad_prob - delta)).astype(jnp.bfloat16)
        dquery = lax.dot_general(dscore, k, TN, preferred_element_type=jnp.float32) * SCALE
        dkey = jnp.dot(dscore, q, preferred_element_type=jnp.float32) * SCALE
        dvalue = jnp.dot(probs.astype(jnp.bfloat16), g, preferred_element_type=jnp.float32)
        for half in range(2):
            for j in range(GROUP):
                at = slice((h * GROUP + j) * HEAD_DIM, (h * GROUP + j + 1) * HEAD_DIM)
                row = (half * GROUP + j) * BLK
                grad = g[row : row + BLK].astype(jnp.float32)
                total = grad + gain[:, at] * dquery[row : row + BLK]
                result[half, :, at] = total.astype(jnp.bfloat16)
        for d in range(4):
            rows_at = slice(2 * BLK * d, 2 * BLK * (d + 1))
            backs[d][:, k_at] = dkey[rows_at].astype(backs[d].dtype)
            backs[d][:, v_at] = dvalue[rows_at].astype(backs[d].dtype)
        for s in range(4):
            rows_at = slice(8 * BLK + BLK * s, 8 * BLK + BLK * (s + 1))
            parts[s][:, k_at] = dkey[rows_at].astype(parts[s].dtype)
            parts[s][:, v_at] = dvalue[rows_at].astype(parts[s].dtype)


def attention(tick, meta, gain, keep, recv, grads, pairs, strided):
    wide = 2 * HALF_KV

    def at(lead, *rest):
        return pl.BlockSpec((None,) + rest, lambda n: (lead, 0, 0))

    whole = pl.BlockSpec(memory_space=pltpu.VMEM)
    args = [meta, gain, keep, recv]
    specs = [
        pl.BlockSpec(memory_space=pltpu.SMEM),
        whole,
        at(tick, BLK, HALF_FEAT),
        at(tick, BLK, HALF_FEAT),
    ]
    if grads is None:
        args += [keep, recv]
        specs += [at(2, BLK, HALF_FEAT), at(2, BLK, HALF_FEAT)]
    else:
        args += [grads, grads, keep, recv]
        specs += [at(0, BLK, HALF_FEAT), at(1, BLK, HALF_FEAT)]
        specs += [at(3, BLK, HALF_FEAT), at(3, BLK, HALF_FEAT)]
    args += list(pairs) + list(strided)
    specs += [at(tick, 2 * BLK, wide)] * 4 + [at(tick, BLK, wide)] * 4
    bf16, f32 = jnp.bfloat16, jnp.float32
    out_shape = [
        jax.ShapeDtypeStruct((2, BLK, HALF_FEAT), bf16),
        jax.ShapeDtypeStruct((2 * BLK, wide), f32),
        jax.ShapeDtypeStruct((2 * BLK, wide), bf16),
        jax.ShapeDtypeStruct((2 * BLK, wide), bf16),
        jax.ShapeDtypeStruct((2 * BLK, wide), bf16),
        jax.ShapeDtypeStruct((BLK, wide), f32),
        jax.ShapeDtypeStruct((BLK, wide), bf16),
        jax.ShapeDtypeStruct((BLK, wide), bf16),
        jax.ShapeDtypeStruct((BLK, wide), bf16),
    ]
    return pl.pallas_call(
        functools.partial(attention_kernel, grads is not None),
        out_shape=out_shape,
        grid=(1,),
        in_specs=specs,
        out_specs=[whole] * len(out_shape),
        compiler_params=pltpu.CompilerParams(vmem_limit_bytes=32 << 20),
        cost_estimate=pl.CostEstimate(
            flops=2 * 5 * 2 * 512 * 768 * 128, bytes_accessed=4 << 20, transcendentals=2 * 512 * 768
        ),
        name="attention",
    )(*args)


def body(inputs, saved_keys, saved_values, query_gain, first_grads, head_grads, window, stride):
    index = lax.axis_index("ctx")
    section = lax.axis_index("pp")
    last = lax.axis_size("pp") - 1
    core = index % 2
    place = (index // 2) % 4
    even_row = (index // 8) % 2 == 0
    ticks = inputs.shape[1]
    f32, bf16 = jnp.float32, jnp.bfloat16

    def halves(array):
        cut = array.shape[-1] // 2
        low, high = array[..., :cut], array[..., cut:]
        return jnp.where(core == 0, low, high), jnp.where(core == 0, high, low)

    key_keep, key_give = halves(saved_keys[0])
    value_keep, value_give = halves(saved_values[0])
    kv_keep = jnp.concatenate([key_keep, value_keep], axis=-1)
    kv_recv = sibling(jnp.concatenate([key_give, value_give], axis=-1))
    stacked = jnp.concatenate([inputs[0], first_grads, head_grads], axis=0)
    keep, give = halves(stacked)
    recv = sibling(give)
    gain = jnp.where(core == 0, query_gain[:, :HALF_FEAT], query_gain[:, HALF_FEAT:])
    heads = jnp.where(core == 0, window[0, :2], window[0, 2:])
    steps = jnp.where(core == 0, stride[0, :2], stride[0, 2:])
    top = jnp.where(section == last, 1, 0)
    meta = jnp.concatenate([jnp.stack([index, top]).astype(jnp.int32), heads, steps])

    pair = jnp.concatenate([kv_keep, kv_recv], axis=1)
    pairs = [pair]
    for d in range(1, 4):
        pairs.append(route(pair, "ctx", lambda i: i + 2 * d))

    def pick(array):
        return jnp.where(core == 0, array[:, :BLK], array[:, BLK:])

    chosen = pick(pairs[0])
    for d in range(1, 4):
        chosen = jnp.where(place == d, pick(pairs[d]), chosen)
    above = route(chosen, "ctx", lambda i: i + 8 if (i // 8) % 2 == 0 else None)
    chosen = jnp.where(even_row, chosen, above)
    strided = [chosen]
    for s in range(1, 4):
        strided.append(route(chosen, "ctx", lambda i: i + STRIDE * s))

    results, totals = [], []
    grads = None
    for tick in range(ticks):
        outs = attention(tick, meta, gain, keep, recv, grads, pairs, strided)
        result, own, backs, parts = outs[0], outs[1], outs[2:5], outs[5:9]
        if tick < ticks - 1:
            grads = route(result, "pp", lambda i: i - 1)
        results.append(result)
        total = parts[0]
        for s in range(1, 4):
            total = total + route(parts[s], "ctx", lambda i: i - STRIDE * s).astype(f32)
        below = route(
            total.astype(bf16), "ctx", lambda i: i - 8 if (i // 8) % 2 == 1 else None
        )
        total = jnp.where(even_row, total + below.astype(f32), 0.0)
        zero = jnp.zeros_like(total)
        spread = jnp.concatenate(
            [jnp.where(core == 0, total, zero), jnp.where(core == 0, zero, total)], axis=0
        )
        final = own + jnp.where(place == 0, spread, 0.0)
        for d in range(1, 4):
            piece = backs[d - 1].astype(f32) + jnp.where(place == d, spread, 0.0)
            final = final + route(piece.astype(bf16), "ctx", lambda i: i - 2 * d).astype(f32)
        totals.append(final.astype(bf16))

    def join(mine, other):
        return jnp.concatenate(
            [jnp.where(core == 0, mine, other), jnp.where(core == 0, other, mine)], axis=-1
        )

    grads_out = [join(r[0], sibling(r[1])) for r in results]
    key_grads, value_grads = [], []
    for total in totals:
        mine, other = total[:BLK], sibling(total[BLK:])
        key_grads.append(join(mine[:, :HALF_KV], other[:, :HALF_KV]))
        value_grads.append(join(mine[:, HALF_KV:], other[:, HALF_KV:]))
    return (
        jnp.stack(grads_out, axis=0)[None],
        jnp.stack(key_grads, axis=0)[None],
        jnp.stack(value_grads, axis=0)[None],
    )


def solution(mesh):
    in_specs = (
        P("pp", None, "ctx", None),
        P("pp", None, "ctx", None),
        P("pp", None, "ctx", None),
        P("pp", None),
        P("pp", "ctx", None),
        P(None, "ctx", None),
        P("pp", None),
        P("pp", None),
    )
    out_specs = (P("pp", None, "ctx", None), P("pp", None, "ctx", None), P("pp", None, "ctx", None))
    return jax.shard_map(body, mesh=mesh, in_specs=in_specs, out_specs=out_specs, check_vma=False)
```

time: 534 us -> 126 us (0.24)
  the two profiles are of different devices: /device:TPU:25 before, /device:TPU:145 now
where the time goes in v1:
time: 126 us; the launch traced here: 125 us
  starting transfers between devices  83 us (66%)
  waiting for transfers between devices  25.4 us (20%)
  Pallas kernels  8 us (6%)
  other arithmetic  6.26 us (5%)
  between operations  1.31 us (1%)
    ppermute x28, starting transfers between devices, route(): lax.ppermute(array, axis, [(a, b) for a, b in pairs if b is not None and...  83 us
    ppermute x28, waiting for transfers between devices, route(): lax.ppermute(array, axis, [(a, b) for a, b in pairs if b is not None and...  25.4 us
    pallas_call x2, Pallas kernels, attention(): pl.pallas_call(functools.partial(attention_kernel, grads is not None), ou...  8 us
  transfers between devices with their start and end apart: 28, of which 8 were waited for; matrix products, arithmetic and copies ran while one was open for 2% of the time, Pallas kernels for 3%

profile of v1, /device:TPU:145, one launch (start us, length us, event | category | flops | bytes accessed | tf_op | source)
XLA Modules:
  0.0 124.7 jit_solution(99718169696427261)
XLA Ops:
  2.6 2.6 %collective-permute-start.1 = (bf16[2,64,512]{2,1,0:T(8,128)(2,1)S(1)}, bf16[2,64,512]{2,1,0:T(8,128)(2,1)S(1)}, u32[]{:S(2)}, u32[]{:S(2)}) collective-permute-start(bf16[2,64,512]{2,1,0:T(8,128)(2,1)S(1)} %pad_maximum_fusion.4), channel_id=1, source_target_pairs={{0,8},{8,0},{16,24},{24,16},{32,40},{40,32},{48,56},{56,48},{64,72... | collective-permute-start | bytes 393224 | tf_op jit(solution)/shard_map/ppermute | solution.py:28
  6.3 4.4 %collective-permute-start.4 = (bf16[2,128,512]{2,1,0:T(8,128)(2,1)S(1)}, bf16[2,128,512]{2,1,0:T(8,128)(2,1)S(1)}, u32[]{:S(2)}, u32[]{:S(2)}) collective-permute-start(bf16[2,128,512]{2,1,0:T(8,128)(2,1)S(1)} %pad_maximum_fusion.1.refs_6_.refs_8_), channel_id=1, source_target_pairs={{0,48},{8,56},{16,64},{24,72},{32,80},{40,88},{48,96},{56,104},{64... | collective-permute-start | bytes 786440 | tf_op jit(solution)/shard_map/ppermute | solution.py:28
  10.7 3.4 %collective-permute-start.3 = (bf16[2,128,512]{2,1,0:T(8,128)(2,1)S(1)}, bf16[2,128,512]{2,1,0:T(8,128)(2,1)S(1)}, u32[]{:S(2)}, u32[]{:S(2)}) collective-permute-start(bf16[2,128,512]{2,1,0:T(8,128)(2,1)S(1)} %pad_maximum_fusion.1.refs_6_.refs_8_), channel_id=1, source_target_pairs={{0,32},{8,40},{16,48},{24,56},{32,64},{40,72},{48,80},{56,88},{64,... | collective-permute-start | bytes 786440 | tf_op jit(solution)/shard_map/ppermute | solution.py:28
  14.1 2.5 %collective-permute-start.2 = (bf16[2,128,512]{2,1,0:T(8,128)(2,1)S(1)}, bf16[2,128,512]{2,1,0:T(8,128)(2,1)S(1)}, u32[]{:S(2)}, u32[]{:S(2)}) collective-permute-start(bf16[2,128,512]{2,1,0:T(8,128)(2,1)S(1)} %pad_maximum_fusion.1.refs_6_.refs_8_), channel_id=1, source_target_pairs={{0,16},{8,24},{16,32},{24,40},{32,48},{40,56},{48,64},{56,72},{64,... | collective-permute-start | bytes 786440 | tf_op jit(solution)/shard_map/ppermute | solution.py:28
  16.7 3.0 %collective-permute-start = (bf16[4,64,1024]{2,1,0:T(8,128)(2,1)S(1)}, bf16[4,64,1024]{2,1,0:T(8,128)(2,1)S(1)}, u32[]{:S(2)}, u32[]{:S(2)}) collective-permute-start(bf16[4,64,1024]{2,1,0:T(8,128)(2,1)S(1)} %get-tuple-element.43), channel_id=1, source_target_pairs={{0,8},{8,0},{16,24},{24,16},{32,40},{40,32},{48,56},{56,48},{64,72... | collective-permute-start | bytes 1572872 | tf_op jit(solution)/shard_map/ppermute | solution.py:28
  20.5 3.5 %collective-permute-done.3.refs_8_.refs_10_ = bf16[2,128,512]{2,1,0:T(8,128)(2,1)S(1)} collective-permute-done((bf16[2,128,512]{2,1,0:T(8,128)(2,1)S(1)}, bf16[2,128,512]{2,1,0:T(8,128)(2,1)S(1)}, u32[]{:S(2)}, u32[]{:S(2)}) %collective-permute-start.3) | collective-permute-done | bytes 262176 | tf_op jit(solution)/shard_map/ppermute | solution.py:28
  24.0 5.6 %collective-permute-done.2.refs_7_.refs_9_ = bf16[2,128,512]{2,1,0:T(8,128)(2,1)S(1)} collective-permute-done((bf16[2,128,512]{2,1,0:T(8,128)(2,1)S(1)}, bf16[2,128,512]{2,1,0:T(8,128)(2,1)S(1)}, u32[]{:S(2)}, u32[]{:S(2)}) %collective-permute-start.2) | collective-permute-done | bytes 262176 | tf_op jit(solution)/shard_map/ppermute | solution.py:28
  29.7 3.2 %collective-permute-start.5 = (bf16[2,64,512]{2,1,0:T(8,128)(2,1)S(1)}, bf16[2,64,512]{2,1,0:T(8,128)(2,1)S(1)}, u32[]{:S(2)}, u32[]{:S(2)}) collective-permute-start(bf16[2,64,512]{2,1,0:T(8,128)(2,1)S(1)} %fusion.2), channel_id=1, source_target_pairs={{0,64},{8,72},{16,80},{24,88},{32,96},{40,104},{48,112},{56,120},{... | collective-permute-start | bytes 393224 | tf_op jit(solution)/shard_map/ppermute | solution.py:28
  35.6 5.4 %collective-permute-start.7 = (bf16[2,64,512]{2,1,0:T(8,128)(2,1)S(1)}, bf16[2,64,512]{2,1,0:T(8,128)(2,1)S(1)}, u32[]{:S(2)}, u32[]{:S(2)}) collective-permute-start(bf16[2,64,512]{2,1,0:T(8,128)(2,1)S(1)} %broadcast_select_fusion.2.refs_10_.refs_12_), channel_id=1, source_target_pairs={{0,256},{8,264},{16,272},{24,280},{32,288},{40,296},{48,304},{56,3... | collective-permute-start | bytes 393224 | tf_op jit(solution)/shard_map/ppermute | solution.py:28
  41.0 1.9 %collective-permute-start.6 = (bf16[2,64,512]{2,1,0:T(8,128)(2,1)S(1)}, bf16[2,64,512]{2,1,0:T(8,128)(2,1)S(1)}, u32[]{:S(2)}, u32[]{:S(2)}) collective-permute-start(bf16[2,64,512]{2,1,0:T(8,128)(2,1)S(1)} %broadcast_select_fusion.2.refs_10_.refs_12_), channel_id=1, source_target_pairs={{0,128},{8,136},{16,144},{24,152},{32,160},{40,168},{48,176},{56,1... | collective-permute-start | bytes 393224 | tf_op jit(solution)/shard_map/ppermute | solution.py:28
  43.1 6.0 %collective-permute-done.6.refs_11_.refs_13_ = bf16[2,64,512]{2,1,0:T(8,128)(2,1)S(1)} collective-permute-done((bf16[2,64,512]{2,1,0:T(8,128)(2,1)S(1)}, bf16[2,64,512]{2,1,0:T(8,128)(2,1)S(1)}, u32[]{:S(2)}, u32[]{:S(2)}) %collective-permute-start.6) | collective-permute-done | bytes 131104 | tf_op jit(solution)/shard_map/ppermute | solution.py:28
  49.1 4.0 %attention.2 = (bf16[2,64,1024]{2,1,0:T(8,128)(2,1)S(1)}, f32[128,512]{1,0:T(8,128)S(1)}, bf16[128,512]{1,0:T(8,128)(2,1)S(1)}, bf16[128,512]{1,0:T(8,128)(2,1)S...) custom-call(s32[6]{0:T(128)S(1)} %pad_add_fusion.refs_0_, ...), custom_call_target="tpu_custom_call" | custom-call | flops 1006632960 | bytes 4194304 | tf_op jit(solution)/shard_map/attention/pallas_call | solution.py:154
  58.9 5.9 %collective-permute-start.9 = (bf16[64,1024]{1,0:T(8,128)(2,1)S(1)}, bf16[64,1024]{1,0:T(8,128)(2,1)S(1)}, u32[]{:S(2)}, u32[]{:S(2)}) collective-permute-start(bf16[64,1024]{1,0:T(8,128)(2,1)S(1)} %slice_bitcast_fusion.1), channel_id=1, source_target_pairs={{0,8},{8,0},{16,24},{24,16},{32,40},{40,32},{48,56},{56,48},{64,72... | collective-permute-start | bytes 393224 | tf_op jit(solution)/shard_map/ppermute | solution.py:28
  66.2 4.0 %attention.3 = (bf16[2,64,1024]{2,1,0:T(8,128)(2,1)S(1)}, f32[128,512]{1,0:T(8,128)S(1)}, bf16[128,512]{1,0:T(8,128)(2,1)S(1)}, bf16[128,512]{1,0:T(8,128)(2,1)S...) custom-call(s32[6]{0:T(128)S(1)} %pad_add_fusion.refs_0_, ...), custom_call_target="tpu_custom_call" | custom-call | flops 1006632960 | bytes 4194304 | tf_op jit(solution)/shard_map/attention/pallas_call | solution.py:154
  70.3 2.9 %collective-permute-start.20 = (bf16[64,512]{1,0:T(8,128)(2,1)S(1)}, bf16[64,512]{1,0:T(8,128)(2,1)S(1)}, u32[]{:S(2)}, u32[]{:S(2)}) collective-permute-start(bf16[64,512]{1,0:T(8,128)(2,1)S(1)} %get-tuple-element.33), channel_id=1, source_target_pairs={{128,0},{136,8},{144,16},{152,24},{160,32},{168,40},{176,48},{184,... | collective-permute-start | bytes 196616 | tf_op jit(solution)/shard_map/ppermute | solution.py:28
  75.2 3.0 %collective-permute-done.20 = bf16[64,512]{1,0:T(8,128)(2,1)S(1)} collective-permute-done((bf16[64,512]{1,0:T(8,128)(2,1)S(1)}, bf16[64,512]{1,0:T(8,128)(2,1)S(1)}, u32[]{:S(2)}, u32[]{:S(2)}) %collective-permute-start.20) | collective-permute-done | bytes 65568 | tf_op jit(solution)/shard_map/ppermute | solution.py:28
  78.1 7.2 %collective-permute-start.11 = (bf16[64,1024]{1,0:T(8,128)(2,1)S(1)}, bf16[64,1024]{1,0:T(8,128)(2,1)S(1)}, u32[]{:S(2)}, u32[]{:S(2)}) collective-permute-start(bf16[64,1024]{1,0:T(8,128)(2,1)S(1)} %slice_bitcast_fusion), channel_id=1, source_target_pairs={{0,8},{8,0},{16,24},{24,16},{32,40},{40,32},{48,56},{56,48},{64,72... | collective-permute-start | bytes 393224 | tf_op jit(solution)/shard_map/ppermute | solution.py:28
  87.7 4.0 %collective-permute-done.23 = bf16[64,512]{1,0:T(8,128)(2,1)S(1)} collective-permute-done((bf16[64,512]{1,0:T(8,128)(2,1)S(1)}, bf16[64,512]{1,0:T(8,128)(2,1)S(1)}, u32[]{:S(2)}, u32[]{:S(2)}) %collective-permute-start.23) | collective-permute-done | bytes 65568 | tf_op jit(solution)/shard_map/ppermute | solution.py:28
  95.7 3.9 %collective-permute-start.18 = (bf16[128,512]{1,0:T(8,128)(2,1)S(1)}, bf16[128,512]{1,0:T(8,128)(2,1)S(1)}, u32[]{:S(2)}, u32[]{:S(2)}) collective-permute-start(bf16[128,512]{1,0:T(8,128)(2,1)S(1)} %get-tuple-element.51), channel_id=1, source_target_pairs={{48,0},{56,8},{64,16},{72,24},{80,32},{88,40},{96,48},{104,56},{11... | collective-permute-start | bytes 393224 | tf_op jit(solution)/shard_map/ppermute | solution.py:28
  99.8 4.2 %collective-permute-start.24 = (bf16[128,512]{1,0:T(8,128)(2,1)S(1)}, bf16[128,512]{1,0:T(8,128)(2,1)S(1)}, u32[]{:S(2)}, u32[]{:S(2)}) collective-permute-start(bf16[128,512]{1,0:T(8,128)(2,1)S(1)} %get-tuple-element.52), channel_id=1, source_target_pairs={{16,0},{24,8},{32,16},{40,24},{48,32},{56,40},{64,48},{72,56},{80,... | collective-permute-start | bytes 393224 | tf_op jit(solution)/shard_map/ppermute | solution.py:28
  104.0 4.6 %collective-permute-start.25 = (bf16[128,512]{1,0:T(8,128)(2,1)S(1)}, bf16[128,512]{1,0:T(8,128)(2,1)S(1)}, u32[]{:S(2)}, u32[]{:S(2)}) collective-permute-start(bf16[128,512]{1,0:T(8,128)(2,1)S(1)} %get-tuple-element.53), channel_id=1, source_target_pairs={{32,0},{40,8},{48,16},{56,24},{64,32},{72,40},{80,48},{88,56},{96,... | collective-permute-start | bytes 393224 | tf_op jit(solution)/shard_map/ppermute | solution.py:28
  108.6 1.9 %collective-permute-start.26 = (bf16[128,512]{1,0:T(8,128)(2,1)S(1)}, bf16[128,512]{1,0:T(8,128)(2,1)S(1)}, u32[]{:S(2)}, u32[]{:S(2)}) collective-permute-start(bf16[128,512]{1,0:T(8,128)(2,1)S(1)} %get-tuple-element.54), channel_id=1, source_target_pairs={{48,0},{56,8},{64,16},{72,24},{80,32},{88,40},{96,48},{104,56},{11... | collective-permute-start | bytes 393224 | tf_op jit(solution)/shard_map/ppermute | solution.py:28
  110.7 5.6 %collective-permute-start.19 = (bf16[64,512]{1,0:T(8,128)(2,1)S(1)}, bf16[64,512]{1,0:T(8,128)(2,1)S(1)}, u32[]{:S(2)}, u32[]{:S(2)}) collective-permute-start(bf16[64,512]{1,0:T(8,128)(2,1)S(1)} %slice.147), channel_id=1, source_target_pairs={{0,8},{8,0},{16,24},{24,16},{32,40},{40,32},{48,56},{56,48},{64,72... | collective-permute-start | bytes 196616 | tf_op jit(solution)/shard_map/ppermute | solution.py:28
  117.0 5.4 %collective-permute-start.27 = (bf16[64,512]{1,0:T(8,128)(2,1)S(1)}, bf16[64,512]{1,0:T(8,128)(2,1)S(1)}, u32[]{:S(2)}, u32[]{:S(2)}) collective-permute-start(bf16[64,512]{1,0:T(8,128)(2,1)S(1)} %slice.150), channel_id=1, source_target_pairs={{0,8},{8,0},{16,24},{24,16},{32,40},{40,32},{48,56},{56,48},{64,72... | collective-permute-start | bytes 196616 | tf_op jit(solution)/shard_map/ppermute | solution.py:28
  (79 shorter events, 25.1 us)
Async XLA Ops:
  6.3 14.2 %collective-permute-start.4 = (bf16[2,128,512]{2,1,0:T(8,128)(2,1)S(1)}, bf16[2,128,512]{2,1,0:T(8,128)(2,1)S(1)}, u32[]{:S(2)}, u32[]{:S(2)}) collective-permute-start(bf16[2,128,512]{2,1,0:T(8,128)(2,1)S(1)} %pad_maximum_fusion.1.refs_6_.refs_8_), channel_id=1, source_target_pairs={{0,48},{8,56},{16,64},{24,72},{32,80},{40,88},{48,96},{56,104},{64... | collective-permute-start | bytes 786440 | tf_op jit(solution)/shard_map/ppermute | solution.py:28
  10.7 13.3 %collective-permute-start.3 = (bf16[2,128,512]{2,1,0:T(8,128)(2,1)S(1)}, bf16[2,128,512]{2,1,0:T(8,128)(2,1)S(1)}, u32[]{:S(2)}, u32[]{:S(2)}) collective-permute-start(bf16[2,128,512]{2,1,0:T(8,128)(2,1)S(1)} %pad_maximum_fusion.1.refs_6_.refs_8_), channel_id=1, source_target_pairs={{0,32},{8,40},{16,48},{24,56},{32,64},{40,72},{48,80},{56,88},{64,... | collective-permute-start | bytes 786440 | tf_op jit(solution)/shard_map/ppermute | solution.py:28
  14.1 15.5 %collective-permute-start.2 = (bf16[2,128,512]{2,1,0:T(8,128)(2,1)S(1)}, bf16[2,128,512]{2,1,0:T(8,128)(2,1)S(1)}, u32[]{:S(2)}, u32[]{:S(2)}) collective-permute-start(bf16[2,128,512]{2,1,0:T(8,128)(2,1)S(1)} %pad_maximum_fusion.1.refs_6_.refs_8_), channel_id=1, source_target_pairs={{0,16},{8,24},{16,32},{24,40},{32,48},{40,56},{48,64},{56,72},{64,... | collective-permute-start | bytes 786440 | tf_op jit(solution)/shard_map/ppermute | solution.py:28
  16.7 26.3 %collective-permute-start = (bf16[4,64,1024]{2,1,0:T(8,128)(2,1)S(1)}, bf16[4,64,1024]{2,1,0:T(8,128)(2,1)S(1)}, u32[]{:S(2)}, u32[]{:S(2)}) collective-permute-start(bf16[4,64,1024]{2,1,0:T(8,128)(2,1)S(1)} %get-tuple-element.43), channel_id=1, source_target_pairs={{0,8},{8,0},{16,24},{24,16},{32,40},{40,32},{48,56},{56,48},{64,72... | collective-permute-start | bytes 1572872 | tf_op jit(solution)/shard_map/ppermute | solution.py:28
  34.9 8.2 %collective-permute-start.8 = (bf16[2,64,512]{2,1,0:T(8,128)(2,1)S(1)}, bf16[2,64,512]{2,1,0:T(8,128)(2,1)S(1)}, u32[]{:S(2)}, u32[]{:S(2)}) collective-permute-start(bf16[2,64,512]{2,1,0:T(8,128)(2,1)S(1)} %broadcast_select_fusion.2.refs_10_.refs_12_), channel_id=1, source_target_pairs={{0,384},{8,392},{16,400},{24,408},{32,416},{40,424},{48,432},{56,4... | collective-permute-start | bytes 393224 | tf_op jit(solution)/shard_map/ppermute | solution.py:28
  35.6 7.5 %collective-permute-start.7 = (bf16[2,64,512]{2,1,0:T(8,128)(2,1)S(1)}, bf16[2,64,512]{2,1,0:T(8,128)(2,1)S(1)}, u32[]{:S(2)}, u32[]{:S(2)}) collective-permute-start(bf16[2,64,512]{2,1,0:T(8,128)(2,1)S(1)} %broadcast_select_fusion.2.refs_10_.refs_12_), channel_id=1, source_target_pairs={{0,256},{8,264},{16,272},{24,280},{32,288},{40,296},{48,304},{56,3... | collective-permute-start | bytes 393224 | tf_op jit(solution)/shard_map/ppermute | solution.py:28
  41.0 8.1 %collective-permute-start.6 = (bf16[2,64,512]{2,1,0:T(8,128)(2,1)S(1)}, bf16[2,64,512]{2,1,0:T(8,128)(2,1)S(1)}, u32[]{:S(2)}, u32[]{:S(2)}) collective-permute-start(bf16[2,64,512]{2,1,0:T(8,128)(2,1)S(1)} %broadcast_select_fusion.2.refs_10_.refs_12_), channel_id=1, source_target_pairs={{0,128},{8,136},{16,144},{24,152},{32,160},{40,168},{48,176},{56,1... | collective-permute-start | bytes 393224 | tf_op jit(solution)/shard_map/ppermute | solution.py:28
  53.1 11.8 %collective-permute-start.12 = (bf16[64,512]{1,0:T(8,128)(2,1)S(1)}, bf16[64,512]{1,0:T(8,128)(2,1)S(1)}, u32[]{:S(2)}, u32[]{:S(2)}) collective-permute-start(bf16[64,512]{1,0:T(8,128)(2,1)S(1)} %get-tuple-element.25), channel_id=1, source_target_pairs={{128,0},{136,8},{144,16},{152,24},{160,32},{168,40},{176,48},{184,... | collective-permute-start | bytes 196616 | tf_op jit(solution)/shard_map/ppermute | solution.py:28
  55.0 9.9 %collective-permute-start.13 = (bf16[64,512]{1,0:T(8,128)(2,1)S(1)}, bf16[64,512]{1,0:T(8,128)(2,1)S(1)}, u32[]{:S(2)}, u32[]{:S(2)}) collective-permute-start(bf16[64,512]{1,0:T(8,128)(2,1)S(1)} %get-tuple-element.26), channel_id=1, source_target_pairs={{256,0},{264,8},{272,16},{280,24},{288,32},{296,40},{304,48},{312,... | collective-permute-start | bytes 196616 | tf_op jit(solution)/shard_map/ppermute | solution.py:28
  56.3 8.6 %collective-permute-start.14 = (bf16[64,512]{1,0:T(8,128)(2,1)S(1)}, bf16[64,512]{1,0:T(8,128)(2,1)S(1)}, u32[]{:S(2)}, u32[]{:S(2)}) collective-permute-start(bf16[64,512]{1,0:T(8,128)(2,1)S(1)} %get-tuple-element.27), channel_id=1, source_target_pairs={{384,0},{392,8},{400,16},{408,24},{416,32},{424,40},{432,48},{440,... | collective-permute-start | bytes 196616 | tf_op jit(solution)/shard_map/ppermute | solution.py:28
  57.0 9.3 %collective-permute-start.10 = (bf16[2,64,1024]{2,1,0:T(8,128)(2,1)S(1)}, bf16[2,64,1024]{2,1,0:T(8,128)(2,1)S(1)}, u32[]{:S(2)}, u32[]{:S(2)}) collective-permute-start(bf16[2,64,1024]{2,1,0:T(8,128)(2,1)S(1)} %get-tuple-element.21), channel_id=1, source_target_pairs={{1,0},{2,1},{3,2},{4,3},{5,4},{6,5},{7,6},{9,8},{10,9},{11,10},{12... | collective-permute-start | bytes 786440 | tf_op jit(solution)/shard_map/ppermute | solution.py:28
  58.9 27.8 %collective-permute-start.9 = (bf16[64,1024]{1,0:T(8,128)(2,1)S(1)}, bf16[64,1024]{1,0:T(8,128)(2,1)S(1)}, u32[]{:S(2)}, u32[]{:S(2)}) collective-permute-start(bf16[64,1024]{1,0:T(8,128)(2,1)S(1)} %slice_bitcast_fusion.1), channel_id=1, source_target_pairs={{0,8},{8,0},{16,24},{24,16},{32,40},{40,32},{48,56},{56,48},{64,72... | collective-permute-start | bytes 393224 | tf_op jit(solution)/shard_map/ppermute | solution.py:28
  64.9 22.8 %collective-permute-start.15 = (bf16[64,512]{1,0:T(8,128)(2,1)S(1)}, bf16[64,512]{1,0:T(8,128)(2,1)S(1)}, u32[]{:S(2)}, u32[]{:S(2)}) collective-permute-start(bf16[64,512]{1,0:T(8,128)(2,1)S(1)} %get-tuple-element.39), channel_id=1, source_target_pairs={{64,0},{72,8},{80,16},{88,24},{96,32},{104,40},{112,48},{120,56},{... | collective-permute-start | bytes 196616 | tf_op jit(solution)/shard_map/ppermute | solution.py:28
  70.3 7.9 %collective-permute-start.20 = (bf16[64,512]{1,0:T(8,128)(2,1)S(1)}, bf16[64,512]{1,0:T(8,128)(2,1)S(1)}, u32[]{:S(2)}, u32[]{:S(2)}) collective-permute-start(bf16[64,512]{1,0:T(8,128)(2,1)S(1)} %get-tuple-element.33), channel_id=1, source_target_pairs={{128,0},{136,8},{144,16},{152,24},{160,32},{168,40},{176,48},{184,... | collective-permute-start | bytes 196616 | tf_op jit(solution)/shard_map/ppermute | solution.py:28
  73.2 12.2 %collective-permute-start.21 = (bf16[64,512]{1,0:T(8,128)(2,1)S(1)}, bf16[64,512]{1,0:T(8,128)(2,1)S(1)}, u32[]{:S(2)}, u32[]{:S(2)}) collective-permute-start(bf16[64,512]{1,0:T(8,128)(2,1)S(1)} %get-tuple-element.34), channel_id=1, source_target_pairs={{256,0},{264,8},{272,16},{280,24},{288,32},{296,40},{304,48},{312,... | collective-permute-start | bytes 196616 | tf_op jit(solution)/shard_map/ppermute | solution.py:28
  74.5 10.9 %collective-permute-start.22 = (bf16[64,512]{1,0:T(8,128)(2,1)S(1)}, bf16[64,512]{1,0:T(8,128)(2,1)S(1)}, u32[]{:S(2)}, u32[]{:S(2)}) collective-permute-start(bf16[64,512]{1,0:T(8,128)(2,1)S(1)} %get-tuple-element.35), channel_id=1, source_target_pairs={{384,0},{392,8},{400,16},{408,24},{416,32},{424,40},{432,48},{440,... | collective-permute-start | bytes 196616 | tf_op jit(solution)/shard_map/ppermute | solution.py:28
  78.1 8.6 %collective-permute-start.11 = (bf16[64,1024]{1,0:T(8,128)(2,1)S(1)}, bf16[64,1024]{1,0:T(8,128)(2,1)S(1)}, u32[]{:S(2)}, u32[]{:S(2)}) collective-permute-start(bf16[64,1024]{1,0:T(8,128)(2,1)S(1)} %slice_bitcast_fusion), channel_id=1, source_target_pairs={{0,8},{8,0},{16,24},{24,16},{32,40},{40,32},{48,56},{56,48},{64,72... | collective-permute-start | bytes 393224 | tf_op jit(solution)/shard_map/ppermute | solution.py:28
  91.9 16.7 %collective-permute-start.16 = (bf16[128,512]{1,0:T(8,128)(2,1)S(1)}, bf16[128,512]{1,0:T(8,128)(2,1)S(1)}, u32[]{:S(2)}, u32[]{:S(2)}) collective-permute-start(bf16[128,512]{1,0:T(8,128)(2,1)S(1)} %get-tuple-element.49), channel_id=1, source_target_pairs={{16,0},{24,8},{32,16},{40,24},{48,32},{56,40},{64,48},{72,56},{80,... | collective-permute-start | bytes 393224 | tf_op jit(solution)/shard_map/ppermute | solution.py:28
  93.8 16.8 %collective-permute-start.17 = (bf16[128,512]{1,0:T(8,128)(2,1)S(1)}, bf16[128,512]{1,0:T(8,128)(2,1)S(1)}, u32[]{:S(2)}, u32[]{:S(2)}) collective-permute-start(bf16[128,512]{1,0:T(8,128)(2,1)S(1)} %get-tuple-element.50), channel_id=1, source_target_pairs={{32,0},{40,8},{48,16},{56,24},{64,32},{72,40},{80,48},{88,56},{96,... | collective-permute-start | bytes 393224 | tf_op jit(solution)/shard_map/ppermute | solution.py:28
  95.7 14.8 %collective-permute-start.18 = (bf16[128,512]{1,0:T(8,128)(2,1)S(1)}, bf16[128,512]{1,0:T(8,128)(2,1)S(1)}, u32[]{:S(2)}, u32[]{:S(2)}) collective-permute-start(bf16[128,512]{1,0:T(8,128)(2,1)S(1)} %get-tuple-element.51), channel_id=1, source_target_pairs={{48,0},{56,8},{64,16},{72,24},{80,32},{88,40},{96,48},{104,56},{11... | collective-permute-start | bytes 393224 | tf_op jit(solution)/shard_map/ppermute | solution.py:28
  99.8 16.6 %collective-permute-start.24 = (bf16[128,512]{1,0:T(8,128)(2,1)S(1)}, bf16[128,512]{1,0:T(8,128)(2,1)S(1)}, u32[]{:S(2)}, u32[]{:S(2)}) collective-permute-start(bf16[128,512]{1,0:T(8,128)(2,1)S(1)} %get-tuple-element.52), channel_id=1, source_target_pairs={{16,0},{24,8},{32,16},{40,24},{48,32},{56,40},{64,48},{72,56},{80,... | collective-permute-start | bytes 393224 | tf_op jit(solution)/shard_map/ppermute | solution.py:28
  104.0 12.3 %collective-permute-start.25 = (bf16[128,512]{1,0:T(8,128)(2,1)S(1)}, bf16[128,512]{1,0:T(8,128)(2,1)S(1)}, u32[]{:S(2)}, u32[]{:S(2)}) collective-permute-start(bf16[128,512]{1,0:T(8,128)(2,1)S(1)} %get-tuple-element.53), channel_id=1, source_target_pairs={{32,0},{40,8},{48,16},{56,24},{64,32},{72,40},{80,48},{88,56},{96,... | collective-permute-start | bytes 393224 | tf_op jit(solution)/shard_map/ppermute | solution.py:28
  108.6 8.3 %collective-permute-start.26 = (bf16[128,512]{1,0:T(8,128)(2,1)S(1)}, bf16[128,512]{1,0:T(8,128)(2,1)S(1)}, u32[]{:S(2)}, u32[]{:S(2)}) collective-permute-start(bf16[128,512]{1,0:T(8,128)(2,1)S(1)} %get-tuple-element.54), channel_id=1, source_target_pairs={{48,0},{56,8},{64,16},{72,24},{80,32},{88,40},{96,48},{104,56},{11... | collective-permute-start | bytes 393224 | tf_op jit(solution)/shard_map/ppermute | solution.py:28
  110.7 11.8 %collective-permute-start.19 = (bf16[64,512]{1,0:T(8,128)(2,1)S(1)}, bf16[64,512]{1,0:T(8,128)(2,1)S(1)}, u32[]{:S(2)}, u32[]{:S(2)}) collective-permute-start(bf16[64,512]{1,0:T(8,128)(2,1)S(1)} %slice.147), channel_id=1, source_target_pairs={{0,8},{8,0},{16,24},{24,16},{32,40},{40,32},{48,56},{56,48},{64,72... | collective-permute-start | bytes 196616 | tf_op jit(solution)/shard_map/ppermute | solution.py:28
  (9 other events, 52.6 us)

commit v2 on v1

--- a/solution.py
+++ b/solution.py
@@ -39,7 +39,13 @@
         h_mine, h_other = refs[:2]
         refs = refs[2:]
     pairs, strided = refs[:4], refs[4:8]
-    result, own, back1, back2, back3, part0, part1, part2, part3 = refs[8:]
+    refs = refs[8:]
+    if has_head:
+        for old, new in zip(refs[:4], refs[5:9]):
+            new[0] = old[...]
+        refs = refs[4:]
+        refs = refs[:1] + tuple(r.at[1] for r in refs[1:5]) + refs[5:]
+    both, other, back1, back2, back3, own, part0, part1, part2, part3 = refs
     backs = (own, back1, back2, back3)
     parts = (part0, part1, part2, part3)
     index = meta[0]
@@ -105,7 +111,10 @@
                 row = (half * GROUP + j) * BLK
                 grad = g[row : row + BLK].astype(jnp.float32)
                 total = grad + gain[:, at] * dquery[row : row + BLK]
-                result[half, :, at] = total.astype(jnp.bfloat16)
+                total = total.astype(jnp.bfloat16)
+                both[half, :, at] = total
+                if half == 1:
+                    other[:, at] = total
         for d in range(4):
             rows_at = slice(2 * BLK * d, 2 * BLK * (d + 1))
             backs[d][:, k_at] = dkey[rows_at].astype(backs[d].dtype)
@@ -116,20 +125,21 @@
             parts[s][:, v_at] = dvalue[rows_at].astype(parts[s].dtype)
 
 
-def attention(tick, meta, gain, keep, recv, grads, pairs, strided):
-    wide = 2 * HALF_KV
-
+WHOLE = pl.BlockSpec(memory_space=pltpu.VMEM)
+SCALAR = pl.BlockSpec(memory_space=pltpu.SMEM)
+WIDE = 2 * HALF_KV
+
+
+def shape(dims, dtype):
+    return jax.ShapeDtypeStruct(dims, dtype)
+
+
+def attention(tick, meta, gain, keep, recv, grads, pairs, strided, earlier):
     def at(lead, *rest):
         return pl.BlockSpec((None,) + rest, lambda n: (lead, 0, 0))
 
-    whole = pl.BlockSpec(memory_space=pltpu.VMEM)
     args = [meta, gain, keep, recv]
-    specs = [
-        pl.BlockSpec(memory_space=pltpu.SMEM),
-        whole,
-        at(tick, BLK, HALF_FEAT),
-        at(tick, BLK, HALF_FEAT),
-    ]
+    specs = [SCALAR, WHOLE, at(tick, BLK, HALF_FEAT), at(tick, BLK, HALF_FEAT)]
     if grads is None:
         args += [keep, recv]
         specs += [at(2, BLK, HALF_FEAT), at(2, BLK, HALF_FEAT)]
@@ -138,25 +148,23 @@
         specs += [at(0, BLK, HALF_FEAT), at(1, BLK, HALF_FEAT)]
         specs += [at(3, BLK, HALF_FEAT), at(3, BLK, HALF_FEAT)]
     args += list(pairs) + list(strided)
-    specs += [at(tick, 2 * BLK, wide)] * 4 + [at(tick, BLK, wide)] * 4
+    specs += [at(tick, 2 * BLK, WIDE)] * 4 + [at(tick, BLK, WIDE)] * 4
     bf16, f32 = jnp.bfloat16, jnp.float32
-    out_shape = [
-        jax.ShapeDtypeStruct((2, BLK, HALF_FEAT), bf16),
-        jax.ShapeDtypeStruct((2 * BLK, wide), f32),
-        jax.ShapeDtypeStruct((2 * BLK, wide), bf16),
-        jax.ShapeDtypeStruct((2 * BLK, wide), bf16),
-        jax.ShapeDtypeStruct((2 * BLK, wide), bf16),
-        jax.ShapeDtypeStruct((BLK, wide), f32),
-        jax.ShapeDtypeStruct((BLK, wide), bf16),
-        jax.ShapeDtypeStruct((BLK, wide), bf16),
-        jax.ShapeDtypeStruct((BLK, wide), bf16),
-    ]
+    out_shape = [shape((2, BLK, HALF_FEAT), bf16)]
+    if earlier is None:
+        out_shape += [shape((BLK, HALF_FEAT), bf16)] + [shape((2 * BLK, WIDE), bf16)] * 3
+    else:
+        args += earlier
+        specs += [WHOLE] * 4
+        out_shape += [shape((2, BLK, HALF_FEAT), bf16)] + [shape((2, 2 * BLK, WIDE), bf16)] * 3
+    out_shape += [shape((2 * BLK, WIDE), f32), shape((BLK, WIDE), f32)]
+    out_shape += [shape((BLK, WIDE), bf16)] * 3
     return pl.pallas_call(
         functools.partial(attention_kernel, grads is not None),
         out_shape=out_shape,
         grid=(1,),
         in_specs=specs,
-        out_specs=[whole] * len(out_shape),
+        out_specs=[WHOLE] * len(out_shape),
         compiler_params=pltpu.CompilerParams(vmem_limit_bytes=32 << 20),
         cost_estimate=pl.CostEstimate(
             flops=2 * 5 * 2 * 512 * 768 * 128, bytes_accessed=4 << 20, transcendentals=2 * 512 * 768
@@ -165,27 +173,125 @@
     )(*args)
 
 
+def simple(kernel, out_shape, args, scalars=1):
+    size = sum(a.size * a.dtype.itemsize for a in list(args) + list(out_shape))
+    return pl.pallas_call(
+        kernel,
+        out_shape=out_shape,
+        in_specs=[SCALAR] * scalars + [WHOLE] * (len(args) - scalars),
+        out_specs=[WHOLE] * len(out_shape),
+        compiler_params=pltpu.CompilerParams(vmem_limit_bytes=16 << 20),
+        cost_estimate=pl.CostEstimate(flops=size, bytes_accessed=size, transcendentals=0),
+        name=kernel.__name__,
+    )(*args)
+
+
+def column_sum(*refs):
+    wide_out, send_out = refs[8:]
+    for t in range(2):
+        total = refs[4 * t][...]
+        for s in range(1, 4):
+            total = total + refs[4 * t + s][...].astype(jnp.float32)
+        wide_out[t] = total
+        send_out[t] = total.astype(jnp.bfloat16)
+
+
+def split_keys(meta, keys, values, keep, give):
+    swap = meta[0] % 2 == 1
+    for source, at in ((keys, 0), (values, HALF_KV)):
+        low, high = source[0, :, :, :HALF_KV], source[0, :, :, HALF_KV:]
+        keep[:, :, at : at + HALF_KV] = jnp.where(swap, high, low)
+        give[:, :, at : at + HALF_KV] = jnp.where(swap, low, high)
+
+
+def split_rows(meta, inputs, first, head, keep, give):
+    swap = meta[0] % 2 == 1
+    for n, source in enumerate((inputs.at[0, 0], inputs.at[0, 1], first.at[0], head.at[0])):
+        low, high = source[:, :HALF_FEAT], source[:, HALF_FEAT:]
+        keep[n] = jnp.where(swap, high, low)
+        give[n] = jnp.where(swap, low, high)
+
+
+def pair_keys(meta, keep, recv, up_low, up_high, pair, start):
+    core = meta[0] % 2
+    even = (meta[0] // 8) % 2 == 0
+    pair[:, :BLK] = keep[...]
+    pair[:, BLK:] = recv[...]
+    near = jnp.where(core == 0, keep[...], recv[...])
+    above = jnp.where(core == 0, up_low[...], up_high[...])
+    start[...] = jnp.where(even, near, above)
+
+
+def row_sum(meta, *refs):
+    total, x1, x2, x3, own0, own1, back1, back2, back3 = refs[:9]
+    mine_out, other_out, strided_out = refs[9:]
+    index = meta[0]
+    owner = (index // 2) % 4 == 0
+    even = (index // 8) % 2 == 0
+    first = (owner & even & (index % 2 == 0)).astype(jnp.float32)
+    second = (owner & even & (index % 2 == 1)).astype(jnp.float32)
+    for t, own in enumerate((own0, own1)):
+        strided = total[t]
+        for x in (x1, x2, x3):
+            strided = strided + x[t].astype(jnp.float32)
+        strided_out[t] = strided.astype(jnp.bfloat16)
+        near = own[...]
+        for back in (back1, back2, back3):
+            near = near + back[t].astype(jnp.float32)
+        mine_out[t] = near[:BLK] + first * strided
+        other_out[t] = (near[BLK:] + second * strided).astype(jnp.bfloat16)
+
+
+def finish(meta, mine, other, low, high, keys_out, values_out):
+    swap = meta[0] % 2 == 1
+    for t in range(2):
+        own = (mine[t] + low[t].astype(jnp.float32)).astype(jnp.bfloat16)
+        far = (other[t].astype(jnp.float32) + high[t].astype(jnp.float32)).astype(jnp.bfloat16)
+        left, right = jnp.where(swap, far, own), jnp.where(swap, own, far)
+        for out, at in ((keys_out, 0), (values_out, HALF_KV)):
+            out[0, t, :, :HALF_KV] = left[:, at : at + HALF_KV]
+            out[0, t, :, HALF_KV:] = right[:, at : at + HALF_KV]
+
+
+def join_rows(meta, mine0, mine1, other, out):
+    swap = meta[0] % 2 == 1
+    for t, mine in enumerate((mine0, mine1)):
+        near, far = mine[0], other[t]
+        out[0, t, :, :HALF_FEAT] = jnp.where(swap, far, near)
+        out[0, t, :, HALF_FEAT:] = jnp.where(swap, near, far)
+
+
 def body(inputs, saved_keys, saved_values, query_gain, first_grads, head_grads, window, stride):
     index = lax.axis_index("ctx")
     section = lax.axis_index("pp")
     last = lax.axis_size("pp") - 1
     core = index % 2
     place = (index // 2) % 4
-    even_row = (index // 8) % 2 == 0
-    ticks = inputs.shape[1]
     f32, bf16 = jnp.float32, jnp.bfloat16
 
-    def halves(array):
-        cut = array.shape[-1] // 2
-        low, high = array[..., :cut], array[..., cut:]
-        return jnp.where(core == 0, low, high), jnp.where(core == 0, high, low)
-
-    key_keep, key_give = halves(saved_keys[0])
-    value_keep, value_give = halves(saved_values[0])
-    kv_keep = jnp.concatenate([key_keep, value_keep], axis=-1)
-    kv_recv = sibling(jnp.concatenate([key_give, value_give], axis=-1))
-    stacked = jnp.concatenate([inputs[0], first_grads, head_grads], axis=0)
-    keep, give = halves(stacked)
+    def ctx(array, move, when=lambda i: True):
+        return route(array, "ctx", lambda i: move(i) if when(i) else None)
+
+    spot = index.astype(jnp.int32).reshape(1)
+    half = shape((2, BLK, WIDE), bf16)
+    kv_keep, kv_give = simple(split_keys, [half, half], [spot, saved_keys, saved_values])
+    kv_recv = sibling(kv_give)
+    up_low = ctx(kv_keep, lambda i: i + 8, lambda i: i % STRIDE == 0)
+    up_high = ctx(kv_give, lambda i: i + 9, lambda i: i % STRIDE == 0)
+    pair, start = simple(
+        pair_keys,
+        [shape((2, 2 * BLK, WIDE), bf16), half],
+        [spot, kv_keep, kv_recv, up_low, up_high],
+    )
+    chosen = start
+    for d in range(1, 4):
+        across = ctx(start, lambda i: i + 2 * d, lambda i: (i // 2) % 4 == 0)
+        chosen = jnp.where(place == d, across, chosen)
+    pairs = [pair] + [ctx(pair, lambda i: i + 2 * d) for d in range(1, 4)]
+    strided = [chosen] + [ctx(chosen, lambda i: i + STRIDE * s) for s in range(1, 4)]
+
+    four = shape((4, BLK, HALF_FEAT), bf16)
+    keep, give = simple(split_rows, [four, four], [spot, inputs, first_grads, head_grads])
     recv = sibling(give)
     gain = jnp.where(core == 0, query_gain[:, :HALF_FEAT], query_gain[:, HALF_FEAT:])
     heads = jnp.where(core == 0, window[0, :2], window[0, 2:])
@@ -193,64 +299,31 @@
     top = jnp.where(section == last, 1, 0)
     meta = jnp.concatenate([jnp.stack([index, top]).astype(jnp.int32), heads, steps])
 
-    pair = jnp.concatenate([kv_keep, kv_recv], axis=1)
-    pairs = [pair]
-    for d in range(1, 4):
-        pairs.append(route(pair, "ctx", lambda i: i + 2 * d))
-
-    def pick(array):
-        return jnp.where(core == 0, array[:, :BLK], array[:, BLK:])
-
-    chosen = pick(pairs[0])
-    for d in range(1, 4):
-        chosen = jnp.where(place == d, pick(pairs[d]), chosen)
-    above = route(chosen, "ctx", lambda i: i + 8 if (i // 8) % 2 == 0 else None)
-    chosen = jnp.where(even_row, chosen, above)
-    strided = [chosen]
-    for s in range(1, 4):
-        strided.append(route(chosen, "ctx", lambda i: i + STRIDE * s))
-
-    results, totals = [], []
-    grads = None
-    for tick in range(ticks):
-        outs = attention(tick, meta, gain, keep, recv, grads, pairs, strided)
-        result, own, backs, parts = outs[0], outs[1], outs[2:5], outs[5:9]
-        if tick < ticks - 1:
-            grads = route(result, "pp", lambda i: i - 1)
-        results.append(result)
-        total = parts[0]
-        for s in range(1, 4):
-            total = total + route(parts[s], "ctx", lambda i: i - STRIDE * s).astype(f32)
-        below = route(
-            total.astype(bf16), "ctx", lambda i: i - 8 if (i // 8) % 2 == 1 else None
-        )
-        total = jnp.where(even_row, total + below.astype(f32), 0.0)
-        zero = jnp.zeros_like(total)
-        spread = jnp.concatenate(
-            [jnp.where(core == 0, total, zero), jnp.where(core == 0, zero, total)], axis=0
-        )
-        final = own + jnp.where(place == 0, spread, 0.0)
-        for d in range(1, 4):
-            piece = backs[d - 1].astype(f32) + jnp.where(place == d, spread, 0.0)
-            final = final + route(piece.astype(bf16), "ctx", lambda i: i - 2 * d).astype(f32)
-        totals.append(final.astype(bf16))
-
-    def join(mine, other):
-        return jnp.concatenate(
-            [jnp.where(core == 0, mine, other), jnp.where(core == 0, other, mine)], axis=-1
-        )
-
-    grads_out = [join(r[0], sibling(r[1])) for r in results]
-    key_grads, value_grads = [], []
-    for total in totals:
-        mine, other = total[:BLK], sibling(total[BLK:])
-        key_grads.append(join(mine[:, :HALF_KV], other[:, :HALF_KV]))
-        value_grads.append(join(mine[:, HALF_KV:], other[:, HALF_KV:]))
-    return (
-        jnp.stack(grads_out, axis=0)[None],
-        jnp.stack(key_grads, axis=0)[None],
-        jnp.stack(value_grads, axis=0)[None],
+    first = attention(0, meta, gain, keep, recv, None, pairs, strided, None)
+    grads = route(first[0], "pp", lambda i: i - 1)
+    second = attention(1, meta, gain, keep, recv, grads, pairs, strided, first[1:5])
+    columns = []
+    for outs in (first, second):
+        columns.append(outs[6])
+        columns += [ctx(outs[6 + s], lambda i: i - STRIDE * s) for s in range(1, 4)]
+    backs = [ctx(second[1 + d], lambda i: i - 2 * d) for d in range(1, 4)]
+    other_rows = sibling(second[1])
+
+    wide = shape((2, BLK, WIDE), f32)
+    total, send = simple(column_sum, [wide, half], columns, 0)
+    rows = [ctx(send, lambda i: i - 2 * d, lambda i: (i // 2) % 4 == d) for d in range(1, 4)]
+    mine, other, down = simple(
+        row_sum, [wide, half, half], [spot, total] + rows + [first[5], second[5]] + backs
     )
+    other = sibling(other)
+    low = ctx(down, lambda i: i - 8, lambda i: i % STRIDE == 8)
+    high = ctx(down, lambda i: i - 9, lambda i: i % STRIDE == 9)
+    keys_shape = shape(saved_keys.shape, bf16)
+    key_grads, value_grads = simple(finish, [keys_shape, keys_shape], [spot, mine, other, low, high])
+    (grads_out,) = simple(
+        join_rows, [shape(inputs.shape, bf16)], [spot, first[0], second[0], other_rows]
+    )
+    return grads_out, key_grads, value_grads
 
 
 def solution(mesh):

time: 126 us -> 119 us (0.944)
  the two profiles are of different devices: /device:TPU:145 before, /device:TPU:192 now
where the time goes in v2:
time: 119 us; the launch traced here: 118 us
  starting transfers between devices  56.5 us (47%)
  waiting for transfers between devices  47.8 us (40%)
  Pallas kernels  10 us (8%)
  local copies, waits for them, and re-layouts  2.83 us (2%)
    ppermute x30, starting transfers between devices, route(): lax.ppermute(array, axis, [(a, b) for a, b in pairs if b is not None and...  56.5 us
    ppermute x30, waiting for transfers between devices, route(): lax.ppermute(array, axis, [(a, b) for a, b in pairs if b is not None and...  47.8 us
    pallas_call x2, Pallas kernels, attention(): pl.pallas_call(functools.partial(attention_kernel, grads is not None), ou...  8 us
    unnamed x16, local copies, waits for them, and re-layouts  2.83 us
  transfers between devices with their start and end apart: 30, of which 17 were waited for; matrix products, arithmetic and copies ran while one was open for 0% of the time, Pallas kernels for 4%

profile of v2, /device:TPU:192, one launch (start us, length us, event | category | flops | bytes accessed | tf_op | source)
XLA Modules:
  0.0 118.4 jit_solution(4176700142999457175)
XLA Ops:
  2.5 3.5 %collective-permute-start.2 = (bf16[2,64,512]{2,1,0:T(8,128)(2,1)S(1)}, bf16[2,64,512]{2,1,0:T(8,128)(2,1)S(1)}, u32[]{:S(2)}, u32[]{:S(2)}) collective-permute-start(bf16[2,64,512]{2,1,0:T(8,128)(2,1)S(1)} %get-tuple-element.38.keep), channel_id=1, source_target_pairs={{0,64},{128,192},{256,320},{384,448},{1,65},{129,193},{257,321},{3... | collective-permute-start | bytes 393224 | tf_op jit(solution)/shard_map/ppermute | solution.py:28
  7.5 1.9 %collective-permute-start.1 = (bf16[2,64,512]{2,1,0:T(8,128)(2,1)S(1)}, bf16[2,64,512]{2,1,0:T(8,128)(2,1)S(1)}, u32[]{:S(2)}, u32[]{:S(2)}) collective-permute-start(bf16[2,64,512]{2,1,0:T(8,128)(2,1)S(1)} %get-tuple-element.39), channel_id=1, source_target_pairs={{0,8},{8,0},{16,24},{24,16},{32,40},{40,32},{48,56},{56,48},{64,72... | collective-permute-start | bytes 393224 | tf_op jit(solution)/shard_map/ppermute | solution.py:28
  15.7 2.1 %collective-permute-start = (bf16[4,64,1024]{2,1,0:T(8,128)(2,1)S(1)}, bf16[4,64,1024]{2,1,0:T(8,128)(2,1)S(1)}, u32[]{:S(2)}, u32[]{:S(2)}) collective-permute-start(bf16[4,64,1024]{2,1,0:T(8,128)(2,1)S(1)} %get-tuple-element.37), channel_id=1, source_target_pairs={{0,8},{8,0},{16,24},{24,16},{32,40},{40,32},{48,56},{56,48},{64,72... | collective-permute-start | bytes 1572872 | tf_op jit(solution)/shard_map/ppermute | solution.py:28
  18.2 5.3 %collective-permute-start.12 = (bf16[2,64,512]{2,1,0:T(8,128)(2,1)S(1)}, bf16[2,64,512]{2,1,0:T(8,128)(2,1)S(1)}, u32[]{:S(2)}, u32[]{:S(2)}) collective-permute-start(bf16[2,64,512]{2,1,0:T(8,128)(2,1)S(1)} %select_select_fusion.refs_10_.refs_12_), channel_id=1, source_target_pairs={{0,384},{8,392},{16,400},{24,408},{32,416},{40,424},{48,432},{56,4... | collective-permute-start | bytes 393224 | tf_op jit(solution)/shard_map/ppermute | solution.py:28
  23.5 2.2 %collective-permute-start.11 = (bf16[2,64,512]{2,1,0:T(8,128)(2,1)S(1)}, bf16[2,64,512]{2,1,0:T(8,128)(2,1)S(1)}, u32[]{:S(2)}, u32[]{:S(2)}) collective-permute-start(bf16[2,64,512]{2,1,0:T(8,128)(2,1)S(1)} %select_select_fusion.refs_10_.refs_12_), channel_id=1, source_target_pairs={{0,256},{8,264},{16,272},{24,280},{32,288},{40,296},{48,304},{56,3... | collective-permute-start | bytes 393224 | tf_op jit(solution)/shard_map/ppermute | solution.py:28
  25.8 5.6 %collective-permute-start.6 = (bf16[2,128,512]{2,1,0:T(8,128)(2,1)S(1)}, bf16[2,128,512]{2,1,0:T(8,128)(2,1)S(1)}, u32[]{:S(2)}, u32[]{:S(2)}) collective-permute-start(bf16[2,128,512]{2,1,0:T(8,128)(2,1)S(1)} %get-tuple-element.40.refs_6_.refs_8_), channel_id=1, source_target_pairs={{0,48},{8,56},{16,64},{24,72},{32,80},{40,88},{48,96},{56,104},{64... | collective-permute-start | bytes 786440 | tf_op jit(solution)/shard_map/ppermute | solution.py:28
  31.4 1.6 %collective-permute-start.5 = (bf16[2,128,512]{2,1,0:T(8,128)(2,1)S(1)}, bf16[2,128,512]{2,1,0:T(8,128)(2,1)S(1)}, u32[]{:S(2)}, u32[]{:S(2)}) collective-permute-start(bf16[2,128,512]{2,1,0:T(8,128)(2,1)S(1)} %get-tuple-element.40.refs_6_.refs_8_), channel_id=1, source_target_pairs={{0,32},{8,40},{16,48},{24,56},{32,64},{40,72},{48,80},{56,88},{64,... | collective-permute-start | bytes 786440 | tf_op jit(solution)/shard_map/ppermute | solution.py:28
  33.0 2.3 %collective-permute-done.12.refs_13_.refs_15_ = bf16[2,64,512]{2,1,0:T(8,128)(2,1)S(1)} collective-permute-done((bf16[2,64,512]{2,1,0:T(8,128)(2,1)S(1)}, bf16[2,64,512]{2,1,0:T(8,128)(2,1)S(1)}, u32[]{:S(2)}, u32[]{:S(2)}) %collective-permute-start.12) | collective-permute-done | bytes 131104 | tf_op jit(solution)/shard_map/ppermute | solution.py:28
  36.7 3.3 %collective-permute-start.10 = (bf16[2,64,512]{2,1,0:T(8,128)(2,1)S(1)}, bf16[2,64,512]{2,1,0:T(8,128)(2,1)S(1)}, u32[]{:S(2)}, u32[]{:S(2)}) collective-permute-start(bf16[2,64,512]{2,1,0:T(8,128)(2,1)S(1)} %select_select_fusion.refs_10_.refs_12_), channel_id=1, source_target_pairs={{0,128},{8,136},{16,144},{24,152},{32,160},{40,168},{48,176},{56,1... | collective-permute-start | bytes 393224 | tf_op jit(solution)/shard_map/ppermute | solution.py:28
  40.2 2.3 %collective-permute-done.10.refs_11_.refs_13_ = bf16[2,64,512]{2,1,0:T(8,128)(2,1)S(1)} collective-permute-done((bf16[2,64,512]{2,1,0:T(8,128)(2,1)S(1)}, bf16[2,64,512]{2,1,0:T(8,128)(2,1)S(1)}, u32[]{:S(2)}, u32[]{:S(2)}) %collective-permute-start.10) | collective-permute-done | bytes 131104 | tf_op jit(solution)/shard_map/ppermute | solution.py:28
  43.7 4.0 %attention.2 = (bf16[2,64,1024]{2,1,0:T(8,128)(2,1)S(1)}, bf16[64,1024]{1,0:T(8,128)(2,1)S(1)}, bf16[128,512]{1,0:T(8,128)(2,1)S(1)}, bf16[128,512]{1,0:T(8,128)...) custom-call(s32[6]{0:T(128)S(1)} %pad_add_fusion.refs_0_, ...), custom_call_target="tpu_custom_call" | custom-call | flops 1006632960 | bytes 4194304 | tf_op jit(solution)/shard_map/attention/pallas_call | solution.py:162
  47.7 1.9 %collective-permute-start.13 = (bf16[2,64,1024]{2,1,0:T(8,128)(2,1)S(1)}, bf16[2,64,1024]{2,1,0:T(8,128)(2,1)S(1)}, u32[]{:S(2)}, u32[]{:S(2)}) collective-permute-start(bf16[2,64,1024]{2,1,0:T(8,128)(2,1)S(1)} %get-tuple-element.42.mine0), channel_id=1, source_target_pairs={{1,0},{2,1},{3,2},{4,3},{5,4},{6,5},{7,6},{9,8},{10,9},{11,10},{12... | collective-permute-start | bytes 786440 | tf_op jit(solution)/shard_map/ppermute | solution.py:28
  53.5 5.1 %collective-permute-done.13.refs_4_.refs_5_ = bf16[2,64,1024]{2,1,0:T(8,128)(2,1)S(1)} collective-permute-done((bf16[2,64,1024]{2,1,0:T(8,128)(2,1)S(1)}, bf16[2,64,1024]{2,1,0:T(8,128)(2,1)S(1)}, u32[]{:S(2)}, u32[]{:S(2)}) %collective-permute-start.13) | collective-permute-done | bytes 262176 | tf_op jit(solution)/shard_map/ppermute | solution.py:28
  58.6 4.0 %attention.3 = (bf16[2,64,1024]{2,1,0:T(8,128)(2,1)S(1)}, bf16[2,64,1024]{2,1,0:T(8,128)(2,1)S(1)}, bf16[2,128,512]{2,1,0:T(8,128)(2,1)S(1)}, bf16[2,128,512]{2,...) custom-call(s32[6]{0:T(128)S(1)} %pad_add_fusion.refs_0_, ...), custom_call_target="tpu_custom_call" | custom-call | flops 1006632960 | bytes 4194304 | tf_op jit(solution)/shard_map/attention/pallas_call | solution.py:162
  67.6 3.6 %collective-permute-done.16.refs_2_ = bf16[64,512]{1,0:T(8,128)(2,1)S(1)} collective-permute-done((bf16[64,512]{1,0:T(8,128)(2,1)S(1)}, bf16[64,512]{1,0:T(8,128)(2,1)S(1)}, u32[]{:S(2)}, u32[]{:S(2)}) %collective-permute-start.16) | collective-permute-done | bytes 65568 | tf_op jit(solution)/shard_map/ppermute | solution.py:28
  73.1 5.2 %collective-permute-done.18.refs_5_ = bf16[64,512]{1,0:T(8,128)(2,1)S(1)} collective-permute-done((bf16[64,512]{1,0:T(8,128)(2,1)S(1)}, bf16[64,512]{1,0:T(8,128)(2,1)S(1)}, u32[]{:S(2)}, u32[]{:S(2)}) %collective-permute-start.18) | collective-permute-done | bytes 65568 | tf_op jit(solution)/shard_map/ppermute | solution.py:28
  78.3 4.9 %collective-permute-done.19.refs_6_ = bf16[64,512]{1,0:T(8,128)(2,1)S(1)} collective-permute-done((bf16[64,512]{1,0:T(8,128)(2,1)S(1)}, bf16[64,512]{1,0:T(8,128)(2,1)S(1)}, u32[]{:S(2)}, u32[]{:S(2)}) %collective-permute-start.19) | collective-permute-done | bytes 65568 | tf_op jit(solution)/shard_map/ppermute | solution.py:28
  83.2 1.9 %collective-permute-done.20.refs_7_ = bf16[64,512]{1,0:T(8,128)(2,1)S(1)} collective-permute-done((bf16[64,512]{1,0:T(8,128)(2,1)S(1)}, bf16[64,512]{1,0:T(8,128)(2,1)S(1)}, u32[]{:S(2)}, u32[]{:S(2)}) %collective-permute-start.20) | collective-permute-done | bytes 65568 | tf_op jit(solution)/shard_map/ppermute | solution.py:28
  90.3 7.5 %collective-permute-done.23.refs_3_ = bf16[2,64,512]{2,1,0:T(8,128)(2,1)S(1)} collective-permute-done((bf16[2,64,512]{2,1,0:T(8,128)(2,1)S(1)}, bf16[2,64,512]{2,1,0:T(8,128)(2,1)S(1)}, u32[]{:S(2)}, u32[]{:S(2)}) %collective-permute-start.23) | collective-permute-done | bytes 131104 | tf_op jit(solution)/shard_map/ppermute | solution.py:28
  99.1 5.8 %collective-permute-done.22.refs_2_ = bf16[2,64,512]{2,1,0:T(8,128)(2,1)S(1)} collective-permute-done((bf16[2,64,512]{2,1,0:T(8,128)(2,1)S(1)}, bf16[2,64,512]{2,1,0:T(8,128)(2,1)S(1)}, u32[]{:S(2)}, u32[]{:S(2)}) %collective-permute-start.22) | collective-permute-done | bytes 131104 | tf_op jit(solution)/shard_map/ppermute | solution.py:28
  104.9 1.9 %collective-permute-start.14 = (bf16[2,64,1024]{2,1,0:T(8,128)(2,1)S(1)}, bf16[2,64,1024]{2,1,0:T(8,128)(2,1)S(1)}, u32[]{:S(2)}, u32[]{:S(2)}) collective-permute-start(bf16[2,64,1024]{2,1,0:T(8,128)(2,1)S(1)} %get-tuple-element.48), channel_id=1, source_target_pairs={{0,8},{8,0},{16,24},{24,16},{32,40},{40,32},{48,56},{56,48},{64,72... | collective-permute-start | bytes 786440 | tf_op jit(solution)/shard_map/ppermute | solution.py:28
  107.1 2.4 %collective-permute-start.27 = (bf16[2,64,512]{2,1,0:T(8,128)(2,1)S(1)}, bf16[2,64,512]{2,1,0:T(8,128)(2,1)S(1)}, u32[]{:S(2)}, u32[]{:S(2)}) collective-permute-start(bf16[2,64,512]{2,1,0:T(8,128)(2,1)S(1)} %get-tuple-element.65), channel_id=1, source_target_pairs={{0,8},{8,0},{16,24},{24,16},{32,40},{40,32},{48,56},{56,48},{64,72... | collective-permute-start | bytes 393224 | tf_op jit(solution)/shard_map/ppermute | solution.py:28
  113.0 2.8 %collective-permute-done.29.high = bf16[2,64,512]{2,1,0:T(8,128)(2,1)S(1)} collective-permute-done((bf16[2,64,512]{2,1,0:T(8,128)(2,1)S(1)}, bf16[2,64,512]{2,1,0:T(8,128)(2,1)S(1)}, u32[]{:S(2)}, u32[]{:S(2)}) %collective-permute-start.29) | collective-permute-done | bytes 131104 | tf_op jit(solution)/shard_map/ppermute | solution.py:28
  115.8 1.9 %collective-permute-done.28.low = bf16[2,64,512]{2,1,0:T(8,128)(2,1)S(1)} collective-permute-done((bf16[2,64,512]{2,1,0:T(8,128)(2,1)S(1)}, bf16[2,64,512]{2,1,0:T(8,128)(2,1)S(1)}, u32[]{:S(2)}, u32[]{:S(2)}) %collective-permute-start.28) | collective-permute-done | bytes 131104 | tf_op jit(solution)/shard_map/ppermute | solution.py:28
  (65 shorter events, 34.3 us)
Async XLA Ops:
  2.5 6.9 %collective-permute-start.2 = (bf16[2,64,512]{2,1,0:T(8,128)(2,1)S(1)}, bf16[2,64,512]{2,1,0:T(8,128)(2,1)S(1)}, u32[]{:S(2)}, u32[]{:S(2)}) collective-permute-start(bf16[2,64,512]{2,1,0:T(8,128)(2,1)S(1)} %get-tuple-element.38.keep), channel_id=1, source_target_pairs={{0,64},{128,192},{256,320},{384,448},{1,65},{129,193},{257,321},{3... | collective-permute-start | bytes 393224 | tf_op jit(solution)/shard_map/ppermute | solution.py:28
  10.8 7.1 %collective-permute-start.9 = (bf16[2,64,512]{2,1,0:T(8,128)(2,1)S(1)}, bf16[2,64,512]{2,1,0:T(8,128)(2,1)S(1)}, u32[]{:S(2)}, u32[]{:S(2)}) collective-permute-start(bf16[2,64,512]{2,1,0:T(8,128)(2,1)S(1)} %get-tuple-element.41), channel_id=1, source_target_pairs={{0,16},{8,24},{64,80},{72,88},{128,144},{136,152},{192,208},{200,2... | collective-permute-start | bytes 393224 | tf_op jit(solution)/shard_map/ppermute | solution.py:28
  15.7 28.0 %collective-permute-start = (bf16[4,64,1024]{2,1,0:T(8,128)(2,1)S(1)}, bf16[4,64,1024]{2,1,0:T(8,128)(2,1)S(1)}, u32[]{:S(2)}, u32[]{:S(2)}) collective-permute-start(bf16[4,64,1024]{2,1,0:T(8,128)(2,1)S(1)} %get-tuple-element.37), channel_id=1, source_target_pairs={{0,8},{8,0},{16,24},{24,16},{32,40},{40,32},{48,56},{56,48},{64,72... | collective-permute-start | bytes 1572872 | tf_op jit(solution)/shard_map/ppermute | solution.py:28
  18.2 17.1 %collective-permute-start.12 = (bf16[2,64,512]{2,1,0:T(8,128)(2,1)S(1)}, bf16[2,64,512]{2,1,0:T(8,128)(2,1)S(1)}, u32[]{:S(2)}, u32[]{:S(2)}) collective-permute-start(bf16[2,64,512]{2,1,0:T(8,128)(2,1)S(1)} %select_select_fusion.refs_10_.refs_12_), channel_id=1, source_target_pairs={{0,384},{8,392},{16,400},{24,408},{32,416},{40,424},{48,432},{56,4... | collective-permute-start | bytes 393224 | tf_op jit(solution)/shard_map/ppermute | solution.py:28
  23.5 13.2 %collective-permute-start.11 = (bf16[2,64,512]{2,1,0:T(8,128)(2,1)S(1)}, bf16[2,64,512]{2,1,0:T(8,128)(2,1)S(1)}, u32[]{:S(2)}, u32[]{:S(2)}) collective-permute-start(bf16[2,64,512]{2,1,0:T(8,128)(2,1)S(1)} %select_select_fusion.refs_10_.refs_12_), channel_id=1, source_target_pairs={{0,256},{8,264},{16,272},{24,280},{32,288},{40,296},{48,304},{56,3... | collective-permute-start | bytes 393224 | tf_op jit(solution)/shard_map/ppermute | solution.py:28
  25.8 16.7 %collective-permute-start.6 = (bf16[2,128,512]{2,1,0:T(8,128)(2,1)S(1)}, bf16[2,128,512]{2,1,0:T(8,128)(2,1)S(1)}, u32[]{:S(2)}, u32[]{:S(2)}) collective-permute-start(bf16[2,128,512]{2,1,0:T(8,128)(2,1)S(1)} %get-tuple-element.40.refs_6_.refs_8_), channel_id=1, source_target_pairs={{0,48},{8,56},{16,64},{24,72},{32,80},{40,88},{48,96},{56,104},{64... | collective-permute-start | bytes 786440 | tf_op jit(solution)/shard_map/ppermute | solution.py:28
  31.4 11.1 %collective-permute-start.5 = (bf16[2,128,512]{2,1,0:T(8,128)(2,1)S(1)}, bf16[2,128,512]{2,1,0:T(8,128)(2,1)S(1)}, u32[]{:S(2)}, u32[]{:S(2)}) collective-permute-start(bf16[2,128,512]{2,1,0:T(8,128)(2,1)S(1)} %get-tuple-element.40.refs_6_.refs_8_), channel_id=1, source_target_pairs={{0,32},{8,40},{16,48},{24,56},{32,64},{40,72},{48,80},{56,88},{64,... | collective-permute-start | bytes 786440 | tf_op jit(solution)/shard_map/ppermute | solution.py:28
  35.3 8.4 %collective-permute-start.4 = (bf16[2,128,512]{2,1,0:T(8,128)(2,1)S(1)}, bf16[2,128,512]{2,1,0:T(8,128)(2,1)S(1)}, u32[]{:S(2)}, u32[]{:S(2)}) collective-permute-start(bf16[2,128,512]{2,1,0:T(8,128)(2,1)S(1)} %get-tuple-element.40.refs_6_.refs_8_), channel_id=1, source_target_pairs={{0,16},{8,24},{16,32},{24,40},{32,48},{40,56},{48,64},{56,72},{64,... | collective-permute-start | bytes 786440 | tf_op jit(solution)/shard_map/ppermute | solution.py:28
  47.7 10.9 %collective-permute-start.13 = (bf16[2,64,1024]{2,1,0:T(8,128)(2,1)S(1)}, bf16[2,64,1024]{2,1,0:T(8,128)(2,1)S(1)}, u32[]{:S(2)}, u32[]{:S(2)}) collective-permute-start(bf16[2,64,1024]{2,1,0:T(8,128)(2,1)S(1)} %get-tuple-element.42.mine0), channel_id=1, source_target_pairs={{1,0},{2,1},{3,2},{4,3},{5,4},{6,5},{7,6},{9,8},{10,9},{11,10},{12... | collective-permute-start | bytes 786440 | tf_op jit(solution)/shard_map/ppermute | solution.py:28
  49.6 16.7 %collective-permute-start.15 = (bf16[64,512]{1,0:T(8,128)(2,1)S(1)}, bf16[64,512]{1,0:T(8,128)(2,1)S(1)}, u32[]{:S(2)}, u32[]{:S(2)}) collective-permute-start(bf16[64,512]{1,0:T(8,128)(2,1)S(1)} %get-tuple-element.50), channel_id=1, source_target_pairs={{128,0},{136,8},{144,16},{152,24},{160,32},{168,40},{176,48},{184,... | collective-permute-start | bytes 196616 | tf_op jit(solution)/shard_map/ppermute | solution.py:28
  50.9 20.2 %collective-permute-start.16 = (bf16[64,512]{1,0:T(8,128)(2,1)S(1)}, bf16[64,512]{1,0:T(8,128)(2,1)S(1)}, u32[]{:S(2)}, u32[]{:S(2)}) collective-permute-start(bf16[64,512]{1,0:T(8,128)(2,1)S(1)} %get-tuple-element.51), channel_id=1, source_target_pairs={{256,0},{264,8},{272,16},{280,24},{288,32},{296,40},{304,48},{312,... | collective-permute-start | bytes 196616 | tf_op jit(solution)/shard_map/ppermute | solution.py:28
  52.2 20.9 %collective-permute-start.17 = (bf16[64,512]{1,0:T(8,128)(2,1)S(1)}, bf16[64,512]{1,0:T(8,128)(2,1)S(1)}, u32[]{:S(2)}, u32[]{:S(2)}) collective-permute-start(bf16[64,512]{1,0:T(8,128)(2,1)S(1)} %get-tuple-element.52), channel_id=1, source_target_pairs={{384,0},{392,8},{400,16},{408,24},{416,32},{424,40},{432,48},{440,... | collective-permute-start | bytes 196616 | tf_op jit(solution)/shard_map/ppermute | solution.py:28
  62.7 15.6 %collective-permute-start.18 = (bf16[64,512]{1,0:T(8,128)(2,1)S(1)}, bf16[64,512]{1,0:T(8,128)(2,1)S(1)}, u32[]{:S(2)}, u32[]{:S(2)}) collective-permute-start(bf16[64,512]{1,0:T(8,128)(2,1)S(1)} %get-tuple-element.54), channel_id=1, source_target_pairs={{128,0},{136,8},{144,16},{152,24},{160,32},{168,40},{176,48},{184,... | collective-permute-start | bytes 196616 | tf_op jit(solution)/shard_map/ppermute | solution.py:28
  64.0 19.2 %collective-permute-start.19 = (bf16[64,512]{1,0:T(8,128)(2,1)S(1)}, bf16[64,512]{1,0:T(8,128)(2,1)S(1)}, u32[]{:S(2)}, u32[]{:S(2)}) collective-permute-start(bf16[64,512]{1,0:T(8,128)(2,1)S(1)} %get-tuple-element.55), channel_id=1, source_target_pairs={{256,0},{264,8},{272,16},{280,24},{288,32},{296,40},{304,48},{312,... | collective-permute-start | bytes 196616 | tf_op jit(solution)/shard_map/ppermute | solution.py:28
  66.3 18.8 %collective-permute-start.20 = (bf16[64,512]{1,0:T(8,128)(2,1)S(1)}, bf16[64,512]{1,0:T(8,128)(2,1)S(1)}, u32[]{:S(2)}, u32[]{:S(2)}) collective-permute-start(bf16[64,512]{1,0:T(8,128)(2,1)S(1)} %get-tuple-element.56), channel_id=1, source_target_pairs={{384,0},{392,8},{400,16},{408,24},{416,32},{424,40},{432,48},{440,... | collective-permute-start | bytes 196616 | tf_op jit(solution)/shard_map/ppermute | solution.py:28
  71.2 35.7 %collective-permute-start.24 = (bf16[2,128,512]{2,1,0:T(8,128)(2,1)S(1)}, bf16[2,128,512]{2,1,0:T(8,128)(2,1)S(1)}, u32[]{:S(2)}, u32[]{:S(2)}) collective-permute-start(bf16[2,128,512]{2,1,0:T(8,128)(2,1)S(1)} %get-tuple-element.61), channel_id=1, source_target_pairs={{16,0},{24,8},{32,16},{40,24},{48,32},{56,40},{64,48},{72,56},{80,... | collective-permute-start | bytes 786440 | tf_op jit(solution)/shard_map/ppermute | solution.py:28
  85.1 12.7 %collective-permute-start.23 = (bf16[2,64,512]{2,1,0:T(8,128)(2,1)S(1)}, bf16[2,64,512]{2,1,0:T(8,128)(2,1)S(1)}, u32[]{:S(2)}, u32[]{:S(2)}) collective-permute-start(bf16[2,64,512]{2,1,0:T(8,128)(2,1)S(1)} %get-tuple-element.58), channel_id=1, source_target_pairs={{48,0},{56,8},{112,64},{120,72},{176,128},{184,136},{240,192},{248... | collective-permute-start | bytes 393224 | tf_op jit(solution)/shard_map/ppermute | solution.py:28
  86.4 20.4 %collective-permute-start.25 = (bf16[2,128,512]{2,1,0:T(8,128)(2,1)S(1)}, bf16[2,128,512]{2,1,0:T(8,128)(2,1)S(1)}, u32[]{:S(2)}, u32[]{:S(2)}) collective-permute-start(bf16[2,128,512]{2,1,0:T(8,128)(2,1)S(1)} %get-tuple-element.62), channel_id=1, source_target_pairs={{32,0},{40,8},{48,16},{56,24},{64,32},{72,40},{80,48},{88,56},{96,... | collective-permute-start | bytes 786440 | tf_op jit(solution)/shard_map/ppermute | solution.py:28
  87.7 19.1 %collective-permute-start.26 = (bf16[2,128,512]{2,1,0:T(8,128)(2,1)S(1)}, bf16[2,128,512]{2,1,0:T(8,128)(2,1)S(1)}, u32[]{:S(2)}, u32[]{:S(2)}) collective-permute-start(bf16[2,128,512]{2,1,0:T(8,128)(2,1)S(1)} %get-tuple-element.63), channel_id=1, source_target_pairs={{48,0},{56,8},{64,16},{72,24},{80,32},{88,40},{96,48},{104,56},{11... | collective-permute-start | bytes 786440 | tf_op jit(solution)/shard_map/ppermute | solution.py:28
  89.0 15.9 %collective-permute-start.22 = (bf16[2,64,512]{2,1,0:T(8,128)(2,1)S(1)}, bf16[2,64,512]{2,1,0:T(8,128)(2,1)S(1)}, u32[]{:S(2)}, u32[]{:S(2)}) collective-permute-start(bf16[2,64,512]{2,1,0:T(8,128)(2,1)S(1)} %get-tuple-element.58), channel_id=1, source_target_pairs={{32,0},{40,8},{96,64},{104,72},{160,128},{168,136},{224,192},{232,... | collective-permute-start | bytes 393224 | tf_op jit(solution)/shard_map/ppermute | solution.py:28
  97.8 9.0 %collective-permute-start.21 = (bf16[2,64,512]{2,1,0:T(8,128)(2,1)S(1)}, bf16[2,64,512]{2,1,0:T(8,128)(2,1)S(1)}, u32[]{:S(2)}, u32[]{:S(2)}) collective-permute-start(bf16[2,64,512]{2,1,0:T(8,128)(2,1)S(1)} %get-tuple-element.58), channel_id=1, source_target_pairs={{16,0},{24,8},{80,64},{88,72},{144,128},{152,136},{208,192},{216,2... | collective-permute-start | bytes 393224 | tf_op jit(solution)/shard_map/ppermute | solution.py:28
  104.9 7.2 %collective-permute-start.14 = (bf16[2,64,1024]{2,1,0:T(8,128)(2,1)S(1)}, bf16[2,64,1024]{2,1,0:T(8,128)(2,1)S(1)}, u32[]{:S(2)}, u32[]{:S(2)}) collective-permute-start(bf16[2,64,1024]{2,1,0:T(8,128)(2,1)S(1)} %get-tuple-element.48), channel_id=1, source_target_pairs={{0,8},{8,0},{16,24},{24,16},{32,40},{40,32},{48,56},{56,48},{64,72... | collective-permute-start | bytes 786440 | tf_op jit(solution)/shard_map/ppermute | solution.py:28
  109.5 6.3 %collective-permute-start.29 = (bf16[2,64,512]{2,1,0:T(8,128)(2,1)S(1)}, bf16[2,64,512]{2,1,0:T(8,128)(2,1)S(1)}, u32[]{:S(2)}, u32[]{:S(2)}) collective-permute-start(bf16[2,64,512]{2,1,0:T(8,128)(2,1)S(1)} %get-tuple-element.66), channel_id=1, source_target_pairs={{72,0},{200,128},{328,256},{456,384},{73,1},{201,129},{329,257},{4... | collective-permute-start | bytes 393224 | tf_op jit(solution)/shard_map/ppermute | solution.py:28
  110.8 6.9 %collective-permute-start.28 = (bf16[2,64,512]{2,1,0:T(8,128)(2,1)S(1)}, bf16[2,64,512]{2,1,0:T(8,128)(2,1)S(1)}, u32[]{:S(2)}, u32[]{:S(2)}) collective-permute-start(bf16[2,64,512]{2,1,0:T(8,128)(2,1)S(1)} %get-tuple-element.66), channel_id=1, source_target_pairs={{64,0},{192,128},{320,256},{448,384},{65,1},{193,129},{321,257},{4... | collective-permute-start | bytes 393224 | tf_op jit(solution)/shard_map/ppermute | solution.py:28
  (14 other events, 91.8 us)

commit v3 on v2

--- a/solution.py
+++ b/solution.py
@@ -16,6 +16,8 @@
 HALF_KV = HALF_HEADS * HEAD_DIM
 HALF_FEAT = HALF_HEADS * GROUP * HEAD_DIM
 SCALE = HEAD_DIM**-0.5
+TA = 3
+TB = 2
 LOG2E = 1.4426950408889634
 NEG = -1e30
 NT = (((1,), (1,)), ((), ()))
@@ -32,20 +34,17 @@
     return route(array, "ctx", lambda i: i ^ 1)
 
 
-def attention_kernel(has_head, *refs):
-    meta, gain, q_mine, q_other, g_mine, g_other = refs[:6]
-    refs = refs[6:]
-    if has_head:
-        h_mine, h_other = refs[:2]
-        refs = refs[2:]
+def attention_kernel(tick, meta, gain, keep, recv, *refs):
+    if tick:
+        grads, refs = refs[0], refs[1:]
     pairs, strided = refs[:4], refs[4:8]
     refs = refs[8:]
-    if has_head:
-        for old, new in zip(refs[:4], refs[5:9]):
+    if tick:
+        for old, new in zip(refs[:7], refs[8:15]):
             new[0] = old[...]
-        refs = refs[4:]
-        refs = refs[:1] + tuple(r.at[1] for r in refs[1:5]) + refs[5:]
-    both, other, back1, back2, back3, own, part0, part1, part2, part3 = refs
+        refs = refs[7:]
+        refs = refs[:1] + tuple(r.at[1] for r in refs[1:8]) + refs[8:]
+    both, other, back1, back2, back3, part1, part2, part3, own, part0 = refs
     backs = (own, back1, back2, back3)
     parts = (part0, part1, part2, part3)
     index = meta[0]
@@ -55,15 +54,17 @@
         window = meta[2 + h]
         stride = meta[4 + h]
         q_rows, g_rows = [], []
-        for half, (q_ref, g_ref) in enumerate(((q_mine, g_mine), (q_other, g_other))):
+        for half, source in enumerate((keep, recv)):
             for j in range(GROUP):
+                near = slice(j * HEAD_DIM, (j + 1) * HEAD_DIM)
                 at = slice((h * GROUP + j) * HEAD_DIM, (h * GROUP + j + 1) * HEAD_DIM)
-                q_rows.append((q_ref[:, at].astype(jnp.float32) * gain[:, at]).astype(jnp.bfloat16))
-                grad = g_ref[:, at]
-                if has_head:
-                    top = (h_mine, h_other)[half][:, at]
-                    grad = jnp.where(meta[1] == 1, top, grad)
-                g_rows.append(grad)
+                rows = source[2 + 2 * tick + h, :, near].astype(jnp.float32)
+                q_rows.append((rows * gain[:, at]).astype(jnp.bfloat16))
+                if tick:
+                    top = source[8 + h, :, near]
+                    g_rows.append(jnp.where(meta[1] == 1, top, grads[half, :, at]))
+                else:
+                    g_rows.append(source[6 + h, :, near])
         q = jnp.concatenate(q_rows, axis=0)
         g = jnp.concatenate(g_rows, axis=0)
         k_at = slice(h * HEAD_DIM, (h + 1) * HEAD_DIM)
@@ -139,28 +140,24 @@
         return pl.BlockSpec((None,) + rest, lambda n: (lead, 0, 0))
 
     args = [meta, gain, keep, recv]
-    specs = [SCALAR, WHOLE, at(tick, BLK, HALF_FEAT), at(tick, BLK, HALF_FEAT)]
-    if grads is None:
-        args += [keep, recv]
-        specs += [at(2, BLK, HALF_FEAT), at(2, BLK, HALF_FEAT)]
-    else:
-        args += [grads, grads, keep, recv]
-        specs += [at(0, BLK, HALF_FEAT), at(1, BLK, HALF_FEAT)]
-        specs += [at(3, BLK, HALF_FEAT), at(3, BLK, HALF_FEAT)]
+    specs = [SCALAR, WHOLE, WHOLE, WHOLE]
+    if tick:
+        args.append(grads)
+        specs.append(WHOLE)
     args += list(pairs) + list(strided)
     specs += [at(tick, 2 * BLK, WIDE)] * 4 + [at(tick, BLK, WIDE)] * 4
     bf16, f32 = jnp.bfloat16, jnp.float32
     out_shape = [shape((2, BLK, HALF_FEAT), bf16)]
-    if earlier is None:
-        out_shape += [shape((BLK, HALF_FEAT), bf16)] + [shape((2 * BLK, WIDE), bf16)] * 3
-    else:
+    lead = (2,) if tick else ()
+    if tick:
         args += earlier
-        specs += [WHOLE] * 4
-        out_shape += [shape((2, BLK, HALF_FEAT), bf16)] + [shape((2, 2 * BLK, WIDE), bf16)] * 3
+        specs += [WHOLE] * 7
+    out_shape.append(shape(lead + (BLK, HALF_FEAT), bf16))
+    out_shape += [shape(lead + (2 * BLK, WIDE), bf16)] * 3
+    out_shape += [shape(lead + (BLK, WIDE), bf16)] * 3
     out_shape += [shape((2 * BLK, WIDE), f32), shape((BLK, WIDE), f32)]
-    out_shape += [shape((BLK, WIDE), bf16)] * 3
     return pl.pallas_call(
-        functools.partial(attention_kernel, grads is not None),
+        functools.partial(attention_kernel, tick),
         out_shape=out_shape,
         grid=(1,),
         in_specs=specs,
@@ -186,33 +183,34 @@
     )(*args)
 
 
-def column_sum(*refs):
-    wide_out, send_out = refs[8:]
-    for t in range(2):
-        total = refs[4 * t][...]
-        for s in range(1, 4):
-            total = total + refs[4 * t + s][...].astype(jnp.float32)
+def column_sum(own0, own1, x1, x2, x3, wide_out, send_out):
+    for t, own in enumerate((own0, own1)):
+        total = own[...]
+        for x in (x1, x2, x3):
+            total = total + x[t].astype(jnp.float32)
         wide_out[t] = total
         send_out[t] = total.astype(jnp.bfloat16)
 
 
-def split_keys(meta, keys, values, keep, give):
+def split_all(meta, keys, values, inputs, first, head, keep, give, kv_keep, kv_give):
     swap = meta[0] % 2 == 1
     for source, at in ((keys, 0), (values, HALF_KV)):
         low, high = source[0, :, :, :HALF_KV], source[0, :, :, HALF_KV:]
-        keep[:, :, at : at + HALF_KV] = jnp.where(swap, high, low)
-        give[:, :, at : at + HALF_KV] = jnp.where(swap, low, high)
-
-
-def split_rows(meta, inputs, first, head, keep, give):
-    swap = meta[0] % 2 == 1
+        mine, far = jnp.where(swap, high, low), jnp.where(swap, low, high)
+        keep[:2, :, at : at + HALF_KV] = mine
+        give[:2, :, at : at + HALF_KV] = far
+        kv_keep[:, :, at : at + HALF_KV] = mine
+        kv_give[:, :, at : at + HALF_KV] = far
     for n, source in enumerate((inputs.at[0, 0], inputs.at[0, 1], first.at[0], head.at[0])):
-        low, high = source[:, :HALF_FEAT], source[:, HALF_FEAT:]
-        keep[n] = jnp.where(swap, high, low)
-        give[n] = jnp.where(swap, low, high)
+        for h in range(HALF_HEADS):
+            low = source[:, h * WIDE : (h + 1) * WIDE]
+            high = source[:, HALF_FEAT + h * WIDE : HALF_FEAT + (h + 1) * WIDE]
+            keep[2 + 2 * n + h] = jnp.where(swap, high, low)
+            give[2 + 2 * n + h] = jnp.where(swap, low, high)
 
 
 def pair_keys(meta, keep, recv, up_low, up_high, pair, start):
+    keep, recv = keep.at[:2], recv.at[:2]
     core = meta[0] % 2
     even = (meta[0] // 8) % 2 == 0
     pair[:, :BLK] = keep[...]
@@ -222,9 +220,16 @@
     start[...] = jnp.where(even, near, above)
 
 
+def choose(meta, start, x1, x2, x3, out):
+    place = (meta[0] // 2) % 4
+    near = jnp.where(place == 0, start[...], x1[...])
+    far = jnp.where(place == 2, x2[...], x3[...])
+    out[...] = jnp.where(place < 2, near, far)
+
+
 def row_sum(meta, *refs):
-    total, x1, x2, x3, own0, own1, back1, back2, back3 = refs[:9]
-    mine_out, other_out, strided_out = refs[9:]
+    total, x1, x2, x3, own0, own1, back1, back2, back3, far_rows = refs[:10]
+    mine_out, swap_out, strided_out = refs[10:]
     index = meta[0]
     owner = (index // 2) % 4 == 0
     even = (index // 8) % 2 == 0
@@ -239,26 +244,23 @@
         for back in (back1, back2, back3):
             near = near + back[t].astype(jnp.float32)
         mine_out[t] = near[:BLK] + first * strided
-        other_out[t] = (near[BLK:] + second * strided).astype(jnp.bfloat16)
-
-
-def finish(meta, mine, other, low, high, keys_out, values_out):
+        swap_out[t, :, :HALF_FEAT] = far_rows[t]
+        swap_out[t, :, HALF_FEAT:] = (near[BLK:] + second * strided).astype(jnp.bfloat16)
+
+
+def finish(meta, mine, swapped, low, high, mine0, mine1, rows_out, keys_out, values_out):
     swap = meta[0] % 2 == 1
-    for t in range(2):
+    for t, rows in enumerate((mine0, mine1)):
+        other = swapped[t, :, HALF_FEAT:].astype(jnp.float32)
         own = (mine[t] + low[t].astype(jnp.float32)).astype(jnp.bfloat16)
-        far = (other[t].astype(jnp.float32) + high[t].astype(jnp.float32)).astype(jnp.bfloat16)
+        far = (other + high[t].astype(jnp.float32)).astype(jnp.bfloat16)
         left, right = jnp.where(swap, far, own), jnp.where(swap, own, far)
         for out, at in ((keys_out, 0), (values_out, HALF_KV)):
             out[0, t, :, :HALF_KV] = left[:, at : at + HALF_KV]
             out[0, t, :, HALF_KV:] = right[:, at : at + HALF_KV]
-
-
-def join_rows(meta, mine0, mine1, other, out):
-    swap = meta[0] % 2 == 1
-    for t, mine in enumerate((mine0, mine1)):
-        near, far = mine[0], other[t]
-        out[0, t, :, :HALF_FEAT] = jnp.where(swap, far, near)
-        out[0, t, :, HALF_FEAT:] = jnp.where(swap, near, far)
+        near, far = rows[0], swapped[t, :, :HALF_FEAT]
+        rows_out[0, t, :, :HALF_FEAT] = jnp.where(swap, far, near)
+        rows_out[0, t, :, HALF_FEAT:] = jnp.where(swap, near, far)
 
 
 def body(inputs, saved_keys, saved_values, query_gain, first_grads, head_grads, window, stride):
@@ -274,25 +276,30 @@
 
     spot = index.astype(jnp.int32).reshape(1)
     half = shape((2, BLK, WIDE), bf16)
-    kv_keep, kv_give = simple(split_keys, [half, half], [spot, saved_keys, saved_values])
-    kv_recv = sibling(kv_give)
+    ten = shape((10, BLK, WIDE), bf16)
+    keep, give, kv_keep, kv_give = simple(
+        split_all,
+        [ten, ten, half, half],
+        [spot, saved_keys, saved_values, inputs, first_grads, head_grads],
+    )
+    recv = sibling(give)
     up_low = ctx(kv_keep, lambda i: i + 8, lambda i: i % STRIDE == 0)
     up_high = ctx(kv_give, lambda i: i + 9, lambda i: i % STRIDE == 0)
     pair, start = simple(
         pair_keys,
         [shape((2, 2 * BLK, WIDE), bf16), half],
-        [spot, kv_keep, kv_recv, up_low, up_high],
-    )
-    chosen = start
-    for d in range(1, 4):
-        across = ctx(start, lambda i: i + 2 * d, lambda i: (i // 2) % 4 == 0)
-        chosen = jnp.where(place == d, across, chosen)
+        [spot, keep, recv, up_low, up_high],
+    )
+    across = [ctx(start, lambda i: i + 2 * d, lambda i: (i // 2) % 4 == 0) for d in range(1, 4)]
+    (chosen,) = simple(choose, [half], [spot, start] + across)
     pairs = [pair] + [ctx(pair, lambda i: i + 2 * d) for d in range(1, 4)]
-    strided = [chosen] + [ctx(chosen, lambda i: i + STRIDE * s) for s in range(1, 4)]
-
-    four = shape((4, BLK, HALF_FEAT), bf16)
-    keep, give = simple(split_rows, [four, four], [spot, inputs, first_grads, head_grads])
-    recv = sibling(give)
+    strided = [chosen]
+    for s in range(1, 4):
+        sent = chosen
+        if s == 1:
+            sent, pairs[TA] = lax.optimization_barrier((chosen, pairs[TA]))
+        strided.append(ctx(sent, lambda i: i + STRIDE * s))
+
     gain = jnp.where(core == 0, query_gain[:, :HALF_FEAT], query_gain[:, HALF_FEAT:])
     heads = jnp.where(core == 0, window[0, :2], window[0, 2:])
     steps = jnp.where(core == 0, stride[0, :2], stride[0, 2:])
@@ -301,27 +308,32 @@
 
     first = attention(0, meta, gain, keep, recv, None, pairs, strided, None)
     grads = route(first[0], "pp", lambda i: i - 1)
-    second = attention(1, meta, gain, keep, recv, grads, pairs, strided, first[1:5])
-    columns = []
-    for outs in (first, second):
-        columns.append(outs[6])
-        columns += [ctx(outs[6 + s], lambda i: i - STRIDE * s) for s in range(1, 4)]
+    second = attention(1, meta, gain, keep, recv, grads, pairs, strided, first[1:8])
+    columns = [first[9], second[9]]
+    columns += [ctx(second[4 + s], lambda i: i - STRIDE * s) for s in range(1, 4)]
     backs = [ctx(second[1 + d], lambda i: i - 2 * d) for d in range(1, 4)]
-    other_rows = sibling(second[1])
 
     wide = shape((2, BLK, WIDE), f32)
     total, send = simple(column_sum, [wide, half], columns, 0)
-    rows = [ctx(send, lambda i: i - 2 * d, lambda i: (i // 2) % 4 == d) for d in range(1, 4)]
-    mine, other, down = simple(
-        row_sum, [wide, half, half], [spot, total] + rows + [first[5], second[5]] + backs
-    )
-    other = sibling(other)
+    rows = []
+    for d in range(1, 4):
+        sent = send
+        if d == 1:
+            sent, backs[TB] = lax.optimization_barrier((send, backs[TB]))
+        rows.append(ctx(sent, lambda i: i - 2 * d, lambda i: (i // 2) % 4 == d))
+    mine, swap, down = simple(
+        row_sum,
+        [wide, shape((2, BLK, HALF_FEAT + WIDE), bf16), half],
+        [spot, total] + rows + [first[8], second[8]] + backs + [second[1]],
+    )
+    swapped = sibling(swap)
     low = ctx(down, lambda i: i - 8, lambda i: i % STRIDE == 8)
     high = ctx(down, lambda i: i - 9, lambda i: i % STRIDE == 9)
     keys_shape = shape(saved_keys.shape, bf16)
-    key_grads, value_grads = simple(finish, [keys_shape, keys_shape], [spot, mine, other, low, high])
-    (grads_out,) = simple(
-        join_rows, [shape(inputs.shape, bf16)], [spot, first[0], second[0], other_rows]
+    grads_out, key_grads, value_grads = simple(
+        finish,
+        [shape(inputs.shape, bf16), keys_shape, keys_shape],
+        [spot, mine, swapped, low, high, first[0], second[0]],
     )
     return grads_out, key_grads, value_grads
 

time: 119 us -> 121 us (1.017)
  the two profiles are of different devices: /device:TPU:192 before, /device:TPU:224 now
where the time goes in v3:
time: 121 us
  starting transfers between devices  65.8 us (54%)
  waiting for transfers between devices  39.4 us (33%)
  Pallas kernels  9.44 us (8%)
  local copies, waits for them, and re-layouts  4.76 us (4%)
    ppermute x25, starting transfers between devices, route(): lax.ppermute(array, axis, [(a, b) for a, b in pairs if b is not None and...  65.8 us
    ppermute x25, waiting for transfers between devices, route(): lax.ppermute(array, axis, [(a, b) for a, b in pairs if b is not None and...  39.4 us
    pallas_call x2, Pallas kernels, attention(): pl.pallas_call(functools.partial(attention_kernel, tick), out_shape=out_s...  8 us
    unnamed x16, local copies, waits for them, and re-layouts  4.76 us
  transfers between devices with their start and end apart: 25, of which 11 were waited for; matrix products, arithmetic and copies ran while one was open for 0% of the time, Pallas kernels for 0%

profile of v3, /device:TPU:224, one launch (start us, length us, event | category | flops | bytes accessed | tf_op | source)
XLA Modules:
  0.0 120.6 jit_solution(15803051982987355560)
XLA Ops:
  5.5 1.9 %collective-permute-start = (bf16[10,64,512]{2,1,0:T(8,128)(2,1)S(1)}, bf16[10,64,512]{2,1,0:T(8,128)(2,1)S(1)}, u32[]{:S(2)}, u32[]{:S(2)}) collective-permute-start(bf16[10,64,512]{2,1,0:T(8,128)(2,1)S(1)} %get-tuple-element.39), channel_id=1, source_target_pairs={{0,8},{8,0},{16,24},{24,16},{32,40},{40,32},{48,56},{56,48},{64,72... | collective-permute-start | bytes 1966088 | tf_op jit(solution)/shard_map/ppermute | solution.py:30
  7.4 2.6 %collective-permute-start.1 = (bf16[2,64,512]{2,1,0:T(8,128)(2,1)S(1)}, bf16[2,64,512]{2,1,0:T(8,128)(2,1)S(1)}, u32[]{:S(2)}, u32[]{:S(2)}) collective-permute-start(bf16[2,64,512]{2,1,0:T(8,128)(2,1)S(1)} %get-tuple-element.40), channel_id=1, source_target_pairs={{0,64},{128,192},{256,320},{384,448},{1,65},{129,193},{257,321},{3... | collective-permute-start | bytes 393224 | tf_op jit(solution)/shard_map/ppermute | solution.py:30
  12.5 1.4 %collective-permute-done.2.up_high = bf16[2,64,512]{2,1,0:T(8,128)(2,1)S(1)} collective-permute-done((bf16[2,64,512]{2,1,0:T(8,128)(2,1)S(1)}, bf16[2,64,512]{2,1,0:T(8,128)(2,1)S(1)}, u32[]{:S(2)}, u32[]{:S(2)}) %collective-permute-start.2) | collective-permute-done | bytes 131104 | tf_op jit(solution)/shard_map/ppermute | solution.py:30
  14.0 1.9 %collective-permute-start.8 = (bf16[2,128,512]{2,1,0:T(8,128)(2,1)S(1)}, bf16[2,128,512]{2,1,0:T(8,128)(2,1)S(1)}, u32[]{:S(2)}, u32[]{:S(2)}) collective-permute-start(bf16[2,128,512]{2,1,0:T(8,128)(2,1)S(1)} %get-tuple-element.42.refs_0_.refs_1_), channel_id=1, source_target_pairs={{0,48},{8,56},{16,64},{24,72},{32,80},{40,88},{48,96},{56,104},{64... | collective-permute-start | bytes 786440 | tf_op jit(solution)/shard_map/ppermute | solution.py:30
  18.5 3.2 %collective-permute-start.5 = (bf16[2,64,512]{2,1,0:T(8,128)(2,1)S(1)}, bf16[2,64,512]{2,1,0:T(8,128)(2,1)S(1)}, u32[]{:S(2)}, u32[]{:S(2)}) collective-permute-start(bf16[2,64,512]{2,1,0:T(8,128)(2,1)S(1)} %get-tuple-element.43.start), channel_id=1, source_target_pairs={{0,16},{8,24},{64,80},{72,88},{128,144},{136,152},{192,208},{200,2... | collective-permute-start | bytes 393224 | tf_op jit(solution)/shard_map/ppermute | solution.py:30
  21.7 1.9 %collective-permute-start.4 = (bf16[2,128,512]{2,1,0:T(8,128)(2,1)S(1)}, bf16[2,128,512]{2,1,0:T(8,128)(2,1)S(1)}, u32[]{:S(2)}, u32[]{:S(2)}) collective-permute-start(bf16[2,128,512]{2,1,0:T(8,128)(2,1)S(1)} %get-tuple-element.42.refs_0_.refs_1_), channel_id=1, source_target_pairs={{0,32},{8,40},{16,48},{24,56},{32,64},{40,72},{48,80},{56,88},{64,... | collective-permute-start | bytes 786440 | tf_op jit(solution)/shard_map/ppermute | solution.py:30
  23.7 1.9 %collective-permute-start.3 = (bf16[2,128,512]{2,1,0:T(8,128)(2,1)S(1)}, bf16[2,128,512]{2,1,0:T(8,128)(2,1)S(1)}, u32[]{:S(2)}, u32[]{:S(2)}) collective-permute-start(bf16[2,128,512]{2,1,0:T(8,128)(2,1)S(1)} %get-tuple-element.42.refs_0_.refs_1_), channel_id=1, source_target_pairs={{0,16},{8,24},{16,32},{24,40},{32,48},{40,56},{48,64},{56,72},{64,... | collective-permute-start | bytes 786440 | tf_op jit(solution)/shard_map/ppermute | solution.py:30
  27.7 3.3 %collective-permute-start.9 = (bf16[2,64,512]{2,1,0:T(8,128)(2,1)S(1)}, bf16[2,64,512]{2,1,0:T(8,128)(2,1)S(1)}, u32[]{:S(2)}, u32[]{:S(2)}) collective-permute-start(bf16[2,64,512]{2,1,0:T(8,128)(2,1)S(1)} %choose.1.refs_4_.refs_5_), channel_id=1, source_target_pairs={{0,128},{8,136},{16,144},{24,152},{32,160},{40,168},{48,176},{56,1... | collective-permute-start | bytes 393224 | tf_op jit(solution)/shard_map/ppermute | solution.py:30
  31.2 7.1 %collective-permute-done.10.refs_6_.refs_7_ = bf16[2,64,512]{2,1,0:T(8,128)(2,1)S(1)} collective-permute-done((bf16[2,64,512]{2,1,0:T(8,128)(2,1)S(1)}, bf16[2,64,512]{2,1,0:T(8,128)(2,1)S(1)}, u32[]{:S(2)}, u32[]{:S(2)}) %collective-permute-start.10) | collective-permute-done | bytes 131104 | tf_op jit(solution)/shard_map/ppermute | solution.py:30
  39.4 3.5 %collective-permute-done.9.refs_5_.refs_6_ = bf16[2,64,512]{2,1,0:T(8,128)(2,1)S(1)} collective-permute-done((bf16[2,64,512]{2,1,0:T(8,128)(2,1)S(1)}, bf16[2,64,512]{2,1,0:T(8,128)(2,1)S(1)}, u32[]{:S(2)}, u32[]{:S(2)}) %collective-permute-start.9) | collective-permute-done | bytes 131104 | tf_op jit(solution)/shard_map/ppermute | solution.py:30
  42.9 4.0 %attention.2 = (bf16[2,64,1024]{2,1,0:T(8,128)(2,1)S(1)}, bf16[64,1024]{1,0:T(8,128)(2,1)S(1)}, bf16[128,512]{1,0:T(8,128)(2,1)S(1)}, bf16[128,512]{1,0:T(8,128)...) custom-call(s32[6]{0:T(128)S(1)} %pad_add_fusion.meta, ...), custom_call_target="tpu_custom_call" | custom-call | flops 1006632960 | bytes 4194304 | tf_op jit(solution)/shard_map/attention/pallas_call | solution.py:159
  46.9 1.9 %collective-permute-start.12 = (bf16[2,64,1024]{2,1,0:T(8,128)(2,1)S(1)}, bf16[2,64,1024]{2,1,0:T(8,128)(2,1)S(1)}, u32[]{:S(2)}, u32[]{:S(2)}) collective-permute-start(bf16[2,64,1024]{2,1,0:T(8,128)(2,1)S(1)} %get-tuple-element.47.mine0), channel_id=1, source_target_pairs={{1,0},{2,1},{3,2},{4,3},{5,4},{6,5},{7,6},{9,8},{10,9},{11,10},{12... | collective-permute-start | bytes 786440 | tf_op jit(solution)/shard_map/ppermute | solution.py:30
  48.8 9.8 %collective-permute-done.12.refs_0_ = bf16[2,64,1024]{2,1,0:T(8,128)(2,1)S(1)} collective-permute-done((bf16[2,64,1024]{2,1,0:T(8,128)(2,1)S(1)}, bf16[2,64,1024]{2,1,0:T(8,128)(2,1)S(1)}, u32[]{:S(2)}, u32[]{:S(2)}) %collective-permute-start.12) | collective-permute-done | bytes 262176 | tf_op jit(solution)/shard_map/ppermute | solution.py:30
  58.6 4.0 %attention.3 = (bf16[2,64,1024]{2,1,0:T(8,128)(2,1)S(1)}, bf16[2,64,1024]{2,1,0:T(8,128)(2,1)S(1)}, bf16[2,128,512]{2,1,0:T(8,128)(2,1)S(1)}, bf16[2,128,512]{2,...) custom-call(s32[6]{0:T(128)S(1)} %pad_add_fusion.meta, ...), custom_call_target="tpu_custom_call" | custom-call | flops 1006632960 | bytes 4194304 | tf_op jit(solution)/shard_map/attention/pallas_call | solution.py:159
  62.7 5.4 %collective-permute-start.16 = (bf16[2,128,512]{2,1,0:T(8,128)(2,1)S(1)}, bf16[2,128,512]{2,1,0:T(8,128)(2,1)S(1)}, u32[]{:S(2)}, u32[]{:S(2)}) collective-permute-start(bf16[2,128,512]{2,1,0:T(8,128)(2,1)S(1)} %get-tuple-element.61), channel_id=1, source_target_pairs={{48,0},{56,8},{64,16},{72,24},{80,32},{88,40},{96,48},{104,56},{11... | collective-permute-start | bytes 786440 | tf_op jit(solution)/shard_map/ppermute | solution.py:30
  68.0 1.9 %collective-permute-start.13 = (bf16[2,64,512]{2,1,0:T(8,128)(2,1)S(1)}, bf16[2,64,512]{2,1,0:T(8,128)(2,1)S(1)}, u32[]{:S(2)}, u32[]{:S(2)}) collective-permute-start(bf16[2,64,512]{2,1,0:T(8,128)(2,1)S(1)} %get-tuple-element.56), channel_id=1, source_target_pairs={{128,0},{136,8},{144,16},{152,24},{160,32},{168,40},{176,48},{184,... | collective-permute-start | bytes 393224 | tf_op jit(solution)/shard_map/ppermute | solution.py:30
  72.0 9.2 %collective-permute-start.20 = (bf16[2,128,512]{2,1,0:T(8,128)(2,1)S(1)}, bf16[2,128,512]{2,1,0:T(8,128)(2,1)S(1)}, u32[]{:S(2)}, u32[]{:S(2)}) collective-permute-start(bf16[2,128,512]{2,1,0:T(8,128)(2,1)S(1)} %get-tuple-element.65), channel_id=1, source_target_pairs={{16,0},{24,8},{32,16},{40,24},{48,32},{56,40},{64,48},{72,56},{80,... | collective-permute-start | bytes 786440 | tf_op jit(solution)/shard_map/ppermute | solution.py:30
  81.2 4.0 %collective-permute-done.13.x1 = bf16[2,64,512]{2,1,0:T(8,128)(2,1)S(1)} collective-permute-done((bf16[2,64,512]{2,1,0:T(8,128)(2,1)S(1)}, bf16[2,64,512]{2,1,0:T(8,128)(2,1)S(1)}, u32[]{:S(2)}, u32[]{:S(2)}) %collective-permute-start.13) | collective-permute-done | bytes 131104 | tf_op jit(solution)/shard_map/ppermute | solution.py:30
  85.1 14.4 %collective-permute-start.21 = (bf16[2,128,512]{2,1,0:T(8,128)(2,1)S(1)}, bf16[2,128,512]{2,1,0:T(8,128)(2,1)S(1)}, u32[]{:S(2)}, u32[]{:S(2)}) collective-permute-start(bf16[2,128,512]{2,1,0:T(8,128)(2,1)S(1)} %get-tuple-element.66), channel_id=1, source_target_pairs={{32,0},{40,8},{48,16},{56,24},{64,32},{72,40},{80,48},{88,56},{96,... | collective-permute-start | bytes 786440 | tf_op jit(solution)/shard_map/ppermute | solution.py:30
  103.5 4.2 %collective-permute-done.19.refs_3_ = bf16[2,64,512]{2,1,0:T(8,128)(2,1)S(1)} collective-permute-done((bf16[2,64,512]{2,1,0:T(8,128)(2,1)S(1)}, bf16[2,64,512]{2,1,0:T(8,128)(2,1)S(1)}, u32[]{:S(2)}, u32[]{:S(2)}) %collective-permute-start.19) | collective-permute-done | bytes 131104 | tf_op jit(solution)/shard_map/ppermute | solution.py:30
  107.7 1.6 %collective-permute-done.18.refs_2_ = bf16[2,64,512]{2,1,0:T(8,128)(2,1)S(1)} collective-permute-done((bf16[2,64,512]{2,1,0:T(8,128)(2,1)S(1)}, bf16[2,64,512]{2,1,0:T(8,128)(2,1)S(1)}, u32[]{:S(2)}, u32[]{:S(2)}) %collective-permute-start.18) | collective-permute-done | bytes 131104 | tf_op jit(solution)/shard_map/ppermute | solution.py:30
  109.5 1.9 %collective-permute-start.22 = (bf16[2,64,1536]{2,1,0:T(8,128)(2,1)S(1)}, bf16[2,64,1536]{2,1,0:T(8,128)(2,1)S(1)}, u32[]{:S(2)}, u32[]{:S(2)}) collective-permute-start(bf16[2,64,1536]{2,1,0:T(8,128)(2,1)S(1)} %get-tuple-element.70), channel_id=1, source_target_pairs={{0,8},{8,0},{16,24},{24,16},{32,40},{40,32},{48,56},{56,48},{64,72... | collective-permute-start | bytes 1179656 | tf_op jit(solution)/shard_map/ppermute | solution.py:30
  114.1 3.7 %collective-permute-done.24.high = bf16[2,64,512]{2,1,0:T(8,128)(2,1)S(1)} collective-permute-done((bf16[2,64,512]{2,1,0:T(8,128)(2,1)S(1)}, bf16[2,64,512]{2,1,0:T(8,128)(2,1)S(1)}, u32[]{:S(2)}, u32[]{:S(2)}) %collective-permute-start.24) | collective-permute-done | bytes 131104 | tf_op jit(solution)/shard_map/ppermute | solution.py:30
  117.8 1.9 %collective-permute-done.23.low = bf16[2,64,512]{2,1,0:T(8,128)(2,1)S(1)} collective-permute-done((bf16[2,64,512]{2,1,0:T(8,128)(2,1)S(1)}, bf16[2,64,512]{2,1,0:T(8,128)(2,1)S(1)}, u32[]{:S(2)}, u32[]{:S(2)}) %collective-permute-start.23) | collective-permute-done | bytes 131104 | tf_op jit(solution)/shard_map/ppermute | solution.py:30
  (53 shorter events, 22.9 us)
Async XLA Ops:
  5.5 8.4 %collective-permute-start = (bf16[10,64,512]{2,1,0:T(8,128)(2,1)S(1)}, bf16[10,64,512]{2,1,0:T(8,128)(2,1)S(1)}, u32[]{:S(2)}, u32[]{:S(2)}) collective-permute-start(bf16[10,64,512]{2,1,0:T(8,128)(2,1)S(1)} %get-tuple-element.39), channel_id=1, source_target_pairs={{0,8},{8,0},{16,24},{24,16},{32,40},{40,32},{48,56},{56,48},{64,72... | collective-permute-start | bytes 1966088 | tf_op jit(solution)/shard_map/ppermute | solution.py:30
  7.4 5.1 %collective-permute-start.1 = (bf16[2,64,512]{2,1,0:T(8,128)(2,1)S(1)}, bf16[2,64,512]{2,1,0:T(8,128)(2,1)S(1)}, u32[]{:S(2)}, u32[]{:S(2)}) collective-permute-start(bf16[2,64,512]{2,1,0:T(8,128)(2,1)S(1)} %get-tuple-element.40), channel_id=1, source_target_pairs={{0,64},{128,192},{256,320},{384,448},{1,65},{129,193},{257,321},{3... | collective-permute-start | bytes 393224 | tf_op jit(solution)/shard_map/ppermute | solution.py:30
  14.0 13.7 %collective-permute-start.8 = (bf16[2,128,512]{2,1,0:T(8,128)(2,1)S(1)}, bf16[2,128,512]{2,1,0:T(8,128)(2,1)S(1)}, u32[]{:S(2)}, u32[]{:S(2)}) collective-permute-start(bf16[2,128,512]{2,1,0:T(8,128)(2,1)S(1)} %get-tuple-element.42.refs_0_.refs_1_), channel_id=1, source_target_pairs={{0,48},{8,56},{16,64},{24,72},{32,80},{40,88},{48,96},{56,104},{64... | collective-permute-start | bytes 786440 | tf_op jit(solution)/shard_map/ppermute | solution.py:30
  15.9 7.8 %collective-permute-start.7 = (bf16[2,64,512]{2,1,0:T(8,128)(2,1)S(1)}, bf16[2,64,512]{2,1,0:T(8,128)(2,1)S(1)}, u32[]{:S(2)}, u32[]{:S(2)}) collective-permute-start(bf16[2,64,512]{2,1,0:T(8,128)(2,1)S(1)} %get-tuple-element.43.start), channel_id=1, source_target_pairs={{0,48},{8,56},{64,112},{72,120},{128,176},{136,184},{192,240},{200... | collective-permute-start | bytes 393224 | tf_op jit(solution)/shard_map/ppermute | solution.py:30
  17.2 8.4 %collective-permute-start.6 = (bf16[2,64,512]{2,1,0:T(8,128)(2,1)S(1)}, bf16[2,64,512]{2,1,0:T(8,128)(2,1)S(1)}, u32[]{:S(2)}, u32[]{:S(2)}) collective-permute-start(bf16[2,64,512]{2,1,0:T(8,128)(2,1)S(1)} %get-tuple-element.43.start), channel_id=1, source_target_pairs={{0,32},{8,40},{64,96},{72,104},{128,160},{136,168},{192,224},{200,... | collective-permute-start | bytes 393224 | tf_op jit(solution)/shard_map/ppermute | solution.py:30
  18.5 7.1 %collective-permute-start.5 = (bf16[2,64,512]{2,1,0:T(8,128)(2,1)S(1)}, bf16[2,64,512]{2,1,0:T(8,128)(2,1)S(1)}, u32[]{:S(2)}, u32[]{:S(2)}) collective-permute-start(bf16[2,64,512]{2,1,0:T(8,128)(2,1)S(1)} %get-tuple-element.43.start), channel_id=1, source_target_pairs={{0,16},{8,24},{64,80},{72,88},{128,144},{136,152},{192,208},{200,2... | collective-permute-start | bytes 393224 | tf_op jit(solution)/shard_map/ppermute | solution.py:30
  21.7 16.6 %collective-permute-start.4 = (bf16[2,128,512]{2,1,0:T(8,128)(2,1)S(1)}, bf16[2,128,512]{2,1,0:T(8,128)(2,1)S(1)}, u32[]{:S(2)}, u32[]{:S(2)}) collective-permute-start(bf16[2,128,512]{2,1,0:T(8,128)(2,1)S(1)} %get-tuple-element.42.refs_0_.refs_1_), channel_id=1, source_target_pairs={{0,32},{8,40},{16,48},{24,56},{32,64},{40,72},{48,80},{56,88},{64,... | collective-permute-start | bytes 786440 | tf_op jit(solution)/shard_map/ppermute | solution.py:30
  23.7 15.7 %collective-permute-start.3 = (bf16[2,128,512]{2,1,0:T(8,128)(2,1)S(1)}, bf16[2,128,512]{2,1,0:T(8,128)(2,1)S(1)}, u32[]{:S(2)}, u32[]{:S(2)}) collective-permute-start(bf16[2,128,512]{2,1,0:T(8,128)(2,1)S(1)} %get-tuple-element.42.refs_0_.refs_1_), channel_id=1, source_target_pairs={{0,16},{8,24},{16,32},{24,40},{32,48},{40,56},{48,64},{56,72},{64,... | collective-permute-start | bytes 786440 | tf_op jit(solution)/shard_map/ppermute | solution.py:30
  25.7 5.5 %collective-permute-start.11 = (bf16[2,64,512]{2,1,0:T(8,128)(2,1)S(1)}, bf16[2,64,512]{2,1,0:T(8,128)(2,1)S(1)}, u32[]{:S(2)}, u32[]{:S(2)}) collective-permute-start(bf16[2,64,512]{2,1,0:T(8,128)(2,1)S(1)} %choose.1.refs_4_.refs_5_), channel_id=1, source_target_pairs={{0,384},{8,392},{16,400},{24,408},{32,416},{40,424},{48,432},{56,4... | collective-permute-start | bytes 393224 | tf_op jit(solution)/shard_map/ppermute | solution.py:30
  26.4 12.0 %collective-permute-start.10 = (bf16[2,64,512]{2,1,0:T(8,128)(2,1)S(1)}, bf16[2,64,512]{2,1,0:T(8,128)(2,1)S(1)}, u32[]{:S(2)}, u32[]{:S(2)}) collective-permute-start(bf16[2,64,512]{2,1,0:T(8,128)(2,1)S(1)} %choose.1.refs_4_.refs_5_), channel_id=1, source_target_pairs={{0,256},{8,264},{16,272},{24,280},{32,288},{40,296},{48,304},{56,3... | collective-permute-start | bytes 393224 | tf_op jit(solution)/shard_map/ppermute | solution.py:30
  27.7 15.2 %collective-permute-start.9 = (bf16[2,64,512]{2,1,0:T(8,128)(2,1)S(1)}, bf16[2,64,512]{2,1,0:T(8,128)(2,1)S(1)}, u32[]{:S(2)}, u32[]{:S(2)}) collective-permute-start(bf16[2,64,512]{2,1,0:T(8,128)(2,1)S(1)} %choose.1.refs_4_.refs_5_), channel_id=1, source_target_pairs={{0,128},{8,136},{16,144},{24,152},{32,160},{40,168},{48,176},{56,1... | collective-permute-start | bytes 393224 | tf_op jit(solution)/shard_map/ppermute | solution.py:30
  46.9 11.7 %collective-permute-start.12 = (bf16[2,64,1024]{2,1,0:T(8,128)(2,1)S(1)}, bf16[2,64,1024]{2,1,0:T(8,128)(2,1)S(1)}, u32[]{:S(2)}, u32[]{:S(2)}) collective-permute-start(bf16[2,64,1024]{2,1,0:T(8,128)(2,1)S(1)} %get-tuple-element.47.mine0), channel_id=1, source_target_pairs={{1,0},{2,1},{3,2},{4,3},{5,4},{6,5},{7,6},{9,8},{10,9},{11,10},{12... | collective-permute-start | bytes 786440 | tf_op jit(solution)/shard_map/ppermute | solution.py:30
  62.7 39.6 %collective-permute-start.16 = (bf16[2,128,512]{2,1,0:T(8,128)(2,1)S(1)}, bf16[2,128,512]{2,1,0:T(8,128)(2,1)S(1)}, u32[]{:S(2)}, u32[]{:S(2)}) collective-permute-start(bf16[2,128,512]{2,1,0:T(8,128)(2,1)S(1)} %get-tuple-element.61), channel_id=1, source_target_pairs={{48,0},{56,8},{64,16},{72,24},{80,32},{88,40},{96,48},{104,56},{11... | collective-permute-start | bytes 786440 | tf_op jit(solution)/shard_map/ppermute | solution.py:30
  68.0 17.1 %collective-permute-start.13 = (bf16[2,64,512]{2,1,0:T(8,128)(2,1)S(1)}, bf16[2,64,512]{2,1,0:T(8,128)(2,1)S(1)}, u32[]{:S(2)}, u32[]{:S(2)}) collective-permute-start(bf16[2,64,512]{2,1,0:T(8,128)(2,1)S(1)} %get-tuple-element.56), channel_id=1, source_target_pairs={{128,0},{136,8},{144,16},{152,24},{160,32},{168,40},{176,48},{184,... | collective-permute-start | bytes 393224 | tf_op jit(solution)/shard_map/ppermute | solution.py:30
  70.0 29.6 %collective-permute-start.14 = (bf16[2,64,512]{2,1,0:T(8,128)(2,1)S(1)}, bf16[2,64,512]{2,1,0:T(8,128)(2,1)S(1)}, u32[]{:S(2)}, u32[]{:S(2)}) collective-permute-start(bf16[2,64,512]{2,1,0:T(8,128)(2,1)S(1)} %get-tuple-element.57), channel_id=1, source_target_pairs={{256,0},{264,8},{272,16},{280,24},{288,32},{296,40},{304,48},{312,... | collective-permute-start | bytes 393224 | tf_op jit(solution)/shard_map/ppermute | solution.py:30
  71.3 28.3 %collective-permute-start.15 = (bf16[2,64,512]{2,1,0:T(8,128)(2,1)S(1)}, bf16[2,64,512]{2,1,0:T(8,128)(2,1)S(1)}, u32[]{:S(2)}, u32[]{:S(2)}) collective-permute-start(bf16[2,64,512]{2,1,0:T(8,128)(2,1)S(1)} %get-tuple-element.58), channel_id=1, source_target_pairs={{384,0},{392,8},{400,16},{408,24},{416,32},{424,40},{432,48},{440,... | collective-permute-start | bytes 393224 | tf_op jit(solution)/shard_map/ppermute | solution.py:30
  72.0 37.4 %collective-permute-start.20 = (bf16[2,128,512]{2,1,0:T(8,128)(2,1)S(1)}, bf16[2,128,512]{2,1,0:T(8,128)(2,1)S(1)}, u32[]{:S(2)}, u32[]{:S(2)}) collective-permute-start(bf16[2,128,512]{2,1,0:T(8,128)(2,1)S(1)} %get-tuple-element.65), channel_id=1, source_target_pairs={{16,0},{24,8},{32,16},{40,24},{48,32},{56,40},{64,48},{72,56},{80,... | collective-permute-start | bytes 786440 | tf_op jit(solution)/shard_map/ppermute | solution.py:30
  85.1 24.2 %collective-permute-start.21 = (bf16[2,128,512]{2,1,0:T(8,128)(2,1)S(1)}, bf16[2,128,512]{2,1,0:T(8,128)(2,1)S(1)}, u32[]{:S(2)}, u32[]{:S(2)}) collective-permute-start(bf16[2,128,512]{2,1,0:T(8,128)(2,1)S(1)} %get-tuple-element.66), channel_id=1, source_target_pairs={{32,0},{40,8},{48,16},{56,24},{64,32},{72,40},{80,48},{88,56},{96,... | collective-permute-start | bytes 786440 | tf_op jit(solution)/shard_map/ppermute | solution.py:30
  99.6 8.1 %collective-permute-start.19 = (bf16[2,64,512]{2,1,0:T(8,128)(2,1)S(1)}, bf16[2,64,512]{2,1,0:T(8,128)(2,1)S(1)}, u32[]{:S(2)}, u32[]{:S(2)}) collective-permute-start(bf16[2,64,512]{2,1,0:T(8,128)(2,1)S(1)} %get-tuple-element.62), channel_id=1, source_target_pairs={{48,0},{56,8},{112,64},{120,72},{176,128},{184,136},{240,192},{248... | collective-permute-start | bytes 393224 | tf_op jit(solution)/shard_map/ppermute | solution.py:30
  100.9 8.4 %collective-permute-start.18 = (bf16[2,64,512]{2,1,0:T(8,128)(2,1)S(1)}, bf16[2,64,512]{2,1,0:T(8,128)(2,1)S(1)}, u32[]{:S(2)}, u32[]{:S(2)}) collective-permute-start(bf16[2,64,512]{2,1,0:T(8,128)(2,1)S(1)} %get-tuple-element.62), channel_id=1, source_target_pairs={{32,0},{40,8},{96,64},{104,72},{160,128},{168,136},{224,192},{232,... | collective-permute-start | bytes 393224 | tf_op jit(solution)/shard_map/ppermute | solution.py:30
  102.2 7.1 %collective-permute-start.17 = (bf16[2,64,512]{2,1,0:T(8,128)(2,1)S(1)}, bf16[2,64,512]{2,1,0:T(8,128)(2,1)S(1)}, u32[]{:S(2)}, u32[]{:S(2)}) collective-permute-start(bf16[2,64,512]{2,1,0:T(8,128)(2,1)S(1)} %get-tuple-element.62), channel_id=1, source_target_pairs={{16,0},{24,8},{80,64},{88,72},{144,128},{152,136},{208,192},{216,2... | collective-permute-start | bytes 393224 | tf_op jit(solution)/shard_map/ppermute | solution.py:30
  109.5 10.1 %collective-permute-start.22 = (bf16[2,64,1536]{2,1,0:T(8,128)(2,1)S(1)}, bf16[2,64,1536]{2,1,0:T(8,128)(2,1)S(1)}, u32[]{:S(2)}, u32[]{:S(2)}) collective-permute-start(bf16[2,64,1536]{2,1,0:T(8,128)(2,1)S(1)} %get-tuple-element.70), channel_id=1, source_target_pairs={{0,8},{8,0},{16,24},{24,16},{32,40},{40,32},{48,56},{56,48},{64,72... | collective-permute-start | bytes 1179656 | tf_op jit(solution)/shard_map/ppermute | solution.py:30
  111.5 6.3 %collective-permute-start.24 = (bf16[2,64,512]{2,1,0:T(8,128)(2,1)S(1)}, bf16[2,64,512]{2,1,0:T(8,128)(2,1)S(1)}, u32[]{:S(2)}, u32[]{:S(2)}) collective-permute-start(bf16[2,64,512]{2,1,0:T(8,128)(2,1)S(1)} %get-tuple-element.71), channel_id=1, source_target_pairs={{72,0},{200,128},{328,256},{456,384},{73,1},{201,129},{329,257},{4... | collective-permute-start | bytes 393224 | tf_op jit(solution)/shard_map/ppermute | solution.py:30
  112.8 6.9 %collective-permute-start.23 = (bf16[2,64,512]{2,1,0:T(8,128)(2,1)S(1)}, bf16[2,64,512]{2,1,0:T(8,128)(2,1)S(1)}, u32[]{:S(2)}, u32[]{:S(2)}) collective-permute-start(bf16[2,64,512]{2,1,0:T(8,128)(2,1)S(1)} %get-tuple-element.71), channel_id=1, source_target_pairs={{64,0},{192,128},{320,256},{448,384},{65,1},{193,129},{321,257},{4... | collective-permute-start | bytes 393224 | tf_op jit(solution)/shard_map/ppermute | solution.py:30
  (9 other events, 25.2 us)

commit v4 on v3

--- a/solution.py
+++ b/solution.py
@@ -16,8 +16,6 @@
 HALF_KV = HALF_HEADS * HEAD_DIM
 HALF_FEAT = HALF_HEADS * GROUP * HEAD_DIM
 SCALE = HEAD_DIM**-0.5
-TA = 3
-TB = 2
 LOG2E = 1.4426950408889634
 NEG = -1e30
 NT = (((1,), (1,)), ((), ()))
@@ -40,13 +38,13 @@
     pairs, strided = refs[:4], refs[4:8]
     refs = refs[8:]
     if tick:
-        for old, new in zip(refs[:7], refs[8:15]):
+        for old, new in zip(refs[:4], refs[6:10]):
             new[0] = old[...]
-        refs = refs[7:]
-        refs = refs[:1] + tuple(r.at[1] for r in refs[1:8]) + refs[8:]
-    both, other, back1, back2, back3, part1, part2, part3, own, part0 = refs
+        refs[10][:, 0] = refs[4][...]
+        refs = refs[5:]
+        refs = refs[:1] + tuple(r.at[1] for r in refs[1:5]) + refs[5:]
+    both, other, back1, back2, back3, parts, own = refs
     backs = (own, back1, back2, back3)
-    parts = (part0, part1, part2, part3)
     index = meta[0]
     blocks = (index, jnp.bitwise_xor(index, 1))
     group = index // STRIDE
@@ -122,8 +120,10 @@
             backs[d][:, v_at] = dvalue[rows_at].astype(backs[d].dtype)
         for s in range(4):
             rows_at = slice(8 * BLK + BLK * s, 8 * BLK + BLK * (s + 1))
-            parts[s][:, k_at] = dkey[rows_at].astype(parts[s].dtype)
-            parts[s][:, v_at] = dvalue[rows_at].astype(parts[s].dtype)
+            spot = jnp.bitwise_and(group - s, 3)
+            part = parts.at[spot, 1] if tick else parts.at[spot]
+            part[:, k_at] = dkey[rows_at].astype(jnp.bfloat16)
+            part[:, v_at] = dvalue[rows_at].astype(jnp.bfloat16)
 
 
 WHOLE = pl.BlockSpec(memory_space=pltpu.VMEM)
@@ -145,17 +145,17 @@
         args.append(grads)
         specs.append(WHOLE)
     args += list(pairs) + list(strided)
-    specs += [at(tick, 2 * BLK, WIDE)] * 4 + [at(tick, BLK, WIDE)] * 4
+    specs += [at(tick, 2 * BLK, WIDE)] * 4 + [WHOLE] * 4
     bf16, f32 = jnp.bfloat16, jnp.float32
     out_shape = [shape((2, BLK, HALF_FEAT), bf16)]
     lead = (2,) if tick else ()
     if tick:
         args += earlier
-        specs += [WHOLE] * 7
+        specs += [WHOLE] * 5
     out_shape.append(shape(lead + (BLK, HALF_FEAT), bf16))
     out_shape += [shape(lead + (2 * BLK, WIDE), bf16)] * 3
-    out_shape += [shape(lead + (BLK, WIDE), bf16)] * 3
-    out_shape += [shape((2 * BLK, WIDE), f32), shape((BLK, WIDE), f32)]
+    out_shape.append(shape((4,) + lead + (BLK, WIDE), bf16))
+    out_shape.append(shape((2 * BLK, WIDE), f32))
     return pl.pallas_call(
         functools.partial(attention_kernel, tick),
         out_shape=out_shape,
@@ -170,26 +170,22 @@
     )(*args)
 
 
-def simple(kernel, out_shape, args, scalars=1):
+def simple(kernel, out_shape, args, blocked=False):
     size = sum(a.size * a.dtype.itemsize for a in list(args) + list(out_shape))
+
+    def all_of(array):
+        return pl.BlockSpec(array.shape, lambda n: (0,) * array.ndim)
+
     return pl.pallas_call(
         kernel,
         out_shape=out_shape,
-        in_specs=[SCALAR] * scalars + [WHOLE] * (len(args) - scalars),
+        grid=(1,),
+        in_specs=[SCALAR] + [all_of(a) if blocked else WHOLE for a in args[1:]],
         out_specs=[WHOLE] * len(out_shape),
         compiler_params=pltpu.CompilerParams(vmem_limit_bytes=16 << 20),
         cost_estimate=pl.CostEstimate(flops=size, bytes_accessed=size, transcendentals=0),
         name=kernel.__name__,
     )(*args)
-
-
-def column_sum(own0, own1, x1, x2, x3, wide_out, send_out):
-    for t, own in enumerate((own0, own1)):
-        total = own[...]
-        for x in (x1, x2, x3):
-            total = total + x[t].astype(jnp.float32)
-        wide_out[t] = total
-        send_out[t] = total.astype(jnp.bfloat16)
 
 
 def split_all(meta, keys, values, inputs, first, head, keep, give, kv_keep, kv_give):
@@ -220,40 +216,41 @@
     start[...] = jnp.where(even, near, above)
 
 
-def choose(meta, start, x1, x2, x3, out):
+def choose(meta, start, x1, x2, x3, *outs):
     place = (meta[0] // 2) % 4
-    near = jnp.where(place == 0, start[...], x1[...])
-    far = jnp.where(place == 2, x2[...], x3[...])
-    out[...] = jnp.where(place < 2, near, far)
-
-
-def row_sum(meta, *refs):
-    total, x1, x2, x3, own0, own1, back1, back2, back3, far_rows = refs[:10]
-    mine_out, swap_out, strided_out = refs[10:]
-    index = meta[0]
-    owner = (index // 2) % 4 == 0
-    even = (index // 8) % 2 == 0
-    first = (owner & even & (index % 2 == 0)).astype(jnp.float32)
-    second = (owner & even & (index % 2 == 1)).astype(jnp.float32)
+    for t, out in enumerate(outs):
+        near = jnp.where(place == 0, start[t], x1[t])
+        far = jnp.where(place == 2, x2[t], x3[t])
+        out[...] = jnp.where(place < 2, near, far)
+
+
+def fold(meta, pieces, own0, own1, back1, back2, back3, far_rows, sums, mine, swap):
+    total = pieces[0].astype(jnp.float32)
+    for n in range(1, 32):
+        total = total + pieces[n].astype(jnp.float32)
+    total = total.astype(jnp.bfloat16)
+    for n in range(STRIDE):
+        sums[n] = total
     for t, own in enumerate((own0, own1)):
-        strided = total[t]
-        for x in (x1, x2, x3):
-            strided = strided + x[t].astype(jnp.float32)
-        strided_out[t] = strided.astype(jnp.bfloat16)
         near = own[...]
         for back in (back1, back2, back3):
             near = near + back[t].astype(jnp.float32)
-        mine_out[t] = near[:BLK] + first * strided
-        swap_out[t, :, :HALF_FEAT] = far_rows[t]
-        swap_out[t, :, HALF_FEAT:] = (near[BLK:] + second * strided).astype(jnp.bfloat16)
-
-
-def finish(meta, mine, swapped, low, high, mine0, mine1, rows_out, keys_out, values_out):
+        mine[t] = near[:BLK]
+        swap[t, :, :HALF_FEAT] = far_rows[t]
+        swap[t, :, HALF_FEAT:] = near[BLK:].astype(jnp.bfloat16)
+
+
+def finish(meta, mine, swapped, sums, mine0, mine1, rows_out, keys_out, values_out):
     swap = meta[0] % 2 == 1
+    owner = meta[0] % STRIDE == 0
     for t, rows in enumerate((mine0, mine1)):
-        other = swapped[t, :, HALF_FEAT:].astype(jnp.float32)
-        own = (mine[t] + low[t].astype(jnp.float32)).astype(jnp.bfloat16)
-        far = (other + high[t].astype(jnp.float32)).astype(jnp.bfloat16)
+        strided = []
+        for half in range(2):
+            quarters = [sums[2 * (4 * t + n) + half] for n in range(4)]
+            whole = jnp.concatenate(quarters, axis=0).astype(jnp.float32)
+            strided.append(jnp.where(owner, whole, 0.0))
+        own = (mine[t] + strided[0]).astype(jnp.bfloat16)
+        far = (swapped[t, :, HALF_FEAT:].astype(jnp.float32) + strided[1]).astype(jnp.bfloat16)
         left, right = jnp.where(swap, far, own), jnp.where(swap, own, far)
         for out, at in ((keys_out, 0), (values_out, HALF_KV)):
             out[0, t, :, :HALF_KV] = left[:, at : at + HALF_KV]
@@ -281,6 +278,7 @@
         split_all,
         [ten, ten, half, half],
         [spot, saved_keys, saved_values, inputs, first_grads, head_grads],
+        blocked=True,
     )
     recv = sibling(give)
     up_low = ctx(kv_keep, lambda i: i + 8, lambda i: i % STRIDE == 0)
@@ -291,14 +289,11 @@
         [spot, keep, recv, up_low, up_high],
     )
     across = [ctx(start, lambda i: i + 2 * d, lambda i: (i // 2) % 4 == 0) for d in range(1, 4)]
-    (chosen,) = simple(choose, [half], [spot, start] + across)
+    chosen = simple(choose, [shape((BLK, WIDE), bf16)] * 2, [spot, start] + across)
     pairs = [pair] + [ctx(pair, lambda i: i + 2 * d) for d in range(1, 4)]
-    strided = [chosen]
-    for s in range(1, 4):
-        sent = chosen
-        if s == 1:
-            sent, pairs[TA] = lax.optimization_barrier((chosen, pairs[TA]))
-        strided.append(ctx(sent, lambda i: i + STRIDE * s))
+
+    def columns(block):
+        return [ctx(block, lambda i: i + STRIDE * s) for s in range(1, 4)]
 
     gain = jnp.where(core == 0, query_gain[:, :HALF_FEAT], query_gain[:, HALF_FEAT:])
     heads = jnp.where(core == 0, window[0, :2], window[0, 2:])
@@ -306,34 +301,34 @@
     top = jnp.where(section == last, 1, 0)
     meta = jnp.concatenate([jnp.stack([index, top]).astype(jnp.int32), heads, steps])
 
+    strided = [chosen[0]] + columns(chosen[0])
     first = attention(0, meta, gain, keep, recv, None, pairs, strided, None)
     grads = route(first[0], "pp", lambda i: i - 1)
-    second = attention(1, meta, gain, keep, recv, grads, pairs, strided, first[1:8])
-    columns = [first[9], second[9]]
-    columns += [ctx(second[4 + s], lambda i: i - STRIDE * s) for s in range(1, 4)]
+    late, own = lax.optimization_barrier((chosen[1], first[6]))
+    strided = [late] + columns(late)
+    second = attention(1, meta, gain, keep, recv, grads, pairs, strided, first[1:6])
     backs = [ctx(second[1 + d], lambda i: i - 2 * d) for d in range(1, 4)]
-
-    wide = shape((2, BLK, WIDE), f32)
-    total, send = simple(column_sum, [wide, half], columns, 0)
-    rows = []
-    for d in range(1, 4):
-        sent = send
-        if d == 1:
-            sent, backs[TB] = lax.optimization_barrier((send, backs[TB]))
-        rows.append(ctx(sent, lambda i: i - 2 * d, lambda i: (i // 2) % 4 == d))
-    mine, swap, down = simple(
-        row_sum,
-        [wide, shape((2, BLK, HALF_FEAT + WIDE), bf16), half],
-        [spot, total] + rows + [first[8], second[8]] + backs + [second[1]],
+    size = lax.axis_size("ctx")
+    teams = [[2 * n + k for n in range(size // 2)] for k in range(2)]
+    pieces = second[5].reshape(32, 16, WIDE)
+    pieces = lax.all_to_all(pieces, "ctx", 0, 0, tiled=True, axis_index_groups=teams)
+    sums, mine, swap = simple(
+        fold,
+        [
+            shape((STRIDE, 16, WIDE), bf16),
+            shape((2, BLK, WIDE), f32),
+            shape((2, BLK, HALF_FEAT + WIDE), bf16),
+        ],
+        [spot, pieces, own, second[6]] + backs + [second[1]],
     )
     swapped = sibling(swap)
-    low = ctx(down, lambda i: i - 8, lambda i: i % STRIDE == 8)
-    high = ctx(down, lambda i: i - 9, lambda i: i % STRIDE == 9)
+    groups = [[STRIDE * k + n for n in range(STRIDE)] for k in range(size // STRIDE)]
+    sums = lax.all_to_all(sums, "ctx", 0, 0, tiled=True, axis_index_groups=groups)
     keys_shape = shape(saved_keys.shape, bf16)
     grads_out, key_grads, value_grads = simple(
         finish,
         [shape(inputs.shape, bf16), keys_shape, keys_shape],
-        [spot, mine, swapped, low, high, first[0], second[0]],
+        [spot, mine, swapped, sums, first[0], second[0]],
     )
     return grads_out, key_grads, value_grads
 

time: 121 us -> 131 us (1.083)
  the two profiles are of different devices: /device:TPU:224 before, /device:TPU:464 now
where the time goes in v4:
time: 131 us; the launch traced here: 130 us
  starting transfers between devices  67 us (51%)
  waiting for transfers between devices  42.9 us (33%)
  Pallas kernels  10.8 us (8%)
  local copies, waits for them, and re-layouts  7.88 us (6%)
    ppermute x20, starting transfers between devices, route(): lax.ppermute(array, axis, [(a, b) for a, b in pairs if b is not None and...  52.4 us
    ppermute x20, waiting for transfers between devices, route(): lax.ppermute(array, axis, [(a, b) for a, b in pairs if b is not None and...  38.5 us
    pallas_call x2, Pallas kernels, attention(): pl.pallas_call(functools.partial(attention_kernel, tick), out_shape=out_s...  8.86 us
    all_to_all x1, starting transfers between devices, body(): lax.all_to_all(sums, 'ctx', 0, 0, tiled=True, axis_index_groups=groups)  8.39 us
    unnamed x32, local copies, waits for them, and re-layouts  7.88 us
    all_to_all x1, starting transfers between devices, body(): lax.all_to_all(pieces, 'ctx', 0, 0, tiled=True, axis_index_groups=teams)  6.15 us
    all_to_all x1, waiting for transfers between devices, body(): lax.all_to_all(sums, 'ctx', 0, 0, tiled=True, axis_index_groups=groups)  4.41 us
  transfers between devices with their start and end apart: 22, of which 12 were waited for; matrix products, arithmetic and copies ran while one was open for 0% of the time, Pallas kernels for 0%

profile of v4, /device:TPU:464, one launch (start us, length us, event | category | flops | bytes accessed | tf_op | source)
XLA Modules:
  0.0 129.7 jit_solution(17296421081609004578)
XLA Ops:
  5.5 1.9 %collective-permute-start = (bf16[10,64,512]{2,1,0:T(8,128)(2,1)S(1)}, bf16[10,64,512]{2,1,0:T(8,128)(2,1)S(1)}, u32[]{:S(2)}, u32[]{:S(2)}) collective-permute-start(bf16[10,64,512]{2,1,0:T(8,128)(2,1)S(1)} %get-tuple-element.31), channel_id=1, source_target_pairs={{0,8},{8,0},{16,24},{24,16},{32,40},{40,32},{48,56},{56,48},{64,72... | collective-permute-start | bytes 1966088 | tf_op jit(solution)/shard_map/ppermute | solution.py:28
  7.4 3.5 %collective-permute-start.1 = (bf16[2,64,512]{2,1,0:T(8,128)(2,1)S(1)}, bf16[2,64,512]{2,1,0:T(8,128)(2,1)S(1)}, u32[]{:S(2)}, u32[]{:S(2)}) collective-permute-start(bf16[2,64,512]{2,1,0:T(8,128)(2,1)S(1)} %get-tuple-element.32), channel_id=1, source_target_pairs={{0,64},{128,192},{256,320},{384,448},{1,65},{129,193},{257,321},{3... | collective-permute-start | bytes 393224 | tf_op jit(solution)/shard_map/ppermute | solution.py:28
  22.7 4.4 %collective-permute-start.3 = (bf16[2,128,512]{2,1,0:T(8,128)(2,1)S(1)}, bf16[2,128,512]{2,1,0:T(8,128)(2,1)S(1)}, u32[]{:S(2)}, u32[]{:S(2)}) collective-permute-start(bf16[2,128,512]{2,1,0:T(8,128)(2,1)S(1)} %get-tuple-element.34.refs_0_.refs_1_), channel_id=1, source_target_pairs={{0,16},{8,24},{16,32},{24,40},{32,48},{40,56},{48,64},{56,72},{64,... | collective-permute-start | bytes 786440 | tf_op jit(solution)/shard_map/ppermute | solution.py:28
  28.0 5.7 %collective-permute-start.10 = (bf16[64,512]{1,0:T(8,128)(2,1)S(1)}, bf16[64,512]{1,0:T(8,128)(2,1)S(1)}, u32[]{:S(2)}, u32[]{:S(2)}) collective-permute-start(bf16[64,512]{1,0:T(8,128)(2,1)S(1)} %get-tuple-element.36.refs_4_), channel_id=1, source_target_pairs={{0,256},{8,264},{16,272},{24,280},{32,288},{40,296},{48,304},{56,3... | collective-permute-start | bytes 196616 | tf_op jit(solution)/shard_map/ppermute | solution.py:28
  33.6 1.9 %collective-permute-start.9 = (bf16[64,512]{1,0:T(8,128)(2,1)S(1)}, bf16[64,512]{1,0:T(8,128)(2,1)S(1)}, u32[]{:S(2)}, u32[]{:S(2)}) collective-permute-start(bf16[64,512]{1,0:T(8,128)(2,1)S(1)} %get-tuple-element.36.refs_4_), channel_id=1, source_target_pairs={{0,128},{8,136},{16,144},{24,152},{32,160},{40,168},{48,176},{56,1... | collective-permute-start | bytes 196616 | tf_op jit(solution)/shard_map/ppermute | solution.py:28
  35.6 3.2 %collective-permute-done.10.refs_6_ = bf16[64,512]{1,0:T(8,128)(2,1)S(1)} collective-permute-done((bf16[64,512]{1,0:T(8,128)(2,1)S(1)}, bf16[64,512]{1,0:T(8,128)(2,1)S(1)}, u32[]{:S(2)}, u32[]{:S(2)}) %collective-permute-start.10) | collective-permute-done | bytes 65568 | tf_op jit(solution)/shard_map/ppermute | solution.py:28
  38.8 3.2 %collective-permute-done.9.refs_5_ = bf16[64,512]{1,0:T(8,128)(2,1)S(1)} collective-permute-done((bf16[64,512]{1,0:T(8,128)(2,1)S(1)}, bf16[64,512]{1,0:T(8,128)(2,1)S(1)}, u32[]{:S(2)}, u32[]{:S(2)}) %collective-permute-start.9) | collective-permute-done | bytes 65568 | tf_op jit(solution)/shard_map/ppermute | solution.py:28
  42.0 2.3 %collective-permute-done.3.refs_1_.refs_2_ = bf16[2,128,512]{2,1,0:T(8,128)(2,1)S(1)} collective-permute-done((bf16[2,128,512]{2,1,0:T(8,128)(2,1)S(1)}, bf16[2,128,512]{2,1,0:T(8,128)(2,1)S(1)}, u32[]{:S(2)}, u32[]{:S(2)}) %collective-permute-start.3) | collective-permute-done | bytes 262176 | tf_op jit(solution)/shard_map/ppermute | solution.py:28
  44.3 4.0 %attention.2 = (bf16[2,64,1024]{2,1,0:T(8,128)(2,1)S(1)}, bf16[64,1024]{1,0:T(8,128)(2,1)S(1)}, bf16[128,512]{1,0:T(8,128)(2,1)S(1)}, bf16[128,512]{1,0:T(8,128)...) custom-call(s32[6]{0:T(128)S(1)} %pad_add_fusion.meta, ...), custom_call_target="tpu_custom_call" | custom-call | flops 1006632960 | bytes 4194304 | tf_op jit(solution)/shard_map/attention/pallas_call | solution.py:159
  48.3 2.5 %collective-permute-start.12 = (bf16[2,64,1024]{2,1,0:T(8,128)(2,1)S(1)}, bf16[2,64,1024]{2,1,0:T(8,128)(2,1)S(1)}, u32[]{:S(2)}, u32[]{:S(2)}) collective-permute-start(bf16[2,64,1024]{2,1,0:T(8,128)(2,1)S(1)} %get-tuple-element.37.mine0), channel_id=1, source_target_pairs={{1,0},{2,1},{3,2},{4,3},{5,4},{6,5},{7,6},{9,8},{10,9},{11,10},{12... | collective-permute-start | bytes 786440 | tf_op jit(solution)/shard_map/ppermute | solution.py:28
  51.5 7.8 %collective-permute-start.14 = (bf16[64,512]{1,0:T(8,128)(2,1)S(1)}, bf16[64,512]{1,0:T(8,128)(2,1)S(1)}, u32[]{:S(2)}, u32[]{:S(2)}) collective-permute-start(bf16[64,512]{1,0:T(8,128)(2,1)S(1)} %get-tuple-element.40.refs_5_), channel_id=1, source_target_pairs={{0,256},{8,264},{16,272},{24,280},{32,288},{40,296},{48,304},{56,3... | collective-permute-start | bytes 196616 | tf_op jit(solution)/shard_map/ppermute | solution.py:28
  59.3 1.9 %collective-permute-start.13 = (bf16[64,512]{1,0:T(8,128)(2,1)S(1)}, bf16[64,512]{1,0:T(8,128)(2,1)S(1)}, u32[]{:S(2)}, u32[]{:S(2)}) collective-permute-start(bf16[64,512]{1,0:T(8,128)(2,1)S(1)} %get-tuple-element.40.refs_5_), channel_id=1, source_target_pairs={{0,128},{8,136},{16,144},{24,152},{32,160},{40,168},{48,176},{56,1... | collective-permute-start | bytes 196616 | tf_op jit(solution)/shard_map/ppermute | solution.py:28
  62.5 3.8 %collective-permute-done.13.refs_6_ = bf16[64,512]{1,0:T(8,128)(2,1)S(1)} collective-permute-done((bf16[64,512]{1,0:T(8,128)(2,1)S(1)}, bf16[64,512]{1,0:T(8,128)(2,1)S(1)}, u32[]{:S(2)}, u32[]{:S(2)}) %collective-permute-start.13) | collective-permute-done | bytes 65568 | tf_op jit(solution)/shard_map/ppermute | solution.py:28
  67.3 4.9 %attention.3 = (bf16[2,64,1024]{2,1,0:T(8,128)(2,1)S(1)}, bf16[2,64,1024]{2,1,0:T(8,128)(2,1)S(1)}, bf16[2,128,512]{2,1,0:T(8,128)(2,1)S(1)}, bf16[2,128,512]{2,...) custom-call(s32[6]{0:T(128)S(1)} %pad_add_fusion.meta, ...), custom_call_target="tpu_custom_call" | custom-call | flops 1006632960 | bytes 4194304 | tf_op jit(solution)/shard_map/attention/pallas_call | solution.py:159
  74.3 6.2 %all-to-all-start = ((bf16[32,16,512]{2,1,0:T(8,128)(2,1)}), bf16[32,16,512]{2,1,0:T(8,128)(2,1)S(1)}, u32[]{:S(2)}, u32[]{:S(2)}) async-start(bf16[32,16,512]{2,1,0:T(8,128)(2,1)} %bitcast.4), calls=%async_computation | async-start | bytes 1048576 | tf_op jit(solution)/shard_map/all_to_all | solution.py:314
  80.5 4.6 %collective-permute-start.16 = (bf16[2,128,512]{2,1,0:T(8,128)(2,1)S(1)}, bf16[2,128,512]{2,1,0:T(8,128)(2,1)S(1)}, u32[]{:S(2)}, u32[]{:S(2)}) collective-permute-start(bf16[2,128,512]{2,1,0:T(8,128)(2,1)S(1)} %copy-done.12), channel_id=1, source_target_pairs={{16,0},{24,8},{32,16},{40,24},{48,32},{56,40},{64,48},{72,56},{80,... | collective-permute-start | bytes 786440 | tf_op jit(solution)/shard_map/ppermute | solution.py:28
  85.1 2.8 %collective-permute-start.17 = (bf16[2,128,512]{2,1,0:T(8,128)(2,1)S(1)}, bf16[2,128,512]{2,1,0:T(8,128)(2,1)S(1)}, u32[]{:S(2)}, u32[]{:S(2)}) collective-permute-start(bf16[2,128,512]{2,1,0:T(8,128)(2,1)S(1)} %copy-done.10), channel_id=1, source_target_pairs={{32,0},{40,8},{48,16},{56,24},{64,32},{72,40},{80,48},{88,56},{96,... | collective-permute-start | bytes 786440 | tf_op jit(solution)/shard_map/ppermute | solution.py:28
  87.9 2.8 %collective-permute-start.18 = (bf16[2,128,512]{2,1,0:T(8,128)(2,1)S(1)}, bf16[2,128,512]{2,1,0:T(8,128)(2,1)S(1)}, u32[]{:S(2)}, u32[]{:S(2)}) collective-permute-start(bf16[2,128,512]{2,1,0:T(8,128)(2,1)S(1)} %copy-done.8), channel_id=1, source_target_pairs={{48,0},{56,8},{64,16},{72,24},{80,32},{88,40},{96,48},{104,56},{11... | collective-permute-start | bytes 786440 | tf_op jit(solution)/shard_map/ppermute | solution.py:28
  90.6 8.8 %collective-permute-done.16.back1 = bf16[2,128,512]{2,1,0:T(8,128)(2,1)S(1)} collective-permute-done((bf16[2,128,512]{2,1,0:T(8,128)(2,1)S(1)}, bf16[2,128,512]{2,1,0:T(8,128)(2,1)S(1)}, u32[]{:S(2)}, u32[]{:S(2)}) %collective-permute-start.16) | collective-permute-done | bytes 262176 | tf_op jit(solution)/shard_map/ppermute | solution.py:28
  99.4 7.6 %collective-permute-done.17.back2 = bf16[2,128,512]{2,1,0:T(8,128)(2,1)S(1)} collective-permute-done((bf16[2,128,512]{2,1,0:T(8,128)(2,1)S(1)}, bf16[2,128,512]{2,1,0:T(8,128)(2,1)S(1)}, u32[]{:S(2)}, u32[]{:S(2)}) %collective-permute-start.17) | collective-permute-done | bytes 262176 | tf_op jit(solution)/shard_map/ppermute | solution.py:28
  107.1 4.4 %collective-permute-done.18.back3 = bf16[2,128,512]{2,1,0:T(8,128)(2,1)S(1)} collective-permute-done((bf16[2,128,512]{2,1,0:T(8,128)(2,1)S(1)}, bf16[2,128,512]{2,1,0:T(8,128)(2,1)S(1)}, u32[]{:S(2)}, u32[]{:S(2)}) %collective-permute-start.18) | collective-permute-done | bytes 262176 | tf_op jit(solution)/shard_map/ppermute | solution.py:28
  112.3 8.4 %all-to-all-start.1 = ((bf16[16,16,512]{2,1,0:T(8,128)(2,1)}), bf16[16,16,512]{2,1,0:T(8,128)(2,1)S(1)}, u32[]{:S(2)}, u32[]{:S(2)}) async-start(bf16[16,16,512]{2,1,0:T(8,128)(2,1)} %get-tuple-element.55), calls=%async_computation.1 | async-start | bytes 524288 | tf_op jit(solution)/shard_map/all_to_all | solution.py:326
  120.7 2.3 %collective-permute-start.19 = (bf16[2,64,1536]{2,1,0:T(8,128)(2,1)S(1)}, bf16[2,64,1536]{2,1,0:T(8,128)(2,1)S(1)}, u32[]{:S(2)}, u32[]{:S(2)}) collective-permute-start(bf16[2,64,1536]{2,1,0:T(8,128)(2,1)S(1)} %get-tuple-element.54), channel_id=1, source_target_pairs={{0,8},{8,0},{16,24},{24,16},{32,40},{40,32},{48,56},{56,48},{64,72... | collective-permute-start | bytes 1179656 | tf_op jit(solution)/shard_map/ppermute | solution.py:28
  124.3 4.4 %all-to-all-done.1.sums = bf16[16,16,512]{2,1,0:T(8,128)(2,1)S(1)} async-done(((bf16[16,16,512]{2,1,0:T(8,128)(2,1)}), bf16[16,16,512]{2,1,0:T(8,128)(2,1)S(1)}, u32[]{:S(2)}, u32[]{:S(2)}) %all-to-all-start.1) | async-done | bytes 262176 | tf_op jit(solution)/shard_map/all_to_all | solution.py:326
  (62 shorter events, 25.6 us)
Async XLA Ops:
  5.5 9.3 %collective-permute-start = (bf16[10,64,512]{2,1,0:T(8,128)(2,1)S(1)}, bf16[10,64,512]{2,1,0:T(8,128)(2,1)S(1)}, u32[]{:S(2)}, u32[]{:S(2)}) collective-permute-start(bf16[10,64,512]{2,1,0:T(8,128)(2,1)S(1)} %get-tuple-element.31), channel_id=1, source_target_pairs={{0,8},{8,0},{16,24},{24,16},{32,40},{40,32},{48,56},{56,48},{64,72... | collective-permute-start | bytes 1966088 | tf_op jit(solution)/shard_map/ppermute | solution.py:28
  7.4 6.0 %collective-permute-start.1 = (bf16[2,64,512]{2,1,0:T(8,128)(2,1)S(1)}, bf16[2,64,512]{2,1,0:T(8,128)(2,1)S(1)}, u32[]{:S(2)}, u32[]{:S(2)}) collective-permute-start(bf16[2,64,512]{2,1,0:T(8,128)(2,1)S(1)} %get-tuple-element.32), channel_id=1, source_target_pairs={{0,64},{128,192},{256,320},{384,448},{1,65},{129,193},{257,321},{3... | collective-permute-start | bytes 393224 | tf_op jit(solution)/shard_map/ppermute | solution.py:28
  10.9 3.9 %collective-permute-start.2 = (bf16[2,64,512]{2,1,0:T(8,128)(2,1)S(1)}, bf16[2,64,512]{2,1,0:T(8,128)(2,1)S(1)}, u32[]{:S(2)}, u32[]{:S(2)}) collective-permute-start(bf16[2,64,512]{2,1,0:T(8,128)(2,1)S(1)} %get-tuple-element.33), channel_id=1, source_target_pairs={{0,72},{128,200},{256,328},{384,456},{1,73},{129,201},{257,329},{3... | collective-permute-start | bytes 393224 | tf_op jit(solution)/shard_map/ppermute | solution.py:28
  14.8 7.8 %collective-permute-start.8 = (bf16[2,64,512]{2,1,0:T(8,128)(2,1)S(1)}, bf16[2,64,512]{2,1,0:T(8,128)(2,1)S(1)}, u32[]{:S(2)}, u32[]{:S(2)}) collective-permute-start(bf16[2,64,512]{2,1,0:T(8,128)(2,1)S(1)} %get-tuple-element.35.start), channel_id=1, source_target_pairs={{0,48},{8,56},{64,112},{72,120},{128,176},{136,184},{192,240},{200... | collective-permute-start | bytes 393224 | tf_op jit(solution)/shard_map/ppermute | solution.py:28
  16.1 11.0 %collective-permute-start.7 = (bf16[2,64,512]{2,1,0:T(8,128)(2,1)S(1)}, bf16[2,64,512]{2,1,0:T(8,128)(2,1)S(1)}, u32[]{:S(2)}, u32[]{:S(2)}) collective-permute-start(bf16[2,64,512]{2,1,0:T(8,128)(2,1)S(1)} %get-tuple-element.35.start), channel_id=1, source_target_pairs={{0,32},{8,40},{64,96},{72,104},{128,160},{136,168},{192,224},{200,... | collective-permute-start | bytes 393224 | tf_op jit(solution)/shard_map/ppermute | solution.py:28
  17.5 9.7 %collective-permute-start.6 = (bf16[2,64,512]{2,1,0:T(8,128)(2,1)S(1)}, bf16[2,64,512]{2,1,0:T(8,128)(2,1)S(1)}, u32[]{:S(2)}, u32[]{:S(2)}) collective-permute-start(bf16[2,64,512]{2,1,0:T(8,128)(2,1)S(1)} %get-tuple-element.35.start), channel_id=1, source_target_pairs={{0,16},{8,24},{64,80},{72,88},{128,144},{136,152},{192,208},{200,2... | collective-permute-start | bytes 393224 | tf_op jit(solution)/shard_map/ppermute | solution.py:28
  18.8 23.2 %collective-permute-start.5 = (bf16[2,128,512]{2,1,0:T(8,128)(2,1)S(1)}, bf16[2,128,512]{2,1,0:T(8,128)(2,1)S(1)}, u32[]{:S(2)}, u32[]{:S(2)}) collective-permute-start(bf16[2,128,512]{2,1,0:T(8,128)(2,1)S(1)} %get-tuple-element.34.refs_0_.refs_1_), channel_id=1, source_target_pairs={{0,48},{8,56},{16,64},{24,72},{32,80},{40,88},{48,96},{56,104},{64... | collective-permute-start | bytes 786440 | tf_op jit(solution)/shard_map/ppermute | solution.py:28
  20.7 21.3 %collective-permute-start.4 = (bf16[2,128,512]{2,1,0:T(8,128)(2,1)S(1)}, bf16[2,128,512]{2,1,0:T(8,128)(2,1)S(1)}, u32[]{:S(2)}, u32[]{:S(2)}) collective-permute-start(bf16[2,128,512]{2,1,0:T(8,128)(2,1)S(1)} %get-tuple-element.34.refs_0_.refs_1_), channel_id=1, source_target_pairs={{0,32},{8,40},{16,48},{24,56},{32,64},{40,72},{48,80},{56,88},{64,... | collective-permute-start | bytes 786440 | tf_op jit(solution)/shard_map/ppermute | solution.py:28
  22.7 21.6 %collective-permute-start.3 = (bf16[2,128,512]{2,1,0:T(8,128)(2,1)S(1)}, bf16[2,128,512]{2,1,0:T(8,128)(2,1)S(1)}, u32[]{:S(2)}, u32[]{:S(2)}) collective-permute-start(bf16[2,128,512]{2,1,0:T(8,128)(2,1)S(1)} %get-tuple-element.34.refs_0_.refs_1_), channel_id=1, source_target_pairs={{0,16},{8,24},{16,32},{24,40},{32,48},{40,56},{48,64},{56,72},{64,... | collective-permute-start | bytes 786440 | tf_op jit(solution)/shard_map/ppermute | solution.py:28
  27.2 6.4 %collective-permute-start.11 = (bf16[64,512]{1,0:T(8,128)(2,1)S(1)}, bf16[64,512]{1,0:T(8,128)(2,1)S(1)}, u32[]{:S(2)}, u32[]{:S(2)}) collective-permute-start(bf16[64,512]{1,0:T(8,128)(2,1)S(1)} %get-tuple-element.36.refs_4_), channel_id=1, source_target_pairs={{0,384},{8,392},{16,400},{24,408},{32,416},{40,424},{48,432},{56,4... | collective-permute-start | bytes 196616 | tf_op jit(solution)/shard_map/ppermute | solution.py:28
  28.0 10.8 %collective-permute-start.10 = (bf16[64,512]{1,0:T(8,128)(2,1)S(1)}, bf16[64,512]{1,0:T(8,128)(2,1)S(1)}, u32[]{:S(2)}, u32[]{:S(2)}) collective-permute-start(bf16[64,512]{1,0:T(8,128)(2,1)S(1)} %get-tuple-element.36.refs_4_), channel_id=1, source_target_pairs={{0,256},{8,264},{16,272},{24,280},{32,288},{40,296},{48,304},{56,3... | collective-permute-start | bytes 196616 | tf_op jit(solution)/shard_map/ppermute | solution.py:28
  33.6 8.4 %collective-permute-start.9 = (bf16[64,512]{1,0:T(8,128)(2,1)S(1)}, bf16[64,512]{1,0:T(8,128)(2,1)S(1)}, u32[]{:S(2)}, u32[]{:S(2)}) collective-permute-start(bf16[64,512]{1,0:T(8,128)(2,1)S(1)} %get-tuple-element.36.refs_4_), channel_id=1, source_target_pairs={{0,128},{8,136},{16,144},{24,152},{32,160},{40,168},{48,176},{56,1... | collective-permute-start | bytes 196616 | tf_op jit(solution)/shard_map/ppermute | solution.py:28
  48.3 18.0 %collective-permute-start.12 = (bf16[2,64,1024]{2,1,0:T(8,128)(2,1)S(1)}, bf16[2,64,1024]{2,1,0:T(8,128)(2,1)S(1)}, u32[]{:S(2)}, u32[]{:S(2)}) collective-permute-start(bf16[2,64,1024]{2,1,0:T(8,128)(2,1)S(1)} %get-tuple-element.37.mine0), channel_id=1, source_target_pairs={{1,0},{2,1},{3,2},{4,3},{5,4},{6,5},{7,6},{9,8},{10,9},{11,10},{12... | collective-permute-start | bytes 786440 | tf_op jit(solution)/shard_map/ppermute | solution.py:28
  50.8 10.4 %collective-permute-start.15 = (bf16[64,512]{1,0:T(8,128)(2,1)S(1)}, bf16[64,512]{1,0:T(8,128)(2,1)S(1)}, u32[]{:S(2)}, u32[]{:S(2)}) collective-permute-start(bf16[64,512]{1,0:T(8,128)(2,1)S(1)} %get-tuple-element.40.refs_5_), channel_id=1, source_target_pairs={{0,384},{8,392},{16,400},{24,408},{32,416},{40,424},{48,432},{56,4... | collective-permute-start | bytes 196616 | tf_op jit(solution)/shard_map/ppermute | solution.py:28
  51.5 11.1 %collective-permute-start.14 = (bf16[64,512]{1,0:T(8,128)(2,1)S(1)}, bf16[64,512]{1,0:T(8,128)(2,1)S(1)}, u32[]{:S(2)}, u32[]{:S(2)}) collective-permute-start(bf16[64,512]{1,0:T(8,128)(2,1)S(1)} %get-tuple-element.40.refs_5_), channel_id=1, source_target_pairs={{0,256},{8,264},{16,272},{24,280},{32,288},{40,296},{48,304},{56,3... | collective-permute-start | bytes 196616 | tf_op jit(solution)/shard_map/ppermute | solution.py:28
  59.3 7.1 %collective-permute-start.13 = (bf16[64,512]{1,0:T(8,128)(2,1)S(1)}, bf16[64,512]{1,0:T(8,128)(2,1)S(1)}, u32[]{:S(2)}, u32[]{:S(2)}) collective-permute-start(bf16[64,512]{1,0:T(8,128)(2,1)S(1)} %get-tuple-element.40.refs_5_), channel_id=1, source_target_pairs={{0,128},{8,136},{16,144},{24,152},{32,160},{40,168},{48,176},{56,1... | collective-permute-start | bytes 196616 | tf_op jit(solution)/shard_map/ppermute | solution.py:28
  74.3 10.8 %copy-start.10 = (bf16[2,128,512]{2,1,0:T(8,128)(2,1)S(1)}, bf16[2,128,512]{2,1,0:T(8,128)(2,1)}, u32[]{:S(2)}) copy-start(bf16[2,128,512]{2,1,0:T(8,128)(2,1)} %copy-done.9) | copy-start | bytes 786436
  74.3 13.5 %copy-start.8 = (bf16[2,128,512]{2,1,0:T(8,128)(2,1)S(1)}, bf16[2,128,512]{2,1,0:T(8,128)(2,1)}, u32[]{:S(2)}) copy-start(bf16[2,128,512]{2,1,0:T(8,128)(2,1)} %copy-done.7) | copy-start | bytes 786436
  74.3 37.1 %all-to-all-start = ((bf16[32,16,512]{2,1,0:T(8,128)(2,1)}), bf16[32,16,512]{2,1,0:T(8,128)(2,1)S(1)}, u32[]{:S(2)}, u32[]{:S(2)}) async-start(bf16[32,16,512]{2,1,0:T(8,128)(2,1)} %bitcast.4), calls=%async_computation | async-start | bytes 1048576 | tf_op jit(solution)/shard_map/all_to_all | solution.py:314
  80.5 18.9 %collective-permute-start.16 = (bf16[2,128,512]{2,1,0:T(8,128)(2,1)S(1)}, bf16[2,128,512]{2,1,0:T(8,128)(2,1)S(1)}, u32[]{:S(2)}, u32[]{:S(2)}) collective-permute-start(bf16[2,128,512]{2,1,0:T(8,128)(2,1)S(1)} %copy-done.12), channel_id=1, source_target_pairs={{16,0},{24,8},{32,16},{40,24},{48,32},{56,40},{64,48},{72,56},{80,... | collective-permute-start | bytes 786440 | tf_op jit(solution)/shard_map/ppermute | solution.py:28
  85.1 22.0 %collective-permute-start.17 = (bf16[2,128,512]{2,1,0:T(8,128)(2,1)S(1)}, bf16[2,128,512]{2,1,0:T(8,128)(2,1)S(1)}, u32[]{:S(2)}, u32[]{:S(2)}) collective-permute-start(bf16[2,128,512]{2,1,0:T(8,128)(2,1)S(1)} %copy-done.10), channel_id=1, source_target_pairs={{32,0},{40,8},{48,16},{56,24},{64,32},{72,40},{80,48},{88,56},{96,... | collective-permute-start | bytes 786440 | tf_op jit(solution)/shard_map/ppermute | solution.py:28
  87.9 23.6 %collective-permute-start.18 = (bf16[2,128,512]{2,1,0:T(8,128)(2,1)S(1)}, bf16[2,128,512]{2,1,0:T(8,128)(2,1)S(1)}, u32[]{:S(2)}, u32[]{:S(2)}) collective-permute-start(bf16[2,128,512]{2,1,0:T(8,128)(2,1)S(1)} %copy-done.8), channel_id=1, source_target_pairs={{48,0},{56,8},{64,16},{72,24},{80,32},{88,40},{96,48},{104,56},{11... | collective-permute-start | bytes 786440 | tf_op jit(solution)/shard_map/ppermute | solution.py:28
  112.3 16.4 %all-to-all-start.1 = ((bf16[16,16,512]{2,1,0:T(8,128)(2,1)}), bf16[16,16,512]{2,1,0:T(8,128)(2,1)S(1)}, u32[]{:S(2)}, u32[]{:S(2)}) async-start(bf16[16,16,512]{2,1,0:T(8,128)(2,1)} %get-tuple-element.55), calls=%async_computation.1 | async-start | bytes 524288 | tf_op jit(solution)/shard_map/all_to_all | solution.py:326
  120.7 3.6 %collective-permute-start.19 = (bf16[2,64,1536]{2,1,0:T(8,128)(2,1)S(1)}, bf16[2,64,1536]{2,1,0:T(8,128)(2,1)S(1)}, u32[]{:S(2)}, u32[]{:S(2)}) collective-permute-start(bf16[2,64,1536]{2,1,0:T(8,128)(2,1)S(1)} %get-tuple-element.54), channel_id=1, source_target_pairs={{0,8},{8,0},{16,24},{24,16},{32,40},{40,32},{48,56},{56,48},{64,72... | collective-permute-start | bytes 1179656 | tf_op jit(solution)/shard_map/ppermute | solution.py:28
  (14 other events, 23.4 us)

commit v5 on v3

--- a/solution.py
+++ b/solution.py
@@ -17,7 +17,6 @@
 HALF_FEAT = HALF_HEADS * GROUP * HEAD_DIM
 SCALE = HEAD_DIM**-0.5
 TA = 3
-TB = 2
 LOG2E = 1.4426950408889634
 NEG = -1e30
 NT = (((1,), (1,)), ((), ()))
@@ -40,11 +39,11 @@
     pairs, strided = refs[:4], refs[4:8]
     refs = refs[8:]
     if tick:
-        for old, new in zip(refs[:7], refs[8:15]):
+        for old, new in zip(refs[:4], refs[5:9]):
             new[0] = old[...]
-        refs = refs[7:]
-        refs = refs[:1] + tuple(r.at[1] for r in refs[1:8]) + refs[8:]
-    both, other, back1, back2, back3, part1, part2, part3, own, part0 = refs
+        refs = refs[4:]
+        refs = refs[:1] + tuple(r.at[1] for r in refs[1:5]) + refs[5:]
+    both, other, back1, back2, back3, own, part0, part1, part2, part3 = refs
     backs = (own, back1, back2, back3)
     parts = (part0, part1, part2, part3)
     index = meta[0]
@@ -127,6 +126,7 @@
 
 
 WHOLE = pl.BlockSpec(memory_space=pltpu.VMEM)
+FAR = pl.BlockSpec(memory_space=pltpu.HBM)
 SCALAR = pl.BlockSpec(memory_space=pltpu.SMEM)
 WIDE = 2 * HALF_KV
 
@@ -148,14 +148,14 @@
     specs += [at(tick, 2 * BLK, WIDE)] * 4 + [at(tick, BLK, WIDE)] * 4
     bf16, f32 = jnp.bfloat16, jnp.float32
     out_shape = [shape((2, BLK, HALF_FEAT), bf16)]
-    lead = (2,) if tick else ()
-    if tick:
+    if earlier is None:
+        out_shape += [shape((BLK, HALF_FEAT), bf16)] + [shape((2 * BLK, WIDE), bf16)] * 3
+    else:
         args += earlier
-        specs += [WHOLE] * 7
-    out_shape.append(shape(lead + (BLK, HALF_FEAT), bf16))
-    out_shape += [shape(lead + (2 * BLK, WIDE), bf16)] * 3
-    out_shape += [shape(lead + (BLK, WIDE), bf16)] * 3
+        specs += [WHOLE] * 4
+        out_shape += [shape((2, BLK, HALF_FEAT), bf16)] + [shape((2, 2 * BLK, WIDE), bf16)] * 3
     out_shape += [shape((2 * BLK, WIDE), f32), shape((BLK, WIDE), f32)]
+    out_shape += [shape((BLK, WIDE), bf16)] * 3
     return pl.pallas_call(
         functools.partial(attention_kernel, tick),
         out_shape=out_shape,
@@ -170,29 +170,46 @@
     )(*args)
 
 
-def simple(kernel, out_shape, args, scalars=1):
+def far_scratch(arrays):
+    buffers = [pltpu.VMEM(a.shape, a.dtype) for a in arrays]
+    return buffers + [pltpu.SemaphoreType.DMA((len(arrays),))]
+
+
+def simple(kernel, out_shape, args, scalars=1, far=False):
     size = sum(a.size * a.dtype.itemsize for a in list(args) + list(out_shape))
     return pl.pallas_call(
         kernel,
         out_shape=out_shape,
-        in_specs=[SCALAR] * scalars + [WHOLE] * (len(args) - scalars),
+        in_specs=[SCALAR] * scalars + [FAR if far else WHOLE] * (len(args) - scalars),
         out_specs=[WHOLE] * len(out_shape),
+        scratch_shapes=far_scratch(args[scalars:]) if far else [],
         compiler_params=pltpu.CompilerParams(vmem_limit_bytes=16 << 20),
         cost_estimate=pl.CostEstimate(flops=size, bytes_accessed=size, transcendentals=0),
         name=kernel.__name__,
     )(*args)
 
 
-def column_sum(own0, own1, x1, x2, x3, wide_out, send_out):
-    for t, own in enumerate((own0, own1)):
-        total = own[...]
-        for x in (x1, x2, x3):
-            total = total + x[t].astype(jnp.float32)
+def column_sum(*refs):
+    wide_out, send_out = refs[8:]
+    for t in range(2):
+        total = refs[4 * t][...]
+        for s in range(1, 4):
+            total = total + refs[4 * t + s][...].astype(jnp.float32)
         wide_out[t] = total
         send_out[t] = total.astype(jnp.bfloat16)
 
 
-def split_all(meta, keys, values, inputs, first, head, keep, give, kv_keep, kv_give):
+def split_all(meta, *refs):
+    sources, (keep, give, kv_keep, kv_give), buffers, sems = refs[:5], refs[5:9], refs[9:14], refs[14]
+    copies = [
+        pltpu.make_async_copy(source, buffer, sems.at[n])
+        for n, (source, buffer) in enumerate(zip(sources, buffers))
+    ]
+    for copy in copies:
+        copy.start()
+    for copy in copies:
+        copy.wait()
+    keys, values, inputs, first, head = buffers
     swap = meta[0] % 2 == 1
     for source, at in ((keys, 0), (values, HALF_KV)):
         low, high = source[0, :, :, :HALF_KV], source[0, :, :, HALF_KV:]
@@ -281,6 +298,7 @@
         split_all,
         [ten, ten, half, half],
         [spot, saved_keys, saved_values, inputs, first_grads, head_grads],
+        far=True,
     )
     recv = sibling(give)
     up_low = ctx(kv_keep, lambda i: i + 8, lambda i: i % STRIDE == 0)
@@ -308,23 +326,22 @@
 
     first = attention(0, meta, gain, keep, recv, None, pairs, strided, None)
     grads = route(first[0], "pp", lambda i: i - 1)
-    second = attention(1, meta, gain, keep, recv, grads, pairs, strided, first[1:8])
-    columns = [first[9], second[9]]
-    columns += [ctx(second[4 + s], lambda i: i - STRIDE * s) for s in range(1, 4)]
+    columns = [ctx(first[6 + s], lambda i: i - STRIDE * s) for s in range(1, 4)]
+    grads, columns = lax.optimization_barrier((grads, columns))
+    second = attention(1, meta, gain, keep, recv, grads, pairs, strided, first[1:5])
+    columns = [first[6]] + columns + [second[6]]
+    columns += [ctx(second[6 + s], lambda i: i - STRIDE * s) for s in range(1, 4)]
     backs = [ctx(second[1 + d], lambda i: i - 2 * d) for d in range(1, 4)]
 
     wide = shape((2, BLK, WIDE), f32)
     total, send = simple(column_sum, [wide, half], columns, 0)
     rows = []
     for d in range(1, 4):
-        sent = send
-        if d == 1:
-            sent, backs[TB] = lax.optimization_barrier((send, backs[TB]))
-        rows.append(ctx(sent, lambda i: i - 2 * d, lambda i: (i // 2) % 4 == d))
+        rows.append(ctx(send, lambda i: i - 2 * d, lambda i: (i // 2) % 4 == d))
     mine, swap, down = simple(
         row_sum,
         [wide, shape((2, BLK, HALF_FEAT + WIDE), bf16), half],
-        [spot, total] + rows + [first[8], second[8]] + backs + [second[1]],
+        [spot, total] + rows + [first[5], second[5]] + backs + [second[1]],
     )
     swapped = sibling(swap)
     low = ctx(down, lambda i: i - 8, lambda i: i % STRIDE == 8)

time: 121 us -> 125 us (1.033)
  the two profiles are of different devices: /device:TPU:224 before, /device:TPU:176 now
where the time goes in v5:
time: 125 us; the launch traced here: 124 us
  starting transfers between devices  74.1 us (59%)
  waiting for transfers between devices  33.9 us (27%)
  Pallas kernels  9.98 us (8%)
  local copies, waits for them, and re-layouts  4.76 us (4%)
    ppermute x28, starting transfers between devices, route(): lax.ppermute(array, axis, [(a, b) for a, b in pairs if b is not None and...  74.1 us
    ppermute x28, waiting for transfers between devices, route(): lax.ppermute(array, axis, [(a, b) for a, b in pairs if b is not None and...  33.9 us
    pallas_call x2, Pallas kernels, attention(): pl.pallas_call(functools.partial(attention_kernel, tick), out_shape=out_s...  8.13 us
    unnamed x16, local copies, waits for them, and re-layouts  4.76 us
  transfers between devices with their start and end apart: 28, of which 11 were waited for; matrix products, arithmetic and copies ran while one was open for 0% of the time, Pallas kernels for 0%

profile of v5, /device:TPU:176, one launch (start us, length us, event | category | flops | bytes accessed | tf_op | source)
XLA Modules:
  0.0 123.9 jit_solution(11197217926332006145)
XLA Ops:
  5.9 1.9 %collective-permute-start = (bf16[10,64,512]{2,1,0:T(8,128)(2,1)S(1)}, bf16[10,64,512]{2,1,0:T(8,128)(2,1)S(1)}, u32[]{:S(2)}, u32[]{:S(2)}) collective-permute-start(bf16[10,64,512]{2,1,0:T(8,128)(2,1)S(1)} %get-tuple-element.41), channel_id=1, source_target_pairs={{0,8},{8,0},{16,24},{24,16},{32,40},{40,32},{48,56},{56,48},{64,72... | collective-permute-start | bytes 1966088 | tf_op jit(solution)/shard_map/ppermute | solution.py:29
  7.9 2.6 %collective-permute-start.1 = (bf16[2,64,512]{2,1,0:T(8,128)(2,1)S(1)}, bf16[2,64,512]{2,1,0:T(8,128)(2,1)S(1)}, u32[]{:S(2)}, u32[]{:S(2)}) collective-permute-start(bf16[2,64,512]{2,1,0:T(8,128)(2,1)S(1)} %get-tuple-element.42), channel_id=1, source_target_pairs={{0,64},{128,192},{256,320},{384,448},{1,65},{129,193},{257,321},{3... | collective-permute-start | bytes 393224 | tf_op jit(solution)/shard_map/ppermute | solution.py:29
  13.0 1.4 %collective-permute-done.2.up_high = bf16[2,64,512]{2,1,0:T(8,128)(2,1)S(1)} collective-permute-done((bf16[2,64,512]{2,1,0:T(8,128)(2,1)S(1)}, bf16[2,64,512]{2,1,0:T(8,128)(2,1)S(1)}, u32[]{:S(2)}, u32[]{:S(2)}) %collective-permute-start.2) | collective-permute-done | bytes 131104 | tf_op jit(solution)/shard_map/ppermute | solution.py:29
  14.4 1.9 %collective-permute-start.8 = (bf16[2,128,512]{2,1,0:T(8,128)(2,1)S(1)}, bf16[2,128,512]{2,1,0:T(8,128)(2,1)S(1)}, u32[]{:S(2)}, u32[]{:S(2)}) collective-permute-start(bf16[2,128,512]{2,1,0:T(8,128)(2,1)S(1)} %get-tuple-element.44.refs_0_.refs_1_), channel_id=1, source_target_pairs={{0,48},{8,56},{16,64},{24,72},{32,80},{40,88},{48,96},{56,104},{64... | collective-permute-start | bytes 786440 | tf_op jit(solution)/shard_map/ppermute | solution.py:29
  17.6 1.3 %collective-permute-start.6 = (bf16[2,64,512]{2,1,0:T(8,128)(2,1)S(1)}, bf16[2,64,512]{2,1,0:T(8,128)(2,1)S(1)}, u32[]{:S(2)}, u32[]{:S(2)}) collective-permute-start(bf16[2,64,512]{2,1,0:T(8,128)(2,1)S(1)} %get-tuple-element.45.start), channel_id=1, source_target_pairs={{0,32},{8,40},{64,96},{72,104},{128,160},{136,168},{192,224},{200,... | collective-permute-start | bytes 393224 | tf_op jit(solution)/shard_map/ppermute | solution.py:29
  18.9 3.2 %collective-permute-start.5 = (bf16[2,64,512]{2,1,0:T(8,128)(2,1)S(1)}, bf16[2,64,512]{2,1,0:T(8,128)(2,1)S(1)}, u32[]{:S(2)}, u32[]{:S(2)}) collective-permute-start(bf16[2,64,512]{2,1,0:T(8,128)(2,1)S(1)} %get-tuple-element.45.start), channel_id=1, source_target_pairs={{0,16},{8,24},{64,80},{72,88},{128,144},{136,152},{192,208},{200,2... | collective-permute-start | bytes 393224 | tf_op jit(solution)/shard_map/ppermute | solution.py:29
  22.2 1.9 %collective-permute-start.4 = (bf16[2,128,512]{2,1,0:T(8,128)(2,1)S(1)}, bf16[2,128,512]{2,1,0:T(8,128)(2,1)S(1)}, u32[]{:S(2)}, u32[]{:S(2)}) collective-permute-start(bf16[2,128,512]{2,1,0:T(8,128)(2,1)S(1)} %get-tuple-element.44.refs_0_.refs_1_), channel_id=1, source_target_pairs={{0,32},{8,40},{16,48},{24,56},{32,64},{40,72},{48,80},{56,88},{64,... | collective-permute-start | bytes 786440 | tf_op jit(solution)/shard_map/ppermute | solution.py:29
  24.1 1.9 %collective-permute-start.3 = (bf16[2,128,512]{2,1,0:T(8,128)(2,1)S(1)}, bf16[2,128,512]{2,1,0:T(8,128)(2,1)S(1)}, u32[]{:S(2)}, u32[]{:S(2)}) collective-permute-start(bf16[2,128,512]{2,1,0:T(8,128)(2,1)S(1)} %get-tuple-element.44.refs_0_.refs_1_), channel_id=1, source_target_pairs={{0,16},{8,24},{16,32},{24,40},{32,48},{40,56},{48,64},{56,72},{64,... | collective-permute-start | bytes 786440 | tf_op jit(solution)/shard_map/ppermute | solution.py:29
  30.2 6.0 %collective-permute-done.11.refs_7_.refs_8_ = bf16[2,64,512]{2,1,0:T(8,128)(2,1)S(1)} collective-permute-done((bf16[2,64,512]{2,1,0:T(8,128)(2,1)S(1)}, bf16[2,64,512]{2,1,0:T(8,128)(2,1)S(1)}, u32[]{:S(2)}, u32[]{:S(2)}) %collective-permute-start.11) | collective-permute-done | bytes 131104 | tf_op jit(solution)/shard_map/ppermute | solution.py:29
  36.2 6.2 %collective-permute-done.10.refs_6_.refs_7_ = bf16[2,64,512]{2,1,0:T(8,128)(2,1)S(1)} collective-permute-done((bf16[2,64,512]{2,1,0:T(8,128)(2,1)S(1)}, bf16[2,64,512]{2,1,0:T(8,128)(2,1)S(1)}, u32[]{:S(2)}, u32[]{:S(2)}) %collective-permute-start.10) | collective-permute-done | bytes 131104 | tf_op jit(solution)/shard_map/ppermute | solution.py:29
  42.4 4.0 %attention.2 = (bf16[2,64,1024]{2,1,0:T(8,128)(2,1)S(1)}, bf16[64,1024]{1,0:T(8,128)(2,1)S(1)}, bf16[128,512]{1,0:T(8,128)(2,1)S(1)}, bf16[128,512]{1,0:T(8,128)...) custom-call(s32[6]{0:T(128)S(1)} %pad_add_fusion.meta, ...), custom_call_target="tpu_custom_call" | custom-call | flops 1006632960 | bytes 4194304 | tf_op jit(solution)/shard_map/attention/pallas_call | solution.py:159
  46.5 1.9 %collective-permute-start.12 = (bf16[2,64,1024]{2,1,0:T(8,128)(2,1)S(1)}, bf16[2,64,1024]{2,1,0:T(8,128)(2,1)S(1)}, u32[]{:S(2)}, u32[]{:S(2)}) collective-permute-start(bf16[2,64,1024]{2,1,0:T(8,128)(2,1)S(1)} %get-tuple-element.49.mine0), channel_id=1, source_target_pairs={{1,0},{2,1},{3,2},{4,3},{5,4},{6,5},{7,6},{9,8},{10,9},{11,10},{12... | collective-permute-start | bytes 786440 | tf_op jit(solution)/shard_map/ppermute | solution.py:29
  48.4 4.9 %collective-permute-start.13 = (bf16[64,512]{1,0:T(8,128)(2,1)S(1)}, bf16[64,512]{1,0:T(8,128)(2,1)S(1)}, u32[]{:S(2)}, u32[]{:S(2)}) collective-permute-start(bf16[64,512]{1,0:T(8,128)(2,1)S(1)} %get-tuple-element.50), channel_id=1, source_target_pairs={{128,0},{136,8},{144,16},{152,24},{160,32},{168,40},{176,48},{184,... | collective-permute-start | bytes 196616 | tf_op jit(solution)/shard_map/ppermute | solution.py:29
  56.0 1.3 %collective-permute-done.14.refs_2_ = bf16[64,512]{1,0:T(8,128)(2,1)S(1)} collective-permute-done((bf16[64,512]{1,0:T(8,128)(2,1)S(1)}, bf16[64,512]{1,0:T(8,128)(2,1)S(1)}, u32[]{:S(2)}, u32[]{:S(2)}) %collective-permute-start.14) | collective-permute-done | bytes 65568 | tf_op jit(solution)/shard_map/ppermute | solution.py:29
  58.5 4.1 %attention.3 = (bf16[2,64,1024]{2,1,0:T(8,128)(2,1)S(1)}, bf16[2,64,1024]{2,1,0:T(8,128)(2,1)S(1)}, bf16[2,128,512]{2,1,0:T(8,128)(2,1)S(1)}, bf16[2,128,512]{2,...) custom-call(s32[6]{0:T(128)S(1)} %pad_add_fusion.meta, ...), custom_call_target="tpu_custom_call" | custom-call | flops 1006632960 | bytes 4194304 | tf_op jit(solution)/shard_map/attention/pallas_call | solution.py:159
  62.6 3.5 %collective-permute-start.16 = (bf16[64,512]{1,0:T(8,128)(2,1)S(1)}, bf16[64,512]{1,0:T(8,128)(2,1)S(1)}, u32[]{:S(2)}, u32[]{:S(2)}) collective-permute-start(bf16[64,512]{1,0:T(8,128)(2,1)S(1)} %get-tuple-element.62), channel_id=1, source_target_pairs={{128,0},{136,8},{144,16},{152,24},{160,32},{168,40},{176,48},{184,... | collective-permute-start | bytes 196616 | tf_op jit(solution)/shard_map/ppermute | solution.py:29
  66.0 7.3 %collective-permute-start.17 = (bf16[64,512]{1,0:T(8,128)(2,1)S(1)}, bf16[64,512]{1,0:T(8,128)(2,1)S(1)}, u32[]{:S(2)}, u32[]{:S(2)}) collective-permute-start(bf16[64,512]{1,0:T(8,128)(2,1)S(1)} %get-tuple-element.63), channel_id=1, source_target_pairs={{256,0},{264,8},{272,16},{280,24},{288,32},{296,40},{304,48},{312,... | collective-permute-start | bytes 196616 | tf_op jit(solution)/shard_map/ppermute | solution.py:29
  74.7 14.4 %collective-permute-start.22 = (bf16[2,128,512]{2,1,0:T(8,128)(2,1)S(1)}, bf16[2,128,512]{2,1,0:T(8,128)(2,1)S(1)}, u32[]{:S(2)}, u32[]{:S(2)}) collective-permute-start(bf16[2,128,512]{2,1,0:T(8,128)(2,1)S(1)} %get-tuple-element.69), channel_id=1, source_target_pairs={{16,0},{24,8},{32,16},{40,24},{48,32},{56,40},{64,48},{72,56},{80,... | collective-permute-start | bytes 786440 | tf_op jit(solution)/shard_map/ppermute | solution.py:29
  90.5 1.9 %collective-permute-start.23 = (bf16[2,128,512]{2,1,0:T(8,128)(2,1)S(1)}, bf16[2,128,512]{2,1,0:T(8,128)(2,1)S(1)}, u32[]{:S(2)}, u32[]{:S(2)}) collective-permute-start(bf16[2,128,512]{2,1,0:T(8,128)(2,1)S(1)} %get-tuple-element.70), channel_id=1, source_target_pairs={{32,0},{40,8},{48,16},{56,24},{64,32},{72,40},{80,48},{88,56},{96,... | collective-permute-start | bytes 786440 | tf_op jit(solution)/shard_map/ppermute | solution.py:29
  92.4 6.6 %collective-permute-start.24 = (bf16[2,128,512]{2,1,0:T(8,128)(2,1)S(1)}, bf16[2,128,512]{2,1,0:T(8,128)(2,1)S(1)}, u32[]{:S(2)}, u32[]{:S(2)}) collective-permute-start(bf16[2,128,512]{2,1,0:T(8,128)(2,1)S(1)} %get-tuple-element.71), channel_id=1, source_target_pairs={{48,0},{56,8},{64,16},{72,24},{80,32},{88,40},{96,48},{104,56},{11... | collective-permute-start | bytes 786440 | tf_op jit(solution)/shard_map/ppermute | solution.py:29
  100.3 2.5 %collective-permute-done.21.refs_3_ = bf16[2,64,512]{2,1,0:T(8,128)(2,1)S(1)} collective-permute-done((bf16[2,64,512]{2,1,0:T(8,128)(2,1)S(1)}, bf16[2,64,512]{2,1,0:T(8,128)(2,1)S(1)}, u32[]{:S(2)}, u32[]{:S(2)}) %collective-permute-start.21) | collective-permute-done | bytes 131104 | tf_op jit(solution)/shard_map/ppermute | solution.py:29
  104.2 6.0 %collective-permute-done.20.refs_2_ = bf16[2,64,512]{2,1,0:T(8,128)(2,1)S(1)} collective-permute-done((bf16[2,64,512]{2,1,0:T(8,128)(2,1)S(1)}, bf16[2,64,512]{2,1,0:T(8,128)(2,1)S(1)}, u32[]{:S(2)}, u32[]{:S(2)}) %collective-permute-start.20) | collective-permute-done | bytes 131104 | tf_op jit(solution)/shard_map/ppermute | solution.py:29
  111.5 1.9 %collective-permute-start.25 = (bf16[2,64,1536]{2,1,0:T(8,128)(2,1)S(1)}, bf16[2,64,1536]{2,1,0:T(8,128)(2,1)S(1)}, u32[]{:S(2)}, u32[]{:S(2)}) collective-permute-start(bf16[2,64,1536]{2,1,0:T(8,128)(2,1)S(1)} %get-tuple-element.74), channel_id=1, source_target_pairs={{0,8},{8,0},{16,24},{24,16},{32,40},{40,32},{48,56},{56,48},{64,72... | collective-permute-start | bytes 1179656 | tf_op jit(solution)/shard_map/ppermute | solution.py:29
  116.1 6.1 %collective-permute-done.27.high = bf16[2,64,512]{2,1,0:T(8,128)(2,1)S(1)} collective-permute-done((bf16[2,64,512]{2,1,0:T(8,128)(2,1)S(1)}, bf16[2,64,512]{2,1,0:T(8,128)(2,1)S(1)}, u32[]{:S(2)}, u32[]{:S(2)}) %collective-permute-start.27) | collective-permute-done | bytes 131104 | tf_op jit(solution)/shard_map/ppermute | solution.py:29
  (59 shorter events, 28.0 us)
Async XLA Ops:
  5.9 8.4 %collective-permute-start = (bf16[10,64,512]{2,1,0:T(8,128)(2,1)S(1)}, bf16[10,64,512]{2,1,0:T(8,128)(2,1)S(1)}, u32[]{:S(2)}, u32[]{:S(2)}) collective-permute-start(bf16[10,64,512]{2,1,0:T(8,128)(2,1)S(1)} %get-tuple-element.41), channel_id=1, source_target_pairs={{0,8},{8,0},{16,24},{24,16},{32,40},{40,32},{48,56},{56,48},{64,72... | collective-permute-start | bytes 1966088 | tf_op jit(solution)/shard_map/ppermute | solution.py:29
  14.4 14.3 %collective-permute-start.8 = (bf16[2,128,512]{2,1,0:T(8,128)(2,1)S(1)}, bf16[2,128,512]{2,1,0:T(8,128)(2,1)S(1)}, u32[]{:S(2)}, u32[]{:S(2)}) collective-permute-start(bf16[2,128,512]{2,1,0:T(8,128)(2,1)S(1)} %get-tuple-element.44.refs_0_.refs_1_), channel_id=1, source_target_pairs={{0,48},{8,56},{16,64},{24,72},{32,80},{40,88},{48,96},{56,104},{64... | collective-permute-start | bytes 786440 | tf_op jit(solution)/shard_map/ppermute | solution.py:29
  16.3 7.8 %collective-permute-start.7 = (bf16[2,64,512]{2,1,0:T(8,128)(2,1)S(1)}, bf16[2,64,512]{2,1,0:T(8,128)(2,1)S(1)}, u32[]{:S(2)}, u32[]{:S(2)}) collective-permute-start(bf16[2,64,512]{2,1,0:T(8,128)(2,1)S(1)} %get-tuple-element.45.start), channel_id=1, source_target_pairs={{0,48},{8,56},{64,112},{72,120},{128,176},{136,184},{192,240},{200... | collective-permute-start | bytes 393224 | tf_op jit(solution)/shard_map/ppermute | solution.py:29
  17.6 8.4 %collective-permute-start.6 = (bf16[2,64,512]{2,1,0:T(8,128)(2,1)S(1)}, bf16[2,64,512]{2,1,0:T(8,128)(2,1)S(1)}, u32[]{:S(2)}, u32[]{:S(2)}) collective-permute-start(bf16[2,64,512]{2,1,0:T(8,128)(2,1)S(1)} %get-tuple-element.45.start), channel_id=1, source_target_pairs={{0,32},{8,40},{64,96},{72,104},{128,160},{136,168},{192,224},{200,... | collective-permute-start | bytes 393224 | tf_op jit(solution)/shard_map/ppermute | solution.py:29
  18.9 7.1 %collective-permute-start.5 = (bf16[2,64,512]{2,1,0:T(8,128)(2,1)S(1)}, bf16[2,64,512]{2,1,0:T(8,128)(2,1)S(1)}, u32[]{:S(2)}, u32[]{:S(2)}) collective-permute-start(bf16[2,64,512]{2,1,0:T(8,128)(2,1)S(1)} %get-tuple-element.45.start), channel_id=1, source_target_pairs={{0,16},{8,24},{64,80},{72,88},{128,144},{136,152},{192,208},{200,2... | collective-permute-start | bytes 393224 | tf_op jit(solution)/shard_map/ppermute | solution.py:29
  22.2 20.2 %collective-permute-start.4 = (bf16[2,128,512]{2,1,0:T(8,128)(2,1)S(1)}, bf16[2,128,512]{2,1,0:T(8,128)(2,1)S(1)}, u32[]{:S(2)}, u32[]{:S(2)}) collective-permute-start(bf16[2,128,512]{2,1,0:T(8,128)(2,1)S(1)} %get-tuple-element.44.refs_0_.refs_1_), channel_id=1, source_target_pairs={{0,32},{8,40},{16,48},{24,56},{32,64},{40,72},{48,80},{56,88},{64,... | collective-permute-start | bytes 786440 | tf_op jit(solution)/shard_map/ppermute | solution.py:29
  24.1 18.3 %collective-permute-start.3 = (bf16[2,128,512]{2,1,0:T(8,128)(2,1)S(1)}, bf16[2,128,512]{2,1,0:T(8,128)(2,1)S(1)}, u32[]{:S(2)}, u32[]{:S(2)}) collective-permute-start(bf16[2,128,512]{2,1,0:T(8,128)(2,1)S(1)} %get-tuple-element.44.refs_0_.refs_1_), channel_id=1, source_target_pairs={{0,16},{8,24},{16,32},{24,40},{32,48},{40,56},{48,64},{56,72},{64,... | collective-permute-start | bytes 786440 | tf_op jit(solution)/shard_map/ppermute | solution.py:29
  26.1 10.1 %collective-permute-start.11 = (bf16[2,64,512]{2,1,0:T(8,128)(2,1)S(1)}, bf16[2,64,512]{2,1,0:T(8,128)(2,1)S(1)}, u32[]{:S(2)}, u32[]{:S(2)}) collective-permute-start(bf16[2,64,512]{2,1,0:T(8,128)(2,1)S(1)} %choose.1.refs_4_.refs_5_), channel_id=1, source_target_pairs={{0,384},{8,392},{16,400},{24,408},{32,416},{40,424},{48,432},{56,4... | collective-permute-start | bytes 393224 | tf_op jit(solution)/shard_map/ppermute | solution.py:29
  27.4 15.0 %collective-permute-start.10 = (bf16[2,64,512]{2,1,0:T(8,128)(2,1)S(1)}, bf16[2,64,512]{2,1,0:T(8,128)(2,1)S(1)}, u32[]{:S(2)}, u32[]{:S(2)}) collective-permute-start(bf16[2,64,512]{2,1,0:T(8,128)(2,1)S(1)} %choose.1.refs_4_.refs_5_), channel_id=1, source_target_pairs={{0,256},{8,264},{16,272},{24,280},{32,288},{40,296},{48,304},{56,3... | collective-permute-start | bytes 393224 | tf_op jit(solution)/shard_map/ppermute | solution.py:29
  28.7 13.7 %collective-permute-start.9 = (bf16[2,64,512]{2,1,0:T(8,128)(2,1)S(1)}, bf16[2,64,512]{2,1,0:T(8,128)(2,1)S(1)}, u32[]{:S(2)}, u32[]{:S(2)}) collective-permute-start(bf16[2,64,512]{2,1,0:T(8,128)(2,1)S(1)} %choose.1.refs_4_.refs_5_), channel_id=1, source_target_pairs={{0,128},{8,136},{16,144},{24,152},{32,160},{40,168},{48,176},{56,1... | collective-permute-start | bytes 393224 | tf_op jit(solution)/shard_map/ppermute | solution.py:29
  46.5 12.0 %collective-permute-start.12 = (bf16[2,64,1024]{2,1,0:T(8,128)(2,1)S(1)}, bf16[2,64,1024]{2,1,0:T(8,128)(2,1)S(1)}, u32[]{:S(2)}, u32[]{:S(2)}) collective-permute-start(bf16[2,64,1024]{2,1,0:T(8,128)(2,1)S(1)} %get-tuple-element.49.mine0), channel_id=1, source_target_pairs={{1,0},{2,1},{3,2},{4,3},{5,4},{6,5},{7,6},{9,8},{10,9},{11,10},{12... | collective-permute-start | bytes 786440 | tf_op jit(solution)/shard_map/ppermute | solution.py:29
  48.4 7.6 %collective-permute-start.13 = (bf16[64,512]{1,0:T(8,128)(2,1)S(1)}, bf16[64,512]{1,0:T(8,128)(2,1)S(1)}, u32[]{:S(2)}, u32[]{:S(2)}) collective-permute-start(bf16[64,512]{1,0:T(8,128)(2,1)S(1)} %get-tuple-element.50), channel_id=1, source_target_pairs={{128,0},{136,8},{144,16},{152,24},{160,32},{168,40},{176,48},{184,... | collective-permute-start | bytes 196616 | tf_op jit(solution)/shard_map/ppermute | solution.py:29
  62.6 26.5 %collective-permute-start.16 = (bf16[64,512]{1,0:T(8,128)(2,1)S(1)}, bf16[64,512]{1,0:T(8,128)(2,1)S(1)}, u32[]{:S(2)}, u32[]{:S(2)}) collective-permute-start(bf16[64,512]{1,0:T(8,128)(2,1)S(1)} %get-tuple-element.62), channel_id=1, source_target_pairs={{128,0},{136,8},{144,16},{152,24},{160,32},{168,40},{176,48},{184,... | collective-permute-start | bytes 196616 | tf_op jit(solution)/shard_map/ppermute | solution.py:29
  66.0 23.1 %collective-permute-start.17 = (bf16[64,512]{1,0:T(8,128)(2,1)S(1)}, bf16[64,512]{1,0:T(8,128)(2,1)S(1)}, u32[]{:S(2)}, u32[]{:S(2)}) collective-permute-start(bf16[64,512]{1,0:T(8,128)(2,1)S(1)} %get-tuple-element.63), channel_id=1, source_target_pairs={{256,0},{264,8},{272,16},{280,24},{288,32},{296,40},{304,48},{312,... | collective-permute-start | bytes 196616 | tf_op jit(solution)/shard_map/ppermute | solution.py:29
  73.4 15.8 %collective-permute-start.18 = (bf16[64,512]{1,0:T(8,128)(2,1)S(1)}, bf16[64,512]{1,0:T(8,128)(2,1)S(1)}, u32[]{:S(2)}, u32[]{:S(2)}) collective-permute-start(bf16[64,512]{1,0:T(8,128)(2,1)S(1)} %get-tuple-element.64), channel_id=1, source_target_pairs={{384,0},{392,8},{400,16},{408,24},{416,32},{424,40},{432,48},{440,... | collective-permute-start | bytes 196616 | tf_op jit(solution)/shard_map/ppermute | solution.py:29
  74.7 35.5 %collective-permute-start.22 = (bf16[2,128,512]{2,1,0:T(8,128)(2,1)S(1)}, bf16[2,128,512]{2,1,0:T(8,128)(2,1)S(1)}, u32[]{:S(2)}, u32[]{:S(2)}) collective-permute-start(bf16[2,128,512]{2,1,0:T(8,128)(2,1)S(1)} %get-tuple-element.69), channel_id=1, source_target_pairs={{16,0},{24,8},{32,16},{40,24},{48,32},{56,40},{64,48},{72,56},{80,... | collective-permute-start | bytes 786440 | tf_op jit(solution)/shard_map/ppermute | solution.py:29
  89.2 13.7 %collective-permute-start.21 = (bf16[2,64,512]{2,1,0:T(8,128)(2,1)S(1)}, bf16[2,64,512]{2,1,0:T(8,128)(2,1)S(1)}, u32[]{:S(2)}, u32[]{:S(2)}) collective-permute-start(bf16[2,64,512]{2,1,0:T(8,128)(2,1)S(1)} %get-tuple-element.66), channel_id=1, source_target_pairs={{48,0},{56,8},{112,64},{120,72},{176,128},{184,136},{240,192},{248... | collective-permute-start | bytes 393224 | tf_op jit(solution)/shard_map/ppermute | solution.py:29
  90.5 19.7 %collective-permute-start.23 = (bf16[2,128,512]{2,1,0:T(8,128)(2,1)S(1)}, bf16[2,128,512]{2,1,0:T(8,128)(2,1)S(1)}, u32[]{:S(2)}, u32[]{:S(2)}) collective-permute-start(bf16[2,128,512]{2,1,0:T(8,128)(2,1)S(1)} %get-tuple-element.70), channel_id=1, source_target_pairs={{32,0},{40,8},{48,16},{56,24},{64,32},{72,40},{80,48},{88,56},{96,... | collective-permute-start | bytes 786440 | tf_op jit(solution)/shard_map/ppermute | solution.py:29
  92.4 18.9 %collective-permute-start.24 = (bf16[2,128,512]{2,1,0:T(8,128)(2,1)S(1)}, bf16[2,128,512]{2,1,0:T(8,128)(2,1)S(1)}, u32[]{:S(2)}, u32[]{:S(2)}) collective-permute-start(bf16[2,128,512]{2,1,0:T(8,128)(2,1)S(1)} %get-tuple-element.71), channel_id=1, source_target_pairs={{48,0},{56,8},{64,16},{72,24},{80,32},{88,40},{96,48},{104,56},{11... | collective-permute-start | bytes 786440 | tf_op jit(solution)/shard_map/ppermute | solution.py:29
  99.0 11.1 %collective-permute-start.20 = (bf16[2,64,512]{2,1,0:T(8,128)(2,1)S(1)}, bf16[2,64,512]{2,1,0:T(8,128)(2,1)S(1)}, u32[]{:S(2)}, u32[]{:S(2)}) collective-permute-start(bf16[2,64,512]{2,1,0:T(8,128)(2,1)S(1)} %get-tuple-element.66), channel_id=1, source_target_pairs={{32,0},{40,8},{96,64},{104,72},{160,128},{168,136},{224,192},{232,... | collective-permute-start | bytes 393224 | tf_op jit(solution)/shard_map/ppermute | solution.py:29
  102.9 7.3 %collective-permute-start.19 = (bf16[2,64,512]{2,1,0:T(8,128)(2,1)S(1)}, bf16[2,64,512]{2,1,0:T(8,128)(2,1)S(1)}, u32[]{:S(2)}, u32[]{:S(2)}) collective-permute-start(bf16[2,64,512]{2,1,0:T(8,128)(2,1)S(1)} %get-tuple-element.66), channel_id=1, source_target_pairs={{16,0},{24,8},{80,64},{88,72},{144,128},{152,136},{208,192},{216,2... | collective-permute-start | bytes 393224 | tf_op jit(solution)/shard_map/ppermute | solution.py:29
  111.5 11.5 %collective-permute-start.25 = (bf16[2,64,1536]{2,1,0:T(8,128)(2,1)S(1)}, bf16[2,64,1536]{2,1,0:T(8,128)(2,1)S(1)}, u32[]{:S(2)}, u32[]{:S(2)}) collective-permute-start(bf16[2,64,1536]{2,1,0:T(8,128)(2,1)S(1)} %get-tuple-element.74), channel_id=1, source_target_pairs={{0,8},{8,0},{16,24},{24,16},{32,40},{40,32},{48,56},{56,48},{64,72... | collective-permute-start | bytes 1179656 | tf_op jit(solution)/shard_map/ppermute | solution.py:29
  113.5 8.7 %collective-permute-start.27 = (bf16[2,64,512]{2,1,0:T(8,128)(2,1)S(1)}, bf16[2,64,512]{2,1,0:T(8,128)(2,1)S(1)}, u32[]{:S(2)}, u32[]{:S(2)}) collective-permute-start(bf16[2,64,512]{2,1,0:T(8,128)(2,1)S(1)} %get-tuple-element.75), channel_id=1, source_target_pairs={{72,0},{200,128},{328,256},{456,384},{73,1},{201,129},{329,257},{4... | collective-permute-start | bytes 393224 | tf_op jit(solution)/shard_map/ppermute | solution.py:29
  114.8 8.2 %collective-permute-start.26 = (bf16[2,64,512]{2,1,0:T(8,128)(2,1)S(1)}, bf16[2,64,512]{2,1,0:T(8,128)(2,1)S(1)}, u32[]{:S(2)}, u32[]{:S(2)}) collective-permute-start(bf16[2,64,512]{2,1,0:T(8,128)(2,1)S(1)} %get-tuple-element.75), channel_id=1, source_target_pairs={{64,0},{192,128},{320,256},{448,384},{65,1},{193,129},{321,257},{4... | collective-permute-start | bytes 393224 | tf_op jit(solution)/shard_map/ppermute | solution.py:29
  (12 other events, 35.2 us)

commit v6 on v3

--- a/solution.py
+++ b/solution.py
@@ -16,8 +16,7 @@
 HALF_KV = HALF_HEADS * HEAD_DIM
 HALF_FEAT = HALF_HEADS * GROUP * HEAD_DIM
 SCALE = HEAD_DIM**-0.5
-TA = 3
-TB = 2
+FARLIM = 56
 LOG2E = 1.4426950408889634
 NEG = -1e30
 NT = (((1,), (1,)), ((), ()))
@@ -127,6 +126,7 @@
 
 
 WHOLE = pl.BlockSpec(memory_space=pltpu.VMEM)
+FAR = pl.BlockSpec(memory_space=pltpu.HBM)
 SCALAR = pl.BlockSpec(memory_space=pltpu.SMEM)
 WIDE = 2 * HALF_KV
 
@@ -170,14 +170,20 @@
     )(*args)
 
 
-def simple(kernel, out_shape, args, scalars=1):
+def far_scratch(arrays):
+    buffers = [pltpu.VMEM(a.shape, a.dtype) for a in arrays]
+    return buffers + [pltpu.SemaphoreType.DMA((len(arrays),))]
+
+
+def simple(kernel, out_shape, args, scalars=1, far=False):
     size = sum(a.size * a.dtype.itemsize for a in list(args) + list(out_shape))
     return pl.pallas_call(
         kernel,
         out_shape=out_shape,
-        in_specs=[SCALAR] * scalars + [WHOLE] * (len(args) - scalars),
+        in_specs=[SCALAR] * scalars + [FAR if far else WHOLE] * (len(args) - scalars),
         out_specs=[WHOLE] * len(out_shape),
-        compiler_params=pltpu.CompilerParams(vmem_limit_bytes=16 << 20),
+        scratch_shapes=far_scratch(args[scalars:]) if far else [],
+        compiler_params=pltpu.CompilerParams(vmem_limit_bytes=(FARLIM if far else 16) << 20),
         cost_estimate=pl.CostEstimate(flops=size, bytes_accessed=size, transcendentals=0),
         name=kernel.__name__,
     )(*args)
@@ -192,15 +198,23 @@
         send_out[t] = total.astype(jnp.bfloat16)
 
 
-def split_all(meta, keys, values, inputs, first, head, keep, give, kv_keep, kv_give):
+def split_all(meta, *refs):
+    sources, (keep, give), buffers, sems = refs[:5], refs[5:7], refs[7:12], refs[12]
+    copies = [
+        pltpu.make_async_copy(source, buffer, sems.at[n])
+        for n, (source, buffer) in enumerate(zip(sources, buffers))
+    ]
+    for copy in copies:
+        copy.start()
+    for copy in copies:
+        copy.wait()
+    keys, values, inputs, first, head = buffers
     swap = meta[0] % 2 == 1
     for source, at in ((keys, 0), (values, HALF_KV)):
         low, high = source[0, :, :, :HALF_KV], source[0, :, :, HALF_KV:]
         mine, far = jnp.where(swap, high, low), jnp.where(swap, low, high)
         keep[:2, :, at : at + HALF_KV] = mine
         give[:2, :, at : at + HALF_KV] = far
-        kv_keep[:, :, at : at + HALF_KV] = mine
-        kv_give[:, :, at : at + HALF_KV] = far
     for n, source in enumerate((inputs.at[0, 0], inputs.at[0, 1], first.at[0], head.at[0])):
         for h in range(HALF_HEADS):
             low = source[:, h * WIDE : (h + 1) * WIDE]
@@ -209,51 +223,49 @@
             give[2 + 2 * n + h] = jnp.where(swap, low, high)
 
 
-def pair_keys(meta, keep, recv, up_low, up_high, pair, start):
-    keep, recv = keep.at[:2], recv.at[:2]
+def pair_keys(meta, keep, recv, pair):
+    pair[:, :BLK] = keep[:2]
+    pair[:, BLK:] = recv[:2]
+
+
+def choose(meta, p0, p1, p2, p3, out):
     core = meta[0] % 2
+    place = (meta[0] // 2) % 4
+    for n, pair in enumerate((p0, p1, p2, p3)):
+        @pl.when(place == n)
+        def _():
+            out[...] = jnp.where(core == 0, pair[:, :BLK], pair[:, BLK:])
+
+
+def add_strided(meta, total, below, back1, back2, back3, own0, own1, out1, out2, out3, near):
+    core = meta[0] % 2
+    place = (meta[0] // 2) % 4
     even = (meta[0] // 8) % 2 == 0
-    pair[:, :BLK] = keep[...]
-    pair[:, BLK:] = recv[...]
-    near = jnp.where(core == 0, keep[...], recv[...])
-    above = jnp.where(core == 0, up_low[...], up_high[...])
-    start[...] = jnp.where(even, near, above)
-
-
-def choose(meta, start, x1, x2, x3, out):
-    place = (meta[0] // 2) % 4
-    near = jnp.where(place == 0, start[...], x1[...])
-    far = jnp.where(place == 2, x2[...], x3[...])
-    out[...] = jnp.where(place < 2, near, far)
-
-
-def row_sum(meta, *refs):
-    total, x1, x2, x3, own0, own1, back1, back2, back3, far_rows = refs[:10]
-    mine_out, swap_out, strided_out = refs[10:]
-    index = meta[0]
-    owner = (index // 2) % 4 == 0
-    even = (index // 8) % 2 == 0
-    first = (owner & even & (index % 2 == 0)).astype(jnp.float32)
-    second = (owner & even & (index % 2 == 1)).astype(jnp.float32)
     for t, own in enumerate((own0, own1)):
-        strided = total[t]
-        for x in (x1, x2, x3):
-            strided = strided + x[t].astype(jnp.float32)
-        strided_out[t] = strided.astype(jnp.bfloat16)
-        near = own[...]
+        strided = total[t] + below[t].astype(jnp.float32)
+        halves = [jnp.where(even & (core == k), strided, 0.0) for k in range(2)]
+        spread = jnp.concatenate(halves, axis=0)
+        near[t] = own[...] + jnp.where(place == 0, spread, 0.0)
+        for d, (back, out) in enumerate(((back1, out1), (back2, out2), (back3, out3))):
+            held = back[t].astype(jnp.float32) + jnp.where(place == d + 1, spread, 0.0)
+            out[t] = held.astype(jnp.bfloat16)
+
+
+def row_sum(meta, near, back1, back2, back3, far_rows, mine_out, swap_out):
+    for t in range(2):
+        total = near[t]
         for back in (back1, back2, back3):
-            near = near + back[t].astype(jnp.float32)
-        mine_out[t] = near[:BLK] + first * strided
+            total = total + back[t].astype(jnp.float32)
+        mine_out[t] = total[:BLK]
         swap_out[t, :, :HALF_FEAT] = far_rows[t]
-        swap_out[t, :, HALF_FEAT:] = (near[BLK:] + second * strided).astype(jnp.bfloat16)
-
-
-def finish(meta, mine, swapped, low, high, mine0, mine1, rows_out, keys_out, values_out):
+        swap_out[t, :, HALF_FEAT:] = total[BLK:].astype(jnp.bfloat16)
+
+
+def finish(meta, mine, swapped, mine0, mine1, rows_out, keys_out, values_out):
     swap = meta[0] % 2 == 1
     for t, rows in enumerate((mine0, mine1)):
-        other = swapped[t, :, HALF_FEAT:].astype(jnp.float32)
-        own = (mine[t] + low[t].astype(jnp.float32)).astype(jnp.bfloat16)
-        far = (other + high[t].astype(jnp.float32)).astype(jnp.bfloat16)
+        own = mine[t].astype(jnp.bfloat16)
+        far = swapped[t, :, HALF_FEAT:]
         left, right = jnp.where(swap, far, own), jnp.where(swap, own, far)
         for out, at in ((keys_out, 0), (values_out, HALF_KV)):
             out[0, t, :, :HALF_KV] = left[:, at : at + HALF_KV]
@@ -277,29 +289,19 @@
     spot = index.astype(jnp.int32).reshape(1)
     half = shape((2, BLK, WIDE), bf16)
     ten = shape((10, BLK, WIDE), bf16)
-    keep, give, kv_keep, kv_give = simple(
+    keep, give = simple(
         split_all,
-        [ten, ten, half, half],
+        [ten, ten],
         [spot, saved_keys, saved_values, inputs, first_grads, head_grads],
+        far=True,
     )
     recv = sibling(give)
-    up_low = ctx(kv_keep, lambda i: i + 8, lambda i: i % STRIDE == 0)
-    up_high = ctx(kv_give, lambda i: i + 9, lambda i: i % STRIDE == 0)
-    pair, start = simple(
-        pair_keys,
-        [shape((2, 2 * BLK, WIDE), bf16), half],
-        [spot, keep, recv, up_low, up_high],
-    )
-    across = [ctx(start, lambda i: i + 2 * d, lambda i: (i // 2) % 4 == 0) for d in range(1, 4)]
-    (chosen,) = simple(choose, [half], [spot, start] + across)
+    (pair,) = simple(pair_keys, [shape((2, 2 * BLK, WIDE), bf16)], [spot, keep, recv])
     pairs = [pair] + [ctx(pair, lambda i: i + 2 * d) for d in range(1, 4)]
-    strided = [chosen]
-    for s in range(1, 4):
-        sent = chosen
-        if s == 1:
-            sent, pairs[TA] = lax.optimization_barrier((chosen, pairs[TA]))
-        strided.append(ctx(sent, lambda i: i + STRIDE * s))
-
+    (chosen,) = simple(choose, [half], [spot] + pairs)
+    above = ctx(chosen, lambda i: i + 8, lambda i: (i // 8) % 2 == 0)
+    chosen = jnp.where((index // 8) % 2 == 0, chosen, above)
+    strided = [chosen] + [ctx(chosen, lambda i: i + STRIDE * s) for s in range(1, 4)]
     gain = jnp.where(core == 0, query_gain[:, :HALF_FEAT], query_gain[:, HALF_FEAT:])
     heads = jnp.where(core == 0, window[0, :2], window[0, 2:])
     steps = jnp.where(core == 0, stride[0, :2], stride[0, 2:])
@@ -311,29 +313,27 @@
     second = attention(1, meta, gain, keep, recv, grads, pairs, strided, first[1:8])
     columns = [first[9], second[9]]
     columns += [ctx(second[4 + s], lambda i: i - STRIDE * s) for s in range(1, 4)]
-    backs = [ctx(second[1 + d], lambda i: i - 2 * d) for d in range(1, 4)]
-
     wide = shape((2, BLK, WIDE), f32)
     total, send = simple(column_sum, [wide, half], columns, 0)
-    rows = []
-    for d in range(1, 4):
-        sent = send
-        if d == 1:
-            sent, backs[TB] = lax.optimization_barrier((send, backs[TB]))
-        rows.append(ctx(sent, lambda i: i - 2 * d, lambda i: (i // 2) % 4 == d))
-    mine, swap, down = simple(
+    below = ctx(send, lambda i: i - 8, lambda i: (i // 8) % 2 == 1)
+    full = shape((2, 2 * BLK, WIDE), bf16)
+    *backs, near = simple(
+        add_strided,
+        [full, full, full, shape((2, 2 * BLK, WIDE), f32)],
+        [spot, total, below] + list(second[2:5]) + [first[8], second[8]],
+    )
+    backs = [ctx(backs[d - 1], lambda i: i - 2 * d) for d in range(1, 4)]
+    mine, swap = simple(
         row_sum,
-        [wide, shape((2, BLK, HALF_FEAT + WIDE), bf16), half],
-        [spot, total] + rows + [first[8], second[8]] + backs + [second[1]],
+        [wide, shape((2, BLK, HALF_FEAT + WIDE), bf16)],
+        [spot, near] + backs + [second[1]],
     )
     swapped = sibling(swap)
-    low = ctx(down, lambda i: i - 8, lambda i: i % STRIDE == 8)
-    high = ctx(down, lambda i: i - 9, lambda i: i % STRIDE == 9)
     keys_shape = shape(saved_keys.shape, bf16)
     grads_out, key_grads, value_grads = simple(
         finish,
         [shape(inputs.shape, bf16), keys_shape, keys_shape],
-        [spot, mine, swapped, low, high, first[0], second[0]],
+        [spot, mine, swapped, first[0], second[0]],
     )
     return grads_out, key_grads, value_grads
 

time: 121 us -> 124 us (1.025)
  the two profiles are of different devices: /device:TPU:224 before, /device:TPU:195 now
where the time goes in v6:
time: 124 us; the launch traced here: 123 us
  waiting for transfers between devices  62.8 us (51%)
  starting transfers between devices  46.1 us (37%)
  Pallas kernels  12 us (10%)
    ppermute x17, waiting for transfers between devices, route(): lax.ppermute(array, axis, [(a, b) for a, b in pairs if b is not None and...  62.8 us
    ppermute x17, starting transfers between devices, route(): lax.ppermute(array, axis, [(a, b) for a, b in pairs if b is not None and...  46.1 us
    pallas_call x2, Pallas kernels, attention(): pl.pallas_call(functools.partial(attention_kernel, tick), out_shape=out_s...  7.99 us
    pallas_call x7, Pallas kernels, simple(): pl.pallas_call(kernel, out_shape=out_shape, in_specs=[SCALAR] * scalars +...  3.98 us
  transfers between devices with their start and end apart: 17, of which 14 were waited for; matrix products, arithmetic and copies ran while one was open for 0% of the time, Pallas kernels for 0%

profile of v6, /device:TPU:195, one launch (start us, length us, event | category | flops | bytes accessed | tf_op | source)
XLA Modules:
  0.0 123.0 jit_solution(1991586371690357889)
XLA Ops:
  0.6 2.5 %split_all.1 = (bf16[10,64,512]{2,1,0:T(8,128)(2,1)}, bf16[10,64,512]{2,1,0:T(8,128)(2,1)}) custom-call(s32[1]{0:T(128)} %bitcast.meta, bf16[1,2,64,512]{3,2,1,0:T(8,128)(2,1)} %refs_0_.1, bf16[1,2,64,512]{3,2,1,0:T(8,128)(2,1)} %refs_1_.1, bf16[1,2,64,2048]{3,2,1,0:T(8,128)(2,1)} %refs_2_.1, bf16[1,64,2048]{2,1,0:T(8,128)(2,1)} %refs_3_.1, ...), custom_call_target="tpu_custom_call" | custom-call | flops 2621444 | bytes 2621444 | tf_op jit(solution)/shard_map/split_all/pallas_call | solution.py:180
  3.2 2.6 %collective-permute-start = (bf16[10,64,512]{2,1,0:T(8,128)(2,1)}, bf16[10,64,512]{2,1,0:T(8,128)(2,1)S(1)}, u32[]{:S(2)}, u32[]{:S(2)}) collective-permute-start(bf16[10,64,512]{2,1,0:T(8,128)(2,1)} %get-tuple-element.34), channel_id=1, source_target_pairs={{0,8},{8,0},{16,24},{24,16},{32,40},{40,32},{48,56},{56,48},{64,72... | collective-permute-start | bytes 1966088 | tf_op jit(solution)/shard_map/ppermute | solution.py:29
  8.8 3.2 %collective-permute-start.3 = (bf16[2,128,512]{2,1,0:T(8,128)(2,1)S(1)}, bf16[2,128,512]{2,1,0:T(8,128)(2,1)S(1)}, u32[]{:S(2)}, u32[]{:S(2)}) collective-permute-start(bf16[2,128,512]{2,1,0:T(8,128)(2,1)S(1)} %pair_keys.1.p0.refs_0_.refs_1_), channel_id=1, source_target_pairs={{0,48},{8,56},{16,64},{24,72},{32,80},{40,88},{48,96},{56,104},{64... | collective-permute-start | bytes 786440 | tf_op jit(solution)/shard_map/ppermute | solution.py:29
  12.0 4.0 %collective-permute-start.2 = (bf16[2,128,512]{2,1,0:T(8,128)(2,1)S(1)}, bf16[2,128,512]{2,1,0:T(8,128)(2,1)S(1)}, u32[]{:S(2)}, u32[]{:S(2)}) collective-permute-start(bf16[2,128,512]{2,1,0:T(8,128)(2,1)S(1)} %pair_keys.1.p0.refs_0_.refs_1_), channel_id=1, source_target_pairs={{0,32},{8,40},{16,48},{24,56},{32,64},{40,72},{48,80},{56,88},{64,... | collective-permute-start | bytes 786440 | tf_op jit(solution)/shard_map/ppermute | solution.py:29
  16.0 3.4 %collective-permute-start.1 = (bf16[2,128,512]{2,1,0:T(8,128)(2,1)S(1)}, bf16[2,128,512]{2,1,0:T(8,128)(2,1)S(1)}, u32[]{:S(2)}, u32[]{:S(2)}) collective-permute-start(bf16[2,128,512]{2,1,0:T(8,128)(2,1)S(1)} %pair_keys.1.p0.refs_0_.refs_1_), channel_id=1, source_target_pairs={{0,16},{8,24},{16,32},{24,40},{32,48},{40,56},{48,64},{56,72},{64,... | collective-permute-start | bytes 786440 | tf_op jit(solution)/shard_map/ppermute | solution.py:29
  21.1 7.1 %collective-permute-done.1.p1.refs_1_.refs_2_ = bf16[2,128,512]{2,1,0:T(8,128)(2,1)S(1)} collective-permute-done((bf16[2,128,512]{2,1,0:T(8,128)(2,1)S(1)}, bf16[2,128,512]{2,1,0:T(8,128)(2,1)S(1)}, u32[]{:S(2)}, u32[]{:S(2)}) %collective-permute-start.1) | collective-permute-done | bytes 262176 | tf_op jit(solution)/shard_map/ppermute | solution.py:29
  28.3 3.2 %collective-permute-start.4 = (bf16[2,64,512]{2,1,0:T(8,128)(2,1)S(1)}, bf16[2,64,512]{2,1,0:T(8,128)(2,1)S(1)}, u32[]{:S(2)}, u32[]{:S(2)}) collective-permute-start(bf16[2,64,512]{2,1,0:T(8,128)(2,1)S(1)} %choose.1), channel_id=1, source_target_pairs={{0,64},{8,72},{16,80},{24,88},{32,96},{40,104},{48,112},{56,120},{... | collective-permute-start | bytes 393224 | tf_op jit(solution)/shard_map/ppermute | solution.py:29
  33.4 3.8 %collective-permute-start.7 = (bf16[2,64,512]{2,1,0:T(8,128)(2,1)S(1)}, bf16[2,64,512]{2,1,0:T(8,128)(2,1)S(1)}, u32[]{:S(2)}, u32[]{:S(2)}) collective-permute-start(bf16[2,64,512]{2,1,0:T(8,128)(2,1)S(1)} %broadcast_select_fusion.refs_4_.refs_5_), channel_id=1, source_target_pairs={{0,384},{8,392},{16,400},{24,408},{32,416},{40,424},{48,432},{56,4... | collective-permute-start | bytes 393224 | tf_op jit(solution)/shard_map/ppermute | solution.py:29
  37.3 2.5 %collective-permute-start.6 = (bf16[2,64,512]{2,1,0:T(8,128)(2,1)S(1)}, bf16[2,64,512]{2,1,0:T(8,128)(2,1)S(1)}, u32[]{:S(2)}, u32[]{:S(2)}) collective-permute-start(bf16[2,64,512]{2,1,0:T(8,128)(2,1)S(1)} %broadcast_select_fusion.refs_4_.refs_5_), channel_id=1, source_target_pairs={{0,256},{8,264},{16,272},{24,280},{32,288},{40,296},{48,304},{56,3... | collective-permute-start | bytes 393224 | tf_op jit(solution)/shard_map/ppermute | solution.py:29
  39.8 2.8 %collective-permute-start.5 = (bf16[2,64,512]{2,1,0:T(8,128)(2,1)S(1)}, bf16[2,64,512]{2,1,0:T(8,128)(2,1)S(1)}, u32[]{:S(2)}, u32[]{:S(2)}) collective-permute-start(bf16[2,64,512]{2,1,0:T(8,128)(2,1)S(1)} %broadcast_select_fusion.refs_4_.refs_5_), channel_id=1, source_target_pairs={{0,128},{8,136},{16,144},{24,152},{32,160},{40,168},{48,176},{56,1... | collective-permute-start | bytes 393224 | tf_op jit(solution)/shard_map/ppermute | solution.py:29
  42.7 3.1 %collective-permute-done.5.refs_5_.refs_6_ = bf16[2,64,512]{2,1,0:T(8,128)(2,1)S(1)} collective-permute-done((bf16[2,64,512]{2,1,0:T(8,128)(2,1)S(1)}, bf16[2,64,512]{2,1,0:T(8,128)(2,1)S(1)}, u32[]{:S(2)}, u32[]{:S(2)}) %collective-permute-start.5) | collective-permute-done | bytes 131104 | tf_op jit(solution)/shard_map/ppermute | solution.py:29
  45.9 4.0 %attention.2 = (bf16[2,64,1024]{2,1,0:T(8,128)(2,1)S(1)}, bf16[64,1024]{1,0:T(8,128)(2,1)S(1)}, bf16[128,512]{1,0:T(8,128)(2,1)S(1)}, bf16[128,512]{1,0:T(8,128)...) custom-call(s32[6]{0:T(128)S(1)} %pad_add_fusion.meta, ...), custom_call_target="tpu_custom_call" | custom-call | flops 1006632960 | bytes 4194304 | tf_op jit(solution)/shard_map/attention/pallas_call | solution.py:159
  49.8 1.9 %collective-permute-start.8 = (bf16[2,64,1024]{2,1,0:T(8,128)(2,1)S(1)}, bf16[2,64,1024]{2,1,0:T(8,128)(2,1)S(1)}, u32[]{:S(2)}, u32[]{:S(2)}) collective-permute-start(bf16[2,64,1024]{2,1,0:T(8,128)(2,1)S(1)} %get-tuple-element.36.mine0), channel_id=1, source_target_pairs={{1,0},{2,1},{3,2},{4,3},{5,4},{6,5},{7,6},{9,8},{10,9},{11,10},{12... | collective-permute-start | bytes 786440 | tf_op jit(solution)/shard_map/ppermute | solution.py:29
  51.7 7.0 %collective-permute-done.8.refs_0_ = bf16[2,64,1024]{2,1,0:T(8,128)(2,1)S(1)} collective-permute-done((bf16[2,64,1024]{2,1,0:T(8,128)(2,1)S(1)}, bf16[2,64,1024]{2,1,0:T(8,128)(2,1)S(1)}, u32[]{:S(2)}, u32[]{:S(2)}) %collective-permute-start.8) | collective-permute-done | bytes 262176 | tf_op jit(solution)/shard_map/ppermute | solution.py:29
  58.8 4.0 %attention.3 = (bf16[2,64,1024]{2,1,0:T(8,128)(2,1)S(1)}, bf16[2,64,1024]{2,1,0:T(8,128)(2,1)S(1)}, bf16[2,128,512]{2,1,0:T(8,128)(2,1)S(1)}, bf16[2,128,512]{2,...) custom-call(s32[6]{0:T(128)S(1)} %pad_add_fusion.meta, ...), custom_call_target="tpu_custom_call" | custom-call | flops 1006632960 | bytes 4194304 | tf_op jit(solution)/shard_map/attention/pallas_call | solution.py:159
  66.7 3.9 %collective-permute-done.9.x1 = bf16[2,64,512]{2,1,0:T(8,128)(2,1)S(1)} collective-permute-done((bf16[2,64,512]{2,1,0:T(8,128)(2,1)S(1)}, bf16[2,64,512]{2,1,0:T(8,128)(2,1)S(1)}, u32[]{:S(2)}, u32[]{:S(2)}) %collective-permute-start.9) | collective-permute-done | bytes 131104 | tf_op jit(solution)/shard_map/ppermute | solution.py:29
  70.6 4.7 %collective-permute-done.10.x2 = bf16[2,64,512]{2,1,0:T(8,128)(2,1)S(1)} collective-permute-done((bf16[2,64,512]{2,1,0:T(8,128)(2,1)S(1)}, bf16[2,64,512]{2,1,0:T(8,128)(2,1)S(1)}, u32[]{:S(2)}, u32[]{:S(2)}) %collective-permute-start.10) | collective-permute-done | bytes 131104 | tf_op jit(solution)/shard_map/ppermute | solution.py:29
  75.3 2.7 %collective-permute-done.11.x3 = bf16[2,64,512]{2,1,0:T(8,128)(2,1)S(1)} collective-permute-done((bf16[2,64,512]{2,1,0:T(8,128)(2,1)S(1)}, bf16[2,64,512]{2,1,0:T(8,128)(2,1)S(1)}, u32[]{:S(2)}, u32[]{:S(2)}) %collective-permute-start.11) | collective-permute-done | bytes 131104 | tf_op jit(solution)/shard_map/ppermute | solution.py:29
  79.4 13.9 %collective-permute-done.12.below = bf16[2,64,512]{2,1,0:T(8,128)(2,1)S(1)} collective-permute-done((bf16[2,64,512]{2,1,0:T(8,128)(2,1)S(1)}, bf16[2,64,512]{2,1,0:T(8,128)(2,1)S(1)}, u32[]{:S(2)}, u32[]{:S(2)}) %collective-permute-start.12) | collective-permute-done | bytes 131104 | tf_op jit(solution)/shard_map/ppermute | solution.py:29
  93.6 5.4 %collective-permute-start.13 = (bf16[2,128,512]{2,1,0:T(8,128)(2,1)S(1)}, bf16[2,128,512]{2,1,0:T(8,128)(2,1)S(1)}, u32[]{:S(2)}, u32[]{:S(2)}) collective-permute-start(bf16[2,128,512]{2,1,0:T(8,128)(2,1)S(1)} %get-tuple-element.56), channel_id=1, source_target_pairs={{16,0},{24,8},{32,16},{40,24},{48,32},{56,40},{64,48},{72,56},{80,... | collective-permute-start | bytes 786440 | tf_op jit(solution)/shard_map/ppermute | solution.py:29
  101.6 3.4 %collective-permute-done.13.back1 = bf16[2,128,512]{2,1,0:T(8,128)(2,1)S(1)} collective-permute-done((bf16[2,128,512]{2,1,0:T(8,128)(2,1)S(1)}, bf16[2,128,512]{2,1,0:T(8,128)(2,1)S(1)}, u32[]{:S(2)}, u32[]{:S(2)}) %collective-permute-start.13) | collective-permute-done | bytes 262176 | tf_op jit(solution)/shard_map/ppermute | solution.py:29
  105.0 2.6 %collective-permute-done.14.back2 = bf16[2,128,512]{2,1,0:T(8,128)(2,1)S(1)} collective-permute-done((bf16[2,128,512]{2,1,0:T(8,128)(2,1)S(1)}, bf16[2,128,512]{2,1,0:T(8,128)(2,1)S(1)}, u32[]{:S(2)}, u32[]{:S(2)}) %collective-permute-start.14) | collective-permute-done | bytes 262176 | tf_op jit(solution)/shard_map/ppermute | solution.py:29
  107.6 7.5 %collective-permute-done.15.back3 = bf16[2,128,512]{2,1,0:T(8,128)(2,1)S(1)} collective-permute-done((bf16[2,128,512]{2,1,0:T(8,128)(2,1)S(1)}, bf16[2,128,512]{2,1,0:T(8,128)(2,1)S(1)}, u32[]{:S(2)}, u32[]{:S(2)}) %collective-permute-start.15) | collective-permute-done | bytes 262176 | tf_op jit(solution)/shard_map/ppermute | solution.py:29
  115.3 5.5 %collective-permute-start.16 = (bf16[2,64,1536]{2,1,0:T(8,128)(2,1)S(1)}, bf16[2,64,1536]{2,1,0:T(8,128)(2,1)S(1)}, u32[]{:S(2)}, u32[]{:S(2)}) collective-permute-start(bf16[2,64,1536]{2,1,0:T(8,128)(2,1)S(1)} %get-tuple-element.61), channel_id=1, source_target_pairs={{0,8},{8,0},{16,24},{24,16},{32,40},{40,32},{48,56},{56,48},{64,72... | collective-permute-start | bytes 1179656 | tf_op jit(solution)/shard_map/ppermute | solution.py:29
  (33 shorter events, 17.2 us)
Async XLA Ops:
  3.2 4.5 %collective-permute-start = (bf16[10,64,512]{2,1,0:T(8,128)(2,1)}, bf16[10,64,512]{2,1,0:T(8,128)(2,1)S(1)}, u32[]{:S(2)}, u32[]{:S(2)}) collective-permute-start(bf16[10,64,512]{2,1,0:T(8,128)(2,1)} %get-tuple-element.34), channel_id=1, source_target_pairs={{0,8},{8,0},{16,24},{24,16},{32,40},{40,32},{48,56},{56,48},{64,72... | collective-permute-start | bytes 1966088 | tf_op jit(solution)/shard_map/ppermute | solution.py:29
  7.7 1.1 copy-start
  8.8 10.7 %collective-permute-start.3 = (bf16[2,128,512]{2,1,0:T(8,128)(2,1)S(1)}, bf16[2,128,512]{2,1,0:T(8,128)(2,1)S(1)}, u32[]{:S(2)}, u32[]{:S(2)}) collective-permute-start(bf16[2,128,512]{2,1,0:T(8,128)(2,1)S(1)} %pair_keys.1.p0.refs_0_.refs_1_), channel_id=1, source_target_pairs={{0,48},{8,56},{16,64},{24,72},{32,80},{40,88},{48,96},{56,104},{64... | collective-permute-start | bytes 786440 | tf_op jit(solution)/shard_map/ppermute | solution.py:29
  12.0 9.1 %collective-permute-start.2 = (bf16[2,128,512]{2,1,0:T(8,128)(2,1)S(1)}, bf16[2,128,512]{2,1,0:T(8,128)(2,1)S(1)}, u32[]{:S(2)}, u32[]{:S(2)}) collective-permute-start(bf16[2,128,512]{2,1,0:T(8,128)(2,1)S(1)} %pair_keys.1.p0.refs_0_.refs_1_), channel_id=1, source_target_pairs={{0,32},{8,40},{16,48},{24,56},{32,64},{40,72},{48,80},{56,88},{64,... | collective-permute-start | bytes 786440 | tf_op jit(solution)/shard_map/ppermute | solution.py:29
  16.0 12.2 %collective-permute-start.1 = (bf16[2,128,512]{2,1,0:T(8,128)(2,1)S(1)}, bf16[2,128,512]{2,1,0:T(8,128)(2,1)S(1)}, u32[]{:S(2)}, u32[]{:S(2)}) collective-permute-start(bf16[2,128,512]{2,1,0:T(8,128)(2,1)S(1)} %pair_keys.1.p0.refs_0_.refs_1_), channel_id=1, source_target_pairs={{0,16},{8,24},{16,32},{24,40},{32,48},{40,56},{48,64},{56,72},{64,... | collective-permute-start | bytes 786440 | tf_op jit(solution)/shard_map/ppermute | solution.py:29
  19.5 12.0 %copy-start.2 = (f32[1,2048]{1,0:T(1,128)S(1)}, f32[1,2048]{1,0:T(1,128)}, u32[]{:S(2)}) copy-start(f32[1,2048]{1,0:T(1,128)} %param.11) | copy-start | bytes 24580
  19.5 26.3 %copy-start.1 = (bf16[10,64,512]{2,1,0:T(8,128)(2,1)S(1)}, bf16[10,64,512]{2,1,0:T(8,128)(2,1)}, u32[]{:S(2)}) copy-start(bf16[10,64,512]{2,1,0:T(8,128)(2,1)} %get-tuple-element.33.keep) | copy-start | bytes 1966084
  28.3 5.1 %collective-permute-start.4 = (bf16[2,64,512]{2,1,0:T(8,128)(2,1)S(1)}, bf16[2,64,512]{2,1,0:T(8,128)(2,1)S(1)}, u32[]{:S(2)}, u32[]{:S(2)}) collective-permute-start(bf16[2,64,512]{2,1,0:T(8,128)(2,1)S(1)} %choose.1), channel_id=1, source_target_pairs={{0,64},{8,72},{16,80},{24,88},{32,96},{40,104},{48,112},{56,120},{... | collective-permute-start | bytes 393224 | tf_op jit(solution)/shard_map/ppermute | solution.py:29
  33.4 9.2 %copy-start.3 = (s32[1,4]{1,0:T(1,128)S(1)}, s32[1,4]{1,0:T(1,128)}, u32[]{:S(2)}) copy-start(s32[1,4]{1,0:T(1,128)} %param.14) | copy-start | bytes 52
  33.4 9.2 %copy-start.4 = (s32[1,4]{1,0:T(1,128)S(1)}, s32[1,4]{1,0:T(1,128)}, u32[]{:S(2)}) copy-start(s32[1,4]{1,0:T(1,128)} %param.15) | copy-start | bytes 52
  33.4 9.3 %collective-permute-start.7 = (bf16[2,64,512]{2,1,0:T(8,128)(2,1)S(1)}, bf16[2,64,512]{2,1,0:T(8,128)(2,1)S(1)}, u32[]{:S(2)}, u32[]{:S(2)}) collective-permute-start(bf16[2,64,512]{2,1,0:T(8,128)(2,1)S(1)} %broadcast_select_fusion.refs_4_.refs_5_), channel_id=1, source_target_pairs={{0,384},{8,392},{16,400},{24,408},{32,416},{40,424},{48,432},{56,4... | collective-permute-start | bytes 393224 | tf_op jit(solution)/shard_map/ppermute | solution.py:29
  37.3 5.5 %collective-permute-start.6 = (bf16[2,64,512]{2,1,0:T(8,128)(2,1)S(1)}, bf16[2,64,512]{2,1,0:T(8,128)(2,1)S(1)}, u32[]{:S(2)}, u32[]{:S(2)}) collective-permute-start(bf16[2,64,512]{2,1,0:T(8,128)(2,1)S(1)} %broadcast_select_fusion.refs_4_.refs_5_), channel_id=1, source_target_pairs={{0,256},{8,264},{16,272},{24,280},{32,288},{40,296},{48,304},{56,3... | collective-permute-start | bytes 393224 | tf_op jit(solution)/shard_map/ppermute | solution.py:29
  39.8 6.1 %collective-permute-start.5 = (bf16[2,64,512]{2,1,0:T(8,128)(2,1)S(1)}, bf16[2,64,512]{2,1,0:T(8,128)(2,1)S(1)}, u32[]{:S(2)}, u32[]{:S(2)}) collective-permute-start(bf16[2,64,512]{2,1,0:T(8,128)(2,1)S(1)} %broadcast_select_fusion.refs_4_.refs_5_), channel_id=1, source_target_pairs={{0,128},{8,136},{16,144},{24,152},{32,160},{40,168},{48,176},{56,1... | collective-permute-start | bytes 393224 | tf_op jit(solution)/shard_map/ppermute | solution.py:29
  49.8 9.0 %collective-permute-start.8 = (bf16[2,64,1024]{2,1,0:T(8,128)(2,1)S(1)}, bf16[2,64,1024]{2,1,0:T(8,128)(2,1)S(1)}, u32[]{:S(2)}, u32[]{:S(2)}) collective-permute-start(bf16[2,64,1024]{2,1,0:T(8,128)(2,1)S(1)} %get-tuple-element.36.mine0), channel_id=1, source_target_pairs={{1,0},{2,1},{3,2},{4,3},{5,4},{6,5},{7,6},{9,8},{10,9},{11,10},{12... | collective-permute-start | bytes 786440 | tf_op jit(solution)/shard_map/ppermute | solution.py:29
  62.8 7.8 %collective-permute-start.9 = (bf16[2,64,512]{2,1,0:T(8,128)(2,1)S(1)}, bf16[2,64,512]{2,1,0:T(8,128)(2,1)S(1)}, u32[]{:S(2)}, u32[]{:S(2)}) collective-permute-start(bf16[2,64,512]{2,1,0:T(8,128)(2,1)S(1)} %get-tuple-element.45), channel_id=1, source_target_pairs={{128,0},{136,8},{144,16},{152,24},{160,32},{168,40},{176,48},{184,... | collective-permute-start | bytes 393224 | tf_op jit(solution)/shard_map/ppermute | solution.py:29
  64.1 11.2 %collective-permute-start.10 = (bf16[2,64,512]{2,1,0:T(8,128)(2,1)S(1)}, bf16[2,64,512]{2,1,0:T(8,128)(2,1)S(1)}, u32[]{:S(2)}, u32[]{:S(2)}) collective-permute-start(bf16[2,64,512]{2,1,0:T(8,128)(2,1)S(1)} %get-tuple-element.46), channel_id=1, source_target_pairs={{256,0},{264,8},{272,16},{280,24},{288,32},{296,40},{304,48},{312,... | collective-permute-start | bytes 393224 | tf_op jit(solution)/shard_map/ppermute | solution.py:29
  65.4 12.6 %collective-permute-start.11 = (bf16[2,64,512]{2,1,0:T(8,128)(2,1)S(1)}, bf16[2,64,512]{2,1,0:T(8,128)(2,1)S(1)}, u32[]{:S(2)}, u32[]{:S(2)}) collective-permute-start(bf16[2,64,512]{2,1,0:T(8,128)(2,1)S(1)} %get-tuple-element.47), channel_id=1, source_target_pairs={{384,0},{392,8},{400,16},{408,24},{416,32},{424,40},{432,48},{440,... | collective-permute-start | bytes 393224 | tf_op jit(solution)/shard_map/ppermute | solution.py:29
  78.1 15.2 %collective-permute-start.12 = (bf16[2,64,512]{2,1,0:T(8,128)(2,1)S(1)}, bf16[2,64,512]{2,1,0:T(8,128)(2,1)S(1)}, u32[]{:S(2)}, u32[]{:S(2)}) collective-permute-start(bf16[2,64,512]{2,1,0:T(8,128)(2,1)S(1)} %get-tuple-element.49), channel_id=1, source_target_pairs={{64,0},{72,8},{80,16},{88,24},{96,32},{104,40},{112,48},{120,56},{... | collective-permute-start | bytes 393224 | tf_op jit(solution)/shard_map/ppermute | solution.py:29
  93.6 11.4 %collective-permute-start.13 = (bf16[2,128,512]{2,1,0:T(8,128)(2,1)S(1)}, bf16[2,128,512]{2,1,0:T(8,128)(2,1)S(1)}, u32[]{:S(2)}, u32[]{:S(2)}) collective-permute-start(bf16[2,128,512]{2,1,0:T(8,128)(2,1)S(1)} %get-tuple-element.56), channel_id=1, source_target_pairs={{16,0},{24,8},{32,16},{40,24},{48,32},{56,40},{64,48},{72,56},{80,... | collective-permute-start | bytes 786440 | tf_op jit(solution)/shard_map/ppermute | solution.py:29
  99.0 8.6 %collective-permute-start.14 = (bf16[2,128,512]{2,1,0:T(8,128)(2,1)S(1)}, bf16[2,128,512]{2,1,0:T(8,128)(2,1)S(1)}, u32[]{:S(2)}, u32[]{:S(2)}) collective-permute-start(bf16[2,128,512]{2,1,0:T(8,128)(2,1)S(1)} %get-tuple-element.57), channel_id=1, source_target_pairs={{32,0},{40,8},{48,16},{56,24},{64,32},{72,40},{80,48},{88,56},{96,... | collective-permute-start | bytes 786440 | tf_op jit(solution)/shard_map/ppermute | solution.py:29
  100.3 14.9 %collective-permute-start.15 = (bf16[2,128,512]{2,1,0:T(8,128)(2,1)S(1)}, bf16[2,128,512]{2,1,0:T(8,128)(2,1)S(1)}, u32[]{:S(2)}, u32[]{:S(2)}) collective-permute-start(bf16[2,128,512]{2,1,0:T(8,128)(2,1)S(1)} %get-tuple-element.58), channel_id=1, source_target_pairs={{48,0},{56,8},{64,16},{72,24},{80,32},{88,40},{96,48},{104,56},{11... | collective-permute-start | bytes 786440 | tf_op jit(solution)/shard_map/ppermute | solution.py:29
  115.3 6.8 %collective-permute-start.16 = (bf16[2,64,1536]{2,1,0:T(8,128)(2,1)S(1)}, bf16[2,64,1536]{2,1,0:T(8,128)(2,1)S(1)}, u32[]{:S(2)}, u32[]{:S(2)}) collective-permute-start(bf16[2,64,1536]{2,1,0:T(8,128)(2,1)S(1)} %get-tuple-element.61), channel_id=1, source_target_pairs={{0,8},{8,0},{16,24},{24,16},{32,40},{40,32},{48,56},{56,48},{64,72... | collective-permute-start | bytes 1179656 | tf_op jit(solution)/shard_map/ppermute | solution.py:29

commit v7 on v6

--- a/solution.py
+++ b/solution.py
@@ -36,19 +36,21 @@
 def attention_kernel(tick, meta, gain, keep, recv, *refs):
     if tick:
         grads, refs = refs[0], refs[1:]
-    pairs, strided = refs[:4], refs[4:8]
-    refs = refs[8:]
+    pairs, shifts = refs[:4], refs[4:12]
+    refs = refs[12:]
     if tick:
-        for old, new in zip(refs[:7], refs[8:15]):
+        for old, new in zip(refs[:8], refs[9:17]):
             new[0] = old[...]
-        refs = refs[7:]
-        refs = refs[:1] + tuple(r.at[1] for r in refs[1:8]) + refs[8:]
-    both, other, back1, back2, back3, part1, part2, part3, own, part0 = refs
+        refs = refs[8:]
+        refs = refs[:1] + tuple(r.at[1] for r in refs[1:9]) + refs[9:]
+    both, other, back1, back2, back3, part0, part1, part2, part3, own = refs
     backs = (own, back1, back2, back3)
     parts = (part0, part1, part2, part3)
     index = meta[0]
     blocks = (index, jnp.bitwise_xor(index, 1))
     group = index // STRIDE
+    even = (index // 8) % 2 == 0
+    strided = [jnp.where(even, shifts[2 * n][...], shifts[2 * n + 1][...]) for n in range(4)]
     for h in range(HALF_HEADS):
         window = meta[2 + h]
         stride = meta[4 + h]
@@ -68,8 +70,8 @@
         g = jnp.concatenate(g_rows, axis=0)
         k_at = slice(h * HEAD_DIM, (h + 1) * HEAD_DIM)
         v_at = slice(HALF_KV + h * HEAD_DIM, HALF_KV + (h + 1) * HEAD_DIM)
-        k = jnp.concatenate([r[:, k_at] for r in pairs + strided], axis=0)
-        v = jnp.concatenate([r[:, v_at] for r in pairs + strided], axis=0)
+        k = jnp.concatenate([r[:, k_at] for r in list(pairs) + strided], axis=0)
+        v = jnp.concatenate([r[:, v_at] for r in list(pairs) + strided], axis=0)
         scores = lax.dot_general(k, q, NT, preferred_element_type=jnp.float32)
         wide = GROUP * BLK
         key_row = lax.broadcasted_iota(jnp.int32, (BLK, wide), 0)
@@ -145,17 +147,17 @@
         args.append(grads)
         specs.append(WHOLE)
     args += list(pairs) + list(strided)
-    specs += [at(tick, 2 * BLK, WIDE)] * 4 + [at(tick, BLK, WIDE)] * 4
+    specs += [at(tick, 2 * BLK, WIDE)] * 4 + [at(tick, BLK, WIDE)] * 8
     bf16, f32 = jnp.bfloat16, jnp.float32
     out_shape = [shape((2, BLK, HALF_FEAT), bf16)]
     lead = (2,) if tick else ()
     if tick:
         args += earlier
-        specs += [WHOLE] * 7
+        specs += [WHOLE] * 8
     out_shape.append(shape(lead + (BLK, HALF_FEAT), bf16))
     out_shape += [shape(lead + (2 * BLK, WIDE), bf16)] * 3
-    out_shape += [shape(lead + (BLK, WIDE), bf16)] * 3
-    out_shape += [shape((2 * BLK, WIDE), f32), shape((BLK, WIDE), f32)]
+    out_shape += [shape(lead + (BLK, WIDE), bf16)] * 4
+    out_shape.append(shape((2 * BLK, WIDE), f32))
     return pl.pallas_call(
         functools.partial(attention_kernel, tick),
         out_shape=out_shape,
@@ -187,15 +189,6 @@
         cost_estimate=pl.CostEstimate(flops=size, bytes_accessed=size, transcendentals=0),
         name=kernel.__name__,
     )(*args)
-
-
-def column_sum(own0, own1, x1, x2, x3, wide_out, send_out):
-    for t, own in enumerate((own0, own1)):
-        total = own[...]
-        for x in (x1, x2, x3):
-            total = total + x[t].astype(jnp.float32)
-        wide_out[t] = total
-        send_out[t] = total.astype(jnp.bfloat16)
 
 
 def split_all(meta, *refs):
@@ -237,12 +230,15 @@
             out[...] = jnp.where(core == 0, pair[:, :BLK], pair[:, BLK:])
 
 
-def add_strided(meta, total, below, back1, back2, back3, own0, own1, out1, out2, out3, near):
+def add_strided(meta, *refs):
+    parts, (back1, back2, back3, own0, own1), (out1, out2, out3, near) = refs[:8], refs[8:13], refs[13:]
     core = meta[0] % 2
     place = (meta[0] // 2) % 4
     even = (meta[0] // 8) % 2 == 0
     for t, own in enumerate((own0, own1)):
-        strided = total[t] + below[t].astype(jnp.float32)
+        strided = parts[0][t].astype(jnp.float32)
+        for part in parts[1:]:
+            strided = strided + part[t].astype(jnp.float32)
         halves = [jnp.where(even & (core == k), strided, 0.0) for k in range(2)]
         spread = jnp.concatenate(halves, axis=0)
         near[t] = own[...] + jnp.where(place == 0, spread, 0.0)
@@ -299,9 +295,10 @@
     (pair,) = simple(pair_keys, [shape((2, 2 * BLK, WIDE), bf16)], [spot, keep, recv])
     pairs = [pair] + [ctx(pair, lambda i: i + 2 * d) for d in range(1, 4)]
     (chosen,) = simple(choose, [half], [spot] + pairs)
-    above = ctx(chosen, lambda i: i + 8, lambda i: (i // 8) % 2 == 0)
-    chosen = jnp.where((index // 8) % 2 == 0, chosen, above)
-    strided = [chosen] + [ctx(chosen, lambda i: i + STRIDE * s) for s in range(1, 4)]
+    def on_even(i):
+        return (i // 8) % 2 == 0
+
+    strided = [chosen] + [ctx(chosen, lambda i: i + 8 * s, on_even) for s in range(1, 8)]
     gain = jnp.where(core == 0, query_gain[:, :HALF_FEAT], query_gain[:, HALF_FEAT:])
     heads = jnp.where(core == 0, window[0, :2], window[0, 2:])
     steps = jnp.where(core == 0, stride[0, :2], stride[0, 2:])
@@ -310,17 +307,16 @@
 
     first = attention(0, meta, gain, keep, recv, None, pairs, strided, None)
     grads = route(first[0], "pp", lambda i: i - 1)
-    second = attention(1, meta, gain, keep, recv, grads, pairs, strided, first[1:8])
-    columns = [first[9], second[9]]
-    columns += [ctx(second[4 + s], lambda i: i - STRIDE * s) for s in range(1, 4)]
+    second = attention(1, meta, gain, keep, recv, grads, pairs, strided, first[1:9])
+    parts = [second[5]]
+    for s in range(1, 8):
+        parts.append(ctx(second[5 + s // 2], lambda i: i - 8 * s, lambda i: on_even(i - 8 * s)))
     wide = shape((2, BLK, WIDE), f32)
-    total, send = simple(column_sum, [wide, half], columns, 0)
-    below = ctx(send, lambda i: i - 8, lambda i: (i // 8) % 2 == 1)
     full = shape((2, 2 * BLK, WIDE), bf16)
     *backs, near = simple(
         add_strided,
         [full, full, full, shape((2, 2 * BLK, WIDE), f32)],
-        [spot, total, below] + list(second[2:5]) + [first[8], second[8]],
+        [spot] + parts + list(second[2:5]) + [first[9], second[9]],
     )
     backs = [ctx(backs[d - 1], lambda i: i - 2 * d) for d in range(1, 4)]
     mine, swap = simple(

time: 124 us -> 134 us (1.081)
  waiting for transfers between devices: 62.8 us -> 69.4 us
  starting transfers between devices: 46.1 us -> 49.8 us
    ppermute x17 -> x23, waiting for transfers between devices: 62.8 us -> 69.4 us  [route(): lax.ppermute(array, axis, [(a, b) for a, b in pairs if b is not None and...]
    ppermute x17 -> x23, starting transfers between devices: 46.1 us -> 49.8 us  [route(): lax.ppermute(array, axis, [(a, b) for a, b in pairs if b is not None and...]
    pallas_call x7 -> x6, Pallas kernels: 3.98 us -> 4.02 us  [simple(): pl.pallas_call(kernel, out_shape=out_shape, in_specs=[SCALAR] * scalars +...]
  transfers between devices with their start and end apart: 17 -> 23, of which waited for: 14 -> 15; matrix products, arithmetic and copies ran while one was open for 0% -> 0% of each run, Pallas kernels for 0% -> 0%
where the time goes in v7:
time: 134 us; the launch traced here: 133 us
  waiting for transfers between devices  69.4 us (52%)
  starting transfers between devices  49.8 us (37%)
  Pallas kernels  12 us (9%)
    ppermute x23, waiting for transfers between devices, route(): lax.ppermute(array, axis, [(a, b) for a, b in pairs if b is not None and...  69.4 us
    ppermute x23, starting transfers between devices, route(): lax.ppermute(array, axis, [(a, b) for a, b in pairs if b is not None and...  49.8 us
    pallas_call x2, Pallas kernels, attention(): pl.pallas_call(functools.partial(attention_kernel, tick), out_shape=out_s...  8 us
    pallas_call x6, Pallas kernels, simple(): pl.pallas_call(kernel, out_shape=out_shape, in_specs=[SCALAR] * scalars +...  4.02 us
  transfers between devices with their start and end apart: 23, of which 15 were waited for; matrix products, arithmetic and copies ran while one was open for 0% of the time, Pallas kernels for 0%

profile of v7, /device:TPU:195, one launch (start us, length us, event | category | flops | bytes accessed | tf_op | source)
XLA Modules:
  0.0 133.4 jit_solution(12960267193829242384)
XLA Ops:
  0.6 2.5 %split_all.1 = (bf16[10,64,512]{2,1,0:T(8,128)(2,1)}, bf16[10,64,512]{2,1,0:T(8,128)(2,1)}) custom-call(s32[1]{0:T(128)} %bitcast.meta, bf16[1,2,64,512]{3,2,1,0:T(8,128)(2,1)} %refs_0_.1, bf16[1,2,64,512]{3,2,1,0:T(8,128)(2,1)} %refs_1_.1, bf16[1,2,64,2048]{3,2,1,0:T(8,128)(2,1)} %refs_2_.1, bf16[1,64,2048]{2,1,0:T(8,128)(2,1)} %refs_3_.1, ...), custom_call_target="tpu_custom_call" | custom-call | flops 2621444 | bytes 2621444 | tf_op jit(solution)/shard_map/split_all/pallas_call | solution.py:182
  3.2 2.6 %collective-permute-start = (bf16[10,64,512]{2,1,0:T(8,128)(2,1)}, bf16[10,64,512]{2,1,0:T(8,128)(2,1)S(1)}, u32[]{:S(2)}, u32[]{:S(2)}) collective-permute-start(bf16[10,64,512]{2,1,0:T(8,128)(2,1)} %get-tuple-element.32), channel_id=1, source_target_pairs={{0,8},{8,0},{16,24},{24,16},{32,40},{40,32},{48,56},{56,48},{64,72... | collective-permute-start | bytes 1966088 | tf_op jit(solution)/shard_map/ppermute | solution.py:29
  5.8 1.9 %collective-permute-done.recv = bf16[10,64,512]{2,1,0:T(8,128)(2,1)S(1)} collective-permute-done((bf16[10,64,512]{2,1,0:T(8,128)(2,1)}, bf16[10,64,512]{2,1,0:T(8,128)(2,1)S(1)}, u32[]{:S(2)}, u32[]{:S(2)}) %collective-permute-start) | collective-permute-done | bytes 655392 | tf_op jit(solution)/shard_map/ppermute | solution.py:29
  8.8 3.3 %collective-permute-start.3 = (bf16[2,128,512]{2,1,0:T(8,128)(2,1)S(1)}, bf16[2,128,512]{2,1,0:T(8,128)(2,1)S(1)}, u32[]{:S(2)}, u32[]{:S(2)}) collective-permute-start(bf16[2,128,512]{2,1,0:T(8,128)(2,1)S(1)} %pair_keys.1.p0.refs_0_.refs_1_), channel_id=1, source_target_pairs={{0,48},{8,56},{16,64},{24,72},{32,80},{40,88},{48,96},{56,104},{64... | collective-permute-start | bytes 786440 | tf_op jit(solution)/shard_map/ppermute | solution.py:29
  12.1 4.0 %collective-permute-start.2 = (bf16[2,128,512]{2,1,0:T(8,128)(2,1)S(1)}, bf16[2,128,512]{2,1,0:T(8,128)(2,1)S(1)}, u32[]{:S(2)}, u32[]{:S(2)}) collective-permute-start(bf16[2,128,512]{2,1,0:T(8,128)(2,1)S(1)} %pair_keys.1.p0.refs_0_.refs_1_), channel_id=1, source_target_pairs={{0,32},{8,40},{16,48},{24,56},{32,64},{40,72},{48,80},{56,88},{64,... | collective-permute-start | bytes 786440 | tf_op jit(solution)/shard_map/ppermute | solution.py:29
  16.2 3.4 %collective-permute-start.1 = (bf16[2,128,512]{2,1,0:T(8,128)(2,1)S(1)}, bf16[2,128,512]{2,1,0:T(8,128)(2,1)S(1)}, u32[]{:S(2)}, u32[]{:S(2)}) collective-permute-start(bf16[2,128,512]{2,1,0:T(8,128)(2,1)S(1)} %pair_keys.1.p0.refs_0_.refs_1_), channel_id=1, source_target_pairs={{0,16},{8,24},{16,32},{24,40},{32,48},{40,56},{48,64},{56,72},{64,... | collective-permute-start | bytes 786440 | tf_op jit(solution)/shard_map/ppermute | solution.py:29
  21.2 7.1 %collective-permute-done.1.p1.refs_1_.refs_2_ = bf16[2,128,512]{2,1,0:T(8,128)(2,1)S(1)} collective-permute-done((bf16[2,128,512]{2,1,0:T(8,128)(2,1)S(1)}, bf16[2,128,512]{2,1,0:T(8,128)(2,1)S(1)}, u32[]{:S(2)}, u32[]{:S(2)}) %collective-permute-start.1) | collective-permute-done | bytes 262176 | tf_op jit(solution)/shard_map/ppermute | solution.py:29
  28.4 3.9 %collective-permute-start.10 = (bf16[2,64,512]{2,1,0:T(8,128)(2,1)S(1)}, bf16[2,64,512]{2,1,0:T(8,128)(2,1)S(1)}, u32[]{:S(2)}, u32[]{:S(2)}) collective-permute-start(bf16[2,64,512]{2,1,0:T(8,128)(2,1)S(1)} %choose.1.refs_4_.refs_5_), channel_id=1, source_target_pairs={{0,448},{8,456},{16,464},{24,472},{32,480},{40,488},{48,496},{56,5... | collective-permute-start | bytes 393224 | tf_op jit(solution)/shard_map/ppermute | solution.py:29
  32.3 1.7 %collective-permute-start.9 = (bf16[2,64,512]{2,1,0:T(8,128)(2,1)S(1)}, bf16[2,64,512]{2,1,0:T(8,128)(2,1)S(1)}, u32[]{:S(2)}, u32[]{:S(2)}) collective-permute-start(bf16[2,64,512]{2,1,0:T(8,128)(2,1)S(1)} %choose.1.refs_4_.refs_5_), channel_id=1, source_target_pairs={{0,384},{8,392},{16,400},{24,408},{32,416},{40,424},{48,432},{56,4... | collective-permute-start | bytes 393224 | tf_op jit(solution)/shard_map/ppermute | solution.py:29
  38.4 3.0 %collective-permute-start.5 = (bf16[2,64,512]{2,1,0:T(8,128)(2,1)S(1)}, bf16[2,64,512]{2,1,0:T(8,128)(2,1)S(1)}, u32[]{:S(2)}, u32[]{:S(2)}) collective-permute-start(bf16[2,64,512]{2,1,0:T(8,128)(2,1)S(1)} %choose.1.refs_4_.refs_5_), channel_id=1, source_target_pairs={{0,128},{8,136},{16,144},{24,152},{32,160},{40,168},{48,176},{56,1... | collective-permute-start | bytes 393224 | tf_op jit(solution)/shard_map/ppermute | solution.py:29
  43.0 1.8 %collective-permute-done.5.refs_6_.refs_7_ = bf16[2,64,512]{2,1,0:T(8,128)(2,1)S(1)} collective-permute-done((bf16[2,64,512]{2,1,0:T(8,128)(2,1)S(1)}, bf16[2,64,512]{2,1,0:T(8,128)(2,1)S(1)}, u32[]{:S(2)}, u32[]{:S(2)}) %collective-permute-start.5) | collective-permute-done | bytes 131104 | tf_op jit(solution)/shard_map/ppermute | solution.py:29
  44.8 2.8 %collective-permute-done.4.refs_5_.refs_6_ = bf16[2,64,512]{2,1,0:T(8,128)(2,1)S(1)} collective-permute-done((bf16[2,64,512]{2,1,0:T(8,128)(2,1)S(1)}, bf16[2,64,512]{2,1,0:T(8,128)(2,1)S(1)}, u32[]{:S(2)}, u32[]{:S(2)}) %collective-permute-start.4) | collective-permute-done | bytes 131104 | tf_op jit(solution)/shard_map/ppermute | solution.py:29
  47.6 4.0 %attention.2 = (bf16[2,64,1024]{2,1,0:T(8,128)(2,1)S(1)}, bf16[64,1024]{1,0:T(8,128)(2,1)S(1)}, bf16[128,512]{1,0:T(8,128)(2,1)S(1)}, bf16[128,512]{1,0:T(8,128)...) custom-call(s32[6]{0:T(128)S(1)} %pad_add_fusion.meta, ...), custom_call_target="tpu_custom_call" | custom-call | flops 1006632960 | bytes 4194304 | tf_op jit(solution)/shard_map/attention/pallas_call | solution.py:161
  51.5 1.9 %collective-permute-start.11 = (bf16[2,64,1024]{2,1,0:T(8,128)(2,1)S(1)}, bf16[2,64,1024]{2,1,0:T(8,128)(2,1)S(1)}, u32[]{:S(2)}, u32[]{:S(2)}) collective-permute-start(bf16[2,64,1024]{2,1,0:T(8,128)(2,1)S(1)} %get-tuple-element.33.mine0), channel_id=1, source_target_pairs={{1,0},{2,1},{3,2},{4,3},{5,4},{6,5},{7,6},{9,8},{10,9},{11,10},{12... | collective-permute-start | bytes 786440 | tf_op jit(solution)/shard_map/ppermute | solution.py:29
  53.5 8.3 %collective-permute-done.11.refs_0_ = bf16[2,64,1024]{2,1,0:T(8,128)(2,1)S(1)} collective-permute-done((bf16[2,64,1024]{2,1,0:T(8,128)(2,1)S(1)}, bf16[2,64,1024]{2,1,0:T(8,128)(2,1)S(1)}, u32[]{:S(2)}, u32[]{:S(2)}) %collective-permute-start.11) | collective-permute-done | bytes 262176 | tf_op jit(solution)/shard_map/ppermute | solution.py:29
  61.8 4.0 %attention.3 = (bf16[2,64,1024]{2,1,0:T(8,128)(2,1)S(1)}, bf16[2,64,1024]{2,1,0:T(8,128)(2,1)S(1)}, bf16[2,128,512]{2,1,0:T(8,128)(2,1)S(1)}, bf16[2,128,512]{2,...) custom-call(s32[6]{0:T(128)S(1)} %pad_add_fusion.meta, ...), custom_call_target="tpu_custom_call" | custom-call | flops 1006632960 | bytes 4194304 | tf_op jit(solution)/shard_map/attention/pallas_call | solution.py:161
  73.7 6.4 %collective-permute-done.14.refs_3_ = bf16[2,64,512]{2,1,0:T(8,128)(2,1)S(1)} collective-permute-done((bf16[2,64,512]{2,1,0:T(8,128)(2,1)S(1)}, bf16[2,64,512]{2,1,0:T(8,128)(2,1)S(1)}, u32[]{:S(2)}, u32[]{:S(2)}) %collective-permute-start.14) | collective-permute-done | bytes 131104 | tf_op jit(solution)/shard_map/ppermute | solution.py:29
  82.1 3.0 %collective-permute-done.16.refs_5_ = bf16[2,64,512]{2,1,0:T(8,128)(2,1)S(1)} collective-permute-done((bf16[2,64,512]{2,1,0:T(8,128)(2,1)S(1)}, bf16[2,64,512]{2,1,0:T(8,128)(2,1)S(1)}, u32[]{:S(2)}, u32[]{:S(2)}) %collective-permute-start.16) | collective-permute-done | bytes 131104 | tf_op jit(solution)/shard_map/ppermute | solution.py:29
  85.1 14.1 %collective-permute-done.18.refs_7_ = bf16[2,64,512]{2,1,0:T(8,128)(2,1)S(1)} collective-permute-done((bf16[2,64,512]{2,1,0:T(8,128)(2,1)S(1)}, bf16[2,64,512]{2,1,0:T(8,128)(2,1)S(1)}, u32[]{:S(2)}, u32[]{:S(2)}) %collective-permute-start.18) | collective-permute-done | bytes 131104 | tf_op jit(solution)/shard_map/ppermute | solution.py:29
  99.6 5.4 %collective-permute-start.19 = (bf16[2,128,512]{2,1,0:T(8,128)(2,1)S(1)}, bf16[2,128,512]{2,1,0:T(8,128)(2,1)S(1)}, u32[]{:S(2)}, u32[]{:S(2)}) collective-permute-start(bf16[2,128,512]{2,1,0:T(8,128)(2,1)S(1)} %get-tuple-element.52), channel_id=1, source_target_pairs={{16,0},{24,8},{32,16},{40,24},{48,32},{56,40},{64,48},{72,56},{80,... | collective-permute-start | bytes 786440 | tf_op jit(solution)/shard_map/ppermute | solution.py:29
  107.6 4.6 %collective-permute-done.19.back1 = bf16[2,128,512]{2,1,0:T(8,128)(2,1)S(1)} collective-permute-done((bf16[2,128,512]{2,1,0:T(8,128)(2,1)S(1)}, bf16[2,128,512]{2,1,0:T(8,128)(2,1)S(1)}, u32[]{:S(2)}, u32[]{:S(2)}) %collective-permute-start.19) | collective-permute-done | bytes 262176 | tf_op jit(solution)/shard_map/ppermute | solution.py:29
  112.2 4.9 %collective-permute-done.20.back2 = bf16[2,128,512]{2,1,0:T(8,128)(2,1)S(1)} collective-permute-done((bf16[2,128,512]{2,1,0:T(8,128)(2,1)S(1)}, bf16[2,128,512]{2,1,0:T(8,128)(2,1)S(1)}, u32[]{:S(2)}, u32[]{:S(2)}) %collective-permute-start.20) | collective-permute-done | bytes 262176 | tf_op jit(solution)/shard_map/ppermute | solution.py:29
  117.2 10.6 %collective-permute-done.21.back3 = bf16[2,128,512]{2,1,0:T(8,128)(2,1)S(1)} collective-permute-done((bf16[2,128,512]{2,1,0:T(8,128)(2,1)S(1)}, bf16[2,128,512]{2,1,0:T(8,128)(2,1)S(1)}, u32[]{:S(2)}, u32[]{:S(2)}) %collective-permute-start.21) | collective-permute-done | bytes 262176 | tf_op jit(solution)/shard_map/ppermute | solution.py:29
  127.9 3.3 %collective-permute-start.22 = (bf16[2,64,1536]{2,1,0:T(8,128)(2,1)S(1)}, bf16[2,64,1536]{2,1,0:T(8,128)(2,1)S(1)}, u32[]{:S(2)}, u32[]{:S(2)}) collective-permute-start(bf16[2,64,1536]{2,1,0:T(8,128)(2,1)S(1)} %get-tuple-element.57), channel_id=1, source_target_pairs={{0,8},{8,0},{16,24},{24,16},{32,40},{40,32},{48,56},{56,48},{64,72... | collective-permute-start | bytes 1179656 | tf_op jit(solution)/shard_map/ppermute | solution.py:29
  (43 shorter events, 23.7 us)
Async XLA Ops:
  3.2 4.5 %collective-permute-start = (bf16[10,64,512]{2,1,0:T(8,128)(2,1)}, bf16[10,64,512]{2,1,0:T(8,128)(2,1)S(1)}, u32[]{:S(2)}, u32[]{:S(2)}) collective-permute-start(bf16[10,64,512]{2,1,0:T(8,128)(2,1)} %get-tuple-element.32), channel_id=1, source_target_pairs={{0,8},{8,0},{16,24},{24,16},{32,40},{40,32},{48,56},{56,48},{64,72... | collective-permute-start | bytes 1966088 | tf_op jit(solution)/shard_map/ppermute | solution.py:29
  8.8 38.8 %copy-start.1 = (bf16[10,64,512]{2,1,0:T(8,128)(2,1)S(1)}, bf16[10,64,512]{2,1,0:T(8,128)(2,1)}, u32[]{:S(2)}) copy-start(bf16[10,64,512]{2,1,0:T(8,128)(2,1)} %get-tuple-element.31.keep) | copy-start | bytes 1966084
  8.8 10.8 %collective-permute-start.3 = (bf16[2,128,512]{2,1,0:T(8,128)(2,1)S(1)}, bf16[2,128,512]{2,1,0:T(8,128)(2,1)S(1)}, u32[]{:S(2)}, u32[]{:S(2)}) collective-permute-start(bf16[2,128,512]{2,1,0:T(8,128)(2,1)S(1)} %pair_keys.1.p0.refs_0_.refs_1_), channel_id=1, source_target_pairs={{0,48},{8,56},{16,64},{24,72},{32,80},{40,88},{48,96},{56,104},{64... | collective-permute-start | bytes 786440 | tf_op jit(solution)/shard_map/ppermute | solution.py:29
  12.1 9.1 %collective-permute-start.2 = (bf16[2,128,512]{2,1,0:T(8,128)(2,1)S(1)}, bf16[2,128,512]{2,1,0:T(8,128)(2,1)S(1)}, u32[]{:S(2)}, u32[]{:S(2)}) collective-permute-start(bf16[2,128,512]{2,1,0:T(8,128)(2,1)S(1)} %pair_keys.1.p0.refs_0_.refs_1_), channel_id=1, source_target_pairs={{0,32},{8,40},{16,48},{24,56},{32,64},{40,72},{48,80},{56,88},{64,... | collective-permute-start | bytes 786440 | tf_op jit(solution)/shard_map/ppermute | solution.py:29
  16.2 12.2 %collective-permute-start.1 = (bf16[2,128,512]{2,1,0:T(8,128)(2,1)S(1)}, bf16[2,128,512]{2,1,0:T(8,128)(2,1)S(1)}, u32[]{:S(2)}, u32[]{:S(2)}) collective-permute-start(bf16[2,128,512]{2,1,0:T(8,128)(2,1)S(1)} %pair_keys.1.p0.refs_0_.refs_1_), channel_id=1, source_target_pairs={{0,16},{8,24},{16,32},{24,40},{32,48},{40,56},{48,64},{56,72},{64,... | collective-permute-start | bytes 786440 | tf_op jit(solution)/shard_map/ppermute | solution.py:29
  28.4 9.9 %collective-permute-start.10 = (bf16[2,64,512]{2,1,0:T(8,128)(2,1)S(1)}, bf16[2,64,512]{2,1,0:T(8,128)(2,1)S(1)}, u32[]{:S(2)}, u32[]{:S(2)}) collective-permute-start(bf16[2,64,512]{2,1,0:T(8,128)(2,1)S(1)} %choose.1.refs_4_.refs_5_), channel_id=1, source_target_pairs={{0,448},{8,456},{16,464},{24,472},{32,480},{40,488},{48,496},{56,5... | collective-permute-start | bytes 393224 | tf_op jit(solution)/shard_map/ppermute | solution.py:29
  32.3 9.1 %collective-permute-start.9 = (bf16[2,64,512]{2,1,0:T(8,128)(2,1)S(1)}, bf16[2,64,512]{2,1,0:T(8,128)(2,1)S(1)}, u32[]{:S(2)}, u32[]{:S(2)}) collective-permute-start(bf16[2,64,512]{2,1,0:T(8,128)(2,1)S(1)} %choose.1.refs_4_.refs_5_), channel_id=1, source_target_pairs={{0,384},{8,392},{16,400},{24,408},{32,416},{40,424},{48,432},{56,4... | collective-permute-start | bytes 393224 | tf_op jit(solution)/shard_map/ppermute | solution.py:29
  34.1 8.9 %collective-permute-start.8 = (bf16[2,64,512]{2,1,0:T(8,128)(2,1)S(1)}, bf16[2,64,512]{2,1,0:T(8,128)(2,1)S(1)}, u32[]{:S(2)}, u32[]{:S(2)}) collective-permute-start(bf16[2,64,512]{2,1,0:T(8,128)(2,1)S(1)} %choose.1.refs_4_.refs_5_), channel_id=1, source_target_pairs={{0,320},{8,328},{16,336},{24,344},{32,352},{40,360},{48,368},{56,3... | collective-permute-start | bytes 393224 | tf_op jit(solution)/shard_map/ppermute | solution.py:29
  35.6 7.4 %collective-permute-start.7 = (bf16[2,64,512]{2,1,0:T(8,128)(2,1)S(1)}, bf16[2,64,512]{2,1,0:T(8,128)(2,1)S(1)}, u32[]{:S(2)}, u32[]{:S(2)}) collective-permute-start(bf16[2,64,512]{2,1,0:T(8,128)(2,1)S(1)} %choose.1.refs_4_.refs_5_), channel_id=1, source_target_pairs={{0,256},{8,264},{16,272},{24,280},{32,288},{40,296},{48,304},{56,3... | collective-permute-start | bytes 393224 | tf_op jit(solution)/shard_map/ppermute | solution.py:29
  37.0 5.9 %collective-permute-start.6 = (bf16[2,64,512]{2,1,0:T(8,128)(2,1)S(1)}, bf16[2,64,512]{2,1,0:T(8,128)(2,1)S(1)}, u32[]{:S(2)}, u32[]{:S(2)}) collective-permute-start(bf16[2,64,512]{2,1,0:T(8,128)(2,1)S(1)} %choose.1.refs_4_.refs_5_), channel_id=1, source_target_pairs={{0,192},{8,200},{16,208},{24,216},{32,224},{40,232},{48,240},{56,2... | collective-permute-start | bytes 393224 | tf_op jit(solution)/shard_map/ppermute | solution.py:29
  38.4 6.4 %collective-permute-start.5 = (bf16[2,64,512]{2,1,0:T(8,128)(2,1)S(1)}, bf16[2,64,512]{2,1,0:T(8,128)(2,1)S(1)}, u32[]{:S(2)}, u32[]{:S(2)}) collective-permute-start(bf16[2,64,512]{2,1,0:T(8,128)(2,1)S(1)} %choose.1.refs_4_.refs_5_), channel_id=1, source_target_pairs={{0,128},{8,136},{16,144},{24,152},{32,160},{40,168},{48,176},{56,1... | collective-permute-start | bytes 393224 | tf_op jit(solution)/shard_map/ppermute | solution.py:29
  41.4 6.2 %collective-permute-start.4 = (bf16[2,64,512]{2,1,0:T(8,128)(2,1)S(1)}, bf16[2,64,512]{2,1,0:T(8,128)(2,1)S(1)}, u32[]{:S(2)}, u32[]{:S(2)}) collective-permute-start(bf16[2,64,512]{2,1,0:T(8,128)(2,1)S(1)} %choose.1.refs_4_.refs_5_), channel_id=1, source_target_pairs={{0,64},{8,72},{16,80},{24,88},{32,96},{40,104},{48,112},{56,120},{... | collective-permute-start | bytes 393224 | tf_op jit(solution)/shard_map/ppermute | solution.py:29
  51.5 10.2 %collective-permute-start.11 = (bf16[2,64,1024]{2,1,0:T(8,128)(2,1)S(1)}, bf16[2,64,1024]{2,1,0:T(8,128)(2,1)S(1)}, u32[]{:S(2)}, u32[]{:S(2)}) collective-permute-start(bf16[2,64,1024]{2,1,0:T(8,128)(2,1)S(1)} %get-tuple-element.33.mine0), channel_id=1, source_target_pairs={{1,0},{2,1},{3,2},{4,3},{5,4},{6,5},{7,6},{9,8},{10,9},{11,10},{12... | collective-permute-start | bytes 786440 | tf_op jit(solution)/shard_map/ppermute | solution.py:29
  65.8 6.5 %collective-permute-start.12 = (bf16[2,64,512]{2,1,0:T(8,128)(2,1)S(1)}, bf16[2,64,512]{2,1,0:T(8,128)(2,1)S(1)}, u32[]{:S(2)}, u32[]{:S(2)}) collective-permute-start(bf16[2,64,512]{2,1,0:T(8,128)(2,1)S(1)} %get-tuple-element.42.refs_0_), channel_id=1, source_target_pairs={{64,0},{72,8},{80,16},{88,24},{96,32},{104,40},{112,48},{120,56},{... | collective-permute-start | bytes 393224 | tf_op jit(solution)/shard_map/ppermute | solution.py:29
  67.1 12.9 %collective-permute-start.14 = (bf16[2,64,512]{2,1,0:T(8,128)(2,1)S(1)}, bf16[2,64,512]{2,1,0:T(8,128)(2,1)S(1)}, u32[]{:S(2)}, u32[]{:S(2)}) collective-permute-start(bf16[2,64,512]{2,1,0:T(8,128)(2,1)S(1)} %get-tuple-element.43), channel_id=1, source_target_pairs={{192,0},{200,8},{208,16},{216,24},{224,32},{232,40},{240,48},{248,... | collective-permute-start | bytes 393224 | tf_op jit(solution)/shard_map/ppermute | solution.py:29
  68.4 13.7 %collective-permute-start.13 = (bf16[2,64,512]{2,1,0:T(8,128)(2,1)S(1)}, bf16[2,64,512]{2,1,0:T(8,128)(2,1)S(1)}, u32[]{:S(2)}, u32[]{:S(2)}) collective-permute-start(bf16[2,64,512]{2,1,0:T(8,128)(2,1)S(1)} %get-tuple-element.43), channel_id=1, source_target_pairs={{128,0},{136,8},{144,16},{152,24},{160,32},{168,40},{176,48},{184,... | collective-permute-start | bytes 393224 | tf_op jit(solution)/shard_map/ppermute | solution.py:29
  69.7 15.3 %collective-permute-start.16 = (bf16[2,64,512]{2,1,0:T(8,128)(2,1)S(1)}, bf16[2,64,512]{2,1,0:T(8,128)(2,1)S(1)}, u32[]{:S(2)}, u32[]{:S(2)}) collective-permute-start(bf16[2,64,512]{2,1,0:T(8,128)(2,1)S(1)} %get-tuple-element.44), channel_id=1, source_target_pairs={{320,0},{328,8},{336,16},{344,24},{352,32},{360,40},{368,48},{376,... | collective-permute-start | bytes 393224 | tf_op jit(solution)/shard_map/ppermute | solution.py:29
  71.0 14.0 %collective-permute-start.15 = (bf16[2,64,512]{2,1,0:T(8,128)(2,1)S(1)}, bf16[2,64,512]{2,1,0:T(8,128)(2,1)S(1)}, u32[]{:S(2)}, u32[]{:S(2)}) collective-permute-start(bf16[2,64,512]{2,1,0:T(8,128)(2,1)S(1)} %get-tuple-element.44), channel_id=1, source_target_pairs={{256,0},{264,8},{272,16},{280,24},{288,32},{296,40},{304,48},{312,... | collective-permute-start | bytes 393224 | tf_op jit(solution)/shard_map/ppermute | solution.py:29
  72.4 26.8 %collective-permute-start.18 = (bf16[2,64,512]{2,1,0:T(8,128)(2,1)S(1)}, bf16[2,64,512]{2,1,0:T(8,128)(2,1)S(1)}, u32[]{:S(2)}, u32[]{:S(2)}) collective-permute-start(bf16[2,64,512]{2,1,0:T(8,128)(2,1)S(1)} %get-tuple-element.45), channel_id=1, source_target_pairs={{448,0},{456,8},{464,16},{472,24},{480,32},{488,40},{496,48},{504,... | collective-permute-start | bytes 393224 | tf_op jit(solution)/shard_map/ppermute | solution.py:29
  80.0 19.2 %collective-permute-start.17 = (bf16[2,64,512]{2,1,0:T(8,128)(2,1)S(1)}, bf16[2,64,512]{2,1,0:T(8,128)(2,1)S(1)}, u32[]{:S(2)}, u32[]{:S(2)}) collective-permute-start(bf16[2,64,512]{2,1,0:T(8,128)(2,1)S(1)} %get-tuple-element.45), channel_id=1, source_target_pairs={{384,0},{392,8},{400,16},{408,24},{416,32},{424,40},{432,48},{440,... | collective-permute-start | bytes 393224 | tf_op jit(solution)/shard_map/ppermute | solution.py:29
  99.6 12.6 %collective-permute-start.19 = (bf16[2,128,512]{2,1,0:T(8,128)(2,1)S(1)}, bf16[2,128,512]{2,1,0:T(8,128)(2,1)S(1)}, u32[]{:S(2)}, u32[]{:S(2)}) collective-permute-start(bf16[2,128,512]{2,1,0:T(8,128)(2,1)S(1)} %get-tuple-element.52), channel_id=1, source_target_pairs={{16,0},{24,8},{32,16},{40,24},{48,32},{56,40},{64,48},{72,56},{80,... | collective-permute-start | bytes 786440 | tf_op jit(solution)/shard_map/ppermute | solution.py:29
  105.0 12.2 %collective-permute-start.20 = (bf16[2,128,512]{2,1,0:T(8,128)(2,1)S(1)}, bf16[2,128,512]{2,1,0:T(8,128)(2,1)S(1)}, u32[]{:S(2)}, u32[]{:S(2)}) collective-permute-start(bf16[2,128,512]{2,1,0:T(8,128)(2,1)S(1)} %get-tuple-element.53), channel_id=1, source_target_pairs={{32,0},{40,8},{48,16},{56,24},{64,32},{72,40},{80,48},{88,56},{96,... | collective-permute-start | bytes 786440 | tf_op jit(solution)/shard_map/ppermute | solution.py:29
  106.3 21.4 %collective-permute-start.21 = (bf16[2,128,512]{2,1,0:T(8,128)(2,1)S(1)}, bf16[2,128,512]{2,1,0:T(8,128)(2,1)S(1)}, u32[]{:S(2)}, u32[]{:S(2)}) collective-permute-start(bf16[2,128,512]{2,1,0:T(8,128)(2,1)S(1)} %get-tuple-element.54), channel_id=1, source_target_pairs={{48,0},{56,8},{64,16},{72,24},{80,32},{88,40},{96,48},{104,56},{11... | collective-permute-start | bytes 786440 | tf_op jit(solution)/shard_map/ppermute | solution.py:29
  127.9 4.6 %collective-permute-start.22 = (bf16[2,64,1536]{2,1,0:T(8,128)(2,1)S(1)}, bf16[2,64,1536]{2,1,0:T(8,128)(2,1)S(1)}, u32[]{:S(2)}, u32[]{:S(2)}) collective-permute-start(bf16[2,64,1536]{2,1,0:T(8,128)(2,1)S(1)} %get-tuple-element.57), channel_id=1, source_target_pairs={{0,8},{8,0},{16,24},{24,16},{32,40},{40,32},{48,56},{56,48},{64,72... | collective-permute-start | bytes 1179656 | tf_op jit(solution)/shard_map/ppermute | solution.py:29
  (4 other events, 32.8 us)

commit v8 on v3

--- a/solution.py
+++ b/solution.py
@@ -16,8 +16,6 @@
 HALF_KV = HALF_HEADS * HEAD_DIM
 HALF_FEAT = HALF_HEADS * GROUP * HEAD_DIM
 SCALE = HEAD_DIM**-0.5
-TA = 3
-TB = 2
 LOG2E = 1.4426950408889634
 NEG = -1e30
 NT = (((1,), (1,)), ((), ()))
@@ -127,6 +125,7 @@
 
 
 WHOLE = pl.BlockSpec(memory_space=pltpu.VMEM)
+FAR = pl.BlockSpec(memory_space=pltpu.HBM)
 SCALAR = pl.BlockSpec(memory_space=pltpu.SMEM)
 WIDE = 2 * HALF_KV
 
@@ -170,14 +169,20 @@
     )(*args)
 
 
-def simple(kernel, out_shape, args, scalars=1):
+def far_scratch(arrays):
+    buffers = [pltpu.VMEM(a.shape, a.dtype) for a in arrays]
+    return buffers + [pltpu.SemaphoreType.DMA((len(arrays),))]
+
+
+def simple(kernel, out_shape, args, scalars=1, far=False):
     size = sum(a.size * a.dtype.itemsize for a in list(args) + list(out_shape))
     return pl.pallas_call(
         kernel,
         out_shape=out_shape,
-        in_specs=[SCALAR] * scalars + [WHOLE] * (len(args) - scalars),
+        in_specs=[SCALAR] * scalars + [FAR if far else WHOLE] * (len(args) - scalars),
         out_specs=[WHOLE] * len(out_shape),
-        compiler_params=pltpu.CompilerParams(vmem_limit_bytes=16 << 20),
+        scratch_shapes=far_scratch(args[scalars:]) if far else [],
+        compiler_params=pltpu.CompilerParams(vmem_limit_bytes=(56 if far else 16) << 20),
         cost_estimate=pl.CostEstimate(flops=size, bytes_accessed=size, transcendentals=0),
         name=kernel.__name__,
     )(*args)
@@ -192,7 +197,17 @@
         send_out[t] = total.astype(jnp.bfloat16)
 
 
-def split_all(meta, keys, values, inputs, first, head, keep, give, kv_keep, kv_give):
+def split_all(meta, *refs):
+    sources, (keep, give, kv_keep, kv_give), buffers, sems = refs[:5], refs[5:9], refs[9:14], refs[14]
+    copies = [
+        pltpu.make_async_copy(source, buffer, sems.at[n])
+        for n, (source, buffer) in enumerate(zip(sources, buffers))
+    ]
+    for copy in copies:
+        copy.start()
+    for copy in copies:
+        copy.wait()
+    keys, values, inputs, first, head = buffers
     swap = meta[0] % 2 == 1
     for source, at in ((keys, 0), (values, HALF_KV)):
         low, high = source[0, :, :, :HALF_KV], source[0, :, :, HALF_KV:]
@@ -209,13 +224,15 @@
             give[2 + 2 * n + h] = jnp.where(swap, low, high)
 
 
-def pair_keys(meta, keep, recv, up_low, up_high, pair, start):
-    keep, recv = keep.at[:2], recv.at[:2]
+def pair_keys(meta, keep, recv, pair):
+    pair[:, :BLK] = keep[:2]
+    pair[:, BLK:] = recv[:2]
+
+
+def first_block(meta, keep, recv, up_low, up_high, start):
     core = meta[0] % 2
     even = (meta[0] // 8) % 2 == 0
-    pair[:, :BLK] = keep[...]
-    pair[:, BLK:] = recv[...]
-    near = jnp.where(core == 0, keep[...], recv[...])
+    near = jnp.where(core == 0, keep[:2], recv[:2])
     above = jnp.where(core == 0, up_low[...], up_high[...])
     start[...] = jnp.where(even, near, above)
 
@@ -281,25 +298,27 @@
         split_all,
         [ten, ten, half, half],
         [spot, saved_keys, saved_values, inputs, first_grads, head_grads],
+        far=True,
     )
     recv = sibling(give)
     up_low = ctx(kv_keep, lambda i: i + 8, lambda i: i % STRIDE == 0)
     up_high = ctx(kv_give, lambda i: i + 9, lambda i: i % STRIDE == 0)
-    pair, start = simple(
-        pair_keys,
-        [shape((2, 2 * BLK, WIDE), bf16), half],
-        [spot, keep, recv, up_low, up_high],
-    )
-    across = [ctx(start, lambda i: i + 2 * d, lambda i: (i // 2) % 4 == 0) for d in range(1, 4)]
+    (pair,) = simple(pair_keys, [shape((2, 2 * BLK, WIDE), bf16)], [spot, keep, recv])
+    pairs = [pair] + [ctx(pair, lambda i: i + 2 * d) for d in range(1, 4)]
+    (start,) = simple(first_block, [half], [spot, keep, recv, up_low, up_high])
+    across = []
+    for d in range(1, 4):
+        sent = start
+        if d == 1:
+            sent, pairs[1] = lax.optimization_barrier((start, pairs[1]))
+        across.append(ctx(sent, lambda i: i + 2 * d, lambda i: (i // 2) % 4 == 0))
     (chosen,) = simple(choose, [half], [spot, start] + across)
-    pairs = [pair] + [ctx(pair, lambda i: i + 2 * d) for d in range(1, 4)]
     strided = [chosen]
     for s in range(1, 4):
         sent = chosen
         if s == 1:
-            sent, pairs[TA] = lax.optimization_barrier((chosen, pairs[TA]))
+            sent, pairs = lax.optimization_barrier((chosen, pairs))
         strided.append(ctx(sent, lambda i: i + STRIDE * s))
-
     gain = jnp.where(core == 0, query_gain[:, :HALF_FEAT], query_gain[:, HALF_FEAT:])
     heads = jnp.where(core == 0, window[0, :2], window[0, 2:])
     steps = jnp.where(core == 0, stride[0, :2], stride[0, 2:])
@@ -309,9 +328,13 @@
     first = attention(0, meta, gain, keep, recv, None, pairs, strided, None)
     grads = route(first[0], "pp", lambda i: i - 1)
     second = attention(1, meta, gain, keep, recv, grads, pairs, strided, first[1:8])
+    backs = [ctx(second[1 + d], lambda i: i - 2 * d) for d in range(1, 4)]
     columns = [first[9], second[9]]
-    columns += [ctx(second[4 + s], lambda i: i - STRIDE * s) for s in range(1, 4)]
-    backs = [ctx(second[1 + d], lambda i: i - 2 * d) for d in range(1, 4)]
+    for s in range(1, 4):
+        sent = second[4 + s]
+        if s == 1:
+            sent, backs[0] = lax.optimization_barrier((sent, backs[0]))
+        columns.append(ctx(sent, lambda i: i - STRIDE * s))
 
     wide = shape((2, BLK, WIDE), f32)
     total, send = simple(column_sum, [wide, half], columns, 0)
@@ -319,7 +342,7 @@
     for d in range(1, 4):
         sent = send
         if d == 1:
-            sent, backs[TB] = lax.optimization_barrier((send, backs[TB]))
+            sent, backs = lax.optimization_barrier((send, backs))
         rows.append(ctx(sent, lambda i: i - 2 * d, lambda i: (i // 2) % 4 == d))
     mine, swap, down = simple(
         row_sum,

time: 121 us -> 129 us (1.066)
  the two profiles are of different devices: /device:TPU:224 before, /device:TPU:192 now
where the time goes in v8:
time: 129 us
  waiting for transfers between devices  62.2 us (48%)
  starting transfers between devices  52.3 us (41%)
  Pallas kernels  11.9 us (9%)
    ppermute x25, waiting for transfers between devices, route(): lax.ppermute(array, axis, [(a, b) for a, b in pairs if b is not None and...  62.2 us
    ppermute x25, starting transfers between devices, route(): lax.ppermute(array, axis, [(a, b) for a, b in pairs if b is not None and...  52.3 us
    pallas_call x2, Pallas kernels, attention(): pl.pallas_call(functools.partial(attention_kernel, tick), out_shape=out_s...  8 us
    pallas_call x7, Pallas kernels, simple(): pl.pallas_call(kernel, out_shape=out_shape, in_specs=[SCALAR] * scalars +...  3.87 us
  transfers between devices with their start and end apart: 25, of which 14 were waited for; matrix products, arithmetic and copies ran while one was open for 0% of the time, Pallas kernels for 0%

profile of v8, /device:TPU:192, one launch (start us, length us, event | category | flops | bytes accessed | tf_op | source)
XLA Modules:
  0.0 128.6 jit_solution(12428607049365449994)
XLA Ops:
  0.6 2.6 %split_all.1 = (bf16[10,64,512]{2,1,0:T(8,128)(2,1)}, bf16[10,64,512]{2,1,0:T(8,128)(2,1)}, bf16[2,64,512]{2,1,0:T(8,128)(2,1)}, bf16[2,64,512]{2,1,0:T(8,128)(2,1)}) custom-call(s32[1]{0:T(128)} %bitcast.meta, bf16[1,2,64,512]{3,2,1,0:T(8,128)(2,1)} %refs_0_.1, bf16[1,2,64,512]{3,2,1,0:T(8,128)(2,1)} %refs_1_.1, bf16[1,2,64,2048]{3,2,1,0:T(8,128)(2,1)} %refs_2_.1, ...), custom_call_target="tpu_custom_call" | custom-call | flops 2883588 | bytes 2883588 | tf_op jit(solution)/shard_map/split_all/pallas_call | solution.py:179
  3.2 1.9 %collective-permute-start = (bf16[10,64,512]{2,1,0:T(8,128)(2,1)}, bf16[10,64,512]{2,1,0:T(8,128)(2,1)S(1)}, u32[]{:S(2)}, u32[]{:S(2)}) collective-permute-start(bf16[10,64,512]{2,1,0:T(8,128)(2,1)} %get-tuple-element.46), channel_id=1, source_target_pairs={{0,8},{8,0},{16,24},{24,16},{32,40},{40,32},{48,56},{56,48},{64,72... | collective-permute-start | bytes 1966088 | tf_op jit(solution)/shard_map/ppermute | solution.py:28
  5.1 2.3 %collective-permute-done.recv = bf16[10,64,512]{2,1,0:T(8,128)(2,1)S(1)} collective-permute-done((bf16[10,64,512]{2,1,0:T(8,128)(2,1)}, bf16[10,64,512]{2,1,0:T(8,128)(2,1)S(1)}, u32[]{:S(2)}, u32[]{:S(2)}) %collective-permute-start) | collective-permute-done | bytes 655392 | tf_op jit(solution)/shard_map/ppermute | solution.py:28
  8.5 3.5 %collective-permute-start.3 = (bf16[2,128,512]{2,1,0:T(8,128)(2,1)S(1)}, bf16[2,128,512]{2,1,0:T(8,128)(2,1)S(1)}, u32[]{:S(2)}, u32[]{:S(2)}) collective-permute-start(bf16[2,128,512]{2,1,0:T(8,128)(2,1)S(1)} %pair_keys.1.refs_0_.refs_1_), channel_id=1, source_target_pairs={{0,16},{8,24},{16,32},{24,40},{32,48},{40,56},{48,64},{56,72},{64,... | collective-permute-start | bytes 786440 | tf_op jit(solution)/shard_map/ppermute | solution.py:28
  12.1 3.5 %collective-permute-start.1 = (bf16[2,64,512]{2,1,0:T(8,128)(2,1)S(1)}, bf16[2,64,512]{2,1,0:T(8,128)(2,1)S(1)}, u32[]{:S(2)}, u32[]{:S(2)}) collective-permute-start(bf16[2,64,512]{2,1,0:T(8,128)(2,1)S(1)} %copy-done.6), channel_id=1, source_target_pairs={{0,64},{128,192},{256,320},{384,448},{1,65},{129,193},{257,321},{3... | collective-permute-start | bytes 393224 | tf_op jit(solution)/shard_map/ppermute | solution.py:28
  18.2 3.7 %collective-permute-start.7 = (bf16[2,128,512]{2,1,0:T(8,128)(2,1)S(1)}, bf16[2,128,512]{2,1,0:T(8,128)(2,1)S(1)}, u32[]{:S(2)}, u32[]{:S(2)}) collective-permute-start(bf16[2,128,512]{2,1,0:T(8,128)(2,1)S(1)} %pair_keys.1.refs_0_.refs_1_), channel_id=1, source_target_pairs={{0,32},{8,40},{16,48},{24,56},{32,64},{40,72},{48,80},{56,88},{64,... | collective-permute-start | bytes 786440 | tf_op jit(solution)/shard_map/ppermute | solution.py:28
  22.0 7.5 %collective-permute-start.6 = (bf16[2,64,512]{2,1,0:T(8,128)(2,1)S(1)}, bf16[2,64,512]{2,1,0:T(8,128)(2,1)S(1)}, u32[]{:S(2)}, u32[]{:S(2)}) collective-permute-start(bf16[2,64,512]{2,1,0:T(8,128)(2,1)S(1)} %first_block.1.start), channel_id=1, source_target_pairs={{0,48},{8,56},{64,112},{72,120},{128,176},{136,184},{192,240},{200... | collective-permute-start | bytes 393224 | tf_op jit(solution)/shard_map/ppermute | solution.py:28
  34.7 3.4 %collective-permute-start.11 = (bf16[2,64,512]{2,1,0:T(8,128)(2,1)S(1)}, bf16[2,64,512]{2,1,0:T(8,128)(2,1)S(1)}, u32[]{:S(2)}, u32[]{:S(2)}) collective-permute-start(bf16[2,64,512]{2,1,0:T(8,128)(2,1)S(1)} %choose.1.refs_4_.refs_5_), channel_id=1, source_target_pairs={{0,384},{8,392},{16,400},{24,408},{32,416},{40,424},{48,432},{56,4... | collective-permute-start | bytes 393224 | tf_op jit(solution)/shard_map/ppermute | solution.py:28
  38.1 2.3 %collective-permute-start.10 = (bf16[2,64,512]{2,1,0:T(8,128)(2,1)S(1)}, bf16[2,64,512]{2,1,0:T(8,128)(2,1)S(1)}, u32[]{:S(2)}, u32[]{:S(2)}) collective-permute-start(bf16[2,64,512]{2,1,0:T(8,128)(2,1)S(1)} %choose.1.refs_4_.refs_5_), channel_id=1, source_target_pairs={{0,256},{8,264},{16,272},{24,280},{32,288},{40,296},{48,304},{56,3... | collective-permute-start | bytes 393224 | tf_op jit(solution)/shard_map/ppermute | solution.py:28
  40.4 3.2 %collective-permute-start.9 = (bf16[2,64,512]{2,1,0:T(8,128)(2,1)S(1)}, bf16[2,64,512]{2,1,0:T(8,128)(2,1)S(1)}, u32[]{:S(2)}, u32[]{:S(2)}) collective-permute-start(bf16[2,64,512]{2,1,0:T(8,128)(2,1)S(1)} %choose.1.refs_4_.refs_5_), channel_id=1, source_target_pairs={{0,128},{8,136},{16,144},{24,152},{32,160},{40,168},{48,176},{56,1... | collective-permute-start | bytes 393224 | tf_op jit(solution)/shard_map/ppermute | solution.py:28
  43.8 2.3 %collective-permute-done.9.refs_5_.refs_6_ = bf16[2,64,512]{2,1,0:T(8,128)(2,1)S(1)} collective-permute-done((bf16[2,64,512]{2,1,0:T(8,128)(2,1)S(1)}, bf16[2,64,512]{2,1,0:T(8,128)(2,1)S(1)}, u32[]{:S(2)}, u32[]{:S(2)}) %collective-permute-start.9) | collective-permute-done | bytes 131104 | tf_op jit(solution)/shard_map/ppermute | solution.py:28
  46.2 1.6 %collective-permute-done.11.refs_7_.refs_8_ = bf16[2,64,512]{2,1,0:T(8,128)(2,1)S(1)} collective-permute-done((bf16[2,64,512]{2,1,0:T(8,128)(2,1)S(1)}, bf16[2,64,512]{2,1,0:T(8,128)(2,1)S(1)}, u32[]{:S(2)}, u32[]{:S(2)}) %collective-permute-start.11) | collective-permute-done | bytes 131104 | tf_op jit(solution)/shard_map/ppermute | solution.py:28
  47.7 4.0 %attention.2 = (bf16[2,64,1024]{2,1,0:T(8,128)(2,1)S(1)}, bf16[64,1024]{1,0:T(8,128)(2,1)S(1)}, bf16[128,512]{1,0:T(8,128)(2,1)S(1)}, bf16[128,512]{1,0:T(8,128)...) custom-call(s32[6]{0:T(128)S(1)} %pad_add_fusion.meta, ...), custom_call_target="tpu_custom_call" | custom-call | flops 1006632960 | bytes 4194304 | tf_op jit(solution)/shard_map/attention/pallas_call | solution.py:158
  51.7 1.9 %collective-permute-start.12 = (bf16[2,64,1024]{2,1,0:T(8,128)(2,1)S(1)}, bf16[2,64,1024]{2,1,0:T(8,128)(2,1)S(1)}, u32[]{:S(2)}, u32[]{:S(2)}) collective-permute-start(bf16[2,64,1024]{2,1,0:T(8,128)(2,1)S(1)} %get-tuple-element.57.mine0), channel_id=1, source_target_pairs={{1,0},{2,1},{3,2},{4,3},{5,4},{6,5},{7,6},{9,8},{10,9},{11,10},{12... | collective-permute-start | bytes 786440 | tf_op jit(solution)/shard_map/ppermute | solution.py:28
  53.6 10.0 %collective-permute-done.12.refs_0_ = bf16[2,64,1024]{2,1,0:T(8,128)(2,1)S(1)} collective-permute-done((bf16[2,64,1024]{2,1,0:T(8,128)(2,1)S(1)}, bf16[2,64,1024]{2,1,0:T(8,128)(2,1)S(1)}, u32[]{:S(2)}, u32[]{:S(2)}) %collective-permute-start.12) | collective-permute-done | bytes 262176 | tf_op jit(solution)/shard_map/ppermute | solution.py:28
  63.7 4.0 %attention.3 = (bf16[2,64,1024]{2,1,0:T(8,128)(2,1)S(1)}, bf16[2,64,1024]{2,1,0:T(8,128)(2,1)S(1)}, bf16[2,128,512]{2,1,0:T(8,128)(2,1)S(1)}, bf16[2,128,512]{2,...) custom-call(s32[6]{0:T(128)S(1)} %pad_add_fusion.meta, ...), custom_call_target="tpu_custom_call" | custom-call | flops 1006632960 | bytes 4194304 | tf_op jit(solution)/shard_map/attention/pallas_call | solution.py:158
  74.2 4.2 %collective-permute-done.13.refs_6_ = bf16[2,128,512]{2,1,0:T(8,128)(2,1)S(1)} collective-permute-done((bf16[2,128,512]{2,1,0:T(8,128)(2,1)S(1)}, bf16[2,128,512]{2,1,0:T(8,128)(2,1)S(1)}, u32[]{:S(2)}, u32[]{:S(2)}) %collective-permute-start.13) | collective-permute-done | bytes 262176 | tf_op jit(solution)/shard_map/ppermute | solution.py:28
  79.7 9.4 %collective-permute-done.15.x2 = bf16[2,64,512]{2,1,0:T(8,128)(2,1)S(1)} collective-permute-done((bf16[2,64,512]{2,1,0:T(8,128)(2,1)S(1)}, bf16[2,64,512]{2,1,0:T(8,128)(2,1)S(1)}, u32[]{:S(2)}, u32[]{:S(2)}) %collective-permute-start.15) | collective-permute-done | bytes 131104 | tf_op jit(solution)/shard_map/ppermute | solution.py:28
  89.0 4.8 %collective-permute-done.16.x3 = bf16[2,64,512]{2,1,0:T(8,128)(2,1)S(1)} collective-permute-done((bf16[2,64,512]{2,1,0:T(8,128)(2,1)S(1)}, bf16[2,64,512]{2,1,0:T(8,128)(2,1)S(1)}, u32[]{:S(2)}, u32[]{:S(2)}) %collective-permute-start.16) | collective-permute-done | bytes 131104 | tf_op jit(solution)/shard_map/ppermute | solution.py:28
  93.9 7.6 %collective-permute-done.14.x1 = bf16[2,64,512]{2,1,0:T(8,128)(2,1)S(1)} collective-permute-done((bf16[2,64,512]{2,1,0:T(8,128)(2,1)S(1)}, bf16[2,64,512]{2,1,0:T(8,128)(2,1)S(1)}, u32[]{:S(2)}, u32[]{:S(2)}) %collective-permute-start.14) | collective-permute-done | bytes 131104 | tf_op jit(solution)/shard_map/ppermute | solution.py:28
  105.4 4.2 %collective-permute-done.21.refs_3_ = bf16[2,64,512]{2,1,0:T(8,128)(2,1)S(1)} collective-permute-done((bf16[2,64,512]{2,1,0:T(8,128)(2,1)S(1)}, bf16[2,64,512]{2,1,0:T(8,128)(2,1)S(1)}, u32[]{:S(2)}, u32[]{:S(2)}) %collective-permute-start.21) | collective-permute-done | bytes 131104 | tf_op jit(solution)/shard_map/ppermute | solution.py:28
  109.6 1.6 %collective-permute-done.20.refs_2_ = bf16[2,64,512]{2,1,0:T(8,128)(2,1)S(1)} collective-permute-done((bf16[2,64,512]{2,1,0:T(8,128)(2,1)S(1)}, bf16[2,64,512]{2,1,0:T(8,128)(2,1)S(1)}, u32[]{:S(2)}, u32[]{:S(2)}) %collective-permute-start.20) | collective-permute-done | bytes 131104 | tf_op jit(solution)/shard_map/ppermute | solution.py:28
  111.4 1.9 %collective-permute-start.22 = (bf16[2,64,1536]{2,1,0:T(8,128)(2,1)S(1)}, bf16[2,64,1536]{2,1,0:T(8,128)(2,1)S(1)}, u32[]{:S(2)}, u32[]{:S(2)}) collective-permute-start(bf16[2,64,1536]{2,1,0:T(8,128)(2,1)S(1)} %get-tuple-element.84), channel_id=1, source_target_pairs={{0,8},{8,0},{16,24},{24,16},{32,40},{40,32},{48,56},{56,48},{64,72... | collective-permute-start | bytes 1179656 | tf_op jit(solution)/shard_map/ppermute | solution.py:28
  115.9 10.9 %collective-permute-done.24.high = bf16[2,64,512]{2,1,0:T(8,128)(2,1)S(1)} collective-permute-done((bf16[2,64,512]{2,1,0:T(8,128)(2,1)S(1)}, bf16[2,64,512]{2,1,0:T(8,128)(2,1)S(1)}, u32[]{:S(2)}, u32[]{:S(2)}) %collective-permute-start.24) | collective-permute-done | bytes 131104 | tf_op jit(solution)/shard_map/ppermute | solution.py:28
  (52 shorter events, 25.4 us)
Async XLA Ops:
  3.2 4.2 %collective-permute-start = (bf16[10,64,512]{2,1,0:T(8,128)(2,1)}, bf16[10,64,512]{2,1,0:T(8,128)(2,1)S(1)}, u32[]{:S(2)}, u32[]{:S(2)}) collective-permute-start(bf16[10,64,512]{2,1,0:T(8,128)(2,1)} %get-tuple-element.46), channel_id=1, source_target_pairs={{0,8},{8,0},{16,24},{24,16},{32,40},{40,32},{48,56},{56,48},{64,72... | collective-permute-start | bytes 1966088 | tf_op jit(solution)/shard_map/ppermute | solution.py:28
  8.5 22.2 %collective-permute-start.3 = (bf16[2,128,512]{2,1,0:T(8,128)(2,1)S(1)}, bf16[2,128,512]{2,1,0:T(8,128)(2,1)S(1)}, u32[]{:S(2)}, u32[]{:S(2)}) collective-permute-start(bf16[2,128,512]{2,1,0:T(8,128)(2,1)S(1)} %pair_keys.1.refs_0_.refs_1_), channel_id=1, source_target_pairs={{0,16},{8,24},{16,32},{24,40},{32,48},{40,56},{48,64},{56,72},{64,... | collective-permute-start | bytes 786440 | tf_op jit(solution)/shard_map/ppermute | solution.py:28
  12.1 9.8 %collective-permute-start.1 = (bf16[2,64,512]{2,1,0:T(8,128)(2,1)S(1)}, bf16[2,64,512]{2,1,0:T(8,128)(2,1)S(1)}, u32[]{:S(2)}, u32[]{:S(2)}) collective-permute-start(bf16[2,64,512]{2,1,0:T(8,128)(2,1)S(1)} %copy-done.6), channel_id=1, source_target_pairs={{0,64},{128,192},{256,320},{384,448},{1,65},{129,193},{257,321},{3... | collective-permute-start | bytes 393224 | tf_op jit(solution)/shard_map/ppermute | solution.py:28
  15.6 6.3 %collective-permute-start.2 = (bf16[2,64,512]{2,1,0:T(8,128)(2,1)S(1)}, bf16[2,64,512]{2,1,0:T(8,128)(2,1)S(1)}, u32[]{:S(2)}, u32[]{:S(2)}) collective-permute-start(bf16[2,64,512]{2,1,0:T(8,128)(2,1)S(1)} %copy-done.5), channel_id=1, source_target_pairs={{0,72},{128,200},{256,328},{384,456},{1,73},{129,201},{257,329},{3... | collective-permute-start | bytes 393224 | tf_op jit(solution)/shard_map/ppermute | solution.py:28
  16.9 23.5 %collective-permute-start.8 = (bf16[2,128,512]{2,1,0:T(8,128)(2,1)S(1)}, bf16[2,128,512]{2,1,0:T(8,128)(2,1)S(1)}, u32[]{:S(2)}, u32[]{:S(2)}) collective-permute-start(bf16[2,128,512]{2,1,0:T(8,128)(2,1)S(1)} %pair_keys.1.refs_0_.refs_1_), channel_id=1, source_target_pairs={{0,48},{8,56},{16,64},{24,72},{32,80},{40,88},{48,96},{56,104},{64... | collective-permute-start | bytes 786440 | tf_op jit(solution)/shard_map/ppermute | solution.py:28
  18.2 22.2 %collective-permute-start.7 = (bf16[2,128,512]{2,1,0:T(8,128)(2,1)S(1)}, bf16[2,128,512]{2,1,0:T(8,128)(2,1)S(1)}, u32[]{:S(2)}, u32[]{:S(2)}) collective-permute-start(bf16[2,128,512]{2,1,0:T(8,128)(2,1)S(1)} %pair_keys.1.refs_0_.refs_1_), channel_id=1, source_target_pairs={{0,32},{8,40},{16,48},{24,56},{32,64},{40,72},{48,80},{56,88},{64,... | collective-permute-start | bytes 786440 | tf_op jit(solution)/shard_map/ppermute | solution.py:28
  22.0 10.1 %collective-permute-start.6 = (bf16[2,64,512]{2,1,0:T(8,128)(2,1)S(1)}, bf16[2,64,512]{2,1,0:T(8,128)(2,1)S(1)}, u32[]{:S(2)}, u32[]{:S(2)}) collective-permute-start(bf16[2,64,512]{2,1,0:T(8,128)(2,1)S(1)} %first_block.1.start), channel_id=1, source_target_pairs={{0,48},{8,56},{64,112},{72,120},{128,176},{136,184},{192,240},{200... | collective-permute-start | bytes 393224 | tf_op jit(solution)/shard_map/ppermute | solution.py:28
  30.8 3.9 %collective-permute-start.4 = (bf16[2,64,512]{2,1,0:T(8,128)(2,1)S(1)}, bf16[2,64,512]{2,1,0:T(8,128)(2,1)S(1)}, u32[]{:S(2)}, u32[]{:S(2)}) collective-permute-start(bf16[2,64,512]{2,1,0:T(8,128)(2,1)S(1)} %first_block.1.start), channel_id=1, source_target_pairs={{0,16},{8,24},{64,80},{72,88},{128,144},{136,152},{192,208},{200,2... | collective-permute-start | bytes 393224 | tf_op jit(solution)/shard_map/ppermute | solution.py:28
  34.7 13.1 %collective-permute-start.11 = (bf16[2,64,512]{2,1,0:T(8,128)(2,1)S(1)}, bf16[2,64,512]{2,1,0:T(8,128)(2,1)S(1)}, u32[]{:S(2)}, u32[]{:S(2)}) collective-permute-start(bf16[2,64,512]{2,1,0:T(8,128)(2,1)S(1)} %choose.1.refs_4_.refs_5_), channel_id=1, source_target_pairs={{0,384},{8,392},{16,400},{24,408},{32,416},{40,424},{48,432},{56,4... | collective-permute-start | bytes 393224 | tf_op jit(solution)/shard_map/ppermute | solution.py:28
  38.1 9.7 %collective-permute-start.10 = (bf16[2,64,512]{2,1,0:T(8,128)(2,1)S(1)}, bf16[2,64,512]{2,1,0:T(8,128)(2,1)S(1)}, u32[]{:S(2)}, u32[]{:S(2)}) collective-permute-start(bf16[2,64,512]{2,1,0:T(8,128)(2,1)S(1)} %choose.1.refs_4_.refs_5_), channel_id=1, source_target_pairs={{0,256},{8,264},{16,272},{24,280},{32,288},{40,296},{48,304},{56,3... | collective-permute-start | bytes 393224 | tf_op jit(solution)/shard_map/ppermute | solution.py:28
  40.4 5.7 %collective-permute-start.9 = (bf16[2,64,512]{2,1,0:T(8,128)(2,1)S(1)}, bf16[2,64,512]{2,1,0:T(8,128)(2,1)S(1)}, u32[]{:S(2)}, u32[]{:S(2)}) collective-permute-start(bf16[2,64,512]{2,1,0:T(8,128)(2,1)S(1)} %choose.1.refs_4_.refs_5_), channel_id=1, source_target_pairs={{0,128},{8,136},{16,144},{24,152},{32,160},{40,168},{48,176},{56,1... | collective-permute-start | bytes 393224 | tf_op jit(solution)/shard_map/ppermute | solution.py:28
  51.7 12.0 %collective-permute-start.12 = (bf16[2,64,1024]{2,1,0:T(8,128)(2,1)S(1)}, bf16[2,64,1024]{2,1,0:T(8,128)(2,1)S(1)}, u32[]{:S(2)}, u32[]{:S(2)}) collective-permute-start(bf16[2,64,1024]{2,1,0:T(8,128)(2,1)S(1)} %get-tuple-element.57.mine0), channel_id=1, source_target_pairs={{1,0},{2,1},{3,2},{4,3},{5,4},{6,5},{7,6},{9,8},{10,9},{11,10},{12... | collective-permute-start | bytes 786440 | tf_op jit(solution)/shard_map/ppermute | solution.py:28
  67.7 10.7 %collective-permute-start.13 = (bf16[2,128,512]{2,1,0:T(8,128)(2,1)S(1)}, bf16[2,128,512]{2,1,0:T(8,128)(2,1)S(1)}, u32[]{:S(2)}, u32[]{:S(2)}) collective-permute-start(bf16[2,128,512]{2,1,0:T(8,128)(2,1)S(1)} %get-tuple-element.67), channel_id=1, source_target_pairs={{16,0},{24,8},{32,16},{40,24},{48,32},{56,40},{64,48},{72,56},{80,... | collective-permute-start | bytes 786440 | tf_op jit(solution)/shard_map/ppermute | solution.py:28
  69.0 35.1 %collective-permute-start.17 = (bf16[2,128,512]{2,1,0:T(8,128)(2,1)S(1)}, bf16[2,128,512]{2,1,0:T(8,128)(2,1)S(1)}, u32[]{:S(2)}, u32[]{:S(2)}) collective-permute-start(bf16[2,128,512]{2,1,0:T(8,128)(2,1)S(1)} %get-tuple-element.74), channel_id=1, source_target_pairs={{32,0},{40,8},{48,16},{56,24},{64,32},{72,40},{80,48},{88,56},{96,... | collective-permute-start | bytes 786440 | tf_op jit(solution)/shard_map/ppermute | solution.py:28
  70.3 33.8 %collective-permute-start.18 = (bf16[2,128,512]{2,1,0:T(8,128)(2,1)S(1)}, bf16[2,128,512]{2,1,0:T(8,128)(2,1)S(1)}, u32[]{:S(2)}, u32[]{:S(2)}) collective-permute-start(bf16[2,128,512]{2,1,0:T(8,128)(2,1)S(1)} %get-tuple-element.75), channel_id=1, source_target_pairs={{48,0},{56,8},{64,16},{72,24},{80,32},{88,40},{96,48},{104,56},{11... | collective-permute-start | bytes 786440 | tf_op jit(solution)/shard_map/ppermute | solution.py:28
  71.6 17.4 %collective-permute-start.15 = (bf16[2,64,512]{2,1,0:T(8,128)(2,1)S(1)}, bf16[2,64,512]{2,1,0:T(8,128)(2,1)S(1)}, u32[]{:S(2)}, u32[]{:S(2)}) collective-permute-start(bf16[2,64,512]{2,1,0:T(8,128)(2,1)S(1)} %get-tuple-element.69), channel_id=1, source_target_pairs={{256,0},{264,8},{272,16},{280,24},{288,32},{296,40},{304,48},{312,... | collective-permute-start | bytes 393224 | tf_op jit(solution)/shard_map/ppermute | solution.py:28
  72.9 20.9 %collective-permute-start.16 = (bf16[2,64,512]{2,1,0:T(8,128)(2,1)S(1)}, bf16[2,64,512]{2,1,0:T(8,128)(2,1)S(1)}, u32[]{:S(2)}, u32[]{:S(2)}) collective-permute-start(bf16[2,64,512]{2,1,0:T(8,128)(2,1)S(1)} %get-tuple-element.70), channel_id=1, source_target_pairs={{384,0},{392,8},{400,16},{408,24},{416,32},{424,40},{432,48},{440,... | collective-permute-start | bytes 393224 | tf_op jit(solution)/shard_map/ppermute | solution.py:28
  78.4 23.0 %collective-permute-start.14 = (bf16[2,64,512]{2,1,0:T(8,128)(2,1)S(1)}, bf16[2,64,512]{2,1,0:T(8,128)(2,1)S(1)}, u32[]{:S(2)}, u32[]{:S(2)}) collective-permute-start(bf16[2,64,512]{2,1,0:T(8,128)(2,1)S(1)} %get-tuple-element.68), channel_id=1, source_target_pairs={{128,0},{136,8},{144,16},{152,24},{160,32},{168,40},{176,48},{184,... | collective-permute-start | bytes 393224 | tf_op jit(solution)/shard_map/ppermute | solution.py:28
  101.5 8.1 %collective-permute-start.21 = (bf16[2,64,512]{2,1,0:T(8,128)(2,1)S(1)}, bf16[2,64,512]{2,1,0:T(8,128)(2,1)S(1)}, u32[]{:S(2)}, u32[]{:S(2)}) collective-permute-start(bf16[2,64,512]{2,1,0:T(8,128)(2,1)S(1)} %get-tuple-element.76), channel_id=1, source_target_pairs={{48,0},{56,8},{112,64},{120,72},{176,128},{184,136},{240,192},{248... | collective-permute-start | bytes 393224 | tf_op jit(solution)/shard_map/ppermute | solution.py:28
  102.8 8.4 %collective-permute-start.20 = (bf16[2,64,512]{2,1,0:T(8,128)(2,1)S(1)}, bf16[2,64,512]{2,1,0:T(8,128)(2,1)S(1)}, u32[]{:S(2)}, u32[]{:S(2)}) collective-permute-start(bf16[2,64,512]{2,1,0:T(8,128)(2,1)S(1)} %get-tuple-element.76), channel_id=1, source_target_pairs={{32,0},{40,8},{96,64},{104,72},{160,128},{168,136},{224,192},{232,... | collective-permute-start | bytes 393224 | tf_op jit(solution)/shard_map/ppermute | solution.py:28
  104.1 7.0 %collective-permute-start.19 = (bf16[2,64,512]{2,1,0:T(8,128)(2,1)S(1)}, bf16[2,64,512]{2,1,0:T(8,128)(2,1)S(1)}, u32[]{:S(2)}, u32[]{:S(2)}) collective-permute-start(bf16[2,64,512]{2,1,0:T(8,128)(2,1)S(1)} %get-tuple-element.76), channel_id=1, source_target_pairs={{16,0},{24,8},{80,64},{88,72},{144,128},{152,136},{208,192},{216,2... | collective-permute-start | bytes 393224 | tf_op jit(solution)/shard_map/ppermute | solution.py:28
  111.4 16.3 %collective-permute-start.22 = (bf16[2,64,1536]{2,1,0:T(8,128)(2,1)S(1)}, bf16[2,64,1536]{2,1,0:T(8,128)(2,1)S(1)}, u32[]{:S(2)}, u32[]{:S(2)}) collective-permute-start(bf16[2,64,1536]{2,1,0:T(8,128)(2,1)S(1)} %get-tuple-element.84), channel_id=1, source_target_pairs={{0,8},{8,0},{16,24},{24,16},{32,40},{40,32},{48,56},{56,48},{64,72... | collective-permute-start | bytes 1179656 | tf_op jit(solution)/shard_map/ppermute | solution.py:28
  113.3 13.5 %collective-permute-start.24 = (bf16[2,64,512]{2,1,0:T(8,128)(2,1)S(1)}, bf16[2,64,512]{2,1,0:T(8,128)(2,1)S(1)}, u32[]{:S(2)}, u32[]{:S(2)}) collective-permute-start(bf16[2,64,512]{2,1,0:T(8,128)(2,1)S(1)} %get-tuple-element.85), channel_id=1, source_target_pairs={{72,0},{200,128},{328,256},{456,384},{73,1},{201,129},{329,257},{4... | collective-permute-start | bytes 393224 | tf_op jit(solution)/shard_map/ppermute | solution.py:28
  114.6 13.0 %collective-permute-start.23 = (bf16[2,64,512]{2,1,0:T(8,128)(2,1)S(1)}, bf16[2,64,512]{2,1,0:T(8,128)(2,1)S(1)}, u32[]{:S(2)}, u32[]{:S(2)}) collective-permute-start(bf16[2,64,512]{2,1,0:T(8,128)(2,1)S(1)} %get-tuple-element.85), channel_id=1, source_target_pairs={{64,0},{192,128},{320,256},{448,384},{65,1},{193,129},{321,257},{4... | collective-permute-start | bytes 393224 | tf_op jit(solution)/shard_map/ppermute | solution.py:28
  (8 other events, 57.2 us)

commit v9 on v3

--- a/solution.py
+++ b/solution.py
@@ -127,6 +127,7 @@
 
 
 WHOLE = pl.BlockSpec(memory_space=pltpu.VMEM)
+FAR = pl.BlockSpec(memory_space=pltpu.HBM)
 SCALAR = pl.BlockSpec(memory_space=pltpu.SMEM)
 WIDE = 2 * HALF_KV
 
@@ -170,14 +171,20 @@
     )(*args)
 
 
-def simple(kernel, out_shape, args, scalars=1):
+def far_scratch(arrays):
+    buffers = [pltpu.VMEM(a.shape, a.dtype) for a in arrays]
+    return buffers + [pltpu.SemaphoreType.DMA((len(arrays),))]
+
+
+def simple(kernel, out_shape, args, scalars=1, far=False):
     size = sum(a.size * a.dtype.itemsize for a in list(args) + list(out_shape))
     return pl.pallas_call(
         kernel,
         out_shape=out_shape,
-        in_specs=[SCALAR] * scalars + [WHOLE] * (len(args) - scalars),
+        in_specs=[SCALAR] * scalars + [FAR if far else WHOLE] * (len(args) - scalars),
         out_specs=[WHOLE] * len(out_shape),
-        compiler_params=pltpu.CompilerParams(vmem_limit_bytes=16 << 20),
+        scratch_shapes=far_scratch(args[scalars:]) if far else [],
+        compiler_params=pltpu.CompilerParams(vmem_limit_bytes=(56 if far else 16) << 20),
         cost_estimate=pl.CostEstimate(flops=size, bytes_accessed=size, transcendentals=0),
         name=kernel.__name__,
     )(*args)
@@ -192,7 +199,17 @@
         send_out[t] = total.astype(jnp.bfloat16)
 
 
-def split_all(meta, keys, values, inputs, first, head, keep, give, kv_keep, kv_give):
+def split_all(meta, *refs):
+    sources, (keep, give, kv_keep, kv_give), buffers, sems = refs[:5], refs[5:9], refs[9:14], refs[14]
+    copies = [
+        pltpu.make_async_copy(source, buffer, sems.at[n])
+        for n, (source, buffer) in enumerate(zip(sources, buffers))
+    ]
+    for copy in copies:
+        copy.start()
+    for copy in copies:
+        copy.wait()
+    keys, values, inputs, first, head = buffers
     swap = meta[0] % 2 == 1
     for source, at in ((keys, 0), (values, HALF_KV)):
         low, high = source[0, :, :, :HALF_KV], source[0, :, :, HALF_KV:]
@@ -281,6 +298,7 @@
         split_all,
         [ten, ten, half, half],
         [spot, saved_keys, saved_values, inputs, first_grads, head_grads],
+        far=True,
     )
     recv = sibling(give)
     up_low = ctx(kv_keep, lambda i: i + 8, lambda i: i % STRIDE == 0)

time: 121 us -> 120 us (level)
  local copies, waits for them, and re-layouts: 4.76 us -> 1.11 us
  Pallas kernels: 9.44 us -> 11.9 us
    unnamed x16 -> x10, local copies, waits for them, and re-layouts: 4.76 us -> 1.11 us
    pallas_call x6, Pallas kernels: 1.44 us -> 3.89 us  [simple(): pl.pallas_call(kernel, out_shape=out_shape, in_specs=[SCALAR] * scalars +...]
where the time goes in v9:
time: 120 us
  starting transfers between devices  65.7 us (55%)
  waiting for transfers between devices  39.8 us (33%)
  Pallas kernels  11.9 us (10%)
    ppermute x25, starting transfers between devices, route(): lax.ppermute(array, axis, [(a, b) for a, b in pairs if b is not None and...  65.7 us
    ppermute x25, waiting for transfers between devices, route(): lax.ppermute(array, axis, [(a, b) for a, b in pairs if b is not None and...  39.8 us
    pallas_call x2, Pallas kernels, attention(): pl.pallas_call(functools.partial(attention_kernel, tick), out_shape=out_s...  8 us
    pallas_call x6, Pallas kernels, simple(): pl.pallas_call(kernel, out_shape=out_shape, in_specs=[SCALAR] * scalars +...  3.89 us
  transfers between devices with their start and end apart: 25, of which 11 were waited for; matrix products, arithmetic and copies ran while one was open for 0% of the time, Pallas kernels for 0%

profile of v9, /device:TPU:224, one launch (start us, length us, event | category | flops | bytes accessed | tf_op | source)
XLA Modules:
  0.0 119.7 jit_solution(15861705398326949794)
XLA Ops:
  0.6 2.6 %split_all.1 = (bf16[10,64,512]{2,1,0:T(8,128)(2,1)}, bf16[10,64,512]{2,1,0:T(8,128)(2,1)}, bf16[2,64,512]{2,1,0:T(8,128)(2,1)}, bf16[2,64,512]{2,1,0:T(8,128)(2,1)}) custom-call(s32[1]{0:T(128)} %bitcast.meta, bf16[1,2,64,512]{3,2,1,0:T(8,128)(2,1)} %refs_0_.1, bf16[1,2,64,512]{3,2,1,0:T(8,128)(2,1)} %refs_1_.1, bf16[1,2,64,2048]{3,2,1,0:T(8,128)(2,1)} %refs_2_.1, ...), custom_call_target="tpu_custom_call" | custom-call | flops 2883588 | bytes 2883588 | tf_op jit(solution)/shard_map/split_all/pallas_call | solution.py:181
  3.2 1.9 %collective-permute-start = (bf16[10,64,512]{2,1,0:T(8,128)(2,1)}, bf16[10,64,512]{2,1,0:T(8,128)(2,1)S(1)}, u32[]{:S(2)}, u32[]{:S(2)}) collective-permute-start(bf16[10,64,512]{2,1,0:T(8,128)(2,1)} %get-tuple-element.39), channel_id=1, source_target_pairs={{0,8},{8,0},{16,24},{24,16},{32,40},{40,32},{48,56},{56,48},{64,72... | collective-permute-start | bytes 1966088 | tf_op jit(solution)/shard_map/ppermute | solution.py:30
  5.1 2.6 %collective-permute-start.1 = (bf16[2,64,512]{2,1,0:T(8,128)(2,1)}, bf16[2,64,512]{2,1,0:T(8,128)(2,1)S(1)}, u32[]{:S(2)}, u32[]{:S(2)}) collective-permute-start(bf16[2,64,512]{2,1,0:T(8,128)(2,1)} %get-tuple-element.40), channel_id=1, source_target_pairs={{0,64},{128,192},{256,320},{384,448},{1,65},{129,193},{257,321},{3... | collective-permute-start | bytes 393224 | tf_op jit(solution)/shard_map/ppermute | solution.py:30
  13.1 2.1 %collective-permute-start.8 = (bf16[2,128,512]{2,1,0:T(8,128)(2,1)S(1)}, bf16[2,128,512]{2,1,0:T(8,128)(2,1)S(1)}, u32[]{:S(2)}, u32[]{:S(2)}) collective-permute-start(bf16[2,128,512]{2,1,0:T(8,128)(2,1)S(1)} %get-tuple-element.42.refs_0_.refs_1_), channel_id=1, source_target_pairs={{0,48},{8,56},{16,64},{24,72},{32,80},{40,88},{48,96},{56,104},{64... | collective-permute-start | bytes 786440 | tf_op jit(solution)/shard_map/ppermute | solution.py:30
  17.8 3.1 %collective-permute-start.5 = (bf16[2,64,512]{2,1,0:T(8,128)(2,1)S(1)}, bf16[2,64,512]{2,1,0:T(8,128)(2,1)S(1)}, u32[]{:S(2)}, u32[]{:S(2)}) collective-permute-start(bf16[2,64,512]{2,1,0:T(8,128)(2,1)S(1)} %get-tuple-element.43.start), channel_id=1, source_target_pairs={{0,16},{8,24},{64,80},{72,88},{128,144},{136,152},{192,208},{200,2... | collective-permute-start | bytes 393224 | tf_op jit(solution)/shard_map/ppermute | solution.py:30
  20.9 1.9 %collective-permute-start.4 = (bf16[2,128,512]{2,1,0:T(8,128)(2,1)S(1)}, bf16[2,128,512]{2,1,0:T(8,128)(2,1)S(1)}, u32[]{:S(2)}, u32[]{:S(2)}) collective-permute-start(bf16[2,128,512]{2,1,0:T(8,128)(2,1)S(1)} %get-tuple-element.42.refs_0_.refs_1_), channel_id=1, source_target_pairs={{0,32},{8,40},{16,48},{24,56},{32,64},{40,72},{48,80},{56,88},{64,... | collective-permute-start | bytes 786440 | tf_op jit(solution)/shard_map/ppermute | solution.py:30
  22.8 1.9 %collective-permute-start.3 = (bf16[2,128,512]{2,1,0:T(8,128)(2,1)S(1)}, bf16[2,128,512]{2,1,0:T(8,128)(2,1)S(1)}, u32[]{:S(2)}, u32[]{:S(2)}) collective-permute-start(bf16[2,128,512]{2,1,0:T(8,128)(2,1)S(1)} %get-tuple-element.42.refs_0_.refs_1_), channel_id=1, source_target_pairs={{0,16},{8,24},{16,32},{24,40},{32,48},{40,56},{48,64},{56,72},{64,... | collective-permute-start | bytes 786440 | tf_op jit(solution)/shard_map/ppermute | solution.py:30
  26.8 3.3 %collective-permute-start.9 = (bf16[2,64,512]{2,1,0:T(8,128)(2,1)S(1)}, bf16[2,64,512]{2,1,0:T(8,128)(2,1)S(1)}, u32[]{:S(2)}, u32[]{:S(2)}) collective-permute-start(bf16[2,64,512]{2,1,0:T(8,128)(2,1)S(1)} %choose.1.refs_4_.refs_5_), channel_id=1, source_target_pairs={{0,128},{8,136},{16,144},{24,152},{32,160},{40,168},{48,176},{56,1... | collective-permute-start | bytes 393224 | tf_op jit(solution)/shard_map/ppermute | solution.py:30
  30.3 7.1 %collective-permute-done.10.refs_6_.refs_7_ = bf16[2,64,512]{2,1,0:T(8,128)(2,1)S(1)} collective-permute-done((bf16[2,64,512]{2,1,0:T(8,128)(2,1)S(1)}, bf16[2,64,512]{2,1,0:T(8,128)(2,1)S(1)}, u32[]{:S(2)}, u32[]{:S(2)}) %collective-permute-start.10) | collective-permute-done | bytes 131104 | tf_op jit(solution)/shard_map/ppermute | solution.py:30
  38.5 3.5 %collective-permute-done.9.refs_5_.refs_6_ = bf16[2,64,512]{2,1,0:T(8,128)(2,1)S(1)} collective-permute-done((bf16[2,64,512]{2,1,0:T(8,128)(2,1)S(1)}, bf16[2,64,512]{2,1,0:T(8,128)(2,1)S(1)}, u32[]{:S(2)}, u32[]{:S(2)}) %collective-permute-start.9) | collective-permute-done | bytes 131104 | tf_op jit(solution)/shard_map/ppermute | solution.py:30
  42.0 4.0 %attention.2 = (bf16[2,64,1024]{2,1,0:T(8,128)(2,1)S(1)}, bf16[64,1024]{1,0:T(8,128)(2,1)S(1)}, bf16[128,512]{1,0:T(8,128)(2,1)S(1)}, bf16[128,512]{1,0:T(8,128)...) custom-call(s32[6]{0:T(128)S(1)} %pad_add_fusion.meta, ...), custom_call_target="tpu_custom_call" | custom-call | flops 1006632960 | bytes 4194304 | tf_op jit(solution)/shard_map/attention/pallas_call | solution.py:160
  46.0 1.9 %collective-permute-start.12 = (bf16[2,64,1024]{2,1,0:T(8,128)(2,1)S(1)}, bf16[2,64,1024]{2,1,0:T(8,128)(2,1)S(1)}, u32[]{:S(2)}, u32[]{:S(2)}) collective-permute-start(bf16[2,64,1024]{2,1,0:T(8,128)(2,1)S(1)} %get-tuple-element.47.mine0), channel_id=1, source_target_pairs={{1,0},{2,1},{3,2},{4,3},{5,4},{6,5},{7,6},{9,8},{10,9},{11,10},{12... | collective-permute-start | bytes 786440 | tf_op jit(solution)/shard_map/ppermute | solution.py:30
  47.9 9.8 %collective-permute-done.12.refs_0_ = bf16[2,64,1024]{2,1,0:T(8,128)(2,1)S(1)} collective-permute-done((bf16[2,64,1024]{2,1,0:T(8,128)(2,1)S(1)}, bf16[2,64,1024]{2,1,0:T(8,128)(2,1)S(1)}, u32[]{:S(2)}, u32[]{:S(2)}) %collective-permute-start.12) | collective-permute-done | bytes 262176 | tf_op jit(solution)/shard_map/ppermute | solution.py:30
  57.8 4.0 %attention.3 = (bf16[2,64,1024]{2,1,0:T(8,128)(2,1)S(1)}, bf16[2,64,1024]{2,1,0:T(8,128)(2,1)S(1)}, bf16[2,128,512]{2,1,0:T(8,128)(2,1)S(1)}, bf16[2,128,512]{2,...) custom-call(s32[6]{0:T(128)S(1)} %pad_add_fusion.meta, ...), custom_call_target="tpu_custom_call" | custom-call | flops 1006632960 | bytes 4194304 | tf_op jit(solution)/shard_map/attention/pallas_call | solution.py:160
  61.8 5.4 %collective-permute-start.16 = (bf16[2,128,512]{2,1,0:T(8,128)(2,1)S(1)}, bf16[2,128,512]{2,1,0:T(8,128)(2,1)S(1)}, u32[]{:S(2)}, u32[]{:S(2)}) collective-permute-start(bf16[2,128,512]{2,1,0:T(8,128)(2,1)S(1)} %get-tuple-element.61), channel_id=1, source_target_pairs={{48,0},{56,8},{64,16},{72,24},{80,32},{88,40},{96,48},{104,56},{11... | collective-permute-start | bytes 786440 | tf_op jit(solution)/shard_map/ppermute | solution.py:30
  67.2 1.9 %collective-permute-start.13 = (bf16[2,64,512]{2,1,0:T(8,128)(2,1)S(1)}, bf16[2,64,512]{2,1,0:T(8,128)(2,1)S(1)}, u32[]{:S(2)}, u32[]{:S(2)}) collective-permute-start(bf16[2,64,512]{2,1,0:T(8,128)(2,1)S(1)} %get-tuple-element.56), channel_id=1, source_target_pairs={{128,0},{136,8},{144,16},{152,24},{160,32},{168,40},{176,48},{184,... | collective-permute-start | bytes 393224 | tf_op jit(solution)/shard_map/ppermute | solution.py:30
  71.1 9.2 %collective-permute-start.20 = (bf16[2,128,512]{2,1,0:T(8,128)(2,1)S(1)}, bf16[2,128,512]{2,1,0:T(8,128)(2,1)S(1)}, u32[]{:S(2)}, u32[]{:S(2)}) collective-permute-start(bf16[2,128,512]{2,1,0:T(8,128)(2,1)S(1)} %get-tuple-element.65), channel_id=1, source_target_pairs={{16,0},{24,8},{32,16},{40,24},{48,32},{56,40},{64,48},{72,56},{80,... | collective-permute-start | bytes 786440 | tf_op jit(solution)/shard_map/ppermute | solution.py:30
  80.3 4.0 %collective-permute-done.13.x1 = bf16[2,64,512]{2,1,0:T(8,128)(2,1)S(1)} collective-permute-done((bf16[2,64,512]{2,1,0:T(8,128)(2,1)S(1)}, bf16[2,64,512]{2,1,0:T(8,128)(2,1)S(1)}, u32[]{:S(2)}, u32[]{:S(2)}) %collective-permute-start.13) | collective-permute-done | bytes 131104 | tf_op jit(solution)/shard_map/ppermute | solution.py:30
  84.3 14.3 %collective-permute-start.21 = (bf16[2,128,512]{2,1,0:T(8,128)(2,1)S(1)}, bf16[2,128,512]{2,1,0:T(8,128)(2,1)S(1)}, u32[]{:S(2)}, u32[]{:S(2)}) collective-permute-start(bf16[2,128,512]{2,1,0:T(8,128)(2,1)S(1)} %get-tuple-element.66), channel_id=1, source_target_pairs={{32,0},{40,8},{48,16},{56,24},{64,32},{72,40},{80,48},{88,56},{96,... | collective-permute-start | bytes 786440 | tf_op jit(solution)/shard_map/ppermute | solution.py:30
  102.7 4.2 %collective-permute-done.19.refs_3_ = bf16[2,64,512]{2,1,0:T(8,128)(2,1)S(1)} collective-permute-done((bf16[2,64,512]{2,1,0:T(8,128)(2,1)S(1)}, bf16[2,64,512]{2,1,0:T(8,128)(2,1)S(1)}, u32[]{:S(2)}, u32[]{:S(2)}) %collective-permute-start.19) | collective-permute-done | bytes 131104 | tf_op jit(solution)/shard_map/ppermute | solution.py:30
  106.9 1.6 %collective-permute-done.18.refs_2_ = bf16[2,64,512]{2,1,0:T(8,128)(2,1)S(1)} collective-permute-done((bf16[2,64,512]{2,1,0:T(8,128)(2,1)S(1)}, bf16[2,64,512]{2,1,0:T(8,128)(2,1)S(1)}, u32[]{:S(2)}, u32[]{:S(2)}) %collective-permute-start.18) | collective-permute-done | bytes 131104 | tf_op jit(solution)/shard_map/ppermute | solution.py:30
  108.7 1.9 %collective-permute-start.22 = (bf16[2,64,1536]{2,1,0:T(8,128)(2,1)S(1)}, bf16[2,64,1536]{2,1,0:T(8,128)(2,1)S(1)}, u32[]{:S(2)}, u32[]{:S(2)}) collective-permute-start(bf16[2,64,1536]{2,1,0:T(8,128)(2,1)S(1)} %get-tuple-element.70), channel_id=1, source_target_pairs={{0,8},{8,0},{16,24},{24,16},{32,40},{40,32},{48,56},{56,48},{64,72... | collective-permute-start | bytes 1179656 | tf_op jit(solution)/shard_map/ppermute | solution.py:30
  113.2 3.7 %collective-permute-done.24.high = bf16[2,64,512]{2,1,0:T(8,128)(2,1)S(1)} collective-permute-done((bf16[2,64,512]{2,1,0:T(8,128)(2,1)S(1)}, bf16[2,64,512]{2,1,0:T(8,128)(2,1)S(1)}, u32[]{:S(2)}, u32[]{:S(2)}) %collective-permute-start.24) | collective-permute-done | bytes 131104 | tf_op jit(solution)/shard_map/ppermute | solution.py:30
  116.9 1.9 %collective-permute-done.23.low = bf16[2,64,512]{2,1,0:T(8,128)(2,1)S(1)} collective-permute-done((bf16[2,64,512]{2,1,0:T(8,128)(2,1)S(1)}, bf16[2,64,512]{2,1,0:T(8,128)(2,1)S(1)}, u32[]{:S(2)}, u32[]{:S(2)}) %collective-permute-start.23) | collective-permute-done | bytes 131104 | tf_op jit(solution)/shard_map/ppermute | solution.py:30
  (47 shorter events, 20.8 us)
Async XLA Ops:
  3.2 8.7 %collective-permute-start = (bf16[10,64,512]{2,1,0:T(8,128)(2,1)}, bf16[10,64,512]{2,1,0:T(8,128)(2,1)S(1)}, u32[]{:S(2)}, u32[]{:S(2)}) collective-permute-start(bf16[10,64,512]{2,1,0:T(8,128)(2,1)} %get-tuple-element.39), channel_id=1, source_target_pairs={{0,8},{8,0},{16,24},{24,16},{32,40},{40,32},{48,56},{56,48},{64,72... | collective-permute-start | bytes 1966088 | tf_op jit(solution)/shard_map/ppermute | solution.py:30
  5.1 5.4 %collective-permute-start.1 = (bf16[2,64,512]{2,1,0:T(8,128)(2,1)}, bf16[2,64,512]{2,1,0:T(8,128)(2,1)S(1)}, u32[]{:S(2)}, u32[]{:S(2)}) collective-permute-start(bf16[2,64,512]{2,1,0:T(8,128)(2,1)} %get-tuple-element.40), channel_id=1, source_target_pairs={{0,64},{128,192},{256,320},{384,448},{1,65},{129,193},{257,321},{3... | collective-permute-start | bytes 393224 | tf_op jit(solution)/shard_map/ppermute | solution.py:30
  13.1 13.7 %collective-permute-start.8 = (bf16[2,128,512]{2,1,0:T(8,128)(2,1)S(1)}, bf16[2,128,512]{2,1,0:T(8,128)(2,1)S(1)}, u32[]{:S(2)}, u32[]{:S(2)}) collective-permute-start(bf16[2,128,512]{2,1,0:T(8,128)(2,1)S(1)} %get-tuple-element.42.refs_0_.refs_1_), channel_id=1, source_target_pairs={{0,48},{8,56},{16,64},{24,72},{32,80},{40,88},{48,96},{56,104},{64... | collective-permute-start | bytes 786440 | tf_op jit(solution)/shard_map/ppermute | solution.py:30
  15.1 7.7 %collective-permute-start.7 = (bf16[2,64,512]{2,1,0:T(8,128)(2,1)S(1)}, bf16[2,64,512]{2,1,0:T(8,128)(2,1)S(1)}, u32[]{:S(2)}, u32[]{:S(2)}) collective-permute-start(bf16[2,64,512]{2,1,0:T(8,128)(2,1)S(1)} %get-tuple-element.43.start), channel_id=1, source_target_pairs={{0,48},{8,56},{64,112},{72,120},{128,176},{136,184},{192,240},{200... | collective-permute-start | bytes 393224 | tf_op jit(solution)/shard_map/ppermute | solution.py:30
  16.4 8.3 %collective-permute-start.6 = (bf16[2,64,512]{2,1,0:T(8,128)(2,1)S(1)}, bf16[2,64,512]{2,1,0:T(8,128)(2,1)S(1)}, u32[]{:S(2)}, u32[]{:S(2)}) collective-permute-start(bf16[2,64,512]{2,1,0:T(8,128)(2,1)S(1)} %get-tuple-element.43.start), channel_id=1, source_target_pairs={{0,32},{8,40},{64,96},{72,104},{128,160},{136,168},{192,224},{200,... | collective-permute-start | bytes 393224 | tf_op jit(solution)/shard_map/ppermute | solution.py:30
  17.8 7.0 %collective-permute-start.5 = (bf16[2,64,512]{2,1,0:T(8,128)(2,1)S(1)}, bf16[2,64,512]{2,1,0:T(8,128)(2,1)S(1)}, u32[]{:S(2)}, u32[]{:S(2)}) collective-permute-start(bf16[2,64,512]{2,1,0:T(8,128)(2,1)S(1)} %get-tuple-element.43.start), channel_id=1, source_target_pairs={{0,16},{8,24},{64,80},{72,88},{128,144},{136,152},{192,208},{200,2... | collective-permute-start | bytes 393224 | tf_op jit(solution)/shard_map/ppermute | solution.py:30
  20.9 16.6 %collective-permute-start.4 = (bf16[2,128,512]{2,1,0:T(8,128)(2,1)S(1)}, bf16[2,128,512]{2,1,0:T(8,128)(2,1)S(1)}, u32[]{:S(2)}, u32[]{:S(2)}) collective-permute-start(bf16[2,128,512]{2,1,0:T(8,128)(2,1)S(1)} %get-tuple-element.42.refs_0_.refs_1_), channel_id=1, source_target_pairs={{0,32},{8,40},{16,48},{24,56},{32,64},{40,72},{48,80},{56,88},{64,... | collective-permute-start | bytes 786440 | tf_op jit(solution)/shard_map/ppermute | solution.py:30
  22.8 15.7 %collective-permute-start.3 = (bf16[2,128,512]{2,1,0:T(8,128)(2,1)S(1)}, bf16[2,128,512]{2,1,0:T(8,128)(2,1)S(1)}, u32[]{:S(2)}, u32[]{:S(2)}) collective-permute-start(bf16[2,128,512]{2,1,0:T(8,128)(2,1)S(1)} %get-tuple-element.42.refs_0_.refs_1_), channel_id=1, source_target_pairs={{0,16},{8,24},{16,32},{24,40},{32,48},{40,56},{48,64},{56,72},{64,... | collective-permute-start | bytes 786440 | tf_op jit(solution)/shard_map/ppermute | solution.py:30
  24.8 5.5 %collective-permute-start.11 = (bf16[2,64,512]{2,1,0:T(8,128)(2,1)S(1)}, bf16[2,64,512]{2,1,0:T(8,128)(2,1)S(1)}, u32[]{:S(2)}, u32[]{:S(2)}) collective-permute-start(bf16[2,64,512]{2,1,0:T(8,128)(2,1)S(1)} %choose.1.refs_4_.refs_5_), channel_id=1, source_target_pairs={{0,384},{8,392},{16,400},{24,408},{32,416},{40,424},{48,432},{56,4... | collective-permute-start | bytes 393224 | tf_op jit(solution)/shard_map/ppermute | solution.py:30
  25.5 12.0 %collective-permute-start.10 = (bf16[2,64,512]{2,1,0:T(8,128)(2,1)S(1)}, bf16[2,64,512]{2,1,0:T(8,128)(2,1)S(1)}, u32[]{:S(2)}, u32[]{:S(2)}) collective-permute-start(bf16[2,64,512]{2,1,0:T(8,128)(2,1)S(1)} %choose.1.refs_4_.refs_5_), channel_id=1, source_target_pairs={{0,256},{8,264},{16,272},{24,280},{32,288},{40,296},{48,304},{56,3... | collective-permute-start | bytes 393224 | tf_op jit(solution)/shard_map/ppermute | solution.py:30
  26.8 15.2 %collective-permute-start.9 = (bf16[2,64,512]{2,1,0:T(8,128)(2,1)S(1)}, bf16[2,64,512]{2,1,0:T(8,128)(2,1)S(1)}, u32[]{:S(2)}, u32[]{:S(2)}) collective-permute-start(bf16[2,64,512]{2,1,0:T(8,128)(2,1)S(1)} %choose.1.refs_4_.refs_5_), channel_id=1, source_target_pairs={{0,128},{8,136},{16,144},{24,152},{32,160},{40,168},{48,176},{56,1... | collective-permute-start | bytes 393224 | tf_op jit(solution)/shard_map/ppermute | solution.py:30
  46.0 11.8 %collective-permute-start.12 = (bf16[2,64,1024]{2,1,0:T(8,128)(2,1)S(1)}, bf16[2,64,1024]{2,1,0:T(8,128)(2,1)S(1)}, u32[]{:S(2)}, u32[]{:S(2)}) collective-permute-start(bf16[2,64,1024]{2,1,0:T(8,128)(2,1)S(1)} %get-tuple-element.47.mine0), channel_id=1, source_target_pairs={{1,0},{2,1},{3,2},{4,3},{5,4},{6,5},{7,6},{9,8},{10,9},{11,10},{12... | collective-permute-start | bytes 786440 | tf_op jit(solution)/shard_map/ppermute | solution.py:30
  61.8 39.6 %collective-permute-start.16 = (bf16[2,128,512]{2,1,0:T(8,128)(2,1)S(1)}, bf16[2,128,512]{2,1,0:T(8,128)(2,1)S(1)}, u32[]{:S(2)}, u32[]{:S(2)}) collective-permute-start(bf16[2,128,512]{2,1,0:T(8,128)(2,1)S(1)} %get-tuple-element.61), channel_id=1, source_target_pairs={{48,0},{56,8},{64,16},{72,24},{80,32},{88,40},{96,48},{104,56},{11... | collective-permute-start | bytes 786440 | tf_op jit(solution)/shard_map/ppermute | solution.py:30
  67.2 17.1 %collective-permute-start.13 = (bf16[2,64,512]{2,1,0:T(8,128)(2,1)S(1)}, bf16[2,64,512]{2,1,0:T(8,128)(2,1)S(1)}, u32[]{:S(2)}, u32[]{:S(2)}) collective-permute-start(bf16[2,64,512]{2,1,0:T(8,128)(2,1)S(1)} %get-tuple-element.56), channel_id=1, source_target_pairs={{128,0},{136,8},{144,16},{152,24},{160,32},{168,40},{176,48},{184,... | collective-permute-start | bytes 393224 | tf_op jit(solution)/shard_map/ppermute | solution.py:30
  69.1 29.6 %collective-permute-start.14 = (bf16[2,64,512]{2,1,0:T(8,128)(2,1)S(1)}, bf16[2,64,512]{2,1,0:T(8,128)(2,1)S(1)}, u32[]{:S(2)}, u32[]{:S(2)}) collective-permute-start(bf16[2,64,512]{2,1,0:T(8,128)(2,1)S(1)} %get-tuple-element.57), channel_id=1, source_target_pairs={{256,0},{264,8},{272,16},{280,24},{288,32},{296,40},{304,48},{312,... | collective-permute-start | bytes 393224 | tf_op jit(solution)/shard_map/ppermute | solution.py:30
  70.4 28.3 %collective-permute-start.15 = (bf16[2,64,512]{2,1,0:T(8,128)(2,1)S(1)}, bf16[2,64,512]{2,1,0:T(8,128)(2,1)S(1)}, u32[]{:S(2)}, u32[]{:S(2)}) collective-permute-start(bf16[2,64,512]{2,1,0:T(8,128)(2,1)S(1)} %get-tuple-element.58), channel_id=1, source_target_pairs={{384,0},{392,8},{400,16},{408,24},{416,32},{424,40},{432,48},{440,... | collective-permute-start | bytes 393224 | tf_op jit(solution)/shard_map/ppermute | solution.py:30
  71.1 37.3 %collective-permute-start.20 = (bf16[2,128,512]{2,1,0:T(8,128)(2,1)S(1)}, bf16[2,128,512]{2,1,0:T(8,128)(2,1)S(1)}, u32[]{:S(2)}, u32[]{:S(2)}) collective-permute-start(bf16[2,128,512]{2,1,0:T(8,128)(2,1)S(1)} %get-tuple-element.65), channel_id=1, source_target_pairs={{16,0},{24,8},{32,16},{40,24},{48,32},{56,40},{64,48},{72,56},{80,... | collective-permute-start | bytes 786440 | tf_op jit(solution)/shard_map/ppermute | solution.py:30
  84.3 24.1 %collective-permute-start.21 = (bf16[2,128,512]{2,1,0:T(8,128)(2,1)S(1)}, bf16[2,128,512]{2,1,0:T(8,128)(2,1)S(1)}, u32[]{:S(2)}, u32[]{:S(2)}) collective-permute-start(bf16[2,128,512]{2,1,0:T(8,128)(2,1)S(1)} %get-tuple-element.66), channel_id=1, source_target_pairs={{32,0},{40,8},{48,16},{56,24},{64,32},{72,40},{80,48},{88,56},{96,... | collective-permute-start | bytes 786440 | tf_op jit(solution)/shard_map/ppermute | solution.py:30
  98.8 8.1 %collective-permute-start.19 = (bf16[2,64,512]{2,1,0:T(8,128)(2,1)S(1)}, bf16[2,64,512]{2,1,0:T(8,128)(2,1)S(1)}, u32[]{:S(2)}, u32[]{:S(2)}) collective-permute-start(bf16[2,64,512]{2,1,0:T(8,128)(2,1)S(1)} %get-tuple-element.62), channel_id=1, source_target_pairs={{48,0},{56,8},{112,64},{120,72},{176,128},{184,136},{240,192},{248... | collective-permute-start | bytes 393224 | tf_op jit(solution)/shard_map/ppermute | solution.py:30
  100.1 8.4 %collective-permute-start.18 = (bf16[2,64,512]{2,1,0:T(8,128)(2,1)S(1)}, bf16[2,64,512]{2,1,0:T(8,128)(2,1)S(1)}, u32[]{:S(2)}, u32[]{:S(2)}) collective-permute-start(bf16[2,64,512]{2,1,0:T(8,128)(2,1)S(1)} %get-tuple-element.62), channel_id=1, source_target_pairs={{32,0},{40,8},{96,64},{104,72},{160,128},{168,136},{224,192},{232,... | collective-permute-start | bytes 393224 | tf_op jit(solution)/shard_map/ppermute | solution.py:30
  101.4 7.1 %collective-permute-start.17 = (bf16[2,64,512]{2,1,0:T(8,128)(2,1)S(1)}, bf16[2,64,512]{2,1,0:T(8,128)(2,1)S(1)}, u32[]{:S(2)}, u32[]{:S(2)}) collective-permute-start(bf16[2,64,512]{2,1,0:T(8,128)(2,1)S(1)} %get-tuple-element.62), channel_id=1, source_target_pairs={{16,0},{24,8},{80,64},{88,72},{144,128},{152,136},{208,192},{216,2... | collective-permute-start | bytes 393224 | tf_op jit(solution)/shard_map/ppermute | solution.py:30
  108.7 10.1 %collective-permute-start.22 = (bf16[2,64,1536]{2,1,0:T(8,128)(2,1)S(1)}, bf16[2,64,1536]{2,1,0:T(8,128)(2,1)S(1)}, u32[]{:S(2)}, u32[]{:S(2)}) collective-permute-start(bf16[2,64,1536]{2,1,0:T(8,128)(2,1)S(1)} %get-tuple-element.70), channel_id=1, source_target_pairs={{0,8},{8,0},{16,24},{24,16},{32,40},{40,32},{48,56},{56,48},{64,72... | collective-permute-start | bytes 1179656 | tf_op jit(solution)/shard_map/ppermute | solution.py:30
  110.6 6.3 %collective-permute-start.24 = (bf16[2,64,512]{2,1,0:T(8,128)(2,1)S(1)}, bf16[2,64,512]{2,1,0:T(8,128)(2,1)S(1)}, u32[]{:S(2)}, u32[]{:S(2)}) collective-permute-start(bf16[2,64,512]{2,1,0:T(8,128)(2,1)S(1)} %get-tuple-element.71), channel_id=1, source_target_pairs={{72,0},{200,128},{328,256},{456,384},{73,1},{201,129},{329,257},{4... | collective-permute-start | bytes 393224 | tf_op jit(solution)/shard_map/ppermute | solution.py:30
  111.9 6.9 %collective-permute-start.23 = (bf16[2,64,512]{2,1,0:T(8,128)(2,1)S(1)}, bf16[2,64,512]{2,1,0:T(8,128)(2,1)S(1)}, u32[]{:S(2)}, u32[]{:S(2)}) collective-permute-start(bf16[2,64,512]{2,1,0:T(8,128)(2,1)S(1)} %get-tuple-element.71), channel_id=1, source_target_pairs={{64,0},{192,128},{320,256},{448,384},{65,1},{193,129},{321,257},{4... | collective-permute-start | bytes 393224 | tf_op jit(solution)/shard_map/ppermute | solution.py:30
  (6 other events, 52.9 us)

commit v10 on v2

--- a/solution.py
+++ b/solution.py
@@ -223,8 +223,8 @@
 
 
 def row_sum(meta, *refs):
-    total, x1, x2, x3, own0, own1, back1, back2, back3 = refs[:9]
-    mine_out, other_out, strided_out = refs[9:]
+    total, x1, x2, x3, own0, own1, back1, back2, back3, far_rows = refs[:10]
+    mine_out, swap_out, strided_out = refs[10:]
     index = meta[0]
     owner = (index // 2) % 4 == 0
     even = (index // 8) % 2 == 0
@@ -239,26 +239,23 @@
         for back in (back1, back2, back3):
             near = near + back[t].astype(jnp.float32)
         mine_out[t] = near[:BLK] + first * strided
-        other_out[t] = (near[BLK:] + second * strided).astype(jnp.bfloat16)
-
-
-def finish(meta, mine, other, low, high, keys_out, values_out):
+        swap_out[t, :, :HALF_FEAT] = far_rows[t]
+        swap_out[t, :, HALF_FEAT:] = (near[BLK:] + second * strided).astype(jnp.bfloat16)
+
+
+def finish(meta, mine, swapped, low, high, mine0, mine1, rows_out, keys_out, values_out):
     swap = meta[0] % 2 == 1
-    for t in range(2):
+    for t, rows in enumerate((mine0, mine1)):
+        other = swapped[t, :, HALF_FEAT:].astype(jnp.float32)
         own = (mine[t] + low[t].astype(jnp.float32)).astype(jnp.bfloat16)
-        far = (other[t].astype(jnp.float32) + high[t].astype(jnp.float32)).astype(jnp.bfloat16)
+        far = (other + high[t].astype(jnp.float32)).astype(jnp.bfloat16)
         left, right = jnp.where(swap, far, own), jnp.where(swap, own, far)
         for out, at in ((keys_out, 0), (values_out, HALF_KV)):
             out[0, t, :, :HALF_KV] = left[:, at : at + HALF_KV]
             out[0, t, :, HALF_KV:] = right[:, at : at + HALF_KV]
-
-
-def join_rows(meta, mine0, mine1, other, out):
-    swap = meta[0] % 2 == 1
-    for t, mine in enumerate((mine0, mine1)):
-        near, far = mine[0], other[t]
-        out[0, t, :, :HALF_FEAT] = jnp.where(swap, far, near)
-        out[0, t, :, HALF_FEAT:] = jnp.where(swap, near, far)
+        near, far = rows[0], swapped[t, :, :HALF_FEAT]
+        rows_out[0, t, :, :HALF_FEAT] = jnp.where(swap, far, near)
+        rows_out[0, t, :, HALF_FEAT:] = jnp.where(swap, near, far)
 
 
 def body(inputs, saved_keys, saved_values, query_gain, first_grads, head_grads, window, stride):
@@ -307,21 +304,23 @@
         columns.append(outs[6])
         columns += [ctx(outs[6 + s], lambda i: i - STRIDE * s) for s in range(1, 4)]
     backs = [ctx(second[1 + d], lambda i: i - 2 * d) for d in range(1, 4)]
-    other_rows = sibling(second[1])
 
     wide = shape((2, BLK, WIDE), f32)
     total, send = simple(column_sum, [wide, half], columns, 0)
     rows = [ctx(send, lambda i: i - 2 * d, lambda i: (i // 2) % 4 == d) for d in range(1, 4)]
-    mine, other, down = simple(
-        row_sum, [wide, half, half], [spot, total] + rows + [first[5], second[5]] + backs
+    mine, swap, down = simple(
+        row_sum,
+        [wide, shape((2, BLK, HALF_FEAT + WIDE), bf16), half],
+        [spot, total] + rows + [first[5], second[5]] + backs + [second[1]],
     )
-    other = sibling(other)
+    swapped = sibling(swap)
     low = ctx(down, lambda i: i - 8, lambda i: i % STRIDE == 8)
     high = ctx(down, lambda i: i - 9, lambda i: i % STRIDE == 9)
     keys_shape = shape(saved_keys.shape, bf16)
-    key_grads, value_grads = simple(finish, [keys_shape, keys_shape], [spot, mine, other, low, high])
-    (grads_out,) = simple(
-        join_rows, [shape(inputs.shape, bf16)], [spot, first[0], second[0], other_rows]
+    grads_out, key_grads, value_grads = simple(
+        finish,
+        [shape(inputs.shape, bf16), keys_shape, keys_shape],
+        [spot, mine, swapped, low, high, first[0], second[0]],
     )
     return grads_out, key_grads, value_grads
 

time: 119 us -> 118 us (level)
  starting transfers between devices: 56.5 us -> 54.1 us
  waiting for transfers between devices: 47.8 us -> 49.9 us
    ppermute x30 -> x29, starting transfers between devices: 56.5 us -> 54.1 us  [route(): lax.ppermute(array, axis, [(a, b) for a, b in pairs if b is not None and...]
    ppermute x30 -> x29, waiting for transfers between devices: 47.8 us -> 49.9 us  [route(): lax.ppermute(array, axis, [(a, b) for a, b in pairs if b is not None and...]
  transfers between devices with their start and end apart: 30 -> 29, of which waited for: 17 -> 18; matrix products, arithmetic and copies ran while one was open for 0% -> 0% of each run, Pallas kernels for 4% -> 4%
where the time goes in v10:
time: 118 us; the launch traced here: 117 us
  starting transfers between devices  54.1 us (46%)
  waiting for transfers between devices  49.9 us (42%)
  Pallas kernels  9.37 us (8%)
  local copies, waits for them, and re-layouts  2.83 us (2%)
    ppermute x29, starting transfers between devices, route(): lax.ppermute(array, axis, [(a, b) for a, b in pairs if b is not None and...  54.1 us
    ppermute x29, waiting for transfers between devices, route(): lax.ppermute(array, axis, [(a, b) for a, b in pairs if b is not None and...  49.9 us
    pallas_call x2, Pallas kernels, attention(): pl.pallas_call(functools.partial(attention_kernel, grads is not None), ou...  8 us
    unnamed x16, local copies, waits for them, and re-layouts  2.83 us
  transfers between devices with their start and end apart: 29, of which 18 were waited for; matrix products, arithmetic and copies ran while one was open for 0% of the time, Pallas kernels for 4%

profile of v10, /device:TPU:192, one launch (start us, length us, event | category | flops | bytes accessed | tf_op | source)
XLA Modules:
  0.0 117.4 jit_solution(12813333287627412466)
XLA Ops:
  2.5 3.5 %collective-permute-start.2 = (bf16[2,64,512]{2,1,0:T(8,128)(2,1)S(1)}, bf16[2,64,512]{2,1,0:T(8,128)(2,1)S(1)}, u32[]{:S(2)}, u32[]{:S(2)}) collective-permute-start(bf16[2,64,512]{2,1,0:T(8,128)(2,1)S(1)} %get-tuple-element.36.keep), channel_id=1, source_target_pairs={{0,64},{128,192},{256,320},{384,448},{1,65},{129,193},{257,321},{3... | collective-permute-start | bytes 393224 | tf_op jit(solution)/shard_map/ppermute | solution.py:28
  6.0 1.4 %collective-permute-start.3 = (bf16[2,64,512]{2,1,0:T(8,128)(2,1)S(1)}, bf16[2,64,512]{2,1,0:T(8,128)(2,1)S(1)}, u32[]{:S(2)}, u32[]{:S(2)}) collective-permute-start(bf16[2,64,512]{2,1,0:T(8,128)(2,1)S(1)} %get-tuple-element.37), channel_id=1, source_target_pairs={{0,72},{128,200},{256,328},{384,456},{1,73},{129,201},{257,329},{3... | collective-permute-start | bytes 393224 | tf_op jit(solution)/shard_map/ppermute | solution.py:28
  7.5 1.9 %collective-permute-start.1 = (bf16[2,64,512]{2,1,0:T(8,128)(2,1)S(1)}, bf16[2,64,512]{2,1,0:T(8,128)(2,1)S(1)}, u32[]{:S(2)}, u32[]{:S(2)}) collective-permute-start(bf16[2,64,512]{2,1,0:T(8,128)(2,1)S(1)} %get-tuple-element.37), channel_id=1, source_target_pairs={{0,8},{8,0},{16,24},{24,16},{32,40},{40,32},{48,56},{56,48},{64,72... | collective-permute-start | bytes 393224 | tf_op jit(solution)/shard_map/ppermute | solution.py:28
  15.7 2.1 %collective-permute-start = (bf16[4,64,1024]{2,1,0:T(8,128)(2,1)S(1)}, bf16[4,64,1024]{2,1,0:T(8,128)(2,1)S(1)}, u32[]{:S(2)}, u32[]{:S(2)}) collective-permute-start(bf16[4,64,1024]{2,1,0:T(8,128)(2,1)S(1)} %get-tuple-element.35), channel_id=1, source_target_pairs={{0,8},{8,0},{16,24},{24,16},{32,40},{40,32},{48,56},{56,48},{64,72... | collective-permute-start | bytes 1572872 | tf_op jit(solution)/shard_map/ppermute | solution.py:28
  18.2 5.3 %collective-permute-start.12 = (bf16[2,64,512]{2,1,0:T(8,128)(2,1)S(1)}, bf16[2,64,512]{2,1,0:T(8,128)(2,1)S(1)}, u32[]{:S(2)}, u32[]{:S(2)}) collective-permute-start(bf16[2,64,512]{2,1,0:T(8,128)(2,1)S(1)} %select_select_fusion.refs_10_.refs_12_), channel_id=1, source_target_pairs={{0,384},{8,392},{16,400},{24,408},{32,416},{40,424},{48,432},{56,4... | collective-permute-start | bytes 393224 | tf_op jit(solution)/shard_map/ppermute | solution.py:28
  23.5 2.2 %collective-permute-start.11 = (bf16[2,64,512]{2,1,0:T(8,128)(2,1)S(1)}, bf16[2,64,512]{2,1,0:T(8,128)(2,1)S(1)}, u32[]{:S(2)}, u32[]{:S(2)}) collective-permute-start(bf16[2,64,512]{2,1,0:T(8,128)(2,1)S(1)} %select_select_fusion.refs_10_.refs_12_), channel_id=1, source_target_pairs={{0,256},{8,264},{16,272},{24,280},{32,288},{40,296},{48,304},{56,3... | collective-permute-start | bytes 393224 | tf_op jit(solution)/shard_map/ppermute | solution.py:28
  25.8 5.6 %collective-permute-start.6 = (bf16[2,128,512]{2,1,0:T(8,128)(2,1)S(1)}, bf16[2,128,512]{2,1,0:T(8,128)(2,1)S(1)}, u32[]{:S(2)}, u32[]{:S(2)}) collective-permute-start(bf16[2,128,512]{2,1,0:T(8,128)(2,1)S(1)} %get-tuple-element.38.refs_6_.refs_8_), channel_id=1, source_target_pairs={{0,48},{8,56},{16,64},{24,72},{32,80},{40,88},{48,96},{56,104},{64... | collective-permute-start | bytes 786440 | tf_op jit(solution)/shard_map/ppermute | solution.py:28
  31.4 1.6 %collective-permute-start.5 = (bf16[2,128,512]{2,1,0:T(8,128)(2,1)S(1)}, bf16[2,128,512]{2,1,0:T(8,128)(2,1)S(1)}, u32[]{:S(2)}, u32[]{:S(2)}) collective-permute-start(bf16[2,128,512]{2,1,0:T(8,128)(2,1)S(1)} %get-tuple-element.38.refs_6_.refs_8_), channel_id=1, source_target_pairs={{0,32},{8,40},{16,48},{24,56},{32,64},{40,72},{48,80},{56,88},{64,... | collective-permute-start | bytes 786440 | tf_op jit(solution)/shard_map/ppermute | solution.py:28
  33.0 2.3 %collective-permute-done.12.refs_13_.refs_15_ = bf16[2,64,512]{2,1,0:T(8,128)(2,1)S(1)} collective-permute-done((bf16[2,64,512]{2,1,0:T(8,128)(2,1)S(1)}, bf16[2,64,512]{2,1,0:T(8,128)(2,1)S(1)}, u32[]{:S(2)}, u32[]{:S(2)}) %collective-permute-start.12) | collective-permute-done | bytes 131104 | tf_op jit(solution)/shard_map/ppermute | solution.py:28
  36.7 3.3 %collective-permute-start.10 = (bf16[2,64,512]{2,1,0:T(8,128)(2,1)S(1)}, bf16[2,64,512]{2,1,0:T(8,128)(2,1)S(1)}, u32[]{:S(2)}, u32[]{:S(2)}) collective-permute-start(bf16[2,64,512]{2,1,0:T(8,128)(2,1)S(1)} %select_select_fusion.refs_10_.refs_12_), channel_id=1, source_target_pairs={{0,128},{8,136},{16,144},{24,152},{32,160},{40,168},{48,176},{56,1... | collective-permute-start | bytes 393224 | tf_op jit(solution)/shard_map/ppermute | solution.py:28
  40.2 2.3 %collective-permute-done.10.refs_11_.refs_13_ = bf16[2,64,512]{2,1,0:T(8,128)(2,1)S(1)} collective-permute-done((bf16[2,64,512]{2,1,0:T(8,128)(2,1)S(1)}, bf16[2,64,512]{2,1,0:T(8,128)(2,1)S(1)}, u32[]{:S(2)}, u32[]{:S(2)}) %collective-permute-start.10) | collective-permute-done | bytes 131104 | tf_op jit(solution)/shard_map/ppermute | solution.py:28
  43.7 4.0 %attention.2 = (bf16[2,64,1024]{2,1,0:T(8,128)(2,1)S(1)}, bf16[64,1024]{1,0:T(8,128)(2,1)S(1)}, bf16[128,512]{1,0:T(8,128)(2,1)S(1)}, bf16[128,512]{1,0:T(8,128)...) custom-call(s32[6]{0:T(128)S(1)} %pad_add_fusion.refs_0_, ...), custom_call_target="tpu_custom_call" | custom-call | flops 1006632960 | bytes 4194304 | tf_op jit(solution)/shard_map/attention/pallas_call | solution.py:162
  47.7 1.9 %collective-permute-start.16 = (bf16[2,64,1024]{2,1,0:T(8,128)(2,1)S(1)}, bf16[2,64,1024]{2,1,0:T(8,128)(2,1)S(1)}, u32[]{:S(2)}, u32[]{:S(2)}) collective-permute-start(bf16[2,64,1024]{2,1,0:T(8,128)(2,1)S(1)} %get-tuple-element.44.mine0), channel_id=1, source_target_pairs={{1,0},{2,1},{3,2},{4,3},{5,4},{6,5},{7,6},{9,8},{10,9},{11,10},{12... | collective-permute-start | bytes 786440 | tf_op jit(solution)/shard_map/ppermute | solution.py:28
  53.5 5.1 %collective-permute-done.16.refs_4_.refs_5_ = bf16[2,64,1024]{2,1,0:T(8,128)(2,1)S(1)} collective-permute-done((bf16[2,64,1024]{2,1,0:T(8,128)(2,1)S(1)}, bf16[2,64,1024]{2,1,0:T(8,128)(2,1)S(1)}, u32[]{:S(2)}, u32[]{:S(2)}) %collective-permute-start.16) | collective-permute-done | bytes 262176 | tf_op jit(solution)/shard_map/ppermute | solution.py:28
  58.6 4.0 %attention.3 = (bf16[2,64,1024]{2,1,0:T(8,128)(2,1)S(1)}, bf16[2,64,1024]{2,1,0:T(8,128)(2,1)S(1)}, bf16[2,128,512]{2,1,0:T(8,128)(2,1)S(1)}, bf16[2,128,512]{2,...) custom-call(s32[6]{0:T(128)S(1)} %pad_add_fusion.refs_0_, ...), custom_call_target="tpu_custom_call" | custom-call | flops 1006632960 | bytes 4194304 | tf_op jit(solution)/shard_map/attention/pallas_call | solution.py:162
  67.6 3.6 %collective-permute-done.14.refs_2_ = bf16[64,512]{1,0:T(8,128)(2,1)S(1)} collective-permute-done((bf16[64,512]{1,0:T(8,128)(2,1)S(1)}, bf16[64,512]{1,0:T(8,128)(2,1)S(1)}, u32[]{:S(2)}, u32[]{:S(2)}) %collective-permute-start.14) | collective-permute-done | bytes 65568 | tf_op jit(solution)/shard_map/ppermute | solution.py:28
  73.1 5.2 %collective-permute-done.17.refs_5_ = bf16[64,512]{1,0:T(8,128)(2,1)S(1)} collective-permute-done((bf16[64,512]{1,0:T(8,128)(2,1)S(1)}, bf16[64,512]{1,0:T(8,128)(2,1)S(1)}, u32[]{:S(2)}, u32[]{:S(2)}) %collective-permute-start.17) | collective-permute-done | bytes 65568 | tf_op jit(solution)/shard_map/ppermute | solution.py:28
  78.3 4.9 %collective-permute-done.18.refs_6_ = bf16[64,512]{1,0:T(8,128)(2,1)S(1)} collective-permute-done((bf16[64,512]{1,0:T(8,128)(2,1)S(1)}, bf16[64,512]{1,0:T(8,128)(2,1)S(1)}, u32[]{:S(2)}, u32[]{:S(2)}) %collective-permute-start.18) | collective-permute-done | bytes 65568 | tf_op jit(solution)/shard_map/ppermute | solution.py:28
  83.2 1.9 %collective-permute-done.19.refs_7_ = bf16[64,512]{1,0:T(8,128)(2,1)S(1)} collective-permute-done((bf16[64,512]{1,0:T(8,128)(2,1)S(1)}, bf16[64,512]{1,0:T(8,128)(2,1)S(1)}, u32[]{:S(2)}, u32[]{:S(2)}) %collective-permute-start.19) | collective-permute-done | bytes 65568 | tf_op jit(solution)/shard_map/ppermute | solution.py:28
  90.3 7.5 %collective-permute-done.22.refs_3_ = bf16[2,64,512]{2,1,0:T(8,128)(2,1)S(1)} collective-permute-done((bf16[2,64,512]{2,1,0:T(8,128)(2,1)S(1)}, bf16[2,64,512]{2,1,0:T(8,128)(2,1)S(1)}, u32[]{:S(2)}, u32[]{:S(2)}) %collective-permute-start.22) | collective-permute-done | bytes 131104 | tf_op jit(solution)/shard_map/ppermute | solution.py:28
  99.1 5.8 %collective-permute-done.21.refs_2_ = bf16[2,64,512]{2,1,0:T(8,128)(2,1)S(1)} collective-permute-done((bf16[2,64,512]{2,1,0:T(8,128)(2,1)S(1)}, bf16[2,64,512]{2,1,0:T(8,128)(2,1)S(1)}, u32[]{:S(2)}, u32[]{:S(2)}) %collective-permute-start.21) | collective-permute-done | bytes 131104 | tf_op jit(solution)/shard_map/ppermute | solution.py:28
  106.4 1.9 %collective-permute-start.26 = (bf16[2,64,1536]{2,1,0:T(8,128)(2,1)S(1)}, bf16[2,64,1536]{2,1,0:T(8,128)(2,1)S(1)}, u32[]{:S(2)}, u32[]{:S(2)}) collective-permute-start(bf16[2,64,1536]{2,1,0:T(8,128)(2,1)S(1)} %get-tuple-element.62), channel_id=1, source_target_pairs={{0,8},{8,0},{16,24},{24,16},{32,40},{40,32},{48,56},{56,48},{64,72... | collective-permute-start | bytes 1179656 | tf_op jit(solution)/shard_map/ppermute | solution.py:28
  110.9 3.7 %collective-permute-done.28.high = bf16[2,64,512]{2,1,0:T(8,128)(2,1)S(1)} collective-permute-done((bf16[2,64,512]{2,1,0:T(8,128)(2,1)S(1)}, bf16[2,64,512]{2,1,0:T(8,128)(2,1)S(1)}, u32[]{:S(2)}, u32[]{:S(2)}) %collective-permute-start.28) | collective-permute-done | bytes 131104 | tf_op jit(solution)/shard_map/ppermute | solution.py:28
  114.6 1.9 %collective-permute-done.27.low = bf16[2,64,512]{2,1,0:T(8,128)(2,1)S(1)} collective-permute-done((bf16[2,64,512]{2,1,0:T(8,128)(2,1)S(1)}, bf16[2,64,512]{2,1,0:T(8,128)(2,1)S(1)}, u32[]{:S(2)}, u32[]{:S(2)}) %collective-permute-start.27) | collective-permute-done | bytes 131104 | tf_op jit(solution)/shard_map/ppermute | solution.py:28
  (62 shorter events, 33.4 us)
Async XLA Ops:
  2.5 6.9 %collective-permute-start.2 = (bf16[2,64,512]{2,1,0:T(8,128)(2,1)S(1)}, bf16[2,64,512]{2,1,0:T(8,128)(2,1)S(1)}, u32[]{:S(2)}, u32[]{:S(2)}) collective-permute-start(bf16[2,64,512]{2,1,0:T(8,128)(2,1)S(1)} %get-tuple-element.36.keep), channel_id=1, source_target_pairs={{0,64},{128,192},{256,320},{384,448},{1,65},{129,193},{257,321},{3... | collective-permute-start | bytes 393224 | tf_op jit(solution)/shard_map/ppermute | solution.py:28
  10.8 7.1 %collective-permute-start.9 = (bf16[2,64,512]{2,1,0:T(8,128)(2,1)S(1)}, bf16[2,64,512]{2,1,0:T(8,128)(2,1)S(1)}, u32[]{:S(2)}, u32[]{:S(2)}) collective-permute-start(bf16[2,64,512]{2,1,0:T(8,128)(2,1)S(1)} %get-tuple-element.39), channel_id=1, source_target_pairs={{0,16},{8,24},{64,80},{72,88},{128,144},{136,152},{192,208},{200,2... | collective-permute-start | bytes 393224 | tf_op jit(solution)/shard_map/ppermute | solution.py:28
  15.7 28.0 %collective-permute-start = (bf16[4,64,1024]{2,1,0:T(8,128)(2,1)S(1)}, bf16[4,64,1024]{2,1,0:T(8,128)(2,1)S(1)}, u32[]{:S(2)}, u32[]{:S(2)}) collective-permute-start(bf16[4,64,1024]{2,1,0:T(8,128)(2,1)S(1)} %get-tuple-element.35), channel_id=1, source_target_pairs={{0,8},{8,0},{16,24},{24,16},{32,40},{40,32},{48,56},{56,48},{64,72... | collective-permute-start | bytes 1572872 | tf_op jit(solution)/shard_map/ppermute | solution.py:28
  18.2 17.1 %collective-permute-start.12 = (bf16[2,64,512]{2,1,0:T(8,128)(2,1)S(1)}, bf16[2,64,512]{2,1,0:T(8,128)(2,1)S(1)}, u32[]{:S(2)}, u32[]{:S(2)}) collective-permute-start(bf16[2,64,512]{2,1,0:T(8,128)(2,1)S(1)} %select_select_fusion.refs_10_.refs_12_), channel_id=1, source_target_pairs={{0,384},{8,392},{16,400},{24,408},{32,416},{40,424},{48,432},{56,4... | collective-permute-start | bytes 393224 | tf_op jit(solution)/shard_map/ppermute | solution.py:28
  23.5 13.2 %collective-permute-start.11 = (bf16[2,64,512]{2,1,0:T(8,128)(2,1)S(1)}, bf16[2,64,512]{2,1,0:T(8,128)(2,1)S(1)}, u32[]{:S(2)}, u32[]{:S(2)}) collective-permute-start(bf16[2,64,512]{2,1,0:T(8,128)(2,1)S(1)} %select_select_fusion.refs_10_.refs_12_), channel_id=1, source_target_pairs={{0,256},{8,264},{16,272},{24,280},{32,288},{40,296},{48,304},{56,3... | collective-permute-start | bytes 393224 | tf_op jit(solution)/shard_map/ppermute | solution.py:28
  25.8 16.7 %collective-permute-start.6 = (bf16[2,128,512]{2,1,0:T(8,128)(2,1)S(1)}, bf16[2,128,512]{2,1,0:T(8,128)(2,1)S(1)}, u32[]{:S(2)}, u32[]{:S(2)}) collective-permute-start(bf16[2,128,512]{2,1,0:T(8,128)(2,1)S(1)} %get-tuple-element.38.refs_6_.refs_8_), channel_id=1, source_target_pairs={{0,48},{8,56},{16,64},{24,72},{32,80},{40,88},{48,96},{56,104},{64... | collective-permute-start | bytes 786440 | tf_op jit(solution)/shard_map/ppermute | solution.py:28
  31.4 11.1 %collective-permute-start.5 = (bf16[2,128,512]{2,1,0:T(8,128)(2,1)S(1)}, bf16[2,128,512]{2,1,0:T(8,128)(2,1)S(1)}, u32[]{:S(2)}, u32[]{:S(2)}) collective-permute-start(bf16[2,128,512]{2,1,0:T(8,128)(2,1)S(1)} %get-tuple-element.38.refs_6_.refs_8_), channel_id=1, source_target_pairs={{0,32},{8,40},{16,48},{24,56},{32,64},{40,72},{48,80},{56,88},{64,... | collective-permute-start | bytes 786440 | tf_op jit(solution)/shard_map/ppermute | solution.py:28
  35.3 8.4 %collective-permute-start.4 = (bf16[2,128,512]{2,1,0:T(8,128)(2,1)S(1)}, bf16[2,128,512]{2,1,0:T(8,128)(2,1)S(1)}, u32[]{:S(2)}, u32[]{:S(2)}) collective-permute-start(bf16[2,128,512]{2,1,0:T(8,128)(2,1)S(1)} %get-tuple-element.38.refs_6_.refs_8_), channel_id=1, source_target_pairs={{0,16},{8,24},{16,32},{24,40},{32,48},{40,56},{48,64},{56,72},{64,... | collective-permute-start | bytes 786440 | tf_op jit(solution)/shard_map/ppermute | solution.py:28
  47.7 10.9 %collective-permute-start.16 = (bf16[2,64,1024]{2,1,0:T(8,128)(2,1)S(1)}, bf16[2,64,1024]{2,1,0:T(8,128)(2,1)S(1)}, u32[]{:S(2)}, u32[]{:S(2)}) collective-permute-start(bf16[2,64,1024]{2,1,0:T(8,128)(2,1)S(1)} %get-tuple-element.44.mine0), channel_id=1, source_target_pairs={{1,0},{2,1},{3,2},{4,3},{5,4},{6,5},{7,6},{9,8},{10,9},{11,10},{12... | collective-permute-start | bytes 786440 | tf_op jit(solution)/shard_map/ppermute | solution.py:28
  49.6 16.7 %collective-permute-start.13 = (bf16[64,512]{1,0:T(8,128)(2,1)S(1)}, bf16[64,512]{1,0:T(8,128)(2,1)S(1)}, u32[]{:S(2)}, u32[]{:S(2)}) collective-permute-start(bf16[64,512]{1,0:T(8,128)(2,1)S(1)} %get-tuple-element.41), channel_id=1, source_target_pairs={{128,0},{136,8},{144,16},{152,24},{160,32},{168,40},{176,48},{184,... | collective-permute-start | bytes 196616 | tf_op jit(solution)/shard_map/ppermute | solution.py:28
  50.9 20.2 %collective-permute-start.14 = (bf16[64,512]{1,0:T(8,128)(2,1)S(1)}, bf16[64,512]{1,0:T(8,128)(2,1)S(1)}, u32[]{:S(2)}, u32[]{:S(2)}) collective-permute-start(bf16[64,512]{1,0:T(8,128)(2,1)S(1)} %get-tuple-element.42), channel_id=1, source_target_pairs={{256,0},{264,8},{272,16},{280,24},{288,32},{296,40},{304,48},{312,... | collective-permute-start | bytes 196616 | tf_op jit(solution)/shard_map/ppermute | solution.py:28
  52.2 20.9 %collective-permute-start.15 = (bf16[64,512]{1,0:T(8,128)(2,1)S(1)}, bf16[64,512]{1,0:T(8,128)(2,1)S(1)}, u32[]{:S(2)}, u32[]{:S(2)}) collective-permute-start(bf16[64,512]{1,0:T(8,128)(2,1)S(1)} %get-tuple-element.43), channel_id=1, source_target_pairs={{384,0},{392,8},{400,16},{408,24},{416,32},{424,40},{432,48},{440,... | collective-permute-start | bytes 196616 | tf_op jit(solution)/shard_map/ppermute | solution.py:28
  62.7 15.6 %collective-permute-start.17 = (bf16[64,512]{1,0:T(8,128)(2,1)S(1)}, bf16[64,512]{1,0:T(8,128)(2,1)S(1)}, u32[]{:S(2)}, u32[]{:S(2)}) collective-permute-start(bf16[64,512]{1,0:T(8,128)(2,1)S(1)} %get-tuple-element.50), channel_id=1, source_target_pairs={{128,0},{136,8},{144,16},{152,24},{160,32},{168,40},{176,48},{184,... | collective-permute-start | bytes 196616 | tf_op jit(solution)/shard_map/ppermute | solution.py:28
  64.0 19.2 %collective-permute-start.18 = (bf16[64,512]{1,0:T(8,128)(2,1)S(1)}, bf16[64,512]{1,0:T(8,128)(2,1)S(1)}, u32[]{:S(2)}, u32[]{:S(2)}) collective-permute-start(bf16[64,512]{1,0:T(8,128)(2,1)S(1)} %get-tuple-element.51), channel_id=1, source_target_pairs={{256,0},{264,8},{272,16},{280,24},{288,32},{296,40},{304,48},{312,... | collective-permute-start | bytes 196616 | tf_op jit(solution)/shard_map/ppermute | solution.py:28
  66.3 18.8 %collective-permute-start.19 = (bf16[64,512]{1,0:T(8,128)(2,1)S(1)}, bf16[64,512]{1,0:T(8,128)(2,1)S(1)}, u32[]{:S(2)}, u32[]{:S(2)}) collective-permute-start(bf16[64,512]{1,0:T(8,128)(2,1)S(1)} %get-tuple-element.52), channel_id=1, source_target_pairs={{384,0},{392,8},{400,16},{408,24},{416,32},{424,40},{432,48},{440,... | collective-permute-start | bytes 196616 | tf_op jit(solution)/shard_map/ppermute | solution.py:28
  71.2 33.8 %collective-permute-start.23 = (bf16[2,128,512]{2,1,0:T(8,128)(2,1)S(1)}, bf16[2,128,512]{2,1,0:T(8,128)(2,1)S(1)}, u32[]{:S(2)}, u32[]{:S(2)}) collective-permute-start(bf16[2,128,512]{2,1,0:T(8,128)(2,1)S(1)} %get-tuple-element.57), channel_id=1, source_target_pairs={{16,0},{24,8},{32,16},{40,24},{48,32},{56,40},{64,48},{72,56},{80,... | collective-permute-start | bytes 786440 | tf_op jit(solution)/shard_map/ppermute | solution.py:28
  85.1 12.7 %collective-permute-start.22 = (bf16[2,64,512]{2,1,0:T(8,128)(2,1)S(1)}, bf16[2,64,512]{2,1,0:T(8,128)(2,1)S(1)}, u32[]{:S(2)}, u32[]{:S(2)}) collective-permute-start(bf16[2,64,512]{2,1,0:T(8,128)(2,1)S(1)} %get-tuple-element.54), channel_id=1, source_target_pairs={{48,0},{56,8},{112,64},{120,72},{176,128},{184,136},{240,192},{248... | collective-permute-start | bytes 393224 | tf_op jit(solution)/shard_map/ppermute | solution.py:28
  86.4 18.5 %collective-permute-start.24 = (bf16[2,128,512]{2,1,0:T(8,128)(2,1)S(1)}, bf16[2,128,512]{2,1,0:T(8,128)(2,1)S(1)}, u32[]{:S(2)}, u32[]{:S(2)}) collective-permute-start(bf16[2,128,512]{2,1,0:T(8,128)(2,1)S(1)} %get-tuple-element.58), channel_id=1, source_target_pairs={{32,0},{40,8},{48,16},{56,24},{64,32},{72,40},{80,48},{88,56},{96,... | collective-permute-start | bytes 786440 | tf_op jit(solution)/shard_map/ppermute | solution.py:28
  87.7 18.4 %collective-permute-start.25 = (bf16[2,128,512]{2,1,0:T(8,128)(2,1)S(1)}, bf16[2,128,512]{2,1,0:T(8,128)(2,1)S(1)}, u32[]{:S(2)}, u32[]{:S(2)}) collective-permute-start(bf16[2,128,512]{2,1,0:T(8,128)(2,1)S(1)} %get-tuple-element.59), channel_id=1, source_target_pairs={{48,0},{56,8},{64,16},{72,24},{80,32},{88,40},{96,48},{104,56},{11... | collective-permute-start | bytes 786440 | tf_op jit(solution)/shard_map/ppermute | solution.py:28
  89.0 15.9 %collective-permute-start.21 = (bf16[2,64,512]{2,1,0:T(8,128)(2,1)S(1)}, bf16[2,64,512]{2,1,0:T(8,128)(2,1)S(1)}, u32[]{:S(2)}, u32[]{:S(2)}) collective-permute-start(bf16[2,64,512]{2,1,0:T(8,128)(2,1)S(1)} %get-tuple-element.54), channel_id=1, source_target_pairs={{32,0},{40,8},{96,64},{104,72},{160,128},{168,136},{224,192},{232,... | collective-permute-start | bytes 393224 | tf_op jit(solution)/shard_map/ppermute | solution.py:28
  97.8 7.1 %collective-permute-start.20 = (bf16[2,64,512]{2,1,0:T(8,128)(2,1)S(1)}, bf16[2,64,512]{2,1,0:T(8,128)(2,1)S(1)}, u32[]{:S(2)}, u32[]{:S(2)}) collective-permute-start(bf16[2,64,512]{2,1,0:T(8,128)(2,1)S(1)} %get-tuple-element.54), channel_id=1, source_target_pairs={{16,0},{24,8},{80,64},{88,72},{144,128},{152,136},{208,192},{216,2... | collective-permute-start | bytes 393224 | tf_op jit(solution)/shard_map/ppermute | solution.py:28
  106.4 10.1 %collective-permute-start.26 = (bf16[2,64,1536]{2,1,0:T(8,128)(2,1)S(1)}, bf16[2,64,1536]{2,1,0:T(8,128)(2,1)S(1)}, u32[]{:S(2)}, u32[]{:S(2)}) collective-permute-start(bf16[2,64,1536]{2,1,0:T(8,128)(2,1)S(1)} %get-tuple-element.62), channel_id=1, source_target_pairs={{0,8},{8,0},{16,24},{24,16},{32,40},{40,32},{48,56},{56,48},{64,72... | collective-permute-start | bytes 1179656 | tf_op jit(solution)/shard_map/ppermute | solution.py:28
  108.3 6.3 %collective-permute-start.28 = (bf16[2,64,512]{2,1,0:T(8,128)(2,1)S(1)}, bf16[2,64,512]{2,1,0:T(8,128)(2,1)S(1)}, u32[]{:S(2)}, u32[]{:S(2)}) collective-permute-start(bf16[2,64,512]{2,1,0:T(8,128)(2,1)S(1)} %get-tuple-element.63), channel_id=1, source_target_pairs={{72,0},{200,128},{328,256},{456,384},{73,1},{201,129},{329,257},{4... | collective-permute-start | bytes 393224 | tf_op jit(solution)/shard_map/ppermute | solution.py:28
  109.6 6.9 %collective-permute-start.27 = (bf16[2,64,512]{2,1,0:T(8,128)(2,1)S(1)}, bf16[2,64,512]{2,1,0:T(8,128)(2,1)S(1)}, u32[]{:S(2)}, u32[]{:S(2)}) collective-permute-start(bf16[2,64,512]{2,1,0:T(8,128)(2,1)S(1)} %get-tuple-element.63), channel_id=1, source_target_pairs={{64,0},{192,128},{320,256},{448,384},{65,1},{193,129},{321,257},{4... | collective-permute-start | bytes 393224 | tf_op jit(solution)/shard_map/ppermute | solution.py:28
  (13 other events, 85.9 us)

commit v11 on v10

--- a/solution.py
+++ b/solution.py
@@ -285,11 +285,12 @@
         across = ctx(start, lambda i: i + 2 * d, lambda i: (i // 2) % 4 == 0)
         chosen = jnp.where(place == d, across, chosen)
     pairs = [pair] + [ctx(pair, lambda i: i + 2 * d) for d in range(1, 4)]
-    strided = [chosen] + [ctx(chosen, lambda i: i + STRIDE * s) for s in range(1, 4)]
 
     four = shape((4, BLK, HALF_FEAT), bf16)
     keep, give = simple(split_rows, [four, four], [spot, inputs, first_grads, head_grads])
     recv = sibling(give)
+    chosen, recv = lax.optimization_barrier((chosen, recv))
+    strided = [chosen] + [ctx(chosen, lambda i: i + STRIDE * s) for s in range(1, 4)]
     gain = jnp.where(core == 0, query_gain[:, :HALF_FEAT], query_gain[:, HALF_FEAT:])
     heads = jnp.where(core == 0, window[0, :2], window[0, 2:])
     steps = jnp.where(core == 0, stride[0, :2], stride[0, 2:])

time: 118 us -> 111 us (0.941)
  the two profiles are of different devices: /device:TPU:192 before, /device:TPU:240 now
where the time goes in v11:
time: 111 us; the launch traced here: 110 us
  starting transfers between devices  64.1 us (58%)
  waiting for transfers between devices  31.4 us (28%)
  Pallas kernels  9.42 us (8%)
  local copies, waits for them, and re-layouts  3.85 us (3%)
  between operations  1.15 us (1%)
    ppermute x29, starting transfers between devices, route(): lax.ppermute(array, axis, [(a, b) for a, b in pairs if b is not None and...  64.1 us
    ppermute x29, waiting for transfers between devices, route(): lax.ppermute(array, axis, [(a, b) for a, b in pairs if b is not None and...  31.4 us
    pallas_call x2, Pallas kernels, attention(): pl.pallas_call(functools.partial(attention_kernel, grads is not None), ou...  8.04 us
    unnamed x16, local copies, waits for them, and re-layouts  3.85 us
  transfers between devices with their start and end apart: 29, of which 10 were waited for; matrix products, arithmetic and copies ran while one was open for 0% of the time, Pallas kernels for 4%

profile of v11, /device:TPU:240, one launch (start us, length us, event | category | flops | bytes accessed | tf_op | source)
XLA Modules:
  0.0 110.1 jit_solution(6725076895694615306)
XLA Ops:
  2.5 2.6 %collective-permute-start.1 = (bf16[2,64,512]{2,1,0:T(8,128)(2,1)S(1)}, bf16[2,64,512]{2,1,0:T(8,128)(2,1)S(1)}, u32[]{:S(2)}, u32[]{:S(2)}) collective-permute-start(bf16[2,64,512]{2,1,0:T(8,128)(2,1)S(1)} %get-tuple-element.37.keep), channel_id=1, source_target_pairs={{0,64},{128,192},{256,320},{384,448},{1,65},{129,193},{257,321},{3... | collective-permute-start | bytes 393224 | tf_op jit(solution)/shard_map/ppermute | solution.py:28
  5.1 1.3 %collective-permute-start.2 = (bf16[2,64,512]{2,1,0:T(8,128)(2,1)S(1)}, bf16[2,64,512]{2,1,0:T(8,128)(2,1)S(1)}, u32[]{:S(2)}, u32[]{:S(2)}) collective-permute-start(bf16[2,64,512]{2,1,0:T(8,128)(2,1)S(1)} %get-tuple-element.38), channel_id=1, source_target_pairs={{0,72},{128,200},{256,328},{384,456},{1,73},{129,201},{257,329},{3... | collective-permute-start | bytes 393224 | tf_op jit(solution)/shard_map/ppermute | solution.py:28
  6.4 1.9 %collective-permute-start = (bf16[2,64,512]{2,1,0:T(8,128)(2,1)S(1)}, bf16[2,64,512]{2,1,0:T(8,128)(2,1)S(1)}, u32[]{:S(2)}, u32[]{:S(2)}) collective-permute-start(bf16[2,64,512]{2,1,0:T(8,128)(2,1)S(1)} %get-tuple-element.38), channel_id=1, source_target_pairs={{0,8},{8,0},{16,24},{24,16},{32,40},{40,32},{48,56},{56,48},{64,72... | collective-permute-start | bytes 393224 | tf_op jit(solution)/shard_map/ppermute | solution.py:28
  10.4 2.4 %collective-permute-start.6 = (bf16[4,64,1024]{2,1,0:T(8,128)(2,1)S(1)}, bf16[4,64,1024]{2,1,0:T(8,128)(2,1)S(1)}, u32[]{:S(2)}, u32[]{:S(2)}) collective-permute-start(bf16[4,64,1024]{2,1,0:T(8,128)(2,1)S(1)} %get-tuple-element.40), channel_id=1, source_target_pairs={{0,8},{8,0},{16,24},{24,16},{32,40},{40,32},{48,56},{56,48},{64,72... | collective-permute-start | bytes 1572872 | tf_op jit(solution)/shard_map/ppermute | solution.py:28
  14.3 1.8 %collective-permute-start.4 = (bf16[2,64,512]{2,1,0:T(8,128)(2,1)S(1)}, bf16[2,64,512]{2,1,0:T(8,128)(2,1)S(1)}, u32[]{:S(2)}, u32[]{:S(2)}) collective-permute-start(bf16[2,64,512]{2,1,0:T(8,128)(2,1)S(1)} %get-tuple-element.39), channel_id=1, source_target_pairs={{0,32},{8,40},{64,96},{72,104},{128,160},{136,168},{192,224},{200,... | collective-permute-start | bytes 393224 | tf_op jit(solution)/shard_map/ppermute | solution.py:28
  17.3 1.9 %collective-permute-start.9 = (bf16[2,128,512]{2,1,0:T(8,128)(2,1)S(1)}, bf16[2,128,512]{2,1,0:T(8,128)(2,1)S(1)}, u32[]{:S(2)}, u32[]{:S(2)}) collective-permute-start(bf16[2,128,512]{2,1,0:T(8,128)(2,1)S(1)} %get-tuple-element.42.refs_6_.refs_8_), channel_id=1, source_target_pairs={{0,48},{8,56},{16,64},{24,72},{32,80},{40,88},{48,96},{56,104},{64... | collective-permute-start | bytes 786440 | tf_op jit(solution)/shard_map/ppermute | solution.py:28
  19.3 1.9 %collective-permute-start.8 = (bf16[2,128,512]{2,1,0:T(8,128)(2,1)S(1)}, bf16[2,128,512]{2,1,0:T(8,128)(2,1)S(1)}, u32[]{:S(2)}, u32[]{:S(2)}) collective-permute-start(bf16[2,128,512]{2,1,0:T(8,128)(2,1)S(1)} %get-tuple-element.42.refs_6_.refs_8_), channel_id=1, source_target_pairs={{0,32},{8,40},{16,48},{24,56},{32,64},{40,72},{48,80},{56,88},{64,... | collective-permute-start | bytes 786440 | tf_op jit(solution)/shard_map/ppermute | solution.py:28
  21.3 4.0 %collective-permute-start.7 = (bf16[2,128,512]{2,1,0:T(8,128)(2,1)S(1)}, bf16[2,128,512]{2,1,0:T(8,128)(2,1)S(1)}, u32[]{:S(2)}, u32[]{:S(2)}) collective-permute-start(bf16[2,128,512]{2,1,0:T(8,128)(2,1)S(1)} %get-tuple-element.42.refs_6_.refs_8_), channel_id=1, source_target_pairs={{0,16},{8,24},{16,32},{24,40},{32,48},{40,56},{48,64},{56,72},{64,... | collective-permute-start | bytes 786440 | tf_op jit(solution)/shard_map/ppermute | solution.py:28
  29.6 2.4 %collective-permute-done.8.refs_8_.refs_10_ = bf16[2,128,512]{2,1,0:T(8,128)(2,1)S(1)} collective-permute-done((bf16[2,128,512]{2,1,0:T(8,128)(2,1)S(1)}, bf16[2,128,512]{2,1,0:T(8,128)(2,1)S(1)}, u32[]{:S(2)}, u32[]{:S(2)}) %collective-permute-start.8) | collective-permute-done | bytes 262176 | tf_op jit(solution)/shard_map/ppermute | solution.py:28
  32.0 9.4 %collective-permute-done.7.refs_7_.refs_9_ = bf16[2,128,512]{2,1,0:T(8,128)(2,1)S(1)} collective-permute-done((bf16[2,128,512]{2,1,0:T(8,128)(2,1)S(1)}, bf16[2,128,512]{2,1,0:T(8,128)(2,1)S(1)}, u32[]{:S(2)}, u32[]{:S(2)}) %collective-permute-start.7) | collective-permute-done | bytes 262176 | tf_op jit(solution)/shard_map/ppermute | solution.py:28
  41.5 2.4 %collective-permute-done.11.refs_12_.refs_14_ = bf16[2,64,512]{2,1,0:T(8,128)(2,1)S(1)} collective-permute-done((bf16[2,64,512]{2,1,0:T(8,128)(2,1)S(1)}, bf16[2,64,512]{2,1,0:T(8,128)(2,1)S(1)}, u32[]{:S(2)}, u32[]{:S(2)}) %collective-permute-start.11) | collective-permute-done | bytes 131104 | tf_op jit(solution)/shard_map/ppermute | solution.py:28
  43.8 4.0 %attention.2 = (bf16[2,64,1024]{2,1,0:T(8,128)(2,1)S(1)}, bf16[64,1024]{1,0:T(8,128)(2,1)S(1)}, bf16[128,512]{1,0:T(8,128)(2,1)S(1)}, bf16[128,512]{1,0:T(8,128)...) custom-call(s32[6]{0:T(128)S(1)} %pad_add_fusion.refs_0_, ...), custom_call_target="tpu_custom_call" | custom-call | flops 1006632960 | bytes 4194304 | tf_op jit(solution)/shard_map/attention/pallas_call | solution.py:162
  47.8 1.9 %collective-permute-start.16 = (bf16[2,64,1024]{2,1,0:T(8,128)(2,1)S(1)}, bf16[2,64,1024]{2,1,0:T(8,128)(2,1)S(1)}, u32[]{:S(2)}, u32[]{:S(2)}) collective-permute-start(bf16[2,64,1024]{2,1,0:T(8,128)(2,1)S(1)} %get-tuple-element.48.mine0), channel_id=1, source_target_pairs={{1,0},{2,1},{3,2},{4,3},{5,4},{6,5},{7,6},{9,8},{10,9},{11,10},{12... | collective-permute-start | bytes 786440 | tf_op jit(solution)/shard_map/ppermute | solution.py:28
  49.8 4.9 %collective-permute-start.13 = (bf16[64,512]{1,0:T(8,128)(2,1)S(1)}, bf16[64,512]{1,0:T(8,128)(2,1)S(1)}, u32[]{:S(2)}, u32[]{:S(2)}) collective-permute-start(bf16[64,512]{1,0:T(8,128)(2,1)S(1)} %get-tuple-element.45), channel_id=1, source_target_pairs={{128,0},{136,8},{144,16},{152,24},{160,32},{168,40},{176,48},{184,... | collective-permute-start | bytes 196616 | tf_op jit(solution)/shard_map/ppermute | solution.py:28
  54.7 3.1 %collective-permute-start.14 = (bf16[64,512]{1,0:T(8,128)(2,1)S(1)}, bf16[64,512]{1,0:T(8,128)(2,1)S(1)}, u32[]{:S(2)}, u32[]{:S(2)}) collective-permute-start(bf16[64,512]{1,0:T(8,128)(2,1)S(1)} %get-tuple-element.46), channel_id=1, source_target_pairs={{256,0},{264,8},{272,16},{280,24},{288,32},{296,40},{304,48},{312,... | collective-permute-start | bytes 196616 | tf_op jit(solution)/shard_map/ppermute | solution.py:28
  59.1 4.1 %attention.3 = (bf16[2,64,1024]{2,1,0:T(8,128)(2,1)S(1)}, bf16[2,64,1024]{2,1,0:T(8,128)(2,1)S(1)}, bf16[2,128,512]{2,1,0:T(8,128)(2,1)S(1)}, bf16[2,128,512]{2,...) custom-call(s32[6]{0:T(128)S(1)} %pad_add_fusion.refs_0_, ...), custom_call_target="tpu_custom_call" | custom-call | flops 1006632960 | bytes 4194304 | tf_op jit(solution)/shard_map/attention/pallas_call | solution.py:162
  63.2 3.8 %collective-permute-start.17 = (bf16[64,512]{1,0:T(8,128)(2,1)S(1)}, bf16[64,512]{1,0:T(8,128)(2,1)S(1)}, u32[]{:S(2)}, u32[]{:S(2)}) collective-permute-start(bf16[64,512]{1,0:T(8,128)(2,1)S(1)} %get-tuple-element.54), channel_id=1, source_target_pairs={{128,0},{136,8},{144,16},{152,24},{160,32},{168,40},{176,48},{184,... | collective-permute-start | bytes 196616 | tf_op jit(solution)/shard_map/ppermute | solution.py:28
  67.0 2.7 %collective-permute-start.18 = (bf16[64,512]{1,0:T(8,128)(2,1)S(1)}, bf16[64,512]{1,0:T(8,128)(2,1)S(1)}, u32[]{:S(2)}, u32[]{:S(2)}) collective-permute-start(bf16[64,512]{1,0:T(8,128)(2,1)S(1)} %get-tuple-element.55), channel_id=1, source_target_pairs={{256,0},{264,8},{272,16},{280,24},{288,32},{296,40},{304,48},{312,... | collective-permute-start | bytes 196616 | tf_op jit(solution)/shard_map/ppermute | solution.py:28
  71.1 2.9 %collective-permute-start.23 = (bf16[2,128,512]{2,1,0:T(8,128)(2,1)S(1)}, bf16[2,128,512]{2,1,0:T(8,128)(2,1)S(1)}, u32[]{:S(2)}, u32[]{:S(2)}) collective-permute-start(bf16[2,128,512]{2,1,0:T(8,128)(2,1)S(1)} %get-tuple-element.61), channel_id=1, source_target_pairs={{16,0},{24,8},{32,16},{40,24},{48,32},{56,40},{64,48},{72,56},{80,... | collective-permute-start | bytes 786440 | tf_op jit(solution)/shard_map/ppermute | solution.py:28
  75.4 1.9 %collective-permute-start.24 = (bf16[2,128,512]{2,1,0:T(8,128)(2,1)S(1)}, bf16[2,128,512]{2,1,0:T(8,128)(2,1)S(1)}, u32[]{:S(2)}, u32[]{:S(2)}) collective-permute-start(bf16[2,128,512]{2,1,0:T(8,128)(2,1)S(1)} %get-tuple-element.62), channel_id=1, source_target_pairs={{32,0},{40,8},{48,16},{56,24},{64,32},{72,40},{80,48},{88,56},{96,... | collective-permute-start | bytes 786440 | tf_op jit(solution)/shard_map/ppermute | solution.py:28
  77.4 7.5 %collective-permute-start.25 = (bf16[2,128,512]{2,1,0:T(8,128)(2,1)S(1)}, bf16[2,128,512]{2,1,0:T(8,128)(2,1)S(1)}, u32[]{:S(2)}, u32[]{:S(2)}) collective-permute-start(bf16[2,128,512]{2,1,0:T(8,128)(2,1)S(1)} %get-tuple-element.63), channel_id=1, source_target_pairs={{48,0},{56,8},{64,16},{72,24},{80,32},{88,40},{96,48},{104,56},{11... | collective-permute-start | bytes 786440 | tf_op jit(solution)/shard_map/ppermute | solution.py:28
  88.7 5.4 %collective-permute-done.21.refs_2_ = bf16[2,64,512]{2,1,0:T(8,128)(2,1)S(1)} collective-permute-done((bf16[2,64,512]{2,1,0:T(8,128)(2,1)S(1)}, bf16[2,64,512]{2,1,0:T(8,128)(2,1)S(1)}, u32[]{:S(2)}, u32[]{:S(2)}) %collective-permute-start.21) | collective-permute-done | bytes 131104 | tf_op jit(solution)/shard_map/ppermute | solution.py:28
  95.4 1.9 %collective-permute-start.26 = (bf16[2,64,1536]{2,1,0:T(8,128)(2,1)S(1)}, bf16[2,64,1536]{2,1,0:T(8,128)(2,1)S(1)}, u32[]{:S(2)}, u32[]{:S(2)}) collective-permute-start(bf16[2,64,1536]{2,1,0:T(8,128)(2,1)S(1)} %get-tuple-element.66), channel_id=1, source_target_pairs={{0,8},{8,0},{16,24},{24,16},{32,40},{40,32},{48,56},{56,48},{64,72... | collective-permute-start | bytes 1179656 | tf_op jit(solution)/shard_map/ppermute | solution.py:28
  100.0 8.4 %collective-permute-done.28.high = bf16[2,64,512]{2,1,0:T(8,128)(2,1)S(1)} collective-permute-done((bf16[2,64,512]{2,1,0:T(8,128)(2,1)S(1)}, bf16[2,64,512]{2,1,0:T(8,128)(2,1)S(1)}, u32[]{:S(2)}, u32[]{:S(2)}) %collective-permute-start.28) | collective-permute-done | bytes 131104 | tf_op jit(solution)/shard_map/ppermute | solution.py:28
  (62 shorter events, 24.3 us)
Async XLA Ops:
  2.5 10.3 %collective-permute-start.1 = (bf16[2,64,512]{2,1,0:T(8,128)(2,1)S(1)}, bf16[2,64,512]{2,1,0:T(8,128)(2,1)S(1)}, u32[]{:S(2)}, u32[]{:S(2)}) collective-permute-start(bf16[2,64,512]{2,1,0:T(8,128)(2,1)S(1)} %get-tuple-element.37.keep), channel_id=1, source_target_pairs={{0,64},{128,192},{256,320},{384,448},{1,65},{129,193},{257,321},{3... | collective-permute-start | bytes 393224 | tf_op jit(solution)/shard_map/ppermute | solution.py:28
  5.1 7.8 %collective-permute-start.2 = (bf16[2,64,512]{2,1,0:T(8,128)(2,1)S(1)}, bf16[2,64,512]{2,1,0:T(8,128)(2,1)S(1)}, u32[]{:S(2)}, u32[]{:S(2)}) collective-permute-start(bf16[2,64,512]{2,1,0:T(8,128)(2,1)S(1)} %get-tuple-element.38), channel_id=1, source_target_pairs={{0,72},{128,200},{256,328},{384,456},{1,73},{129,201},{257,329},{3... | collective-permute-start | bytes 393224 | tf_op jit(solution)/shard_map/ppermute | solution.py:28
  10.4 15.0 %collective-permute-start.6 = (bf16[4,64,1024]{2,1,0:T(8,128)(2,1)S(1)}, bf16[4,64,1024]{2,1,0:T(8,128)(2,1)S(1)}, u32[]{:S(2)}, u32[]{:S(2)}) collective-permute-start(bf16[4,64,1024]{2,1,0:T(8,128)(2,1)S(1)} %get-tuple-element.40), channel_id=1, source_target_pairs={{0,8},{8,0},{16,24},{24,16},{32,40},{40,32},{48,56},{56,48},{64,72... | collective-permute-start | bytes 1572872 | tf_op jit(solution)/shard_map/ppermute | solution.py:28
  16.0 9.3 %collective-permute-start.3 = (bf16[2,64,512]{2,1,0:T(8,128)(2,1)S(1)}, bf16[2,64,512]{2,1,0:T(8,128)(2,1)S(1)}, u32[]{:S(2)}, u32[]{:S(2)}) collective-permute-start(bf16[2,64,512]{2,1,0:T(8,128)(2,1)S(1)} %get-tuple-element.39), channel_id=1, source_target_pairs={{0,48},{8,56},{64,112},{72,120},{128,176},{136,184},{192,240},{200... | collective-permute-start | bytes 393224 | tf_op jit(solution)/shard_map/ppermute | solution.py:28
  17.3 10.8 %collective-permute-start.9 = (bf16[2,128,512]{2,1,0:T(8,128)(2,1)S(1)}, bf16[2,128,512]{2,1,0:T(8,128)(2,1)S(1)}, u32[]{:S(2)}, u32[]{:S(2)}) collective-permute-start(bf16[2,128,512]{2,1,0:T(8,128)(2,1)S(1)} %get-tuple-element.42.refs_6_.refs_8_), channel_id=1, source_target_pairs={{0,48},{8,56},{16,64},{24,72},{32,80},{40,88},{48,96},{56,104},{64... | collective-permute-start | bytes 786440 | tf_op jit(solution)/shard_map/ppermute | solution.py:28
  19.3 12.7 %collective-permute-start.8 = (bf16[2,128,512]{2,1,0:T(8,128)(2,1)S(1)}, bf16[2,128,512]{2,1,0:T(8,128)(2,1)S(1)}, u32[]{:S(2)}, u32[]{:S(2)}) collective-permute-start(bf16[2,128,512]{2,1,0:T(8,128)(2,1)S(1)} %get-tuple-element.42.refs_6_.refs_8_), channel_id=1, source_target_pairs={{0,32},{8,40},{16,48},{24,56},{32,64},{40,72},{48,80},{56,88},{64,... | collective-permute-start | bytes 786440 | tf_op jit(solution)/shard_map/ppermute | solution.py:28
  21.3 20.2 %collective-permute-start.7 = (bf16[2,128,512]{2,1,0:T(8,128)(2,1)S(1)}, bf16[2,128,512]{2,1,0:T(8,128)(2,1)S(1)}, u32[]{:S(2)}, u32[]{:S(2)}) collective-permute-start(bf16[2,128,512]{2,1,0:T(8,128)(2,1)S(1)} %get-tuple-element.42.refs_6_.refs_8_), channel_id=1, source_target_pairs={{0,16},{8,24},{16,32},{24,40},{32,48},{40,56},{48,64},{56,72},{64,... | collective-permute-start | bytes 786440 | tf_op jit(solution)/shard_map/ppermute | solution.py:28
  25.4 16.0 %collective-permute-start.12 = (bf16[2,64,512]{2,1,0:T(8,128)(2,1)S(1)}, bf16[2,64,512]{2,1,0:T(8,128)(2,1)S(1)}, u32[]{:S(2)}, u32[]{:S(2)}) collective-permute-start(bf16[2,64,512]{2,1,0:T(8,128)(2,1)S(1)} %select_select_fusion.refs_10_.refs_12_), channel_id=1, source_target_pairs={{0,384},{8,392},{16,400},{24,408},{32,416},{40,424},{48,432},{56,4... | collective-permute-start | bytes 393224 | tf_op jit(solution)/shard_map/ppermute | solution.py:28
  26.7 17.1 %collective-permute-start.11 = (bf16[2,64,512]{2,1,0:T(8,128)(2,1)S(1)}, bf16[2,64,512]{2,1,0:T(8,128)(2,1)S(1)}, u32[]{:S(2)}, u32[]{:S(2)}) collective-permute-start(bf16[2,64,512]{2,1,0:T(8,128)(2,1)S(1)} %select_select_fusion.refs_10_.refs_12_), channel_id=1, source_target_pairs={{0,256},{8,264},{16,272},{24,280},{32,288},{40,296},{48,304},{56,3... | collective-permute-start | bytes 393224 | tf_op jit(solution)/shard_map/ppermute | solution.py:28
  28.2 15.7 %collective-permute-start.10 = (bf16[2,64,512]{2,1,0:T(8,128)(2,1)S(1)}, bf16[2,64,512]{2,1,0:T(8,128)(2,1)S(1)}, u32[]{:S(2)}, u32[]{:S(2)}) collective-permute-start(bf16[2,64,512]{2,1,0:T(8,128)(2,1)S(1)} %select_select_fusion.refs_10_.refs_12_), channel_id=1, source_target_pairs={{0,128},{8,136},{16,144},{24,152},{32,160},{40,168},{48,176},{56,1... | collective-permute-start | bytes 393224 | tf_op jit(solution)/shard_map/ppermute | solution.py:28
  47.8 11.3 %collective-permute-start.16 = (bf16[2,64,1024]{2,1,0:T(8,128)(2,1)S(1)}, bf16[2,64,1024]{2,1,0:T(8,128)(2,1)S(1)}, u32[]{:S(2)}, u32[]{:S(2)}) collective-permute-start(bf16[2,64,1024]{2,1,0:T(8,128)(2,1)S(1)} %get-tuple-element.48.mine0), channel_id=1, source_target_pairs={{1,0},{2,1},{3,2},{4,3},{5,4},{6,5},{7,6},{9,8},{10,9},{11,10},{12... | collective-permute-start | bytes 786440 | tf_op jit(solution)/shard_map/ppermute | solution.py:28
  49.8 20.0 %collective-permute-start.13 = (bf16[64,512]{1,0:T(8,128)(2,1)S(1)}, bf16[64,512]{1,0:T(8,128)(2,1)S(1)}, u32[]{:S(2)}, u32[]{:S(2)}) collective-permute-start(bf16[64,512]{1,0:T(8,128)(2,1)S(1)} %get-tuple-element.45), channel_id=1, source_target_pairs={{128,0},{136,8},{144,16},{152,24},{160,32},{168,40},{176,48},{184,... | collective-permute-start | bytes 196616 | tf_op jit(solution)/shard_map/ppermute | solution.py:28
  54.7 16.4 %collective-permute-start.14 = (bf16[64,512]{1,0:T(8,128)(2,1)S(1)}, bf16[64,512]{1,0:T(8,128)(2,1)S(1)}, u32[]{:S(2)}, u32[]{:S(2)}) collective-permute-start(bf16[64,512]{1,0:T(8,128)(2,1)S(1)} %get-tuple-element.46), channel_id=1, source_target_pairs={{256,0},{264,8},{272,16},{280,24},{288,32},{296,40},{304,48},{312,... | collective-permute-start | bytes 196616 | tf_op jit(solution)/shard_map/ppermute | solution.py:28
  57.8 16.2 %collective-permute-start.15 = (bf16[64,512]{1,0:T(8,128)(2,1)S(1)}, bf16[64,512]{1,0:T(8,128)(2,1)S(1)}, u32[]{:S(2)}, u32[]{:S(2)}) collective-permute-start(bf16[64,512]{1,0:T(8,128)(2,1)S(1)} %get-tuple-element.47), channel_id=1, source_target_pairs={{384,0},{392,8},{400,16},{408,24},{416,32},{424,40},{432,48},{440,... | collective-permute-start | bytes 196616 | tf_op jit(solution)/shard_map/ppermute | solution.py:28
  63.2 10.8 %collective-permute-start.17 = (bf16[64,512]{1,0:T(8,128)(2,1)S(1)}, bf16[64,512]{1,0:T(8,128)(2,1)S(1)}, u32[]{:S(2)}, u32[]{:S(2)}) collective-permute-start(bf16[64,512]{1,0:T(8,128)(2,1)S(1)} %get-tuple-element.54), channel_id=1, source_target_pairs={{128,0},{136,8},{144,16},{152,24},{160,32},{168,40},{176,48},{184,... | collective-permute-start | bytes 196616 | tf_op jit(solution)/shard_map/ppermute | solution.py:28
  67.0 7.0 %collective-permute-start.18 = (bf16[64,512]{1,0:T(8,128)(2,1)S(1)}, bf16[64,512]{1,0:T(8,128)(2,1)S(1)}, u32[]{:S(2)}, u32[]{:S(2)}) collective-permute-start(bf16[64,512]{1,0:T(8,128)(2,1)S(1)} %get-tuple-element.55), channel_id=1, source_target_pairs={{256,0},{264,8},{272,16},{280,24},{288,32},{296,40},{304,48},{312,... | collective-permute-start | bytes 196616 | tf_op jit(solution)/shard_map/ppermute | solution.py:28
  71.1 23.2 %collective-permute-start.23 = (bf16[2,128,512]{2,1,0:T(8,128)(2,1)S(1)}, bf16[2,128,512]{2,1,0:T(8,128)(2,1)S(1)}, u32[]{:S(2)}, u32[]{:S(2)}) collective-permute-start(bf16[2,128,512]{2,1,0:T(8,128)(2,1)S(1)} %get-tuple-element.61), channel_id=1, source_target_pairs={{16,0},{24,8},{32,16},{40,24},{48,32},{56,40},{64,48},{72,56},{80,... | collective-permute-start | bytes 786440 | tf_op jit(solution)/shard_map/ppermute | solution.py:28
  74.1 13.3 %collective-permute-start.22 = (bf16[2,64,512]{2,1,0:T(8,128)(2,1)S(1)}, bf16[2,64,512]{2,1,0:T(8,128)(2,1)S(1)}, u32[]{:S(2)}, u32[]{:S(2)}) collective-permute-start(bf16[2,64,512]{2,1,0:T(8,128)(2,1)S(1)} %get-tuple-element.58), channel_id=1, source_target_pairs={{48,0},{56,8},{112,64},{120,72},{176,128},{184,136},{240,192},{248... | collective-permute-start | bytes 393224 | tf_op jit(solution)/shard_map/ppermute | solution.py:28
  75.4 18.9 %collective-permute-start.24 = (bf16[2,128,512]{2,1,0:T(8,128)(2,1)S(1)}, bf16[2,128,512]{2,1,0:T(8,128)(2,1)S(1)}, u32[]{:S(2)}, u32[]{:S(2)}) collective-permute-start(bf16[2,128,512]{2,1,0:T(8,128)(2,1)S(1)} %get-tuple-element.62), channel_id=1, source_target_pairs={{32,0},{40,8},{48,16},{56,24},{64,32},{72,40},{80,48},{88,56},{96,... | collective-permute-start | bytes 786440 | tf_op jit(solution)/shard_map/ppermute | solution.py:28
  77.4 17.9 %collective-permute-start.25 = (bf16[2,128,512]{2,1,0:T(8,128)(2,1)S(1)}, bf16[2,128,512]{2,1,0:T(8,128)(2,1)S(1)}, u32[]{:S(2)}, u32[]{:S(2)}) collective-permute-start(bf16[2,128,512]{2,1,0:T(8,128)(2,1)S(1)} %get-tuple-element.63), channel_id=1, source_target_pairs={{48,0},{56,8},{64,16},{72,24},{80,32},{88,40},{96,48},{104,56},{11... | collective-permute-start | bytes 786440 | tf_op jit(solution)/shard_map/ppermute | solution.py:28
  84.9 9.3 %collective-permute-start.21 = (bf16[2,64,512]{2,1,0:T(8,128)(2,1)S(1)}, bf16[2,64,512]{2,1,0:T(8,128)(2,1)S(1)}, u32[]{:S(2)}, u32[]{:S(2)}) collective-permute-start(bf16[2,64,512]{2,1,0:T(8,128)(2,1)S(1)} %get-tuple-element.58), channel_id=1, source_target_pairs={{32,0},{40,8},{96,64},{104,72},{160,128},{168,136},{224,192},{232,... | collective-permute-start | bytes 393224 | tf_op jit(solution)/shard_map/ppermute | solution.py:28
  95.4 13.8 %collective-permute-start.26 = (bf16[2,64,1536]{2,1,0:T(8,128)(2,1)S(1)}, bf16[2,64,1536]{2,1,0:T(8,128)(2,1)S(1)}, u32[]{:S(2)}, u32[]{:S(2)}) collective-permute-start(bf16[2,64,1536]{2,1,0:T(8,128)(2,1)S(1)} %get-tuple-element.66), channel_id=1, source_target_pairs={{0,8},{8,0},{16,24},{24,16},{32,40},{40,32},{48,56},{56,48},{64,72... | collective-permute-start | bytes 1179656 | tf_op jit(solution)/shard_map/ppermute | solution.py:28
  97.4 11.0 %collective-permute-start.28 = (bf16[2,64,512]{2,1,0:T(8,128)(2,1)S(1)}, bf16[2,64,512]{2,1,0:T(8,128)(2,1)S(1)}, u32[]{:S(2)}, u32[]{:S(2)}) collective-permute-start(bf16[2,64,512]{2,1,0:T(8,128)(2,1)S(1)} %get-tuple-element.67), channel_id=1, source_target_pairs={{72,0},{200,128},{328,256},{456,384},{73,1},{201,129},{329,257},{4... | collective-permute-start | bytes 393224 | tf_op jit(solution)/shard_map/ppermute | solution.py:28
  98.7 10.5 %collective-permute-start.27 = (bf16[2,64,512]{2,1,0:T(8,128)(2,1)S(1)}, bf16[2,64,512]{2,1,0:T(8,128)(2,1)S(1)}, u32[]{:S(2)}, u32[]{:S(2)}) collective-permute-start(bf16[2,64,512]{2,1,0:T(8,128)(2,1)S(1)} %get-tuple-element.67), channel_id=1, source_target_pairs={{64,0},{192,128},{320,256},{448,384},{65,1},{193,129},{321,257},{4... | collective-permute-start | bytes 393224 | tf_op jit(solution)/shard_map/ppermute | solution.py:28
  (13 other events, 57.2 us)
